TPU v7x, 32 devices: a whole 2x2x4 slice. The times are simulated.
32 devices in a mesh: img: 2 (over x), gz: 8 (over z, y), gy: 2 (over core).
Axes of the slice: x: 2, y: 2, z: 4, core: 2. Of those that a mesh axis runs over, the one named last changes fastest.
Arguments:
- initial_block: float32 [32, 16, 32, 384], P('img', 'gz', 'gy'), parts along dimension 0, may hold values from -6 to 6, as said below
- concentration: float32 [32, 32, 384], P(('img', 'gz'), 'gy'), parts along dimension 0, may hold values from -1.2 to 1.2
- stiffness: float32 [16, 32, 384], P('gz', 'gy'), may hold values from 0.02 to 0.2
Outputs:
- ritz_values: float32 [16], P('img'), parts along dimension 0
- mode_density: float32 [32, 32, 384], P(('img', 'gz'), 'gy'), parts along dimension 0
- residual_density: float32 [32, 32, 384], P(('img', 'gz'), 'gy'), parts along dimension 0
There are 2 independent parts, one for each index of `img`. A program takes and returns all parts, laid end to end along the dimension named above; an argument that names none is the same for every part. Nothing has to cross between parts.
Inputs may be any that keep to these rules, and one draw needn't show every extreme that they name: `initial_block`: the 16 starting vectors are linearly independent.
All inputs are finite; a program needn't handle non-finite values.
Results may differ from a plain program's by a relative error of at most 0.0003.
Values sent between devices are 32-bit elements; how exact they have to be, the bound alone decides.
No kernel may reach another device: no remote copies, remote signals or barrier semaphores. Data moves between devices by JAX's collectives and lax.ppermute only.
A program may use at most 64 MiB of HBM per device.

v0:
```python
import jax
import jax.numpy as jnp
import numpy as np
from jax import lax
from jax.sharding import PartitionSpec as P

BLOCK = 16
MODES = 8
ITERS = 2
SWEEPS = 8


def with_halo(x, sides, width):
    for axis, dim in sides:
        size, length = (lax.axis_size(axis), x.shape[dim])
        up = [(i, (i + 1) % size) for i in range(size)]
        down = [(j, i) for i, j in up]
        last = lax.slice_in_dim(x, length - width, length, axis=dim)
        initial = lax.slice_in_dim(x, 0, width, axis=dim)
        before = lax.ppermute(last, axis, up)
        after = lax.ppermute(initial, axis, down)
        x = jnp.concatenate([before, x, after], axis=dim)
    return x


def tournament_tables(players_total):
    players = list(range(players_total))
    left_stack = []
    right_stack = []
    unit = np.eye(players_total, dtype=np.float32)
    for round_number in range(players_total - 1):
        left_side = [players[place] for place in range(players_total // 2)]
        right_side = [players[players_total - 1 - place] for place in range(players_total // 2)]
        left_stack.append(unit[:, left_side])
        right_stack.append(unit[:, right_side])
        players = [players[0], players[-1]] + players[1:-1]
    return (np.stack(left_stack), np.stack(right_stack))


def rotate_round(carry, tables):
    highest = lax.Precision.HIGHEST
    matrix, vectors = carry
    left_table, right_table = tables
    diagonal_now = jnp.diagonal(matrix)
    left_diag = jnp.dot(diagonal_now, left_table, precision=highest)
    right_diag = jnp.dot(diagonal_now, right_table, precision=highest)
    coupling = jnp.sum(left_table * jnp.dot(matrix, right_table, precision=highest), axis=0)
    spread = right_diag - left_diag
    divisor = jnp.abs(spread) + jnp.sqrt(spread * spread + 4.0 * coupling * coupling)
    direction = jnp.where(spread >= 0.0, 1.0, -1.0)
    safe_divisor = jnp.where(divisor > 0.0, divisor, 1.0)
    tangent = jnp.where(divisor > 0.0, direction * 2.0 * coupling / safe_divisor, 0.0)
    adjacent = 1.0 / jnp.sqrt(1.0 + tangent * tangent)
    opposite = tangent * adjacent
    cos_full = jnp.dot(left_table + right_table, adjacent, precision=highest)
    both_tables = jnp.concatenate([left_table, right_table], axis=1)
    signed_sin = jnp.concatenate(
        [right_table * opposite[None, :], -left_table * opposite[None, :]], axis=1
    )
    rotation = jnp.diag(cos_full) + jnp.dot(signed_sin, both_tables.T, precision=highest).T
    matrix = jnp.dot(jnp.dot(rotation.T, matrix, precision=highest), rotation, precision=highest)
    vectors = jnp.dot(vectors, rotation, precision=highest)
    return ((matrix, vectors), None)


def symmetric_eigen(matrix):
    left_np, right_np = tournament_tables(BLOCK)
    left_all = jnp.asarray(left_np)
    right_all = jnp.asarray(right_np)

    def sweep(sweep_index, carry):
        result_carry, unused = lax.scan(rotate_round, carry, (left_all, right_all))
        return result_carry

    start = (matrix, jnp.eye(BLOCK, dtype=jnp.float32))
    final_matrix, final_vectors = lax.fori_loop(0, SWEEPS, sweep, start)
    values = jnp.diagonal(final_matrix)
    ranking = jnp.argsort(values)
    return (values[ranking], final_vectors[:, ranking])


def second_along(padded, axis):
    count = padded.shape[axis] - 2
    upper = lax.slice_in_dim(padded, 2, 2 + count, axis=axis)
    lower = lax.slice_in_dim(padded, 0, count, axis=axis)
    middle = lax.slice_in_dim(padded, 1, 1 + count, axis=axis)
    return upper + lower - 2.0 * middle


def x_second(field):
    return jnp.roll(field, -1, 3) + jnp.roll(field, 1, 3) - 2.0 * field


def hessian(block, curvature, stiffness, stiff_rim):
    padded = with_halo(block, (("gz", 1), ("gy", 2)), 2)
    along_z = padded[:, :, 2:-2, :]
    z_flux = stiff_rim[:, 1:-1, :] * second_along(along_z, 1)
    z_term = second_along(z_flux, 1)
    along_y = padded[:, 2:-2, :, :]
    y_flux = stiff_rim[1:-1, :, :] * second_along(along_y, 2)
    y_term = second_along(y_flux, 2)
    x_flux = stiffness * x_second(block)
    x_term = x_second(x_flux)
    return curvature * block + z_term + y_term + x_term


def local(initial_block, concentration, stiffness):
    highest = lax.Precision.HIGHEST
    stiff_rim = with_halo(stiffness, (("gz", 0), ("gy", 1)), 1)
    curvature = 3.0 * concentration * concentration - 1.0
    precondition = curvature + 2.0
    precondition = precondition + (
        stiff_rim[2:, 1:-1, :] + stiff_rim[:-2, 1:-1, :] + 4.0 * stiffness
    )
    precondition = precondition + (
        stiff_rim[1:-1, 2:, :] + stiff_rim[1:-1, :-2, :] + 4.0 * stiffness
    )
    precondition = precondition + (
        jnp.roll(stiffness, -1, 2) + jnp.roll(stiffness, 1, 2) + 4.0 * stiffness
    )
    cells_total = (
        concentration.shape[0]
        * concentration.shape[1]
        * concentration.shape[2]
        * lax.axis_size("gz")
        * lax.axis_size("gy")
    )
    scale_factor = jnp.float32(cells_total / MODES)
    identity = jnp.eye(BLOCK, dtype=jnp.float32)
    search = initial_block
    ritz_all = jnp.zeros((BLOCK,), jnp.float32)
    modes = search[:MODES]
    residuals = search[:MODES]
    for iteration in range(ITERS):
        gram_local = jnp.einsum("azyx,bzyx->ab", search, search, precision=highest)
        gram_matrix = lax.psum(gram_local, ("gz", "gy"))
        lower_factor = jnp.linalg.cholesky(gram_matrix)
        lower_inverse = lax.linalg.triangular_solve(
            lower_factor, identity, left_side=True, lower=True
        )
        basis_vectors = jnp.einsum("ab,bzyx->azyx", lower_inverse, search, precision=highest)
        images = hessian(basis_vectors, curvature, stiffness, stiff_rim)
        projected_local = jnp.einsum("azyx,bzyx->ab", basis_vectors, images, precision=highest)
        projected = lax.psum(projected_local, ("gz", "gy"))
        projected = 0.5 * (projected + projected.T)
        ritz_all, ritz_vectors = symmetric_eigen(projected)
        combination = ritz_vectors[:, :MODES]
        modes = jnp.einsum("azyx,aj->jzyx", basis_vectors, combination, precision=highest)
        mode_images = jnp.einsum("azyx,aj->jzyx", images, combination, precision=highest)
        residuals = mode_images - ritz_all[:MODES, None, None, None] * modes
        corrections = residuals / precondition
        search = jnp.concatenate([modes, corrections], axis=0)
    mode_density = scale_factor * jnp.sum(modes * modes, axis=0)
    residual_density = scale_factor * jnp.sum(residuals * residuals, axis=0)
    return (ritz_all[:MODES], mode_density, residual_density)


def solution(mesh):
    return jax.shard_map(
        local,
        mesh=mesh,
        in_specs=(P("img", "gz", "gy", None), P(("img", "gz"), "gy", None), P("gz", "gy", None)),
        out_specs=(P("img"), P(("img", "gz"), "gy", None), P(("img", "gz"), "gy", None)),
        check_vma=False,
    )
```

profile of v0, /device:TPU:0, one launch (start us, length us, event | category | flops | bytes accessed | tf_op | source)
XLA Modules:
  0.0 766.4 jit_solution(15188571875948156192)
XLA Ops:
  0.6 3.2 convolution_bitcast_fusion.13
  3.8 35.4 %psum.28 = f32[16,16]{0,1:T(8,128)S(1)} all-reduce(f32[16,16]{0,1:T(8,128)S(1)} %convolution_bitcast_fusion.13), channel_id=1, replica_groups=mesh['img'=2,'gz'=8,'gy'=2] {'gz','gy'}, use_global_device_ids=true, to_apply=%region_0.1 | all-reduce | flops 256 | bytes 2048 | tf_op jit(solution)/shard_map/psum | solution.py:136
  39.3 1.5 cholesky.44
  43.6 2.3 fusion.90
  45.9 2.0 collective-permute-start.3
  48.0 4.7 collective-permute-start.1
  57.0 17.7 %collective-permute-done = f32[1,16,384]{2,1,0:T(8,128)S(1)} collective-permute-done((f32[1,16,384]{2,1,0:T(8,128)S(1)}, f32[1,16,384]{2,1,0:T(8,128)S(1)}, u32[]{:S(2)}, u32[]{:S(2)}) %collective-permute-start) | collective-permute-done | bytes 24608 | tf_op jit(solution)/shard_map/ppermute | solution.py:20
  74.8 4.5 collective-permute-done.1
  86.7 31.5 %psum.29 = f32[16,16]{1,0:T(8,128)S(1)} all-reduce(f32[16,16]{1,0:T(8,128)S(1)} %convolution_bitcast_fusion.12), channel_id=1, replica_groups=mesh['img'=2,'gz'=8,'gy'=2] {'gz','gy'}, use_global_device_ids=true, to_apply=%region_3.6 | all-reduce | flops 256 | bytes 2048 | tf_op jit(solution)/shard_map/psum | solution.py:144
  118.3 266.1 %while.57 = (s32[]{:T(128)}, f32[16,16]{1,0:T(8,128)S(1)}, f32[16,16]{0,1:T(8,128)S(1)}, s32[]{:T(128)}, s32[]{:T(128)}, /*index=5*/s32[]{:T(128)}, f32[15,16,8]...) while((s32[]{:T(128)}, f32[16,16]{1,0:T(8,128)S(1)}, ...), condition=%wide.region_8.11_spmd.clone, body=%wide.region_4.0_spmd.sunk.clone.sunk | while | flops 228060 | bytes 55646 | solution.py:76
  118.3 33.3 %while.60 = (s32[]{:T(128)}, f32[16,16]{1,0:T(8,128)S(1)}, f32[16,16]{0,1:T(8,128)S(1)}, s32[]{:T(128)}, f32[15,16,8]{1,2,0:T(8,128)S(1)}, /*index=5*/f32[15,16,8]{1,2,0:T(8,128)S(1)}) while((s32[]{:T(128)}, f32[16,16]{1,0:T(8,128)S(1)}, f32[16,16]{0,1:T(8,128)S(1)}, s32[]{:T(128)}, f32[15,16,8]{1,2,0:T(8,128)S(1)}, ...), condition=%wide.region_7.9_spmd.clone, body=%wide.region_5.8_spmd.sunk.clone.sunk | while | flops 228058 | bytes 55489 | solution.py:72
  151.5 33.3 %while.60 = (s32[]{:T(128)}, f32[16,16]{1,0:T(8,128)S(1)}, f32[16,16]{0,1:T(8,128)S(1)}, s32[]{:T(128)}, f32[15,16,8]{1,2,0:T(8,128)S(1)}, /*index=5*/f32[15,16,8]{1,2,0:T(8,128)S(1)}) while((s32[]{:T(128)}, f32[16,16]{1,0:T(8,128)S(1)}, f32[16,16]{0,1:T(8,128)S(1)}, s32[]{:T(128)}, f32[15,16,8]{1,2,0:T(8,128)S(1)}, ...), condition=%wide.region_7.9_spmd.clone, body=%wide.region_5.8_spmd.sunk.clone.sunk | while | flops 228058 | bytes 55489 | solution.py:72
  184.8 33.3 %while.60 = (s32[]{:T(128)}, f32[16,16]{1,0:T(8,128)S(1)}, f32[16,16]{0,1:T(8,128)S(1)}, s32[]{:T(128)}, f32[15,16,8]{1,2,0:T(8,128)S(1)}, /*index=5*/f32[15,16,8]{1,2,0:T(8,128)S(1)}) while((s32[]{:T(128)}, f32[16,16]{1,0:T(8,128)S(1)}, f32[16,16]{0,1:T(8,128)S(1)}, s32[]{:T(128)}, f32[15,16,8]{1,2,0:T(8,128)S(1)}, ...), condition=%wide.region_7.9_spmd.clone, body=%wide.region_5.8_spmd.sunk.clone.sunk | while | flops 228058 | bytes 55489 | solution.py:72
  218.0 33.3 %while.60 = (s32[]{:T(128)}, f32[16,16]{1,0:T(8,128)S(1)}, f32[16,16]{0,1:T(8,128)S(1)}, s32[]{:T(128)}, f32[15,16,8]{1,2,0:T(8,128)S(1)}, /*index=5*/f32[15,16,8]{1,2,0:T(8,128)S(1)}) while((s32[]{:T(128)}, f32[16,16]{1,0:T(8,128)S(1)}, f32[16,16]{0,1:T(8,128)S(1)}, s32[]{:T(128)}, f32[15,16,8]{1,2,0:T(8,128)S(1)}, ...), condition=%wide.region_7.9_spmd.clone, body=%wide.region_5.8_spmd.sunk.clone.sunk | while | flops 228058 | bytes 55489 | solution.py:72
  251.3 33.3 %while.60 = (s32[]{:T(128)}, f32[16,16]{1,0:T(8,128)S(1)}, f32[16,16]{0,1:T(8,128)S(1)}, s32[]{:T(128)}, f32[15,16,8]{1,2,0:T(8,128)S(1)}, /*index=5*/f32[15,16,8]{1,2,0:T(8,128)S(1)}) while((s32[]{:T(128)}, f32[16,16]{1,0:T(8,128)S(1)}, f32[16,16]{0,1:T(8,128)S(1)}, s32[]{:T(128)}, f32[15,16,8]{1,2,0:T(8,128)S(1)}, ...), condition=%wide.region_7.9_spmd.clone, body=%wide.region_5.8_spmd.sunk.clone.sunk | while | flops 228058 | bytes 55489 | solution.py:72
  284.6 33.3 %while.60 = (s32[]{:T(128)}, f32[16,16]{1,0:T(8,128)S(1)}, f32[16,16]{0,1:T(8,128)S(1)}, s32[]{:T(128)}, f32[15,16,8]{1,2,0:T(8,128)S(1)}, /*index=5*/f32[15,16,8]{1,2,0:T(8,128)S(1)}) while((s32[]{:T(128)}, f32[16,16]{1,0:T(8,128)S(1)}, f32[16,16]{0,1:T(8,128)S(1)}, s32[]{:T(128)}, f32[15,16,8]{1,2,0:T(8,128)S(1)}, ...), condition=%wide.region_7.9_spmd.clone, body=%wide.region_5.8_spmd.sunk.clone.sunk | while | flops 228058 | bytes 55489 | solution.py:72
  317.8 33.3 %while.60 = (s32[]{:T(128)}, f32[16,16]{1,0:T(8,128)S(1)}, f32[16,16]{0,1:T(8,128)S(1)}, s32[]{:T(128)}, f32[15,16,8]{1,2,0:T(8,128)S(1)}, /*index=5*/f32[15,16,8]{1,2,0:T(8,128)S(1)}) while((s32[]{:T(128)}, f32[16,16]{1,0:T(8,128)S(1)}, f32[16,16]{0,1:T(8,128)S(1)}, s32[]{:T(128)}, f32[15,16,8]{1,2,0:T(8,128)S(1)}, ...), condition=%wide.region_7.9_spmd.clone, body=%wide.region_5.8_spmd.sunk.clone.sunk | while | flops 228058 | bytes 55489 | solution.py:72
  351.1 33.3 %while.60 = (s32[]{:T(128)}, f32[16,16]{1,0:T(8,128)S(1)}, f32[16,16]{0,1:T(8,128)S(1)}, s32[]{:T(128)}, f32[15,16,8]{1,2,0:T(8,128)S(1)}, /*index=5*/f32[15,16,8]{1,2,0:T(8,128)S(1)}) while((s32[]{:T(128)}, f32[16,16]{1,0:T(8,128)S(1)}, f32[16,16]{0,1:T(8,128)S(1)}, s32[]{:T(128)}, f32[15,16,8]{1,2,0:T(8,128)S(1)}, ...), condition=%wide.region_7.9_spmd.clone, body=%wide.region_5.8_spmd.sunk.clone.sunk | while | flops 228058 | bytes 55489 | solution.py:72
  389.7 30.0 %psum.30 = f32[16,16]{0,1:T(8,128)S(1)} all-reduce(f32[16,16]{0,1:T(8,128)S(1)} %convolution_bitcast_fusion.11), channel_id=1, replica_groups=mesh['img'=2,'gz'=8,'gy'=2] {'gz','gy'}, use_global_device_ids=true, to_apply=%region_10.13 | all-reduce | flops 256 | bytes 2048 | tf_op jit(solution)/shard_map/psum | solution.py:136
  419.8 1.5 cholesky.55
  424.9 2.0 collective-permute-start.9
  428.1 33.0 %collective-permute-done.8 = f32[16,2,16,384]{3,0,2,1:T(8,128)S(1)} collective-permute-done((f32[16,2,16,384]{3,0,2,1:T(8,128)S(1)}, f32[16,2,16,384]{3,0,2,1:T(8,128)S(1)}, u32[]{:S(2)}, u32[]{:S(2)}) %collective-permute-start.8) | collective-permute-done | bytes 786464 | tf_op jit(solution)/shard_map/ppermute | solution.py:21
  465.1 30.1 %psum.31 = f32[16,16]{0,1:T(8,128)S(1)} all-reduce(f32[16,16]{0,1:T(8,128)S(1)} %convolution_bitcast_fusion.10), channel_id=1, replica_groups=mesh['img'=2,'gz'=8,'gy'=2] {'gz','gy'}, use_global_device_ids=true, to_apply=%region_11.14 | all-reduce | flops 256 | bytes 2048 | tf_op jit(solution)/shard_map/psum | solution.py:144
  495.3 266.0 %while.59 = (s32[]{:T(128)}, f32[16,16]{1,0:T(8,128)S(1)}, f32[16,16]{0,1:T(8,128)S(1)}, s32[]{:T(128)}, s32[]{:T(128)}, /*index=5*/s32[]{:T(128)}, f32[15,16,8]{1,2,0:T(8,128)S(1)}, f32[15,16,8]{1,2,0:T(8,128)S(1)}) while((s32[]{:T(128)}, f32[16,16]{1,0:T(8,128)S(1)}, f32[16,16]{0,1:T(8,128)S(1)}, s32[]{:T(128)}, ...), condition=%wide.region_16.19_spmd.clone, body=%wide.region_12.18_spmd.sunk.clone.sunk | while | flops 228060 | bytes 55630 | solution.py:76
  495.3 33.2 %while.61 = (s32[]{:T(128)}, f32[16,16]{1,0:T(8,128)S(1)}, f32[16,16]{0,1:T(8,128)S(1)}, s32[]{:T(128)}, f32[15,16,8]{1,2,0:T(8,128)S(1)}, /*index=5*/f32[15,16,8]{1,2,0:T(8,128)S(1)}) while((s32[]{:T(128)}, f32[16,16]{1,0:T(8,128)S(1)}, f32[16,16]{0,1:T(8,128)S(1)}, s32[]{:T(128)}, f32[15,16,8]{1,2,0:T(8,128)S(1)}, ...), condition=%wide.region_15.17_spmd.clone, body=%wide.region_13.16_spmd.sunk.clone.sunk | while | flops 228058 | bytes 55489 | solution.py:72
  528.5 33.3 %while.61 = (s32[]{:T(128)}, f32[16,16]{1,0:T(8,128)S(1)}, f32[16,16]{0,1:T(8,128)S(1)}, s32[]{:T(128)}, f32[15,16,8]{1,2,0:T(8,128)S(1)}, /*index=5*/f32[15,16,8]{1,2,0:T(8,128)S(1)}) while((s32[]{:T(128)}, f32[16,16]{1,0:T(8,128)S(1)}, f32[16,16]{0,1:T(8,128)S(1)}, s32[]{:T(128)}, f32[15,16,8]{1,2,0:T(8,128)S(1)}, ...), condition=%wide.region_15.17_spmd.clone, body=%wide.region_13.16_spmd.sunk.clone.sunk | while | flops 228058 | bytes 55489 | solution.py:72
  561.8 33.3 %while.61 = (s32[]{:T(128)}, f32[16,16]{1,0:T(8,128)S(1)}, f32[16,16]{0,1:T(8,128)S(1)}, s32[]{:T(128)}, f32[15,16,8]{1,2,0:T(8,128)S(1)}, /*index=5*/f32[15,16,8]{1,2,0:T(8,128)S(1)}) while((s32[]{:T(128)}, f32[16,16]{1,0:T(8,128)S(1)}, f32[16,16]{0,1:T(8,128)S(1)}, s32[]{:T(128)}, f32[15,16,8]{1,2,0:T(8,128)S(1)}, ...), condition=%wide.region_15.17_spmd.clone, body=%wide.region_13.16_spmd.sunk.clone.sunk | while | flops 228058 | bytes 55489 | solution.py:72
  595.1 33.3 %while.61 = (s32[]{:T(128)}, f32[16,16]{1,0:T(8,128)S(1)}, f32[16,16]{0,1:T(8,128)S(1)}, s32[]{:T(128)}, f32[15,16,8]{1,2,0:T(8,128)S(1)}, /*index=5*/f32[15,16,8]{1,2,0:T(8,128)S(1)}) while((s32[]{:T(128)}, f32[16,16]{1,0:T(8,128)S(1)}, f32[16,16]{0,1:T(8,128)S(1)}, s32[]{:T(128)}, f32[15,16,8]{1,2,0:T(8,128)S(1)}, ...), condition=%wide.region_15.17_spmd.clone, body=%wide.region_13.16_spmd.sunk.clone.sunk | while | flops 228058 | bytes 55489 | solution.py:72
  628.3 33.3 %while.61 = (s32[]{:T(128)}, f32[16,16]{1,0:T(8,128)S(1)}, f32[16,16]{0,1:T(8,128)S(1)}, s32[]{:T(128)}, f32[15,16,8]{1,2,0:T(8,128)S(1)}, /*index=5*/f32[15,16,8]{1,2,0:T(8,128)S(1)}) while((s32[]{:T(128)}, f32[16,16]{1,0:T(8,128)S(1)}, f32[16,16]{0,1:T(8,128)S(1)}, s32[]{:T(128)}, f32[15,16,8]{1,2,0:T(8,128)S(1)}, ...), condition=%wide.region_15.17_spmd.clone, body=%wide.region_13.16_spmd.sunk.clone.sunk | while | flops 228058 | bytes 55489 | solution.py:72
  661.6 33.3 %while.61 = (s32[]{:T(128)}, f32[16,16]{1,0:T(8,128)S(1)}, f32[16,16]{0,1:T(8,128)S(1)}, s32[]{:T(128)}, f32[15,16,8]{1,2,0:T(8,128)S(1)}, /*index=5*/f32[15,16,8]{1,2,0:T(8,128)S(1)}) while((s32[]{:T(128)}, f32[16,16]{1,0:T(8,128)S(1)}, f32[16,16]{0,1:T(8,128)S(1)}, s32[]{:T(128)}, f32[15,16,8]{1,2,0:T(8,128)S(1)}, ...), condition=%wide.region_15.17_spmd.clone, body=%wide.region_13.16_spmd.sunk.clone.sunk | while | flops 228058 | bytes 55489 | solution.py:72
  694.8 33.3 %while.61 = (s32[]{:T(128)}, f32[16,16]{1,0:T(8,128)S(1)}, f32[16,16]{0,1:T(8,128)S(1)}, s32[]{:T(128)}, f32[15,16,8]{1,2,0:T(8,128)S(1)}, /*index=5*/f32[15,16,8]{1,2,0:T(8,128)S(1)}) while((s32[]{:T(128)}, f32[16,16]{1,0:T(8,128)S(1)}, f32[16,16]{0,1:T(8,128)S(1)}, s32[]{:T(128)}, f32[15,16,8]{1,2,0:T(8,128)S(1)}, ...), condition=%wide.region_15.17_spmd.clone, body=%wide.region_13.16_spmd.sunk.clone.sunk | while | flops 228058 | bytes 55489 | solution.py:72
  728.1 33.3 %while.61 = (s32[]{:T(128)}, f32[16,16]{1,0:T(8,128)S(1)}, f32[16,16]{0,1:T(8,128)S(1)}, s32[]{:T(128)}, f32[15,16,8]{1,2,0:T(8,128)S(1)}, /*index=5*/f32[15,16,8]{1,2,0:T(8,128)S(1)}) while((s32[]{:T(128)}, f32[16,16]{1,0:T(8,128)S(1)}, f32[16,16]{0,1:T(8,128)S(1)}, s32[]{:T(128)}, f32[15,16,8]{1,2,0:T(8,128)S(1)}, ...), condition=%wide.region_15.17_spmd.clone, body=%wide.region_13.16_spmd.sunk.clone.sunk | while | flops 228058 | bytes 55489 | solution.py:72
  (3238 shorter events, 558.6 us)
Async XLA Ops:
  0.6 47.3 %copy-start.7 = (f32[2,16,384]{2,1,0:T(8,128)S(1)}, f32[2,16,384]{2,1,0:T(8,128)}, u32[]{:S(2)}) copy-start(f32[2,16,384]{2,1,0:T(8,128)} %param.20) | copy-start | bytes 147460
  45.8 36.5 %collective-permute-start.2 = (f32[16,2,16,384]{3,0,2,1:T(8,128)S(1)}, f32[16,2,16,384]{3,0,2,1:T(8,128)S(1)}, u32[]{:S(2)}, u32[]{:S(2)}) collective-permute-start(f32[16,2,16,384]{3,0,2,1:T(8,128)S(1)} %fusion.90), channel_id=1, source_target_pairs={{2,0},{4,2},{6,4},{8,6},{10,8},{12,10},{14,12},{0,14},{3,1},{5,3},... | collective-permute-start | bytes 2359304 | tf_op jit(solution)/shard_map/ppermute | solution.py:21
  45.9 36.4 %collective-permute-start.3 = (f32[16,2,16,384]{3,0,2,1:T(8,128)S(1)}, f32[16,2,16,384]{3,0,2,1:T(8,128)S(1)}, u32[]{:S(2)}, u32[]{:S(2)}) collective-permute-start(f32[16,2,16,384]{3,0,2,1:T(8,128)S(1)} %fusion.90), channel_id=1, source_target_pairs={{0,2},{2,4},{4,6},{6,8},{8,10},{10,12},{12,14},{14,0},{1,3},{3,5},... | collective-permute-start | bytes 2359304 | tf_op jit(solution)/shard_map/ppermute | solution.py:20
  47.9 26.8 %collective-permute-start = (f32[1,16,384]{2,1,0:T(8,128)S(1)}, f32[1,16,384]{2,1,0:T(8,128)S(1)}, u32[]{:S(2)}, u32[]{:S(2)}) collective-permute-start(f32[1,16,384]{2,1,0:T(8,128)S(1)} %get-tuple-element.262), channel_id=1, source_target_pairs={{0,2},{2,4},{4,6},{6,8},{8,10},{10,12},{12,14},{14,0},{1,3},{3,5},... | collective-permute-start | bytes 73736 | tf_op jit(solution)/shard_map/ppermute | solution.py:20
  48.0 31.3 %collective-permute-start.1 = (f32[1,16,384]{2,1,0:T(8,128)S(1)}, f32[1,16,384]{2,1,0:T(8,128)S(1)}, u32[]{:S(2)}, u32[]{:S(2)}) collective-permute-start(f32[1,16,384]{2,1,0:T(8,128)S(1)} %get-tuple-element.261), channel_id=1, source_target_pairs={{2,0},{4,2},{6,4},{8,6},{10,8},{12,10},{14,12},{0,14},{3,1},{5,3},... | collective-permute-start | bytes 73736 | tf_op jit(solution)/shard_map/ppermute | solution.py:21
  57.0 25.3 %copy-start.2 = (f32[16,16]{0,1:T(8,128)}, f32[16,16]{0,1:T(8,128)S(1)}, u32[]{:S(2)}) copy-start(f32[16,16]{0,1:T(8,128)S(1)} %fusion.111) | copy-start | bytes 3076
  74.8 5.8 copy-start.10
  79.3 1.3 copy-start.11
  79.3 1.2 collective-permute-start.5
  79.4 1.3 collective-permute-start.4
  80.7 0.6 copy-start.12
  82.4 1.6 collective-permute-start.6
  82.8 1.7 collective-permute-start.7
  83.5 1.1 copy-start.5
  83.5 1.4 copy-start.6
  83.5 1.4 copy-start.8
  83.5 1.5 copy-start.9
  85.5 32.7 %copy-start = (f32[15,16,8]{1,2,0:T(8,128)S(1)}, f32[15,16,8]{1,2,0:T(8,128)}, u32[]{:S(2)}) copy-start(f32[15,16,8]{1,2,0:T(8,128)} %constant.142.clone..sunk2.4) | copy-start | bytes 23044
  85.6 32.7 %copy-start.1 = (f32[15,16,8]{1,2,0:T(8,128)S(1)}, f32[15,16,8]{1,2,0:T(8,128)}, u32[]{:S(2)}) copy-start(f32[15,16,8]{1,2,0:T(8,128)} %constant.143.clone..sunk2.4) | copy-start | bytes 23044
  85.6 32.7 %copy-start.4 = (f32[16,16]{0,1:T(8,128)S(1)}, f32[16,16]{0,1:T(8,128)}, u32[]{:S(2)}) copy-start(f32[16,16]{0,1:T(8,128)} %copy-done.2) | copy-start | bytes 3076
  424.8 36.3 %collective-permute-start.8 = (f32[16,2,16,384]{3,0,2,1:T(8,128)S(1)}, f32[16,2,16,384]{3,0,2,1:T(8,128)S(1)}, u32[]{:S(2)}, u32[]{:S(2)}) collective-permute-start(f32[16,2,16,384]{3,0,2,1:T(8,128)S(1)} %fusion.116), channel_id=1, source_target_pairs={{2,0},{4,2},{6,4},{8,6},{10,8},{12,10},{14,12},{0,14},{3,1},{5,3},... | collective-permute-start | bytes 2359304 | tf_op jit(solution)/shard_map/ppermute | solution.py:21
  424.9 36.2 %collective-permute-start.9 = (f32[16,2,16,384]{3,0,2,1:T(8,128)S(1)}, f32[16,2,16,384]{3,0,2,1:T(8,128)S(1)}, u32[]{:S(2)}, u32[]{:S(2)}) collective-permute-start(f32[16,2,16,384]{3,0,2,1:T(8,128)S(1)} %fusion.116), channel_id=1, source_target_pairs={{0,2},{2,4},{4,6},{6,8},{8,10},{10,12},{12,14},{14,0},{1,3},{3,5},... | collective-permute-start | bytes 2359304 | tf_op jit(solution)/shard_map/ppermute | solution.py:20
  461.2 1.6 collective-permute-start.10
  461.2 2.0 collective-permute-start.11
  463.9 31.4 %copy-start.3 = (f32[16,16]{0,1:T(8,128)S(1)}, f32[16,16]{0,1:T(8,128)}, u32[]{:S(2)}) copy-start(f32[16,16]{0,1:T(8,128)} %copy-done.2) | copy-start | bytes 3076
  764.0 2.4 copy-start.13
where the time goes:
time: 767 us; the launch traced here: 766 us
  matrix products  354 us (46%)
  local copies, waits for them, and re-layouts  172 us (22%)
  blocking collectives  127 us (17%)
  waiting for transfers between devices  57.9 us (8%)
  other arithmetic  36.1 us (5%)
  starting transfers between devices  10.6 us (1%)
    gather x240, local copies, waits for them, and re-layouts, rotate_round(): diagonal_now = jnp.diagonal(matrix)  159 us
    psum x2, blocking collectives, local(): gram_matrix = lax.psum(gram_local, ('gz', 'gy'))  65.4 us
    psum x2, blocking collectives, local(): projected = lax.psum(projected_local, ('gz', 'gy'))  61.6 us
    dot_general x240, matrix products, rotate_round(): jnp.dot(matrix, right_table, precision=highest)  58.5 us
    dot_general x240, matrix products, rotate_round(): jnp.dot(rotation.T, matrix, precision=highest)  49.6 us
    dot_general x240, matrix products, rotate_round(): jnp.dot(signed_sin, both_tables.T, precision=highest)  49.5 us
    dot_general x240, matrix products, rotate_round(): vectors = jnp.dot(vectors, rotation, precision=highest)  48.4 us
    ppermute x6, waiting for transfers between devices, with_halo(): after = lax.ppermute(initial, axis, down)  39.2 us
  transfers between devices with their start and end apart: 12, of which 9 were waited for; matrix products, arithmetic and copies ran while one was open for 1% of the time, Pallas kernels for 0%

commit v1 on v0

v1 whole, which is shorter than its diff:
```python
import functools

import jax
import jax.numpy as jnp
from jax import lax
from jax.experimental import pallas as pl
from jax.experimental.pallas import tpu as pltpu
from jax.sharding import PartitionSpec as P

BLOCK = 16
MODES = 8
ITERS = 2
HALF = BLOCK // 2
LANES = 128
MAX_SWEEPS = 14
HIGHEST = lax.Precision.HIGHEST


def neighbour_layers(x, axis, dim, first, last):
    size = lax.axis_size(axis)
    up = [(i, (i + 1) % size) for i in range(size)]
    down = [(j, i) for i, j in up]
    before = lax.ppermute(last, axis, up)
    after = lax.ppermute(first, axis, down)
    return before, after


def edge(x, dim, start, stop):
    return lax.slice_in_dim(x, start, stop, axis=dim)


def grid_sum(x):
    axes = ("gz", "gy")
    total = lax.axis_size("gz") * lax.axis_size("gy")
    if total & (total - 1):
        return lax.psum(x, axes)
    mask = 1
    while mask < total:
        one = lax.ppermute(x, axes, [(i, i ^ mask) for i in range(total)])
        if 2 * mask < total:
            two = lax.ppermute(x, axes, [(i, i ^ (2 * mask)) for i in range(total)])
            three = lax.ppermute(x, axes, [(i, i ^ (3 * mask)) for i in range(total)])
            x = (x + one) + (two + three)
        else:
            x = x + one
        mask *= 4
    return x


def tournament():
    players = list(range(BLOCK))
    rounds = []
    for _ in range(BLOCK - 1):
        rounds.append([(players[k], players[BLOCK - 1 - k]) for k in range(HALF)])
        players = [players[0], players[-1]] + players[1:-1]
    return rounds


def every_sublane(x):
    x = x + pltpu.roll(x, 4, 0)
    x = x + pltpu.roll(x, 2, 0)
    return x + pltpu.roll(x, 1, 0)


def small_kernel(gram_ref, stiff_ref, theta_ref, mix_ref):
    rows = lax.broadcasted_iota(jnp.int32, (BLOCK, LANES), 0)
    lanes = lax.broadcasted_iota(jnp.int32, (BLOCK, LANES), 1)
    unit = jnp.where(rows == lanes, 1.0, 0.0).astype(jnp.float32)
    pad = jnp.zeros((BLOCK, LANES - BLOCK), jnp.float32)
    work = jnp.concatenate([gram_ref[...], pad], axis=1)
    inverse = unit
    for k in range(BLOCK):
        pivot = work[k : k + 1, :]
        pivot_inverse = inverse[k : k + 1, :]
        scale = 1.0 / work[k : k + 1, k : k + 1]
        factor = jnp.where(rows[:, :1] > k, work[:, k : k + 1] * scale, 0.0)
        root = lax.sqrt(scale)
        work = work - factor * pivot
        inverse = inverse - factor * pivot_inverse
        inverse = jnp.where(rows == k, inverse * root, inverse)
    lower_inverse = inverse[:, :BLOCK]
    half_way = jnp.dot(
        lower_inverse, stiff_ref[...], precision=HIGHEST, preferred_element_type=jnp.float32
    )
    projected = lax.dot_general(
        half_way,
        lower_inverse,
        (((1,), (1,)), ((), ())),
        precision=HIGHEST,
        preferred_element_type=jnp.float32,
    )
    eye = unit[:, :BLOCK]
    mean = jnp.sum(jnp.sum(projected * eye, axis=1, keepdims=True), axis=0, keepdims=True) / BLOCK
    traceless = projected - mean * eye
    spread = jnp.sum(
        jnp.sum(traceless * traceless, axis=1, keepdims=True), axis=0, keepdims=True
    )
    scale = 1.25 * jnp.sqrt(spread) + 1e-30
    shifted = eye + traceless / scale

    upper = []
    lower = []
    for k in range(BLOCK):
        column = jnp.broadcast_to(shifted[:, k : k + 1], (BLOCK, LANES))
        upper.append(column[:8])
        lower.append(column[8:])

    def sweep(carry):
        count, _, upper, lower = carry
        upper, lower = list(upper), list(lower)
        norms = [
            every_sublane(upper[k] * upper[k] + lower[k] * lower[k]) for k in range(BLOCK)
        ]
        worst = jnp.zeros((8, LANES), jnp.float32)
        for pairs in tournament():
            for i, j in pairs:
                ui, uj, li, lj = upper[i], upper[j], lower[i], lower[j]
                g = every_sublane(ui * uj + li * lj)
                a, b = norms[i], norms[j]
                d = b - a
                g2 = g * g
                h2 = d * d + 4.0 * g2
                worst = jnp.maximum(worst, g2)
                live = h2 > 1e-28
                ih = lax.rsqrt(jnp.maximum(h2, 1e-28))
                positive = d >= 0.0
                dd = jnp.abs(d)
                c2 = jnp.where(live, 0.5 + 0.5 * dd * ih, 1.0)
                ic = lax.rsqrt(c2)
                c = c2 * ic
                signed = jnp.where(positive, g, -g)
                s = jnp.where(live, signed * ih * ic, 0.0)
                move = 0.5 * (h2 * ih - dd)
                move = jnp.where(positive, move, -move)
                upper[i] = c * ui - s * uj
                lower[i] = c * li - s * lj
                upper[j] = s * ui + c * uj
                lower[j] = s * li + c * lj
                norms[i] = a - move
                norms[j] = b + move
        return count + 1, jnp.max(worst), tuple(upper), tuple(lower)

    def unfinished(carry):
        count, worst, _, _ = carry
        return jnp.logical_and(count < MAX_SWEEPS, worst > 1e-8)

    _, _, upper, lower = lax.while_loop(
        unfinished, sweep, (jnp.int32(0), jnp.float32(1.0), tuple(upper), tuple(lower))
    )
    squares = [every_sublane(upper[k] * upper[k] + lower[k] * lower[k]) for k in range(BLOCK)]
    lane = lanes[:8]
    theta = jnp.zeros((8, LANES), jnp.float32)
    vectors_upper = jnp.zeros((8, LANES), jnp.float32)
    vectors_lower = jnp.zeros((8, LANES), jnp.float32)
    for k in range(BLOCK):
        rank = jnp.zeros((8, LANES), jnp.int32)
        for other in range(BLOCK):
            if other < k:
                rank = rank + jnp.where(squares[other] <= squares[k], 1, 0)
            elif other > k:
                rank = rank + jnp.where(squares[other] < squares[k], 1, 0)
        here = lane == rank
        inverse_norm = lax.rsqrt(squares[k])
        theta = jnp.where(here, squares[k] * inverse_norm, theta)
        vectors_upper = jnp.where(here, upper[k] * inverse_norm, vectors_upper)
        vectors_lower = jnp.where(here, lower[k] * inverse_norm, vectors_lower)
    theta_ref[...] = mean + scale * (theta - 1.0)
    vectors = jnp.concatenate([vectors_upper, vectors_lower], axis=0)
    mix_ref[...] = lax.dot_general(
        lower_inverse,
        vectors,
        (((0,), (0,)), ((), ())),
        precision=HIGHEST,
        preferred_element_type=jnp.float32,
    )


def ritz_pairs(gram, stiff):
    theta, mix = pl.pallas_call(
        small_kernel,
        out_shape=(
            jax.ShapeDtypeStruct((8, LANES), jnp.float32),
            jax.ShapeDtypeStruct((BLOCK, LANES), jnp.float32),
        ),
        in_specs=[pl.BlockSpec(memory_space=pltpu.VMEM)] * 2,
        out_specs=[pl.BlockSpec(memory_space=pltpu.VMEM)] * 2,
        name="ritz_pairs",
    )(gram, stiff)
    return theta[0, :MODES], mix[:, :MODES]


def difference(before, x, after, dim):
    length = x.shape[dim]
    padded = jnp.concatenate([before, x, after], axis=dim)
    return edge(padded, dim, 2, 2 + length) + edge(padded, dim, 0, length) - 2.0 * x


def x_difference(field):
    axis = field.ndim - 1
    return jnp.roll(field, -1, axis) + jnp.roll(field, 1, axis) - 2.0 * field


def weighted_gram(block, near, curvature, stiffness):
    (z_before, z_after), (y_before, y_after) = near
    terms = [
        (block, curvature),
        (difference(z_before, block, z_after, 1), stiffness),
        (difference(y_before, block, y_after, 2), stiffness),
        (x_difference(block), stiffness),
    ]
    total = 0.0
    for field, weight in terms:
        total = total + jnp.einsum("azyx,bzyx->ab", field * weight, field, precision=HIGHEST)
    return total


def hessian(block, near, far, curvature, stiffness, stiff_near):
    total = curvature * block + x_difference(stiffness * x_difference(block))
    for axis in (0, 1):
        dim = axis + 1
        before, after = near[axis]
        far_before, far_after = far[axis]
        rim_before, rim_after = stiff_near[axis]
        wide = jnp.concatenate([before, block, after], axis=dim)
        weights = jnp.concatenate([rim_before, stiffness, rim_after], axis=axis)
        flux = weights * difference(far_before, wide, far_after, dim)
        length = block.shape[dim]
        total = total + (
            edge(flux, dim, 2, 2 + length)
            + edge(flux, dim, 0, length)
            - 2.0 * edge(flux, dim, 1, 1 + length)
        )
    return total


def near_layers(block):
    nz, ny = block.shape[1], block.shape[2]
    return (
        neighbour_layers(block, "gz", 1, edge(block, 1, 0, 1), edge(block, 1, nz - 1, nz)),
        neighbour_layers(block, "gy", 2, edge(block, 2, 0, 1), edge(block, 2, ny - 1, ny)),
    )


def far_layers(block):
    nz, ny = block.shape[1], block.shape[2]
    return (
        neighbour_layers(block, "gz", 1, edge(block, 1, 1, 2), edge(block, 1, nz - 2, nz - 1)),
        neighbour_layers(block, "gy", 2, edge(block, 2, 1, 2), edge(block, 2, ny - 2, ny - 1)),
    )


def combine(mix, block):
    return jnp.einsum("azyx,aj->jzyx", block, mix, precision=HIGHEST)


def combine_pairs(mix, pairs):
    return tuple(tuple(combine(mix, part) for part in pair) for pair in pairs)


def local(initial_block, concentration, stiffness):
    nz, ny, nx = concentration.shape
    curvature = 3.0 * concentration * concentration - 1.0
    cells_total = nz * ny * nx * lax.axis_size("gz") * lax.axis_size("gy")
    scale_factor = jnp.float32(cells_total / MODES)

    near = near_layers(initial_block)
    held, near = lax.optimization_barrier((initial_block, near))
    far = far_layers(held)
    stiff_near = (
        neighbour_layers(stiffness, "gz", 0, stiffness[:1], stiffness[nz - 1 :]),
        neighbour_layers(stiffness, "gy", 1, stiffness[:, :1], stiffness[:, ny - 1 :]),
    )
    precondition = curvature + 2.0
    for axis in (0, 1):
        before, after = stiff_near[axis]
        wide = jnp.concatenate([before, stiffness, after], axis=axis)
        length = stiffness.shape[axis]
        precondition = precondition + (
            edge(wide, axis, 2, 2 + length) + edge(wide, axis, 0, length) + 4.0 * stiffness
        )
    precondition = precondition + (
        jnp.roll(stiffness, -1, 2) + jnp.roll(stiffness, 1, 2) + 4.0 * stiffness
    )

    gram = jnp.einsum("azyx,bzyx->ab", initial_block, initial_block, precision=HIGHEST)
    stiff = weighted_gram(initial_block, near, curvature, stiffness)
    sums = grid_sum(jnp.concatenate([gram, stiff], axis=1))
    theta, mix = ritz_pairs(sums[:, :BLOCK], sums[:, BLOCK:])

    modes = combine(mix, initial_block)
    mode_images = hessian(
        modes, combine_pairs(mix, near), combine_pairs(mix, far), curvature, stiffness, stiff_near
    )
    residuals = mode_images - theta[:, None, None, None] * modes
    corrections = residuals / precondition
    search = jnp.concatenate([modes, corrections], axis=0)

    near = near_layers(corrections)
    held, near = lax.optimization_barrier((corrections, near))
    far = far_layers(held)
    gram = jnp.einsum("azyx,bzyx->ab", search, search, precision=HIGHEST)
    cross = jnp.einsum("azyx,bzyx->ab", mode_images, search, precision=HIGHEST)
    low = weighted_gram(corrections, near, curvature, stiffness)
    stiff = jnp.concatenate(
        [cross, jnp.concatenate([cross[:, MODES:].T, low], axis=1)], axis=0
    )
    sums = grid_sum(jnp.concatenate([gram, stiff], axis=1))
    theta, mix = ritz_pairs(sums[:, :BLOCK], sums[:, BLOCK:])

    correction_images = hessian(corrections, near, far, curvature, stiffness, stiff_near)
    images = jnp.concatenate([mode_images, correction_images], axis=0)
    modes = combine(mix, search)
    residuals = combine(mix, images) - theta[:, None, None, None] * modes
    mode_density = scale_factor * jnp.sum(modes * modes, axis=0)
    residual_density = scale_factor * jnp.sum(residuals * residuals, axis=0)
    return (theta, mode_density, residual_density)


def solution(mesh):
    return jax.shard_map(
        local,
        mesh=mesh,
        in_specs=(P("img", "gz", "gy", None), P(("img", "gz"), "gy", None), P("gz", "gy", None)),
        out_specs=(P("img"), P(("img", "gz"), "gy", None), P(("img", "gz"), "gy", None)),
        check_vma=False,
    )
```

time: 767 us -> 132 us (0.17)
  matrix products: 354 us -> 24.1 us
  local copies, waits for them, and re-layouts: 172 us -> 10.4 us
  blocking collectives: 127 us -> 0 us
  other arithmetic: 36.1 us -> 3.34 us
  starting transfers between devices: 10.6 us -> 37.9 us
  waiting for transfers between devices: 57.9 us -> 35.9 us
  Pallas kernels: 0 us -> 18.1 us
    dot_general x1930 -> x22, matrix products: 354 us -> 24.1 us  [the longest x8 11.8 us: weighted_gram(): jnp.einsum('azyx,bzyx->ab', field * weight, field, precision=HIGHEST)]
    gather x246 -> x0, local copies, waits for them, and re-layouts: 163 us -> none  [the longest x240 159 us: rotate_round(): diagonal_now = jnp.diagonal(matrix)]
    psum x4 -> x0, blocking collectives: 127 us -> none  [the longest x2 65.4 us: local(): gram_matrix = lax.psum(gram_local, ('gz', 'gy'))]
    ppermute x12 -> x32, starting transfers between devices: 10.6 us -> 37.9 us  [the longest x10 20.4 us: neighbour_layers(): after = lax.ppermute(first, axis, down)]
    ppermute x12 -> x32, waiting for transfers between devices: 57.9 us -> 35.9 us  [the longest x10 16.9 us: neighbour_layers(): before = lax.ppermute(last, axis, up)]
    mul x248 -> x7, other arithmetic: 20.5 us -> 1.71 us  [the longest x2 1.15 us: weighted_gram(): field * weight]
    pallas_call x0 -> x2, Pallas kernels: none -> 18.1 us  [ritz_pairs(): pl.pallas_call(small_kernel, out_shape=(jax.ShapeDtypeStruct((8, LANES),...]
    another operation x10 -> x0, other arithmetic: 8.01 us -> none  [the longest x6 4.26 us: local(): lower_factor = jnp.linalg.cholesky(gram_matrix)]
  transfers between devices with their start and end apart: 12 -> 32, of which waited for: 9 -> 14; matrix products, arithmetic and copies ran while one was open for 1% -> 15% of each run, Pallas kernels for 0% -> 7%
where the time goes in v1:
time: 132 us; the launch traced here: 131 us
  starting transfers between devices  37.9 us (29%)
  waiting for transfers between devices  35.9 us (27%)
  matrix products  24.1 us (18%)
  Pallas kernels  18.1 us (14%)
  local copies, waits for them, and re-layouts  10.4 us (8%)
  other arithmetic  3.34 us (3%)
    ppermute x10, starting transfers between devices, neighbour_layers(): after = lax.ppermute(first, axis, down)  20.4 us
    pallas_call x2, Pallas kernels, ritz_pairs(): pl.pallas_call(small_kernel, out_shape=(jax.ShapeDtypeStruct((8, LANES),...  18.1 us
    ppermute x10, waiting for transfers between devices, neighbour_layers(): before = lax.ppermute(last, axis, up)  16.9 us
    dot_general x8, matrix products, weighted_gram(): jnp.einsum('azyx,bzyx->ab', field * weight, field, precision=HIGHEST)  11.8 us
    dot_general x11, matrix products, combine(): return jnp.einsum('azyx,aj->jzyx', block, mix, precision=HIGHEST)  8.79 us
    ppermute x10, waiting for transfers between devices, neighbour_layers(): after = lax.ppermute(first, axis, down)  8.22 us
    ppermute x4, starting transfers between devices, grid_sum(): three = lax.ppermute(x, axes, [(i, i ^ 3 * mask) for i in range(total)])  8.02 us
    ppermute x10, starting transfers between devices, neighbour_layers(): before = lax.ppermute(last, axis, up)  5 us
  transfers between devices with their start and end apart: 32, of which 14 were waited for; matrix products, arithmetic and copies ran while one was open for 15% of the time, Pallas kernels for 7%

profile of v1, /device:TPU:0, one launch (start us, length us, event | category | flops | bytes accessed | tf_op | source)
XLA Modules:
  0.0 130.9 jit_solution(13681945637819884444)
XLA Ops:
  1.4 3.0 %collective-permute-start.10 = (f32[1,16,384]{2,1,0:T(8,128)S(1)}, f32[1,16,384]{2,1,0:T(8,128)S(1)}, u32[]{:S(2)}, u32[]{:S(2)}) collective-permute-start(f32[1,16,384]{2,1,0:T(8,128)S(1)} %get-tuple-element.99), channel_id=1, source_target_pairs={{0,2},{2,4},{4,6},{6,8},{8,10},{10,12},{12,14},{14,0},{1,3},{3,5},... | collective-permute-start | bytes 73736 | tf_op jit(solution)/shard_map/ppermute | solution.py:23
  4.4 3.1 %collective-permute-start.11 = (f32[1,16,384]{2,1,0:T(8,128)S(1)}, f32[1,16,384]{2,1,0:T(8,128)S(1)}, u32[]{:S(2)}, u32[]{:S(2)}) collective-permute-start(f32[1,16,384]{2,1,0:T(8,128)S(1)} %get-tuple-element.98), channel_id=1, source_target_pairs={{2,0},{4,2},{6,4},{8,6},{10,8},{12,10},{14,12},{0,14},{3,1},{5,3},... | collective-permute-start | bytes 73736 | tf_op jit(solution)/shard_map/ppermute | solution.py:24
  8.1 1.2 fusion.115
  10.0 1.4 %convolution_bitcast_fusion.13 = f32[16,16]{1,0:T(8,128)S(1)} fusion(f32[16,2,16,384]{3,2,1,0:T(8,128)S(1)} %copy-done), kind=kOutput, calls=%fused_computation.16 | convolution fusion | flops 37748736 | bytes 787456 | tf_op jit(solution)/shard_map/azyx,bzyx->ab/dot_general | solution.py:285
  11.5 4.8 %collective-permute-start.1 = (f32[16,1,16,384]{3,2,1,0:T(8,128)S(1)}, f32[16,1,16,384]{3,2,1,0:T(8,128)S(1)}, u32[]{:S(2)}, u32[]{:S(2)}) collective-permute-start(f32[16,1,16,384]{3,2,1,0:T(8,128)S(1)} %get-tuple-element.58), channel_id=1, source_target_pairs={{2,0},{4,2},{6,4},{8,6},{10,8},{12,10},{14,12},{0,14},{3,1},{5,3},... | collective-permute-start | bytes 1179656 | tf_op jit(solution)/shard_map/ppermute | solution.py:24
  17.7 9.0 %collective-permute-done = f32[16,1,16,384]{3,2,1,0:T(8,128)S(1)} collective-permute-done((f32[16,1,16,384]{3,2,1,0:T(8,128)S(1)}, f32[16,1,16,384]{3,2,1,0:T(8,128)S(1)}, u32[]{:S(2)}, u32[]{:S(2)}) %collective-permute-start) | collective-permute-done | bytes 393248 | tf_op jit(solution)/shard_map/ppermute | solution.py:23
  26.7 4.4 %collective-permute-done.1 = f32[16,1,16,384]{3,2,1,0:T(8,128)S(1)} collective-permute-done((f32[16,1,16,384]{3,2,1,0:T(8,128)S(1)}, f32[16,1,16,384]{3,2,1,0:T(8,128)S(1)}, u32[]{:S(2)}, u32[]{:S(2)}) %collective-permute-start.1) | collective-permute-done | bytes 393248 | tf_op jit(solution)/shard_map/ppermute | solution.py:24
  32.1 1.9 %convolution_bitcast_fusion.11 = f32[16,16]{1,0:T(8,128)S(1)} fusion(f32[16,2,16,384]{3,2,1,0:T(8,128)S(1)} %get-tuple-element.42, f32[16,2,16,384]{3,2,1,0:T(8,128)S(1)} %get-tuple-element.41), kind=kOutput, calls=%fused_computation.14 | convolution fusion | flops 37748736 | bytes 1573888 | tf_op jit(solution)/shard_map/azyx,bzyx->ab/dot_general | solution.py:213
  34.0 1.9 %convolution_bitcast_fusion.10 = f32[16,16]{1,0:T(8,128)S(1)} fusion(f32[16,2,16,384]{3,2,1,0:T(8,128)S(1)} %get-tuple-element.50, f32[16,2,16,384]{3,2,1,0:T(8,128)S(1)} %get-tuple-element.49), kind=kOutput, calls=%fused_computation.13 | convolution fusion | flops 37748736 | bytes 1573888 | tf_op jit(solution)/shard_map/azyx,bzyx->ab/dot_general | solution.py:213
  35.9 1.9 %convolution_bitcast_fusion.9 = f32[16,16]{1,0:T(8,128)S(1)} fusion(f32[16,2,16,384]{3,2,1,0:T(8,128)S(1)} %get-tuple-element.48, f32[16,2,16,384]{3,2,1,0:T(8,128)S(1)} %get-tuple-element.47), kind=kOutput, calls=%fused_computation.12 | convolution fusion | flops 37748736 | bytes 1573888 | tf_op jit(solution)/shard_map/azyx,bzyx->ab/dot_general | solution.py:213
  37.8 2.0 %fusion.4 = f32[16,16]{1,0:T(8,128)S(1)} fusion(f32[16,16]{1,0:T(8,128)S(1)} %convolution_bitcast_fusion.9, f32[16,16]{1,0:T(8,128)S(1)} %convolution_bitcast_fusion.10, f32[16,16]{1,0:T(8,128)S(1)} %convolution_bitcast_fusion.11, f32[16,2,16,384]{3,2,1,0:T(8,128)S(1)} %get-tuple-element.55, f32[16,2,16,384]{3,2,1,0:T(8,128)S(1)} %copy-done), kind=kOutput, calls=%fused_computation.19 | convolution fusion | flops 37749504 | bytes 1576960 | tf_op jit(solution)/shard_map/azyx,bzyx->ab/dot_general | solution.py:213
  40.0 1.8 %collective-permute-start.6 = (f32[16,32]{1,0:T(8,128)S(1)}, f32[16,32]{1,0:T(8,128)S(1)}, u32[]{:S(2)}, u32[]{:S(2)}) collective-permute-start(f32[16,32]{1,0:T(8,128)S(1)} %pad_maximum_fusion.15), channel_id=1, source_target_pairs={{0,3},{1,2},{2,1},{3,0},{4,7},{5,6},{6,5},{7,4},{8,11},{9,10},{10,... | collective-permute-start | bytes 6152 | tf_op jit(solution)/shard_map/ppermute | solution.py:42
  44.0 4.4 %collective-permute-start.12 = (f32[16,1,16,384]{3,0,2,1:T(8,128)}, f32[16,1,16,384]{3,0,2,1:T(8,128)S(1)}, u32[]{:S(2)}, u32[]{:S(2)}) collective-permute-start(f32[16,1,16,384]{3,0,2,1:T(8,128)} %get-tuple-element.52), channel_id=1, source_target_pairs={{2,0},{4,2},{6,4},{8,6},{10,8},{12,10},{14,12},{0,14},{3,1},{5,3},... | collective-permute-start | bytes 1179656 | tf_op jit(solution)/shard_map/ppermute | solution.py:24
  48.6 4.3 %collective-permute-start.9 = (f32[16,32]{1,0:T(8,128)S(1)}, f32[16,32]{1,0:T(8,128)S(1)}, u32[]{:S(2)}, u32[]{:S(2)}) collective-permute-start(f32[16,32]{1,0:T(8,128)S(1)} %add_add_fusion.3), channel_id=1, source_target_pairs={{0,12},{1,13},{2,14},{3,15},{4,8},{5,9},{6,10},{7,11},{8,4},{9,5},... | collective-permute-start | bytes 6152 | tf_op jit(solution)/shard_map/ppermute | solution.py:42
  53.6 4.1 %collective-permute-done.7 = f32[16,32]{1,0:T(8,128)S(1)} collective-permute-done((f32[16,32]{1,0:T(8,128)S(1)}, f32[16,32]{1,0:T(8,128)S(1)}, u32[]{:S(2)}, u32[]{:S(2)}) %collective-permute-start.7) | collective-permute-done | bytes 2080 | tf_op jit(solution)/shard_map/ppermute | solution.py:39
  58.9 9.1 %ritz_pairs.2 = (f32[8,128]{1,0:T(8,128)}, f32[16,128]{1,0:T(8,128)}) custom-call(f32[16,16]{1,0:T(8,128)} %get-tuple-element.105.gram_ref, f32[16,16]{1,0:T(8,128)} %get-tuple-element.104.stiff_ref), custom_call_target="tpu_custom_call" | custom-call | tf_op jit(solution)/shard_map/ritz_pairs/pallas_call | solution.py:179
  67.9 1.6 %fusion.90 = f32[8,2,16,384]{3,0,2,1:T(8,128)S(1)} fusion(f32[16,128]{1,0:T(8,128)} %get-tuple-element.21, f32[16,2,16,384]{3,2,1,0:T(8,128)S(1)} %copy-done), kind=kOutput, calls=%fused_computation.163 | convolution fusion | flops 18874368 | bytes 1187840 | tf_op jit(solution)/shard_map/azyx,aj->jzyx/dot_general | solution.py:253
  75.1 1.4 %convolution_bitcast_fusion.1 = f32[8,1,16,384]{3,0,2,1:T(8,128)S(1)} fusion(f32[16,1,16,384]{3,0,2,1:T(8,128)} %collective-permute-done.13, f32[16,128]{1,0:T(8,128)S(1)} %copy-done.2), kind=kOutput, calls=%fused_computation.4 | convolution fusion | flops 9437184 | bytes 598016 | tf_op jit(solution)/shard_map/azyx,aj->jzyx/dot_general | solution.py:253
  77.7 1.0 collective-permute-start.18
  78.7 3.7 %collective-permute-start.19 = (f32[8,1,16,384]{3,0,2,1:T(8,128)S(1)}, f32[8,1,16,384]{3,0,2,1:T(8,128)S(1)}, u32[]{:S(2)}, u32[]{:S(2)}) collective-permute-start(f32[8,1,16,384]{3,0,2,1:T(8,128)S(1)} %get-tuple-element.78), channel_id=1, source_target_pairs={{2,0},{4,2},{6,4},{8,6},{10,8},{12,10},{14,12},{0,14},{3,1},{5,3},... | collective-permute-start | bytes 589832 | tf_op jit(solution)/shard_map/ppermute | solution.py:24
  84.1 1.1 convolution_bitcast_fusion.8
  85.3 2.5 %collective-permute-done.18 = f32[8,1,16,384]{3,0,2,1:T(8,128)S(1)} collective-permute-done((f32[8,1,16,384]{3,0,2,1:T(8,128)S(1)}, f32[8,1,16,384]{3,0,2,1:T(8,128)S(1)}, u32[]{:S(2)}, u32[]{:S(2)}) %collective-permute-start.18) | collective-permute-done | bytes 196640 | tf_op jit(solution)/shard_map/ppermute | solution.py:23
  87.8 2.9 %collective-permute-done.19 = f32[8,1,16,384]{3,0,2,1:T(8,128)S(1)} collective-permute-done((f32[8,1,16,384]{3,0,2,1:T(8,128)S(1)}, f32[8,1,16,384]{3,0,2,1:T(8,128)S(1)}, u32[]{:S(2)}, u32[]{:S(2)}) %collective-permute-start.19) | collective-permute-done | bytes 196640 | tf_op jit(solution)/shard_map/ppermute | solution.py:24
  91.3 2.3 %collective-permute-start.28 = (f32[8,1,16,384]{3,0,2,1:T(8,128)S(1)}, f32[8,1,16,384]{3,0,2,1:T(8,128)S(1)}, u32[]{:S(2)}, u32[]{:S(2)}) collective-permute-start(f32[8,1,16,384]{3,0,2,1:T(8,128)S(1)} %get-tuple-element.73), channel_id=1, source_target_pairs={{2,0},{4,2},{6,4},{8,6},{10,8},{12,10},{14,12},{0,14},{3,1},{5,3},... | collective-permute-start | bytes 589832 | tf_op jit(solution)/shard_map/ppermute | solution.py:24
  97.9 4.9 %collective-permute-done.29 = f32[8,1,16,384]{3,0,2,1:T(8,128)S(1)} collective-permute-done((f32[8,1,16,384]{3,0,2,1:T(8,128)S(1)}, f32[8,1,16,384]{3,0,2,1:T(8,128)S(1)}, u32[]{:S(2)}, u32[]{:S(2)}) %collective-permute-start.29) | collective-permute-done | bytes 196640 | tf_op jit(solution)/shard_map/ppermute | solution.py:23
  106.3 1.8 %collective-permute-done.23 = f32[16,32]{1,0:T(8,128)S(1)} collective-permute-done((f32[16,32]{1,0:T(8,128)S(1)}, f32[16,32]{1,0:T(8,128)S(1)}, u32[]{:S(2)}, u32[]{:S(2)}) %collective-permute-start.23) | collective-permute-done | bytes 2080 | tf_op jit(solution)/shard_map/ppermute | solution.py:41
  108.3 1.6 %collective-permute-start.25 = (f32[16,32]{1,0:T(8,128)S(1)}, f32[16,32]{1,0:T(8,128)S(1)}, u32[]{:S(2)}, u32[]{:S(2)}) collective-permute-start(f32[16,32]{1,0:T(8,128)S(1)} %add_add_fusion.1), channel_id=1, source_target_pairs={{0,4},{1,5},{2,6},{3,7},{4,0},{5,1},{6,2},{7,3},{8,12},{9,13},{10,... | collective-permute-start | bytes 6152 | tf_op jit(solution)/shard_map/ppermute | solution.py:39
  109.9 1.9 %collective-permute-start.26 = (f32[16,32]{1,0:T(8,128)S(1)}, f32[16,32]{1,0:T(8,128)S(1)}, u32[]{:S(2)}, u32[]{:S(2)}) collective-permute-start(f32[16,32]{1,0:T(8,128)S(1)} %add_add_fusion.1), channel_id=1, source_target_pairs={{0,8},{1,9},{2,10},{3,11},{4,12},{5,13},{6,14},{7,15},{8,0},{9,1},... | collective-permute-start | bytes 6152 | tf_op jit(solution)/shard_map/ppermute | solution.py:41
  112.7 1.7 %collective-permute-done.26 = f32[16,32]{1,0:T(8,128)S(1)} collective-permute-done((f32[16,32]{1,0:T(8,128)S(1)}, f32[16,32]{1,0:T(8,128)S(1)}, u32[]{:S(2)}, u32[]{:S(2)}) %collective-permute-start.26) | collective-permute-done | bytes 2080 | tf_op jit(solution)/shard_map/ppermute | solution.py:41
  114.5 2.8 %collective-permute-done.27 = f32[16,32]{1,0:T(8,128)S(1)} collective-permute-done((f32[16,32]{1,0:T(8,128)S(1)}, f32[16,32]{1,0:T(8,128)S(1)}, u32[]{:S(2)}, u32[]{:S(2)}) %collective-permute-start.27) | collective-permute-done | bytes 2080 | tf_op jit(solution)/shard_map/ppermute | solution.py:42
  117.9 9.1 %ritz_pairs.3 = (f32[8,128]{1,0:T(8,128)}, f32[16,128]{1,0:T(8,128)}) custom-call(f32[16,16]{1,0:T(8,128)} %get-tuple-element.103.gram_ref, f32[16,16]{1,0:T(8,128)} %get-tuple-element.102.stiff_ref), custom_call_target="tpu_custom_call" | custom-call | tf_op jit(solution)/shard_map/ritz_pairs/pallas_call | solution.py:179
  127.0 1.4 %multiply_reduce_fusion = (f32[2,16,384]{2,1,0:T(8,128)S(1)}, f32[8,2,16,384]{3,0,2,1:T(8,128)S(1)}) fusion(f32[8,2,16,384]{3,0,2,1:T(8,128)S(1)} %get-tuple-element.30, f32[8,2,16,384]{3,0,2,1:T(8,128)S(1)} %fusion.90, f32[16,128]{1,0:T(8,128)} %get-tuple-element.29), kind=kOutput, calls=%fused_computation.117 | convolution fusion | flops 19255296 | bytes 1236992 | tf_op jit(solution)/shard_map/azyx,aj->jzyx/dot_general | solution.py:253
  (125 shorter events, 29.8 us)
Async XLA Ops:
  1.4 14.8 %collective-permute-start.10 = (f32[1,16,384]{2,1,0:T(8,128)S(1)}, f32[1,16,384]{2,1,0:T(8,128)S(1)}, u32[]{:S(2)}, u32[]{:S(2)}) collective-permute-start(f32[1,16,384]{2,1,0:T(8,128)S(1)} %get-tuple-element.99), channel_id=1, source_target_pairs={{0,2},{2,4},{4,6},{6,8},{8,10},{10,12},{12,14},{14,0},{1,3},{3,5},... | collective-permute-start | bytes 73736 | tf_op jit(solution)/shard_map/ppermute | solution.py:23
  4.4 12.4 %collective-permute-start.11 = (f32[1,16,384]{2,1,0:T(8,128)S(1)}, f32[1,16,384]{2,1,0:T(8,128)S(1)}, u32[]{:S(2)}, u32[]{:S(2)}) collective-permute-start(f32[1,16,384]{2,1,0:T(8,128)S(1)} %get-tuple-element.98), channel_id=1, source_target_pairs={{2,0},{4,2},{6,4},{8,6},{10,8},{12,10},{14,12},{0,14},{3,1},{5,3},... | collective-permute-start | bytes 73736 | tf_op jit(solution)/shard_map/ppermute | solution.py:24
  7.5 4.0 %collective-permute-start.14 = (f32[2,1,384]{2,1,0:T(1,128)S(1)}, f32[2,1,384]{2,1,0:T(1,128)S(1)}, u32[]{:S(2)}, u32[]{:S(2)}) collective-permute-start(f32[2,1,384]{2,1,0:T(1,128)S(1)} %get-tuple-element.101), channel_id=1, source_target_pairs={{0,1},{1,0},{2,3},{3,2},{4,5},{5,4},{6,7},{7,6},{8,9},{9,8},{10,11... | collective-permute-start | bytes 9224 | tf_op jit(solution)/shard_map/ppermute | solution.py:23
  7.6 8.6 %collective-permute-start.15 = (f32[2,1,384]{2,1,0:T(1,128)S(1)}, f32[2,1,384]{2,1,0:T(1,128)S(1)}, u32[]{:S(2)}, u32[]{:S(2)}) collective-permute-start(f32[2,1,384]{2,1,0:T(1,128)S(1)} %get-tuple-element.100), channel_id=1, source_target_pairs={{1,0},{0,1},{3,2},{2,3},{5,4},{4,5},{7,6},{6,7},{9,8},{8,9},{11,10... | collective-permute-start | bytes 9224 | tf_op jit(solution)/shard_map/ppermute | solution.py:24
  9.3 17.4 %collective-permute-start = (f32[16,1,16,384]{3,2,1,0:T(8,128)S(1)}, f32[16,1,16,384]{3,2,1,0:T(8,128)S(1)}, u32[]{:S(2)}, u32[]{:S(2)}) collective-permute-start(f32[16,1,16,384]{3,2,1,0:T(8,128)S(1)} %get-tuple-element.59), channel_id=1, source_target_pairs={{0,2},{2,4},{4,6},{6,8},{8,10},{10,12},{12,14},{14,0},{1,3},{3,5},... | collective-permute-start | bytes 1179656 | tf_op jit(solution)/shard_map/ppermute | solution.py:23
  11.5 19.6 %collective-permute-start.1 = (f32[16,1,16,384]{3,2,1,0:T(8,128)S(1)}, f32[16,1,16,384]{3,2,1,0:T(8,128)S(1)}, u32[]{:S(2)}, u32[]{:S(2)}) collective-permute-start(f32[16,1,16,384]{3,2,1,0:T(8,128)S(1)} %get-tuple-element.58), channel_id=1, source_target_pairs={{2,0},{4,2},{6,4},{8,6},{10,8},{12,10},{14,12},{0,14},{3,1},{5,3},... | collective-permute-start | bytes 1179656 | tf_op jit(solution)/shard_map/ppermute | solution.py:24
  16.3 1.2 collective-permute-start.2
  16.3 1.5 %collective-permute-start.3 = (f32[16,2,1,384]{3,0,2,1:T(8,128)S(1)}, f32[16,2,1,384]{3,0,2,1:T(8,128)S(1)}, u32[]{:S(2)}, u32[]{:S(2)}) collective-permute-start(f32[16,2,1,384]{3,0,2,1:T(8,128)S(1)} %copy.175), channel_id=1, source_target_pairs={{1,0},{0,1},{3,2},{2,3},{5,4},{4,5},{7,6},{6,7},{9,8},{8,9},{11,10... | collective-permute-start | bytes 147464 | tf_op jit(solution)/shard_map/ppermute | solution.py:24
  39.9 8.5 %collective-permute-start.4 = (f32[16,32]{1,0:T(8,128)S(1)}, f32[16,32]{1,0:T(8,128)S(1)}, u32[]{:S(2)}, u32[]{:S(2)}) collective-permute-start(f32[16,32]{1,0:T(8,128)S(1)} %pad_maximum_fusion.15), channel_id=1, source_target_pairs={{0,1},{1,0},{2,3},{3,2},{4,5},{5,4},{6,7},{7,6},{8,9},{9,8},{10,11... | collective-permute-start | bytes 6152 | tf_op jit(solution)/shard_map/ppermute | solution.py:39
  40.0 8.5 %collective-permute-start.5 = (f32[16,32]{1,0:T(8,128)S(1)}, f32[16,32]{1,0:T(8,128)S(1)}, u32[]{:S(2)}, u32[]{:S(2)}) collective-permute-start(f32[16,32]{1,0:T(8,128)S(1)} %pad_maximum_fusion.15), channel_id=1, source_target_pairs={{0,2},{1,3},{2,0},{3,1},{4,6},{5,7},{6,4},{7,5},{8,10},{9,11},{10,... | collective-permute-start | bytes 6152 | tf_op jit(solution)/shard_map/ppermute | solution.py:41
  40.0 8.4 %collective-permute-start.6 = (f32[16,32]{1,0:T(8,128)S(1)}, f32[16,32]{1,0:T(8,128)S(1)}, u32[]{:S(2)}, u32[]{:S(2)}) collective-permute-start(f32[16,32]{1,0:T(8,128)S(1)} %pad_maximum_fusion.15), channel_id=1, source_target_pairs={{0,3},{1,2},{2,1},{3,0},{4,7},{5,6},{6,5},{7,4},{8,11},{9,10},{10,... | collective-permute-start | bytes 6152 | tf_op jit(solution)/shard_map/ppermute | solution.py:42
  43.7 31.4 %collective-permute-start.13 = (f32[16,1,16,384]{3,0,2,1:T(8,128)}, f32[16,1,16,384]{3,0,2,1:T(8,128)}, u32[]{:S(2)}, u32[]{:S(2)}) collective-permute-start(f32[16,1,16,384]{3,0,2,1:T(8,128)} %get-tuple-element.51), channel_id=1, source_target_pairs={{0,2},{2,4},{4,6},{6,8},{8,10},{10,12},{12,14},{14,0},{1,3},{3,5},... | collective-permute-start | bytes 1179656 | tf_op jit(solution)/shard_map/ppermute | solution.py:23
  44.0 32.5 %collective-permute-start.12 = (f32[16,1,16,384]{3,0,2,1:T(8,128)}, f32[16,1,16,384]{3,0,2,1:T(8,128)S(1)}, u32[]{:S(2)}, u32[]{:S(2)}) collective-permute-start(f32[16,1,16,384]{3,0,2,1:T(8,128)} %get-tuple-element.52), channel_id=1, source_target_pairs={{2,0},{4,2},{6,4},{8,6},{10,8},{12,10},{14,12},{0,14},{3,1},{5,3},... | collective-permute-start | bytes 1179656 | tf_op jit(solution)/shard_map/ppermute | solution.py:24
  48.5 9.2 %collective-permute-start.7 = (f32[16,32]{1,0:T(8,128)S(1)}, f32[16,32]{1,0:T(8,128)S(1)}, u32[]{:S(2)}, u32[]{:S(2)}) collective-permute-start(f32[16,32]{1,0:T(8,128)S(1)} %add_add_fusion.3), channel_id=1, source_target_pairs={{0,4},{1,5},{2,6},{3,7},{4,0},{5,1},{6,2},{7,3},{8,12},{9,13},{10,... | collective-permute-start | bytes 6152 | tf_op jit(solution)/shard_map/ppermute | solution.py:39
  48.6 9.2 %collective-permute-start.8 = (f32[16,32]{1,0:T(8,128)S(1)}, f32[16,32]{1,0:T(8,128)S(1)}, u32[]{:S(2)}, u32[]{:S(2)}) collective-permute-start(f32[16,32]{1,0:T(8,128)S(1)} %add_add_fusion.3), channel_id=1, source_target_pairs={{0,8},{1,9},{2,10},{3,11},{4,12},{5,13},{6,14},{7,15},{8,0},{9,1},... | collective-permute-start | bytes 6152 | tf_op jit(solution)/shard_map/ppermute | solution.py:41
  48.6 9.6 %collective-permute-start.9 = (f32[16,32]{1,0:T(8,128)S(1)}, f32[16,32]{1,0:T(8,128)S(1)}, u32[]{:S(2)}, u32[]{:S(2)}) collective-permute-start(f32[16,32]{1,0:T(8,128)S(1)} %add_add_fusion.3), channel_id=1, source_target_pairs={{0,12},{1,13},{2,14},{3,15},{4,8},{5,9},{6,10},{7,11},{8,4},{9,5},... | collective-permute-start | bytes 6152 | tf_op jit(solution)/shard_map/ppermute | solution.py:42
  57.7 15.3 %collective-permute-start.17 = (f32[16,2,1,384]{3,0,1,2:T(8,128)}, f32[16,2,1,384]{3,0,1,2:T(8,128)}, u32[]{:S(2)}, u32[]{:S(2)}) collective-permute-start(f32[16,2,1,384]{3,0,1,2:T(8,128)} %get-tuple-element.53), channel_id=1, source_target_pairs={{0,1},{1,0},{2,3},{3,2},{4,5},{5,4},{6,7},{7,6},{8,9},{9,8},{10,11... | collective-permute-start | bytes 147464 | tf_op jit(solution)/shard_map/ppermute | solution.py:23
  57.8 16.3 %collective-permute-start.16 = (f32[16,2,1,384]{3,0,1,2:T(8,128)}, f32[16,2,1,384]{3,0,1,2:T(8,128)}, u32[]{:S(2)}, u32[]{:S(2)}) collective-permute-start(f32[16,2,1,384]{3,0,1,2:T(8,128)} %get-tuple-element.54), channel_id=1, source_target_pairs={{1,0},{0,1},{3,2},{2,3},{5,4},{4,5},{7,6},{6,7},{9,8},{8,9},{11,10... | collective-permute-start | bytes 147464 | tf_op jit(solution)/shard_map/ppermute | solution.py:24
  77.7 10.1 %collective-permute-start.18 = (f32[8,1,16,384]{3,0,2,1:T(8,128)S(1)}, f32[8,1,16,384]{3,0,2,1:T(8,128)S(1)}, u32[]{:S(2)}, u32[]{:S(2)}) collective-permute-start(f32[8,1,16,384]{3,0,2,1:T(8,128)S(1)} %get-tuple-element.79), channel_id=1, source_target_pairs={{0,2},{2,4},{4,6},{6,8},{8,10},{10,12},{12,14},{14,0},{1,3},{3,5},... | collective-permute-start | bytes 589832 | tf_op jit(solution)/shard_map/ppermute | solution.py:23
  78.7 12.0 %collective-permute-start.19 = (f32[8,1,16,384]{3,0,2,1:T(8,128)S(1)}, f32[8,1,16,384]{3,0,2,1:T(8,128)S(1)}, u32[]{:S(2)}, u32[]{:S(2)}) collective-permute-start(f32[8,1,16,384]{3,0,2,1:T(8,128)S(1)} %get-tuple-element.78), channel_id=1, source_target_pairs={{2,0},{4,2},{6,4},{8,6},{10,8},{12,10},{14,12},{0,14},{3,1},{5,3},... | collective-permute-start | bytes 589832 | tf_op jit(solution)/shard_map/ppermute | solution.py:24
  82.5 2.8 %collective-permute-start.20 = (f32[8,2,1,384]{3,0,2,1:T(8,128)S(1)}, f32[8,2,1,384]{3,0,2,1:T(8,128)S(1)}, u32[]{:S(2)}, u32[]{:S(2)}) collective-permute-start(f32[8,2,1,384]{3,0,2,1:T(8,128)S(1)} %get-tuple-element.77), channel_id=1, source_target_pairs={{0,1},{1,0},{2,3},{3,2},{4,5},{5,4},{6,7},{7,6},{8,9},{9,8},{10,11... | collective-permute-start | bytes 73736 | tf_op jit(solution)/shard_map/ppermute | solution.py:23
  82.5 2.8 %collective-permute-start.21 = (f32[8,2,1,384]{3,0,2,1:T(8,128)S(1)}, f32[8,2,1,384]{3,0,2,1:T(8,128)S(1)}, u32[]{:S(2)}, u32[]{:S(2)}) collective-permute-start(f32[8,2,1,384]{3,0,2,1:T(8,128)S(1)} %get-tuple-element.76), channel_id=1, source_target_pairs={{1,0},{0,1},{3,2},{2,3},{5,4},{4,5},{7,6},{6,7},{9,8},{8,9},{11,10... | collective-permute-start | bytes 73736 | tf_op jit(solution)/shard_map/ppermute | solution.py:24
  91.3 6.6 %collective-permute-start.28 = (f32[8,1,16,384]{3,0,2,1:T(8,128)S(1)}, f32[8,1,16,384]{3,0,2,1:T(8,128)S(1)}, u32[]{:S(2)}, u32[]{:S(2)}) collective-permute-start(f32[8,1,16,384]{3,0,2,1:T(8,128)S(1)} %get-tuple-element.73), channel_id=1, source_target_pairs={{2,0},{4,2},{6,4},{8,6},{10,8},{12,10},{14,12},{0,14},{3,1},{5,3},... | collective-permute-start | bytes 589832 | tf_op jit(solution)/shard_map/ppermute | solution.py:24
  93.7 9.2 %collective-permute-start.29 = (f32[8,1,16,384]{3,0,2,1:T(8,128)S(1)}, f32[8,1,16,384]{3,0,2,1:T(8,128)S(1)}, u32[]{:S(2)}, u32[]{:S(2)}) collective-permute-start(f32[8,1,16,384]{3,0,2,1:T(8,128)S(1)} %get-tuple-element.72), channel_id=1, source_target_pairs={{0,2},{2,4},{4,6},{6,8},{8,10},{10,12},{12,14},{14,0},{1,3},{3,5},... | collective-permute-start | bytes 589832 | tf_op jit(solution)/shard_map/ppermute | solution.py:23
  93.7 3.5 %collective-permute-start.30 = (f32[8,2,1,384]{3,0,2,1:T(8,128)S(1)}, f32[8,2,1,384]{3,0,2,1:T(8,128)S(1)}, u32[]{:S(2)}, u32[]{:S(2)}) collective-permute-start(f32[8,2,1,384]{3,0,2,1:T(8,128)S(1)} %get-tuple-element.75), channel_id=1, source_target_pairs={{1,0},{0,1},{3,2},{2,3},{5,4},{4,5},{7,6},{6,7},{9,8},{8,9},{11,10... | collective-permute-start | bytes 73736 | tf_op jit(solution)/shard_map/ppermute | solution.py:24
  93.7 3.5 %collective-permute-start.31 = (f32[8,2,1,384]{3,0,2,1:T(8,128)S(1)}, f32[8,2,1,384]{3,0,2,1:T(8,128)S(1)}, u32[]{:S(2)}, u32[]{:S(2)}) collective-permute-start(f32[8,2,1,384]{3,0,2,1:T(8,128)S(1)} %get-tuple-element.74), channel_id=1, source_target_pairs={{0,1},{1,0},{2,3},{3,2},{4,5},{5,4},{6,7},{7,6},{8,9},{9,8},{10,11... | collective-permute-start | bytes 73736 | tf_op jit(solution)/shard_map/ppermute | solution.py:23
  104.4 1.9 %collective-permute-start.22 = (f32[16,32]{1,0:T(8,128)S(1)}, f32[16,32]{1,0:T(8,128)S(1)}, u32[]{:S(2)}, u32[]{:S(2)}) collective-permute-start(f32[16,32]{1,0:T(8,128)S(1)} %maximum_maximum_fusion), channel_id=1, source_target_pairs={{0,1},{1,0},{2,3},{3,2},{4,5},{5,4},{6,7},{7,6},{8,9},{9,8},{10,11... | collective-permute-start | bytes 6152 | tf_op jit(solution)/shard_map/ppermute | solution.py:39
  104.4 3.7 %collective-permute-start.23 = (f32[16,32]{1,0:T(8,128)S(1)}, f32[16,32]{1,0:T(8,128)S(1)}, u32[]{:S(2)}, u32[]{:S(2)}) collective-permute-start(f32[16,32]{1,0:T(8,128)S(1)} %maximum_maximum_fusion), channel_id=1, source_target_pairs={{0,2},{1,3},{2,0},{3,1},{4,6},{5,7},{6,4},{7,5},{8,10},{9,11},{10,... | collective-permute-start | bytes 6152 | tf_op jit(solution)/shard_map/ppermute | solution.py:41
  105.3 3.1 %collective-permute-start.24 = (f32[16,32]{1,0:T(8,128)S(1)}, f32[16,32]{1,0:T(8,128)S(1)}, u32[]{:S(2)}, u32[]{:S(2)}) collective-permute-start(f32[16,32]{1,0:T(8,128)S(1)} %maximum_maximum_fusion), channel_id=1, source_target_pairs={{0,3},{1,2},{2,1},{3,0},{4,7},{5,6},{6,5},{7,4},{8,11},{9,10},{10,... | collective-permute-start | bytes 6152 | tf_op jit(solution)/shard_map/ppermute | solution.py:42
  108.3 4.4 %collective-permute-start.25 = (f32[16,32]{1,0:T(8,128)S(1)}, f32[16,32]{1,0:T(8,128)S(1)}, u32[]{:S(2)}, u32[]{:S(2)}) collective-permute-start(f32[16,32]{1,0:T(8,128)S(1)} %add_add_fusion.1), channel_id=1, source_target_pairs={{0,4},{1,5},{2,6},{3,7},{4,0},{5,1},{6,2},{7,3},{8,12},{9,13},{10,... | collective-permute-start | bytes 6152 | tf_op jit(solution)/shard_map/ppermute | solution.py:39
  109.9 4.5 %collective-permute-start.26 = (f32[16,32]{1,0:T(8,128)S(1)}, f32[16,32]{1,0:T(8,128)S(1)}, u32[]{:S(2)}, u32[]{:S(2)}) collective-permute-start(f32[16,32]{1,0:T(8,128)S(1)} %add_add_fusion.1), channel_id=1, source_target_pairs={{0,8},{1,9},{2,10},{3,11},{4,12},{5,13},{6,14},{7,15},{8,0},{9,1},... | collective-permute-start | bytes 6152 | tf_op jit(solution)/shard_map/ppermute | solution.py:41
  111.8 5.4 %collective-permute-start.27 = (f32[16,32]{1,0:T(8,128)S(1)}, f32[16,32]{1,0:T(8,128)S(1)}, u32[]{:S(2)}, u32[]{:S(2)}) collective-permute-start(f32[16,32]{1,0:T(8,128)S(1)} %add_add_fusion.1), channel_id=1, source_target_pairs={{0,12},{1,13},{2,14},{3,15},{4,8},{5,9},{6,10},{7,11},{8,4},{9,5},... | collective-permute-start | bytes 6152 | tf_op jit(solution)/shard_map/ppermute | solution.py:42
  (8 other events, 32.5 us)

commit v2 on v0

v2 whole, which is shorter than its diff:
```python
import functools

import jax
import jax.numpy as jnp
from jax import lax
from jax.experimental import pallas as pl
from jax.experimental.pallas import tpu as pltpu
from jax.sharding import PartitionSpec as P

BLOCK = 16
MODES = 8
HALF = BLOCK // 2
LANES = 128
MAX_SWEEPS = 14
HIGHEST = lax.Precision.HIGHEST
VMEM = pl.BlockSpec(memory_space=pltpu.VMEM)


def call(kernel, out_shapes, args, scratch=(), flops=1000000, name=None):
    out_shape = tuple(jax.ShapeDtypeStruct(s, jnp.float32) for s in out_shapes)
    moved = 4 * sum(x.size for x in list(args) + list(out_shape))
    return pl.pallas_call(
        kernel,
        out_shape=out_shape,
        in_specs=[VMEM] * len(args),
        out_specs=[VMEM] * len(out_shape),
        scratch_shapes=list(scratch),
        compiler_params=pltpu.CompilerParams(vmem_limit_bytes=40 * 1024 * 1024),
        cost_estimate=pl.CostEstimate(flops=flops, bytes_accessed=moved, transcendentals=0),
        name=name,
    )(*args)


def from_next(x):
    size = lax.axis_size("gz")
    return lax.ppermute(x, "gz", [((i + 1) % size, i) for i in range(size)])


def from_previous(x):
    size = lax.axis_size("gz")
    return lax.ppermute(x, "gz", [(i, (i + 1) % size) for i in range(size)])


def edge(x, dim, start, stop):
    return lax.slice_in_dim(x, start, stop, axis=dim)


def rows_beside(x, dim):
    size = lax.axis_size("gy")
    length = x.shape[dim]
    first = edge(x, dim, 0, 2)
    last = edge(x, dim, length - 2, length)
    if size == 2:
        rows = jnp.concatenate([last, first], axis=dim)
        return lax.ppermute(rows, "gy", [(0, 1), (1, 0)])
    before = lax.ppermute(last, "gy", [(i, (i + 1) % size) for i in range(size)])
    after = lax.ppermute(first, "gy", [((i + 1) % size, i) for i in range(size)])
    return jnp.concatenate([before, after], axis=dim)


def all_terms(copies):
    return lax.all_to_all(copies, ("gz", "gy"), 0, 0, tiled=True)


def spread_rows(x, k):
    return jnp.broadcast_to(x[k : k + 1, :], (8, LANES))


def every_row(x):
    x = x + pltpu.roll(x, 4, 0)
    x = x + pltpu.roll(x, 2, 0)
    return x + pltpu.roll(x, 1, 0)


def packed_sums(tiles, row):
    low4, low2, low1 = row < 4, (row & 2) == 0, (row & 1) == 0
    tiles = [
        jnp.where(low4, tiles[k], tiles[k + 4])
        + pltpu.roll(jnp.where(low4, tiles[k + 4], tiles[k]), 4, 0)
        for k in range(4)
    ]

    def fold(a, b, low, step):
        other = jnp.where(low, b, a)
        moved = jnp.where(low, pltpu.roll(other, 8 - step, 0), pltpu.roll(other, step, 0))
        return jnp.where(low, a, b) + moved

    tiles = [fold(tiles[k], tiles[k + 2], low2, 2) for k in range(2)]
    return fold(tiles[0], tiles[1], low1, 1)


def tournament():
    players = list(range(BLOCK))
    rounds = []
    for _ in range(BLOCK - 1):
        rounds.append([(players[k], players[BLOCK - 1 - k]) for k in range(HALF)])
        players = [players[0], players[-1]] + players[1:-1]
    return rounds


def ritz_kernel(terms_ref, theta_ref, theta_rows_ref, mix_ref):
    tiles = [terms_ref[k : k + 8, :] for k in range(0, terms_ref.shape[0], 8)]
    while len(tiles) > 1:
        tiles = [sum(tiles[k : k + 2]) for k in range(0, len(tiles), 2)]
    total = tiles[0]
    row = lax.broadcasted_iota(jnp.int32, (8, LANES), 0)
    lane = lax.broadcasted_iota(jnp.int32, (8, LANES), 1)

    def columns(upper, lower):
        return (
            [jnp.broadcast_to(upper[:, k : k + 1], (8, LANES)) for k in range(BLOCK)],
            [jnp.broadcast_to(lower[:, k : k + 1], (8, LANES)) for k in range(BLOCK)],
        )

    def entry(upper, lower, k):
        return spread_rows(upper, k) if k < 8 else spread_rows(lower, k - 8)

    gram_u, gram_l = columns(total[:, :BLOCK], total[:, BLOCK : 2 * BLOCK])
    zero = jnp.zeros((8, LANES), jnp.float32)
    inverse_u = [jnp.where(row == k, 1.0, 0.0).astype(jnp.float32) for k in range(8)] + [zero] * 8
    inverse_l = [zero] * 8 + [
        jnp.where(row == k, 1.0, 0.0).astype(jnp.float32) for k in range(8)
    ]
    for k in range(BLOCK):
        root = lax.rsqrt(entry(gram_u[k], gram_l[k], k))
        gram_u[k] = gram_u[k] * root
        gram_l[k] = gram_l[k] * root
        inverse_u[k] = inverse_u[k] * root
        inverse_l[k] = inverse_l[k] * root
        for i in range(k + 1, BLOCK):
            factor = entry(gram_u[k], gram_l[k], i)
            if i < 8:
                gram_u[i] = gram_u[i] - factor * gram_u[k]
            gram_l[i] = gram_l[i] - factor * gram_l[k]
            inverse_u[i] = inverse_u[i] - factor * inverse_u[k]
            if k >= 8:
                inverse_l[i] = inverse_l[i] - factor * inverse_l[k]
    transposed_u, transposed_l = zero, zero
    for k in range(BLOCK):
        transposed_u = jnp.where(lane == k, inverse_u[k], transposed_u)
        transposed_l = jnp.where(lane == k, inverse_l[k], transposed_l)
    transposed = jnp.concatenate([transposed_u, transposed_l], axis=0)[:, :BLOCK]

    dot = functools.partial(
        lax.dot_general, precision=HIGHEST, preferred_element_type=jnp.float32
    )
    stiff = jnp.concatenate(
        [total[:, 2 * BLOCK : 3 * BLOCK], total[:, 3 * BLOCK : 4 * BLOCK]], axis=0
    )
    half_way = dot(stiff, transposed, (((1,), (0,)), ((), ())))
    projected = dot(transposed, half_way, (((0,), (0,)), ((), ())))

    upper, lower = columns(projected[:8], projected[8:])
    diagonal = zero
    for k in range(8):
        diagonal = diagonal + jnp.where(row == k, upper[k] + lower[k + 8], 0.0)
    mean = every_row(diagonal) * (1.0 / BLOCK)
    size = zero
    for k in range(8):
        upper[k] = upper[k] - jnp.where(row == k, mean, 0.0)
        lower[k + 8] = lower[k + 8] - jnp.where(row == k, mean, 0.0)
    for k in range(BLOCK):
        size = size + (upper[k] * upper[k] + lower[k] * lower[k])
    scale = 1.25 * jnp.sqrt(every_row(size)) + 1e-30
    shrink = 1.0 / scale
    for k in range(BLOCK):
        upper[k] = upper[k] * shrink
        lower[k] = lower[k] * shrink
    for k in range(8):
        upper[k] = upper[k] + jnp.where(row == k, 1.0, 0.0)
        lower[k + 8] = lower[k + 8] + jnp.where(row == k, 1.0, 0.0)

    def squares(upper, lower):
        top = packed_sums([upper[k] * upper[k] + lower[k] * lower[k] for k in range(8)], row)
        bottom = packed_sums(
            [upper[15 - k] * upper[15 - k] + lower[15 - k] * lower[15 - k] for k in range(8)], row
        )
        return top, bottom

    def sweep(carry):
        count, _, upper, lower = carry
        upper, lower = list(upper), list(lower)
        top, bottom = squares(upper, lower)
        worst = zero
        for pairs in tournament():
            g = packed_sums([upper[i] * upper[j] + lower[i] * lower[j] for i, j in pairs], row)
            d = bottom - top
            g2 = g * g
            worst = jnp.maximum(worst, g2)
            dd = jnp.maximum(jnp.abs(d), 1e-18)
            ih = lax.rsqrt(dd * dd + 4.0 * g2)
            c2 = 0.5 + (0.5 * dd) * ih
            ic = lax.rsqrt(c2)
            c = c2 * ic
            s = jnp.where(d >= 0.0, g, -g) * (ih * ic)
            move = (s * ic) * g
            top = top - move
            bottom = bottom + move
            for k, (i, j) in enumerate(pairs):
                ck, sk = spread_rows(c, k), spread_rows(s, k)
                ui, uj, li, lj = upper[i], upper[j], lower[i], lower[j]
                upper[i] = ck * ui - sk * uj
                lower[i] = ck * li - sk * lj
                upper[j] = sk * ui + ck * uj
                lower[j] = sk * li + ck * lj
            next_top = jnp.where(
                row == 0, top, jnp.where(row == 1, pltpu.roll(bottom, 1, 0), pltpu.roll(top, 1, 0))
            )
            bottom = jnp.where(row == 7, top, pltpu.roll(bottom, 7, 0))
            top = next_top
        return count + 1, jnp.max(worst), tuple(upper), tuple(lower)

    def unfinished(carry):
        count, worst, _, _ = carry
        return jnp.logical_and(count < MAX_SWEEPS, worst > 1e-8)

    _, _, upper, lower = lax.while_loop(
        unfinished, sweep, (jnp.int32(0), jnp.float32(1.0), tuple(upper), tuple(lower))
    )

    top, bottom = squares(upper, lower)
    rank_top, rank_bottom = zero, zero
    for k in range(BLOCK):
        mine = spread_rows(top, k) if k < 8 else spread_rows(bottom, 15 - k)
        before_top = (mine < top) | ((mine == top) & (k < row))
        before_bottom = (mine < bottom) | ((mine == bottom) & (k < 15 - row))
        rank_top = rank_top + jnp.where(before_top, 1.0, 0.0)
        rank_bottom = rank_bottom + jnp.where(before_bottom, 1.0, 0.0)
    inverse_top, inverse_bottom = lax.rsqrt(top), lax.rsqrt(bottom)
    value_top, value_bottom = top * inverse_top, bottom * inverse_bottom
    lane_float = lane.astype(jnp.float32)
    theta = zero
    vectors_u, vectors_l = zero, zero
    for k in range(BLOCK):

        def of(first, second):
            return spread_rows(first, k) if k < 8 else spread_rows(second, 15 - k)

        here = lane_float == of(rank_top, rank_bottom)
        inverse_norm = of(inverse_top, inverse_bottom)
        theta = jnp.where(here, of(value_top, value_bottom), theta)
        vectors_u = jnp.where(here, upper[k] * inverse_norm, vectors_u)
        vectors_l = jnp.where(here, lower[k] * inverse_norm, vectors_l)
    theta = mean + scale * (theta - 1.0)
    theta_ref[...] = theta
    on_row = jnp.sum(jnp.where(row == lane, theta, 0.0), axis=1, keepdims=True)
    theta_rows_ref[...] = jnp.broadcast_to(on_row, (8, LANES))
    vectors = jnp.concatenate([vectors_u, vectors_l], axis=0)
    mix = dot(transposed, vectors, (((1,), (0,)), ((), ())))
    for j in range(MODES):
        mix_ref[j] = jnp.broadcast_to(mix[:, j : j + 1], (BLOCK, LANES))


def ritz_pairs(terms):
    return call(
        ritz_kernel,
        [(8, LANES), (8, LANES), (MODES, BLOCK, LANES)],
        [terms],
        flops=10000000,
        name="ritz_pairs",
    )


def inner(a, b):
    return lax.dot_general(
        a, b, (((1,), (1,)), ((), ())), precision=HIGHEST, preferred_element_type=jnp.float32
    )


def folded(products, offset):
    height, width = products.shape
    row = lax.broadcasted_iota(jnp.int32, (height, width), 0)
    column = lax.broadcasted_iota(jnp.int32, (height, width), 1)
    same = jnp.where((row & 7) == (column & 7), products, 0.0)
    sums = jnp.sum(same.reshape(height // 8, 8, width), axis=1)
    row = lax.broadcasted_iota(jnp.int32, (width, LANES), 0)
    lane = lax.broadcasted_iota(jnp.int32, (width, LANES), 1)
    place = jnp.where((row >> 3) + offset == lane, 1.0, 0.0).astype(jnp.float32)
    return jnp.dot(sums, place, precision=HIGHEST, preferred_element_type=jnp.float32)


def rows_of(x):
    return x.reshape(x.shape[0] * x.shape[1], x.shape[2])


def store_y_differences(source_ref, beside_ref, wide_ref, change_ref, z):
    count, _, ny, _ = source_ref.shape

    @pl.loop(0, count)
    def _(a):
        wide_ref[6:8, :] = beside_ref[a, z, :2]
        wide_ref[8 : 8 + ny, :] = source_ref[a, z]
        wide_ref[8 + ny : 10 + ny, :] = beside_ref[a, z, 2:]
        wide = wide_ref[...]
        change = roll(wide, -1, 0) + roll(wide, 1, 0) - 2.0 * wide
        change_ref[a] = change[8 : 8 + ny]


def plane_stiff(field, change, curvature, stiffness):
    rows = rows_of(field)
    along_x = roll(rows, -1, 1) + roll(rows, 1, 1) - 2.0 * rows
    weight = jnp.broadcast_to(stiffness[None], field.shape)
    weight = rows_of(weight)
    along_y = rows_of(change)
    bent = rows_of(field * curvature[None])
    return inner(bent, rows) + inner(along_x * weight, along_x) + inner(along_y * weight, along_y)


def first_local_kernel(block_ref, beside_ref, curvature_ref, stiffness_ref, tile_ref, wide_ref, change_ref):
    nz, ny, nx = curvature_ref.shape
    wide_ref[...] = jnp.zeros(wide_ref.shape, jnp.float32)
    gram = jnp.zeros((8 * BLOCK, 8 * BLOCK), jnp.float32)
    stiff = jnp.zeros((8 * BLOCK, 8 * BLOCK), jnp.float32)
    for z in range(nz):
        store_y_differences(block_ref, beside_ref, wide_ref, change_ref, z)
        for start in range(0, ny, 8):
            part = slice(start, start + 8)
            field = block_ref[:, z, part, :]
            rows = rows_of(field)
            gram = gram + inner(rows, rows)
            stiff = stiff + plane_stiff(
                field, change_ref[:, part, :], curvature_ref[z, part, :], stiffness_ref[z, part, :]
            )
    half = 8 * HALF
    tile_ref[...] = (
        folded(gram[:half], 0)
        + folded(gram[half:], BLOCK)
        + folded(stiff[:half], 2 * BLOCK)
        + folded(stiff[half:], 3 * BLOCK)
    )


def first_local(block, beside, curvature, stiffness):
    nz, ny, nx = curvature.shape
    (tile,) = call(
        first_local_kernel,
        [(8, LANES)],
        [block, beside, curvature, stiffness],
        scratch=[
            pltpu.VMEM((ny + 16, nx), jnp.float32),
            pltpu.VMEM((BLOCK, ny, nx), jnp.float32),
        ],
        flops=100000000,
        name="first_local",
    )
    return tile


def second_local_kernel(
    modes_ref, images_ref, corrections_ref, beside_ref, curvature_ref, stiffness_ref,
    tile_ref, wide_ref, change_ref,
):
    nz, ny, nx = curvature_ref.shape
    wide_ref[...] = jnp.zeros(wide_ref.shape, jnp.float32)
    half = 8 * HALF
    gram = jnp.zeros((2 * half, 2 * half), jnp.float32)
    cross = jnp.zeros((half, 2 * half), jnp.float32)
    back = jnp.zeros((half, half), jnp.float32)
    low = jnp.zeros((half, half), jnp.float32)
    for z in range(nz):
        store_y_differences(corrections_ref, beside_ref, wide_ref, change_ref, z)
        for start in range(0, ny, 8):
            part = slice(start, start + 8)
            field = corrections_ref[:, z, part, :]
            second = rows_of(field)
            rows = jnp.concatenate([rows_of(modes_ref[:, z, part, :]), second], axis=0)
            images = rows_of(images_ref[:, z, part, :])
            gram = gram + inner(rows, rows)
            cross = cross + inner(images, rows)
            back = back + inner(second, images)
            low = low + plane_stiff(
                field, change_ref[:, part, :], curvature_ref[z, part, :], stiffness_ref[z, part, :]
            )
    tile_ref[...] = (
        folded(gram[:half], 0)
        + folded(gram[half:], BLOCK)
        + folded(cross, 2 * BLOCK)
        + (folded(back, 3 * BLOCK) + folded(low, 3 * BLOCK + HALF))
    )


def second_local(modes, images, corrections, beside, curvature, stiffness):
    nz, ny, nx = curvature.shape
    (tile,) = call(
        second_local_kernel,
        [(8, LANES)],
        [modes, images, corrections, beside, curvature, stiffness],
        scratch=[
            pltpu.VMEM((ny + 16, nx), jnp.float32),
            pltpu.VMEM((HALF, ny, nx), jnp.float32),
        ],
        flops=80000000,
        name="second_local",
    )
    return tile


def across_kernel(block_ref, after_ref, layers_ref, tile_ref, copies_ref):
    count, nz, ny, nx = block_ref.shape
    half = 8 * HALF
    stiff = jnp.zeros((8 * count, 8 * count), jnp.float32)

    def layer(k, part):
        return block_ref[:, k, part, :] if k < nz else after_ref[:, k - nz, part, :]

    for z in range(1, nz + 1):
        for start in range(0, ny, 8):
            part = slice(start, start + 8)
            change = (layer(z + 1, part) + layer(z - 1, part)) - 2.0 * layer(z, part)
            weight = layers_ref[z + 1, part, :]
            stiff = stiff + inner(rows_of(change * weight[None]), rows_of(change))
    tile = tile_ref[...]
    if count == BLOCK:
        tile = tile + folded(stiff[:half], 2 * BLOCK) + folded(stiff[half:], 3 * BLOCK)
    else:
        tile = tile + folded(stiff, 3 * BLOCK + HALF)
    for k in range(0, copies_ref.shape[0], 8):
        copies_ref[k : k + 8, :] = tile


def across(block, after, layers, tile):
    total = lax.axis_size("gz") * lax.axis_size("gy")
    (copies,) = call(
        across_kernel,
        [(8 * total, LANES)],
        [block, after, layers, tile],
        flops=25000000,
        name="across",
    )
    return copies


def roll(x, shift, axis):
    return pltpu.roll(x, shift % x.shape[axis], axis)


def apply_hessian(before, own, after, wide, curvature, stiff_layers, stiff_wide, layer):
    layers = before[-2:] + own + after[:2]

    def flux(k):
        middle = layers[k + 2]
        return stiff_layers(k + 1) * ((layers[k + 3] + layers[k + 1]) - 2.0 * middle)

    field = own[layer]
    total = curvature * field + (flux(layer + 1) + flux(layer - 1) - 2.0 * flux(layer))
    change = roll(field, -1, 1) + roll(field, 1, 1) - 2.0 * field
    change = stiff_layers(layer + 1) * change
    total = total + (roll(change, -1, 1) + roll(change, 1, 1) - 2.0 * change)
    change = stiff_wide * (roll(wide, -1, 0) + roll(wide, 1, 0) - 2.0 * wide)
    change = roll(change, -1, 0) + roll(change, 1, 0) - 2.0 * change
    rows = field.shape[0]
    return total + change[8 : 8 + rows]


def update_kernel(
    mix_ref, theta_ref, block_ref, before_ref, after_ref, beside_ref,
    curvature_ref, inverse_ref, stiff_layers_ref, stiff_wide_ref,
    modes_ref, images_ref, corrections_ref, layers_ref, wide_ref,
):
    nz, ny, nx = curvature_ref.shape
    wide_ref[...] = jnp.zeros(wide_ref.shape, jnp.float32)
    for source, offset in ((before_ref, 0), (block_ref, nz), (after_ref, 2 * nz)):

        @pl.loop(0, nz)
        def _(z, source=source, offset=offset):
            for start in range(0, nx, LANES):
                lanes = slice(start, start + LANES)
                parts = [source[a, z, :, lanes] for a in range(BLOCK)]
                for j in range(MODES):
                    mixed = mix_ref[j, 0:1, :] * parts[0]
                    for a in range(1, BLOCK):
                        mixed = mixed + mix_ref[j, a : a + 1, :] * parts[a]
                    layers_ref[j, offset + z, :, lanes] = mixed
                    if source is block_ref:
                        wide_ref[j, z, 8 : 8 + ny, lanes] = mixed

    @pl.loop(0, nz)
    def _(z):
        for start in range(0, nx, LANES):
            lanes = slice(start, start + LANES)
            parts = [beside_ref[a, z, :, lanes] for a in range(BLOCK)]
            for j in range(MODES):
                mixed = mix_ref[j, 0:1, :] * parts[0]
                for a in range(1, BLOCK):
                    mixed = mixed + mix_ref[j, a : a + 1, :] * parts[a]
                wide_ref[j, z, 6:8, lanes] = mixed[:2]
                wide_ref[j, z, 8 + ny : 10 + ny, lanes] = mixed[2:]

    @pl.loop(0, MODES)
    def _(j):
        layers = [layers_ref[j, k] for k in range(3 * nz)]
        theta = jnp.broadcast_to(theta_ref[pl.ds(j, 1), :1], (1, nx))
        for z in range(nz):
            image = apply_hessian(
                layers[:nz], layers[nz : 2 * nz], layers[2 * nz :], wide_ref[j, z],
                curvature_ref[z], lambda k: stiff_layers_ref[k], stiff_wide_ref[z], z,
            )
            mode = layers[nz + z]
            images_ref[j, z] = image
            modes_ref[j, z] = mode
            corrections_ref[j, z] = (image - theta * mode) * inverse_ref[z]


def update(mix, theta_rows, block, before, after, beside, fields):
    curvature, inverse, stiff_layers, stiff_wide = fields
    nz, ny, nx = curvature.shape
    return call(
        update_kernel,
        [(MODES, nz, ny, nx)] * 3,
        [mix, theta_rows, block, before, after, beside, curvature, inverse, stiff_layers, stiff_wide],
        scratch=[
            pltpu.VMEM((MODES, 3 * nz, ny, nx), jnp.float32),
            pltpu.VMEM((MODES, nz, ny + 16, nx), jnp.float32),
        ],
        name="update",
    )


def images_kernel(
    block_ref, before_ref, after_ref, beside_ref,
    curvature_ref, stiff_layers_ref, stiff_wide_ref, images_ref, wide_ref,
):
    nz, ny, nx = curvature_ref.shape
    wide_ref[...] = jnp.zeros(wide_ref.shape, jnp.float32)

    @pl.loop(0, MODES)
    def _(j):
        for z in range(nz):
            wide_ref[z, 6:8, :] = beside_ref[j, z, :2]
            wide_ref[z, 8 : 8 + ny, :] = block_ref[j, z]
            wide_ref[z, 8 + ny : 10 + ny, :] = beside_ref[j, z, 2:]
        before = [before_ref[j, z] for z in range(nz)]
        own = [block_ref[j, z] for z in range(nz)]
        after = [after_ref[j, z] for z in range(nz)]
        for z in range(nz):
            images_ref[j, z] = apply_hessian(
                before, own, after, wide_ref[z],
                curvature_ref[z], lambda k: stiff_layers_ref[k], stiff_wide_ref[z], z,
            )


def images_of(block, before, after, beside, fields):
    curvature, _, stiff_layers, stiff_wide = fields
    nz, ny, nx = curvature.shape
    (images,) = call(
        images_kernel,
        [(MODES, nz, ny, nx)],
        [block, before, after, beside, curvature, stiff_layers, stiff_wide],
        scratch=[pltpu.VMEM((nz, ny + 16, nx), jnp.float32)],
        name="images",
    )
    return images


def density_kernel(
    factor, mix_ref, theta_ref, modes_ref, corrections_ref, first_ref, second_ref,
    mode_density_ref, residual_density_ref,
):
    nz, ny, nx = mode_density_ref.shape

    @pl.loop(0, nz)
    def _(z):
        for start in range(0, nx, LANES):
            lanes = slice(start, start + LANES)
            vectors = [modes_ref[a, z, :, lanes] for a in range(MODES)]
            vectors = vectors + [corrections_ref[a, z, :, lanes] for a in range(MODES)]
            images = [first_ref[a, z, :, lanes] for a in range(MODES)]
            images = images + [second_ref[a, z, :, lanes] for a in range(MODES)]
            mode_sum = jnp.zeros((ny, LANES), jnp.float32)
            residual_sum = jnp.zeros((ny, LANES), jnp.float32)
            for j in range(MODES):
                mode = mix_ref[j, 0:1, :] * vectors[0]
                image = mix_ref[j, 0:1, :] * images[0]
                for a in range(1, BLOCK):
                    mode = mode + mix_ref[j, a : a + 1, :] * vectors[a]
                    image = image + mix_ref[j, a : a + 1, :] * images[a]
                residual = image - theta_ref[j : j + 1, :] * mode
                mode_sum = mode_sum + mode * mode
                residual_sum = residual_sum + residual * residual
            mode_density_ref[z, :, lanes] = factor * mode_sum
            residual_density_ref[z, :, lanes] = factor * residual_sum


def densities(factor, mix, theta_rows, modes, corrections, first, second):
    shape = modes.shape[1:]
    return call(
        functools.partial(density_kernel, factor),
        [shape, shape],
        [mix, theta_rows, modes, corrections, first, second],
        name="densities",
    )


def local(initial_block, concentration, stiffness):
    nz, ny, nx = concentration.shape
    cells_total = nz * ny * nx * lax.axis_size("gz") * lax.axis_size("gy")
    curvature = 3.0 * concentration * concentration - 1.0

    after = from_next(initial_block)
    beside = rows_beside(initial_block, 2)
    tile = first_local(initial_block, beside, curvature, stiffness)

    late, tile = lax.optimization_barrier((stiffness, tile))
    next_stiffness = from_next(late)
    previous_stiffness = from_previous(late)
    beside_stiffness = rows_beside(late, 1)
    layers = jnp.concatenate([previous_stiffness[nz - 1 :], stiffness, next_stiffness[:1]], axis=0)
    blank = jnp.zeros((nz, 6, nx), jnp.float32)
    wide = jnp.concatenate(
        [blank, beside_stiffness[:, :2], stiffness, beside_stiffness[:, 2:], blank], axis=1
    )
    precondition = (curvature + 2.0) + 12.0 * stiffness
    precondition = precondition + (layers[2:] + layers[:-2])
    precondition = precondition + (wide[:, 9 : 9 + ny] + wide[:, 7 : 7 + ny])
    precondition = precondition + (jnp.roll(stiffness, -1, 2) + jnp.roll(stiffness, 1, 2))
    fields = (curvature, 1.0 / precondition, layers, wide)

    held, after, tile, fields = lax.optimization_barrier((initial_block, after, tile, fields))
    layers = fields[2]
    before = from_previous(held)
    terms = all_terms(across(initial_block, after, layers, tile))
    _, theta_rows, mix = ritz_pairs(terms)
    modes, mode_images, corrections = update(
        mix, theta_rows, initial_block, before, after, beside, fields
    )

    after = from_next(corrections)
    beside = rows_beside(corrections, 2)
    tile = second_local(modes, mode_images, corrections, beside, curvature, stiffness)
    held, after, tile = lax.optimization_barrier((corrections, after, tile))
    before = from_previous(held)
    terms = all_terms(across(corrections, after, layers, tile))
    theta, theta_rows, mix = ritz_pairs(terms)
    correction_images = images_of(corrections, before, after, beside, fields)
    mode_density, residual_density = densities(
        float(cells_total / MODES), mix, theta_rows, modes, corrections, mode_images, correction_images
    )
    return (theta[0, :MODES], mode_density, residual_density)


def solution(mesh):
    return jax.shard_map(
        local,
        mesh=mesh,
        in_specs=(P("img", "gz", "gy", None), P(("img", "gz"), "gy", None), P("gz", "gy", None)),
        out_specs=(P("img"), P(("img", "gz"), "gy", None), P(("img", "gz"), "gy", None)),
        check_vma=False,
    )
```

time: 767 us -> 94.6 us (0.12)
  matrix products: 354 us -> 0 us
  local copies, waits for them, and re-layouts: 172 us -> 3.18 us
  blocking collectives: 127 us -> 34.2 us
  waiting for transfers between devices: 57.9 us -> 10 us
  other arithmetic: 36.1 us -> 0.28 us
  Pallas kernels: 0 us -> 30.3 us
    dot_general x1930 -> x0, matrix products: 354 us -> none  [the longest x240 58.5 us: rotate_round(): jnp.dot(matrix, right_table, precision=highest)]
    gather x246 -> x0, local copies, waits for them, and re-layouts: 163 us -> none  [the longest x240 159 us: rotate_round(): diagonal_now = jnp.diagonal(matrix)]
    psum x4 -> x0, blocking collectives: 127 us -> none  [the longest x2 65.4 us: local(): gram_matrix = lax.psum(gram_local, ('gz', 'gy'))]
    ppermute x12 -> x9, waiting for transfers between devices: 57.9 us -> 10 us  [the longest x3 4.84 us: from_next(): return lax.ppermute(x, 'gz', [((i + 1) % size, i) for i in range(size)])]
    all_to_all x0 -> x2, blocking collectives: none -> 34.2 us  [all_terms(): return lax.all_to_all(copies, ('gz', 'gy'), 0, 0, tiled=True)]
    pallas_call x0 -> x9, Pallas kernels: none -> 30.3 us  [call(): pl.pallas_call(kernel, out_shape=out_shape, in_specs=[VMEM] * len(args),...]
    mul x249 -> x0, other arithmetic: 21.1 us -> none  [the longest x240 18.7 us: rotate_round(): right_table * opposite[None, :]]
    another operation x10 -> x0, other arithmetic: 8.01 us -> none  [the longest x6 4.26 us: local(): lower_factor = jnp.linalg.cholesky(gram_matrix)]
  transfers between devices with their start and end apart: 12 -> 9, of which waited for: 9 -> 5; matrix products, arithmetic and copies ran while one was open for 1% -> 3% of each run, Pallas kernels for 0% -> 25%
where the time goes in v2:
time: 94.6 us; the launch traced here: 94.7 us
  blocking collectives  34.2 us (36%)
  Pallas kernels  30.3 us (32%)
  starting transfers between devices  16 us (17%)
  waiting for transfers between devices  10 us (11%)
  local copies, waits for them, and re-layouts  3.18 us (3%)
    all_to_all x2, blocking collectives, all_terms(): return lax.all_to_all(copies, ('gz', 'gy'), 0, 0, tiled=True)  34.2 us
    pallas_call x9, Pallas kernels, call(): pl.pallas_call(kernel, out_shape=out_shape, in_specs=[VMEM] * len(args),...  30.3 us
    ppermute x3, starting transfers between devices, from_next(): return lax.ppermute(x, 'gz', [((i + 1) % size, i) for i in range(size)])  12.3 us
    ppermute x3, waiting for transfers between devices, from_next(): return lax.ppermute(x, 'gz', [((i + 1) % size, i) for i in range(size)])  4.84 us
    ppermute x3, waiting for transfers between devices, from_previous(): return lax.ppermute(x, 'gz', [(i, (i + 1) % size) for i in range(size)])  3.45 us
    ppermute x3, starting transfers between devices, from_previous(): return lax.ppermute(x, 'gz', [(i, (i + 1) % size) for i in range(size)])  3.01 us
  transfers between devices with their start and end apart: 9, of which 5 were waited for; matrix products, arithmetic and copies ran while one was open for 3% of the time, Pallas kernels for 25%

profile of v2, /device:TPU:0, one launch (start us, length us, event | category | flops | bytes accessed | tf_op | source)
XLA Modules:
  0.0 94.7 jit_solution(10348233560264854064)
XLA Ops:
  0.6 6.1 %collective-permute-start = (f32[16,2,16,384]{3,2,1,0:T(8,128)}, f32[16,2,16,384]{3,2,1,0:T(8,128)S(1)}, u32[]{:S(2)}, u32[]{:S(2)}) collective-permute-start(f32[16,2,16,384]{3,2,1,0:T(8,128)} %block_ref.5), channel_id=1, source_target_pairs={{2,0},{4,2},{6,4},{8,6},{10,8},{12,10},{14,12},{0,14},{3,1},{5,3},... | collective-permute-start | bytes 2359304 | tf_op jit(solution)/shard_map/ppermute | solution.py:36
  6.7 1.2 %fusion.7 = (f32[16,2,2,384]{3,2,1,0:T(2,128)S(1)}, f32[16,2,2,384]{3,2,1,0:T(2,128)S(1)}) fusion(f32[16,2,16,384]{3,2,1,0:T(8,128)} %block_ref.5), kind=kLoop, calls=%fused_computation.18 | loop fusion | bytes 393216 | tf_op jit(solution)/shard_map/slice | solution.py:45
  7.9 0.1 pad_maximum_fusion
  8.0 0.0 copy-start.2
  8.0 0.1 collective-permute-start.1
  8.1 1.0 %fusion.10 = (f32[2,16,383]{2,1,0:T(8,128)S(1)}, f32[2,16,383]{2,1,0:T(8,128)S(1)}) fusion(f32[2,16,384]{2,1,0:T(8,128)} %stiffness_ref.3), kind=kLoop, calls=%fused_computation.21 | loop fusion | bytes 196096 | tf_op jit(solution)/shard_map/jit(_roll_static)/slice | solution.py:615
  9.1 0.4 collective-permute-done.1.beside_ref
  9.5 0.3 copy-done.1
  9.8 4.9 %first_local.1.tile_ref = f32[8,128]{1,0:T(8,128)S(1)} custom-call(f32[16,2,16,384]{3,2,1,0:T(8,128)S(1)} %copy-done, f32[16,2,4,384]{3,2,1,0:T(4,128)S(1)} %collective-permute-done.1.beside_ref, f32[2,16,384]{2,1,0:T(8,128)S(1)} %fusion.6.curvature_ref, f32[2,16,384]{2,1,0:T(8,128)S(1)} %copy-done.1), custom_call_target="tpu_custom_call" | custom-call | flops 100000000 | bytes 1085440 | tf_op jit(solution)/shard_map/first_local/pallas_call | solution.py:22
  14.8 0.6 collective-permute-start.4
  15.4 0.1 fusion.9
  15.4 4.7 %collective-permute-start.2 = (f32[2,16,384]{2,1,0:T(8,128)S(1)}, f32[2,16,384]{2,1,0:T(8,128)S(1)}, u32[]{:S(2)}, u32[]{:S(2)}) collective-permute-start(f32[2,16,384]{2,1,0:T(8,128)S(1)} %copy-done.1), channel_id=1, source_target_pairs={{2,0},{4,2},{6,4},{8,6},{10,8},{12,10},{14,12},{0,14},{3,1},{5,3},... | collective-permute-start | bytes 147464 | tf_op jit(solution)/shard_map/ppermute | solution.py:36
  20.2 3.4 %collective-permute-done.3 = f32[2,16,384]{2,1,0:T(8,128)S(1)} collective-permute-done((f32[2,16,384]{2,1,0:T(8,128)S(1)}, f32[2,16,384]{2,1,0:T(8,128)S(1)}, u32[]{:S(2)}, u32[]{:S(2)}) %collective-permute-start.3) | collective-permute-done | bytes 49184 | tf_op jit(solution)/shard_map/ppermute | solution.py:41
  23.7 1.1 %collective-permute-done.2 = f32[2,16,384]{2,1,0:T(8,128)S(1)} collective-permute-done((f32[2,16,384]{2,1,0:T(8,128)S(1)}, f32[2,16,384]{2,1,0:T(8,128)S(1)}, u32[]{:S(2)}, u32[]{:S(2)}) %collective-permute-start.2) | collective-permute-done | bytes 49184 | tf_op jit(solution)/shard_map/ppermute | solution.py:36
  24.8 0.1 fusion.3.inverse_ref
  24.9 1.5 %collective-permute-start.5 = (f32[16,2,16,384]{3,2,1,0:T(8,128)S(1)}, f32[16,2,16,384]{3,2,1,0:T(8,128)S(1)}, u32[]{:S(2)}, u32[]{:S(2)}) collective-permute-start(f32[16,2,16,384]{3,2,1,0:T(8,128)S(1)} %copy-done), channel_id=1, source_target_pairs={{0,2},{2,4},{4,6},{6,8},{8,10},{10,12},{12,14},{14,0},{1,3},{3,5},... | collective-permute-start | bytes 2359304 | tf_op jit(solution)/shard_map/ppermute | solution.py:41
  26.4 1.4 %across.2 = f32[128,128]{1,0:T(8,128)S(1)} custom-call(f32[16,2,16,384]{3,2,1,0:T(8,128)S(1)} %copy-done, f32[16,2,16,384]{3,2,1,0:T(8,128)S(1)} %collective-permute-done.after_ref, f32[4,16,384]{2,1,0:T(8,128)S(1)} %pad_maximum_fusion.1.layers_ref.stiff_layers_ref, f32[8,128]{1,0:T(8,128)S(1)} %first_local.1.tile_ref), custom_call_target="tpu_custom_call" | custom-call | flops 25000000 | bytes 1740800 | tf_op jit(solution)/shard_map/across/pallas_call | solution.py:22
  27.8 22.3 %all_to_all.22 = f32[16,8,128]{2,1,0:T(8,128)S(1)} all-to-all(f32[16,8,128]{2,1,0:T(8,128)S(1)} %bitcast.8), channel_id=1, replica_groups=mesh['img'=2,'gz'=8,'gy'=2] {'gz','gy'}, dimensions={0} | all-to-all | bytes 131072 | tf_op jit(solution)/shard_map/all_to_all | solution.py:62
  50.1 6.3 %ritz_pairs.2 = (f32[8,128]{1,0:T(8,128)}, f32[8,128]{1,0:T(8,128)S(1)}, f32[8,16,128]{2,1,0:T(8,128)S(1)}) custom-call(f32[128,128]{1,0:T(8,128)S(1)} %bitcast.6), custom_call_target="tpu_custom_call" | custom-call | flops 10000000 | bytes 139264 | tf_op jit(solution)/shard_map/ritz_pairs/pallas_call | solution.py:22
  56.4 3.2 %update.1 = (f32[8,2,16,384]{3,2,1,0:T(8,128)S(1)}, f32[8,2,16,384]{3,2,1,0:T(8,128)S(1)}, f32[8,2,16,384]{3,2,1,0:T(8,128)S(1)}) custom-call(f32[8,16,128]{2,1,0:T(8,128)S(1)} %get-tuple-element.30.mix_ref, f32[8,128]{1,0:T(8,128)S(1)} %get-tuple-element.31.theta_ref, f32[16,2,16,384]{3,2,1,0:T(8,128)S(1)} %copy-done, ...), custom_call_target="tpu_custom_call" | custom-call | flops 1000000 | bytes 4100096 | tf_op jit(solution)/shard_map/update/pallas_call | solution.py:22
  59.6 1.5 %collective-permute-start.6 = (f32[8,2,16,384]{3,2,1,0:T(8,128)S(1)}, f32[8,2,16,384]{3,2,1,0:T(8,128)S(1)}, u32[]{:S(2)}, u32[]{:S(2)}) collective-permute-start(f32[8,2,16,384]{3,2,1,0:T(8,128)S(1)} %get-tuple-element.44.corrections_ref.block_ref), channel_id=1, source_target_pairs={{2,0},{4,2},{6,4},{8,6},{10,8},{12,10},{14,12},{0,14},{3,1},{5,3},... | collective-permute-start | bytes 1179656 | tf_op jit(solution)/shard_map/ppermute | solution.py:36
  61.2 0.1 collective-permute-start.7
  61.3 1.3 %collective-permute-done.7.beside_ref = f32[8,2,4,384]{3,2,1,0:T(4,128)S(1)} collective-permute-done((f32[8,2,4,384]{3,2,1,0:T(4,128)S(1)}, f32[8,2,4,384]{3,2,1,0:T(4,128)S(1)}, u32[]{:S(2)}, u32[]{:S(2)}) %collective-permute-start.7) | collective-permute-done | bytes 98336 | tf_op jit(solution)/shard_map/ppermute | solution.py:55
  62.6 4.6 %second_local.1.tile_ref = f32[8,128]{1,0:T(8,128)S(1)} custom-call(f32[8,2,16,384]{3,2,1,0:T(8,128)S(1)} %get-tuple-element.37.modes_ref, f32[8,2,16,384]{3,2,1,0:T(8,128)S(1)} %get-tuple-element.38.images_ref.first_ref, f32[8,2,16,384]{3,2,1,0:T(8,128)S(1)} %get-tuple-element.44.corrections_ref.block_ref, ...), custom_call_target="tpu_custom_call" | custom-call | flops 80000000 | bytes 1380352 | tf_op jit(solution)/shard_map/second_local/pallas_call | solution.py:22
  67.2 3.8 %collective-permute-done.6.after_ref = f32[8,2,16,384]{3,2,1,0:T(8,128)S(1)} collective-permute-done((f32[8,2,16,384]{3,2,1,0:T(8,128)S(1)}, f32[8,2,16,384]{3,2,1,0:T(8,128)S(1)}, u32[]{:S(2)}, u32[]{:S(2)}) %collective-permute-start.6) | collective-permute-done | bytes 393248 | tf_op jit(solution)/shard_map/ppermute | solution.py:36
  71.0 1.5 %collective-permute-start.8 = (f32[8,2,16,384]{3,2,1,0:T(8,128)S(1)}, f32[8,2,16,384]{3,2,1,0:T(8,128)S(1)}, u32[]{:S(2)}, u32[]{:S(2)}) collective-permute-start(f32[8,2,16,384]{3,2,1,0:T(8,128)S(1)} %get-tuple-element.44.corrections_ref.block_ref), channel_id=1, source_target_pairs={{0,2},{2,4},{4,6},{6,8},{8,10},{10,12},{12,14},{14,0},{1,3},{3,5},... | collective-permute-start | bytes 1179656 | tf_op jit(solution)/shard_map/ppermute | solution.py:41
  72.5 0.7 across.3
  73.3 11.9 %all_to_all.23 = f32[16,8,128]{2,1,0:T(8,128)S(1)} all-to-all(f32[16,8,128]{2,1,0:T(8,128)S(1)} %bitcast.9), channel_id=1, replica_groups=mesh['img'=2,'gz'=8,'gy'=2] {'gz','gy'}, dimensions={0} | all-to-all | bytes 131072 | tf_op jit(solution)/shard_map/all_to_all | solution.py:62
  85.1 5.9 %ritz_pairs.3 = (f32[8,128]{1,0:T(8,128)S(1)}, f32[8,128]{1,0:T(8,128)S(1)}, f32[8,16,128]{2,1,0:T(8,128)S(1)}) custom-call(f32[128,128]{1,0:T(8,128)S(1)} %bitcast.7), custom_call_target="tpu_custom_call" | custom-call | flops 10000000 | bytes 139264 | tf_op jit(solution)/shard_map/ritz_pairs/pallas_call | solution.py:22
  91.0 0.5 slice_bitcast_fusion
  91.5 1.5 %images.1.second_ref = f32[8,2,16,384]{3,2,1,0:T(8,128)S(1)} custom-call(f32[8,2,16,384]{3,2,1,0:T(8,128)S(1)} %get-tuple-element.44.corrections_ref.block_ref, f32[8,2,16,384]{3,2,1,0:T(8,128)S(1)} %collective-permute-done.8.before_ref, f32[8,2,16,384]{3,2,1,0:T(8,128)S(1)} %collective-permute-done.6.after_ref, ...), custom_call_target="tpu_custom_call" | custom-call | flops 1000000 | bytes 1916928 | tf_op jit(solution)/shard_map/images/pallas_call | solution.py:22
  93.0 1.7 %densities.1 = (f32[2,16,384]{2,1,0:T(8,128)}, f32[2,16,384]{2,1,0:T(8,128)}) custom-call(f32[8,16,128]{2,1,0:T(8,128)S(1)} %get-tuple-element.42.mix_ref, f32[8,128]{1,0:T(8,128)S(1)} %get-tuple-element.43.theta_ref, f32[8,2,16,384]{3,2,1,0:T(8,128)S(1)} %get-tuple-element.37.modes_ref, f32[8,2,16,384]{3,2,1,0:T(8,128)S(1)} %get-tuple-element.44.corrections_ref.block_ref, ...), custom_call_target="tpu_custom_call" | custom-call | flops 1000000 | bytes 1740800 | tf_op jit(solution)/shard_map/densities/pallas_call | solution.py:22
  (20 shorter events, 0.2 us)
Async XLA Ops:
  0.6 8.9 %copy-start = (f32[16,2,16,384]{3,2,1,0:T(8,128)S(1)}, f32[16,2,16,384]{3,2,1,0:T(8,128)}, u32[]{:S(2)}) copy-start(f32[16,2,16,384]{3,2,1,0:T(8,128)} %block_ref.5) | copy-start | bytes 2359300
  0.6 24.2 %collective-permute-start = (f32[16,2,16,384]{3,2,1,0:T(8,128)}, f32[16,2,16,384]{3,2,1,0:T(8,128)S(1)}, u32[]{:S(2)}, u32[]{:S(2)}) collective-permute-start(f32[16,2,16,384]{3,2,1,0:T(8,128)} %block_ref.5), channel_id=1, source_target_pairs={{2,0},{4,2},{6,4},{8,6},{10,8},{12,10},{14,12},{0,14},{3,1},{5,3},... | collective-permute-start | bytes 2359304 | tf_op jit(solution)/shard_map/ppermute | solution.py:36
  8.0 1.0 %copy-start.2 = (f32[2,16,384]{2,1,0:T(8,128)S(1)}, f32[2,16,384]{2,1,0:T(8,128)}, u32[]{:S(2)}) copy-start(f32[2,16,384]{2,1,0:T(8,128)} %param.4) | copy-start | bytes 147460
  8.0 1.5 %collective-permute-start.1 = (f32[16,2,4,384]{3,2,1,0:T(4,128)S(1)}, f32[16,2,4,384]{3,2,1,0:T(4,128)S(1)}, u32[]{:S(2)}, u32[]{:S(2)}) collective-permute-start(f32[16,2,4,384]{3,2,1,0:T(4,128)S(1)} %pad_maximum_fusion), channel_id=1, source_target_pairs={{0,1},{1,0},{2,3},{3,2},{4,5},{5,4},{6,7},{7,6},{8,9},{9,8},{10,11... | collective-permute-start | bytes 589832 | tf_op jit(solution)/shard_map/ppermute | solution.py:55
  9.0 0.8 copy-start.1
  14.8 5.4 %collective-permute-start.4 = (f32[2,4,384]{2,1,0:T(4,128)S(1)}, f32[2,4,384]{2,1,0:T(4,128)S(1)}, u32[]{:S(2)}, u32[]{:S(2)}) collective-permute-start(f32[2,4,384]{2,1,0:T(4,128)S(1)} %pad_maximum_fusion.7), channel_id=1, source_target_pairs={{0,1},{1,0},{2,3},{3,2},{4,5},{5,4},{6,7},{7,6},{8,9},{9,8},{10,11... | collective-permute-start | bytes 36872 | tf_op jit(solution)/shard_map/ppermute | solution.py:55
  15.4 8.2 %collective-permute-start.3 = (f32[2,16,384]{2,1,0:T(8,128)S(1)}, f32[2,16,384]{2,1,0:T(8,128)S(1)}, u32[]{:S(2)}, u32[]{:S(2)}) collective-permute-start(f32[2,16,384]{2,1,0:T(8,128)S(1)} %copy-done.1), channel_id=1, source_target_pairs={{0,2},{2,4},{4,6},{6,8},{8,10},{10,12},{12,14},{14,0},{1,3},{3,5},... | collective-permute-start | bytes 147464 | tf_op jit(solution)/shard_map/ppermute | solution.py:41
  15.4 9.3 %collective-permute-start.2 = (f32[2,16,384]{2,1,0:T(8,128)S(1)}, f32[2,16,384]{2,1,0:T(8,128)S(1)}, u32[]{:S(2)}, u32[]{:S(2)}) collective-permute-start(f32[2,16,384]{2,1,0:T(8,128)S(1)} %copy-done.1), channel_id=1, source_target_pairs={{2,0},{4,2},{6,4},{8,6},{10,8},{12,10},{14,12},{0,14},{3,1},{5,3},... | collective-permute-start | bytes 147464 | tf_op jit(solution)/shard_map/ppermute | solution.py:36
  24.9 31.5 %collective-permute-start.5 = (f32[16,2,16,384]{3,2,1,0:T(8,128)S(1)}, f32[16,2,16,384]{3,2,1,0:T(8,128)S(1)}, u32[]{:S(2)}, u32[]{:S(2)}) collective-permute-start(f32[16,2,16,384]{3,2,1,0:T(8,128)S(1)} %copy-done), channel_id=1, source_target_pairs={{0,2},{2,4},{4,6},{6,8},{8,10},{10,12},{12,14},{14,0},{1,3},{3,5},... | collective-permute-start | bytes 2359304 | tf_op jit(solution)/shard_map/ppermute | solution.py:41
  59.6 11.4 %collective-permute-start.6 = (f32[8,2,16,384]{3,2,1,0:T(8,128)S(1)}, f32[8,2,16,384]{3,2,1,0:T(8,128)S(1)}, u32[]{:S(2)}, u32[]{:S(2)}) collective-permute-start(f32[8,2,16,384]{3,2,1,0:T(8,128)S(1)} %get-tuple-element.44.corrections_ref.block_ref), channel_id=1, source_target_pairs={{2,0},{4,2},{6,4},{8,6},{10,8},{12,10},{14,12},{0,14},{3,1},{5,3},... | collective-permute-start | bytes 1179656 | tf_op jit(solution)/shard_map/ppermute | solution.py:36
  61.2 1.4 %collective-permute-start.7 = (f32[8,2,4,384]{3,2,1,0:T(4,128)S(1)}, f32[8,2,4,384]{3,2,1,0:T(4,128)S(1)}, u32[]{:S(2)}, u32[]{:S(2)}) collective-permute-start(f32[8,2,4,384]{3,2,1,0:T(4,128)S(1)} %pad_maximum_fusion.2), channel_id=1, source_target_pairs={{0,1},{1,0},{2,3},{3,2},{4,5},{5,4},{6,7},{7,6},{8,9},{9,8},{10,11... | collective-permute-start | bytes 294920 | tf_op jit(solution)/shard_map/ppermute | solution.py:55
  71.0 20.6 %collective-permute-start.8 = (f32[8,2,16,384]{3,2,1,0:T(8,128)S(1)}, f32[8,2,16,384]{3,2,1,0:T(8,128)S(1)}, u32[]{:S(2)}, u32[]{:S(2)}) collective-permute-start(f32[8,2,16,384]{3,2,1,0:T(8,128)S(1)} %get-tuple-element.44.corrections_ref.block_ref), channel_id=1, source_target_pairs={{0,2},{2,4},{4,6},{6,8},{8,10},{10,12},{12,14},{14,0},{1,3},{3,5},... | collective-permute-start | bytes 1179656 | tf_op jit(solution)/shard_map/ppermute | solution.py:41

commit v3 on v2

--- a/solution.py
+++ b/solution.py
@@ -242,7 +242,7 @@
         vectors_u = jnp.where(here, upper[k] * inverse_norm, vectors_u)
         vectors_l = jnp.where(here, lower[k] * inverse_norm, vectors_l)
     theta = mean + scale * (theta - 1.0)
-    theta_ref[...] = theta
+    theta_ref[...] = theta[0, :MODES]
     on_row = jnp.sum(jnp.where(row == lane, theta, 0.0), axis=1, keepdims=True)
     theta_rows_ref[...] = jnp.broadcast_to(on_row, (8, LANES))
     vectors = jnp.concatenate([vectors_u, vectors_l], axis=0)
@@ -254,7 +254,7 @@
 def ritz_pairs(terms):
     return call(
         ritz_kernel,
-        [(8, LANES), (8, LANES), (MODES, BLOCK, LANES)],
+        [(MODES,), (8, LANES), (MODES, BLOCK, LANES)],
         [terms],
         flops=10000000,
         name="ritz_pairs",
@@ -617,8 +617,9 @@
 
     held, after, tile, fields = lax.optimization_barrier((initial_block, after, tile, fields))
     layers = fields[2]
+    terms = all_terms(across(held, after, layers, tile))
+    held, terms = lax.optimization_barrier((initial_block, terms))
     before = from_previous(held)
-    terms = all_terms(across(initial_block, after, layers, tile))
     _, theta_rows, mix = ritz_pairs(terms)
     modes, mode_images, corrections = update(
         mix, theta_rows, initial_block, before, after, beside, fields
@@ -628,14 +629,15 @@
     beside = rows_beside(corrections, 2)
     tile = second_local(modes, mode_images, corrections, beside, curvature, stiffness)
     held, after, tile = lax.optimization_barrier((corrections, after, tile))
+    terms = all_terms(across(held, after, layers, tile))
+    held, terms = lax.optimization_barrier((corrections, terms))
     before = from_previous(held)
-    terms = all_terms(across(corrections, after, layers, tile))
     theta, theta_rows, mix = ritz_pairs(terms)
     correction_images = images_of(corrections, before, after, beside, fields)
     mode_density, residual_density = densities(
         float(cells_total / MODES), mix, theta_rows, modes, corrections, mode_images, correction_images
     )
-    return (theta[0, :MODES], mode_density, residual_density)
+    return (theta, mode_density, residual_density)
 
 
 def solution(mesh):

time: 94.6 us -> 104 us (1.099)
  waiting for transfers between devices: 10 us -> 32.1 us
  blocking collectives: 34.2 us -> 25.4 us
  starting transfers between devices: 16 us -> 12 us
    ppermute x3, waiting for transfers between devices: 3.45 us -> 25.7 us  [from_previous(): return lax.ppermute(x, 'gz', [(i, (i + 1) % size) for i in range(size)])]
    all_to_all x2, blocking collectives: 34.2 us -> 25.4 us  [all_terms(): return lax.all_to_all(copies, ('gz', 'gy'), 0, 0, tiled=True)]
    ppermute x3, starting transfers between devices: 3.01 us -> 0.25 us  [from_previous(): return lax.ppermute(x, 'gz', [(i, (i + 1) % size) for i in range(size)])]
    ppermute x3, starting transfers between devices: 12.3 us -> 11 us  [from_next(): return lax.ppermute(x, 'gz', [((i + 1) % size, i) for i in range(size)])]
  transfers between devices with their start and end apart: 9 -> 9, of which waited for: 5 -> 7; matrix products, arithmetic and copies ran while one was open for 3% -> 3% of each run, Pallas kernels for 25% -> 21%
where the time goes in v3:
time: 104 us
  waiting for transfers between devices  32.1 us (31%)
  Pallas kernels  30.5 us (29%)
  blocking collectives  25.4 us (24%)
  starting transfers between devices  12 us (12%)
  local copies, waits for them, and re-layouts  2.65 us (3%)
    pallas_call x9, Pallas kernels, call(): pl.pallas_call(kernel, out_shape=out_shape, in_specs=[VMEM] * len(args),...  30.5 us
    ppermute x3, waiting for transfers between devices, from_previous(): return lax.ppermute(x, 'gz', [(i, (i + 1) % size) for i in range(size)])  25.7 us
    all_to_all x2, blocking collectives, all_terms(): return lax.all_to_all(copies, ('gz', 'gy'), 0, 0, tiled=True)  25.4 us
    ppermute x3, starting transfers between devices, from_next(): return lax.ppermute(x, 'gz', [((i + 1) % size, i) for i in range(size)])  11 us
    ppermute x3, waiting for transfers between devices, from_next(): return lax.ppermute(x, 'gz', [((i + 1) % size, i) for i in range(size)])  4.64 us
  transfers between devices with their start and end apart: 9, of which 7 were waited for; matrix products, arithmetic and copies ran while one was open for 3% of the time, Pallas kernels for 21%

profile of v3, /device:TPU:0, one launch (start us, length us, event | category | flops | bytes accessed | tf_op | source)
XLA Modules:
  0.0 103.6 jit_solution(9474102721544702209)
XLA Ops:
  0.6 6.1 %collective-permute-start = (f32[16,2,16,384]{3,2,1,0:T(8,128)}, f32[16,2,16,384]{3,2,1,0:T(8,128)S(1)}, u32[]{:S(2)}, u32[]{:S(2)}) collective-permute-start(f32[16,2,16,384]{3,2,1,0:T(8,128)} %block_ref.4), channel_id=1, source_target_pairs={{2,0},{4,2},{6,4},{8,6},{10,8},{12,10},{14,12},{0,14},{3,1},{5,3},... | collective-permute-start | bytes 2359304 | tf_op jit(solution)/shard_map/ppermute | solution.py:36
  6.7 1.2 %fusion.7 = (f32[16,2,2,384]{3,2,1,0:T(2,128)S(1)}, f32[16,2,2,384]{3,2,1,0:T(2,128)S(1)}) fusion(f32[16,2,16,384]{3,2,1,0:T(8,128)} %block_ref.4), kind=kLoop, calls=%fused_computation.17 | loop fusion | bytes 393216 | tf_op jit(solution)/shard_map/slice | solution.py:45
  7.9 0.1 pad_maximum_fusion
  8.0 0.1 collective-permute-start.1
  8.1 1.0 fusion.10
  9.1 0.4 collective-permute-done.1.beside_ref
  9.5 0.3 copy-done.1
  9.8 4.9 %first_local.1.tile_ref = f32[8,128]{1,0:T(8,128)S(1)} custom-call(f32[16,2,16,384]{3,2,1,0:T(8,128)S(1)} %copy-done, f32[16,2,4,384]{3,2,1,0:T(4,128)S(1)} %collective-permute-done.1.beside_ref, f32[2,16,384]{2,1,0:T(8,128)S(1)} %fusion.6.curvature_ref, f32[2,16,384]{2,1,0:T(8,128)S(1)} %copy-done.1), custom_call_target="tpu_custom_call" | custom-call | flops 100000000 | bytes 1085440 | tf_op jit(solution)/shard_map/first_local/pallas_call | solution.py:22
  14.8 0.6 collective-permute-start.4
  15.4 0.1 fusion.9
  15.4 4.7 %collective-permute-start.2 = (f32[2,16,384]{2,1,0:T(8,128)S(1)}, f32[2,16,384]{2,1,0:T(8,128)S(1)}, u32[]{:S(2)}, u32[]{:S(2)}) collective-permute-start(f32[2,16,384]{2,1,0:T(8,128)S(1)} %copy-done.1), channel_id=1, source_target_pairs={{2,0},{4,2},{6,4},{8,6},{10,8},{12,10},{14,12},{0,14},{3,1},{5,3},... | collective-permute-start | bytes 147464 | tf_op jit(solution)/shard_map/ppermute | solution.py:36
  20.2 3.4 %collective-permute-done.3 = f32[2,16,384]{2,1,0:T(8,128)S(1)} collective-permute-done((f32[2,16,384]{2,1,0:T(8,128)S(1)}, f32[2,16,384]{2,1,0:T(8,128)S(1)}, u32[]{:S(2)}, u32[]{:S(2)}) %collective-permute-start.3) | collective-permute-done | bytes 49184 | tf_op jit(solution)/shard_map/ppermute | solution.py:41
  23.7 1.1 %collective-permute-done.2 = f32[2,16,384]{2,1,0:T(8,128)S(1)} collective-permute-done((f32[2,16,384]{2,1,0:T(8,128)S(1)}, f32[2,16,384]{2,1,0:T(8,128)S(1)}, u32[]{:S(2)}, u32[]{:S(2)}) %collective-permute-start.2) | collective-permute-done | bytes 49184 | tf_op jit(solution)/shard_map/ppermute | solution.py:36
  24.8 0.1 fusion.3.inverse_ref
  24.9 1.4 %across.2 = f32[128,128]{1,0:T(8,128)S(1)} custom-call(f32[16,2,16,384]{3,2,1,0:T(8,128)S(1)} %copy-done, f32[16,2,16,384]{3,2,1,0:T(8,128)S(1)} %collective-permute-done.after_ref, f32[4,16,384]{2,1,0:T(8,128)S(1)} %pad_maximum_fusion.1.layers_ref.stiff_layers_ref, f32[8,128]{1,0:T(8,128)S(1)} %first_local.1.tile_ref), custom_call_target="tpu_custom_call" | custom-call | flops 25000000 | bytes 1740800 | tf_op jit(solution)/shard_map/across/pallas_call | solution.py:22
  26.3 14.3 %all_to_all.24 = f32[16,8,128]{2,1,0:T(8,128)S(1)} all-to-all(f32[16,8,128]{2,1,0:T(8,128)S(1)} %bitcast.6), channel_id=1, replica_groups=mesh['img'=2,'gz'=8,'gy'=2] {'gz','gy'}, dimensions={0} | all-to-all | bytes 131072 | tf_op jit(solution)/shard_map/all_to_all | solution.py:62
  40.7 0.1 collective-permute-start.5
  40.8 6.2 %ritz_pairs.2 = (f32[8]{0:T(128)}, f32[8,128]{1,0:T(8,128)S(1)}, f32[8,16,128]{2,1,0:T(8,128)S(1)}) custom-call(f32[128,128]{1,0:T(8,128)S(1)} %bitcast.4), custom_call_target="tpu_custom_call" | custom-call | flops 10000000 | bytes 135200 | tf_op jit(solution)/shard_map/ritz_pairs/pallas_call | solution.py:22
  47.0 15.3 %collective-permute-done.5.before_ref = f32[16,2,16,384]{3,2,1,0:T(8,128)S(1)} collective-permute-done((f32[16,2,16,384]{3,2,1,0:T(8,128)S(1)}, f32[16,2,16,384]{3,2,1,0:T(8,128)S(1)}, u32[]{:S(2)}, u32[]{:S(2)}) %collective-permute-start.5) | collective-permute-done | bytes 786464 | tf_op jit(solution)/shard_map/ppermute | solution.py:41
  62.4 3.1 %update.1 = (f32[8,2,16,384]{3,2,1,0:T(8,128)S(1)}, f32[8,2,16,384]{3,2,1,0:T(8,128)S(1)}, f32[8,2,16,384]{3,2,1,0:T(8,128)S(1)}) custom-call(f32[8,16,128]{2,1,0:T(8,128)S(1)} %get-tuple-element.36.mix_ref, f32[8,128]{1,0:T(8,128)S(1)} %get-tuple-element.37.theta_ref, f32[16,2,16,384]{3,2,1,0:T(8,128)S(1)} %copy-done, ...), custom_call_target="tpu_custom_call" | custom-call | flops 1000000 | bytes 4100096 | tf_op jit(solution)/shard_map/update/pallas_call | solution.py:22
  65.5 0.2 collective-permute-start.6
  65.8 0.1 collective-permute-start.7
  65.9 1.3 %collective-permute-done.7.beside_ref = f32[8,2,4,384]{3,2,1,0:T(4,128)S(1)} collective-permute-done((f32[8,2,4,384]{3,2,1,0:T(4,128)S(1)}, f32[8,2,4,384]{3,2,1,0:T(4,128)S(1)}, u32[]{:S(2)}, u32[]{:S(2)}) %collective-permute-start.7) | collective-permute-done | bytes 98336 | tf_op jit(solution)/shard_map/ppermute | solution.py:55
  67.2 4.6 %second_local.1.tile_ref = f32[8,128]{1,0:T(8,128)S(1)} custom-call(f32[8,2,16,384]{3,2,1,0:T(8,128)S(1)} %get-tuple-element.43.modes_ref, f32[8,2,16,384]{3,2,1,0:T(8,128)S(1)} %get-tuple-element.44.images_ref.first_ref, f32[8,2,16,384]{3,2,1,0:T(8,128)S(1)} %get-tuple-element.52.corrections_ref.block_ref, ...), custom_call_target="tpu_custom_call" | custom-call | flops 80000000 | bytes 1380352 | tf_op jit(solution)/shard_map/second_local/pallas_call | solution.py:22
  71.8 3.6 %collective-permute-done.6.after_ref = f32[8,2,16,384]{3,2,1,0:T(8,128)S(1)} collective-permute-done((f32[8,2,16,384]{3,2,1,0:T(8,128)S(1)}, f32[8,2,16,384]{3,2,1,0:T(8,128)S(1)}, u32[]{:S(2)}, u32[]{:S(2)}) %collective-permute-start.6) | collective-permute-done | bytes 393248 | tf_op jit(solution)/shard_map/ppermute | solution.py:36
  75.4 0.7 across.3
  76.1 11.1 %all_to_all.25 = f32[16,8,128]{2,1,0:T(8,128)S(1)} all-to-all(f32[16,8,128]{2,1,0:T(8,128)S(1)} %bitcast.7), channel_id=1, replica_groups=mesh['img'=2,'gz'=8,'gy'=2] {'gz','gy'}, dimensions={0} | all-to-all | bytes 131072 | tf_op jit(solution)/shard_map/all_to_all | solution.py:62
  87.2 0.1 collective-permute-start.8
  87.3 6.2 %ritz_pairs.3 = (f32[8]{0:T(128)}, f32[8,128]{1,0:T(8,128)S(1)}, f32[8,16,128]{2,1,0:T(8,128)S(1)}) custom-call(f32[128,128]{1,0:T(8,128)S(1)} %bitcast.5), custom_call_target="tpu_custom_call" | custom-call | flops 10000000 | bytes 135200 | tf_op jit(solution)/shard_map/ritz_pairs/pallas_call | solution.py:22
  93.6 6.9 %collective-permute-done.8.before_ref = f32[8,2,16,384]{3,2,1,0:T(8,128)S(1)} collective-permute-done((f32[8,2,16,384]{3,2,1,0:T(8,128)S(1)}, f32[8,2,16,384]{3,2,1,0:T(8,128)S(1)}, u32[]{:S(2)}, u32[]{:S(2)}) %collective-permute-start.8) | collective-permute-done | bytes 393248 | tf_op jit(solution)/shard_map/ppermute | solution.py:41
  100.5 1.5 %images.1.second_ref = f32[8,2,16,384]{3,2,1,0:T(8,128)S(1)} custom-call(f32[8,2,16,384]{3,2,1,0:T(8,128)S(1)} %get-tuple-element.52.corrections_ref.block_ref, f32[8,2,16,384]{3,2,1,0:T(8,128)S(1)} %collective-permute-done.8.before_ref, f32[8,2,16,384]{3,2,1,0:T(8,128)S(1)} %collective-permute-done.6.after_ref, ...), custom_call_target="tpu_custom_call" | custom-call | flops 1000000 | bytes 1916928 | tf_op jit(solution)/shard_map/images/pallas_call | solution.py:22
  102.0 1.6 %densities.1 = (f32[2,16,384]{2,1,0:T(8,128)}, f32[2,16,384]{2,1,0:T(8,128)}) custom-call(f32[8,16,128]{2,1,0:T(8,128)S(1)} %get-tuple-element.50.mix_ref, f32[8,128]{1,0:T(8,128)S(1)} %get-tuple-element.51.theta_ref, f32[8,2,16,384]{3,2,1,0:T(8,128)S(1)} %get-tuple-element.43.modes_ref, f32[8,2,16,384]{3,2,1,0:T(8,128)S(1)} %get-tuple-element.52.corrections_ref.block_ref, ...), custom_call_target="tpu_custom_call" | custom-call | flops 1000000 | bytes 1740800 | tf_op jit(solution)/shard_map/densities/pallas_call | solution.py:22
  (19 shorter events, 0.2 us)
Async XLA Ops:
  0.6 8.9 %copy-start = (f32[16,2,16,384]{3,2,1,0:T(8,128)S(1)}, f32[16,2,16,384]{3,2,1,0:T(8,128)}, u32[]{:S(2)}) copy-start(f32[16,2,16,384]{3,2,1,0:T(8,128)} %block_ref.4) | copy-start | bytes 2359300
  0.6 24.2 %collective-permute-start = (f32[16,2,16,384]{3,2,1,0:T(8,128)}, f32[16,2,16,384]{3,2,1,0:T(8,128)S(1)}, u32[]{:S(2)}, u32[]{:S(2)}) collective-permute-start(f32[16,2,16,384]{3,2,1,0:T(8,128)} %block_ref.4), channel_id=1, source_target_pairs={{2,0},{4,2},{6,4},{8,6},{10,8},{12,10},{14,12},{0,14},{3,1},{5,3},... | collective-permute-start | bytes 2359304 | tf_op jit(solution)/shard_map/ppermute | solution.py:36
  8.0 1.0 %copy-start.2 = (f32[2,16,384]{2,1,0:T(8,128)S(1)}, f32[2,16,384]{2,1,0:T(8,128)}, u32[]{:S(2)}) copy-start(f32[2,16,384]{2,1,0:T(8,128)} %param.4) | copy-start | bytes 147460
  8.0 1.5 %collective-permute-start.1 = (f32[16,2,4,384]{3,2,1,0:T(4,128)S(1)}, f32[16,2,4,384]{3,2,1,0:T(4,128)S(1)}, u32[]{:S(2)}, u32[]{:S(2)}) collective-permute-start(f32[16,2,4,384]{3,2,1,0:T(4,128)S(1)} %pad_maximum_fusion), channel_id=1, source_target_pairs={{0,1},{1,0},{2,3},{3,2},{4,5},{5,4},{6,7},{7,6},{8,9},{9,8},{10,11... | collective-permute-start | bytes 589832 | tf_op jit(solution)/shard_map/ppermute | solution.py:55
  9.0 0.8 copy-start.1
  14.8 5.4 %collective-permute-start.4 = (f32[2,4,384]{2,1,0:T(4,128)S(1)}, f32[2,4,384]{2,1,0:T(4,128)S(1)}, u32[]{:S(2)}, u32[]{:S(2)}) collective-permute-start(f32[2,4,384]{2,1,0:T(4,128)S(1)} %pad_maximum_fusion.7), channel_id=1, source_target_pairs={{0,1},{1,0},{2,3},{3,2},{4,5},{5,4},{6,7},{7,6},{8,9},{9,8},{10,11... | collective-permute-start | bytes 36872 | tf_op jit(solution)/shard_map/ppermute | solution.py:55
  15.4 8.2 %collective-permute-start.3 = (f32[2,16,384]{2,1,0:T(8,128)S(1)}, f32[2,16,384]{2,1,0:T(8,128)S(1)}, u32[]{:S(2)}, u32[]{:S(2)}) collective-permute-start(f32[2,16,384]{2,1,0:T(8,128)S(1)} %copy-done.1), channel_id=1, source_target_pairs={{0,2},{2,4},{4,6},{6,8},{8,10},{10,12},{12,14},{14,0},{1,3},{3,5},... | collective-permute-start | bytes 147464 | tf_op jit(solution)/shard_map/ppermute | solution.py:41
  15.4 9.3 %collective-permute-start.2 = (f32[2,16,384]{2,1,0:T(8,128)S(1)}, f32[2,16,384]{2,1,0:T(8,128)S(1)}, u32[]{:S(2)}, u32[]{:S(2)}) collective-permute-start(f32[2,16,384]{2,1,0:T(8,128)S(1)} %copy-done.1), channel_id=1, source_target_pairs={{2,0},{4,2},{6,4},{8,6},{10,8},{12,10},{14,12},{0,14},{3,1},{5,3},... | collective-permute-start | bytes 147464 | tf_op jit(solution)/shard_map/ppermute | solution.py:36
  40.7 21.7 %collective-permute-start.5 = (f32[16,2,16,384]{3,2,1,0:T(8,128)S(1)}, f32[16,2,16,384]{3,2,1,0:T(8,128)S(1)}, u32[]{:S(2)}, u32[]{:S(2)}) collective-permute-start(f32[16,2,16,384]{3,2,1,0:T(8,128)S(1)} %copy-done), channel_id=1, source_target_pairs={{0,2},{2,4},{4,6},{6,8},{8,10},{10,12},{12,14},{14,0},{1,3},{3,5},... | collective-permute-start | bytes 2359304 | tf_op jit(solution)/shard_map/ppermute | solution.py:41
  65.5 9.9 %collective-permute-start.6 = (f32[8,2,16,384]{3,2,1,0:T(8,128)S(1)}, f32[8,2,16,384]{3,2,1,0:T(8,128)S(1)}, u32[]{:S(2)}, u32[]{:S(2)}) collective-permute-start(f32[8,2,16,384]{3,2,1,0:T(8,128)S(1)} %get-tuple-element.52.corrections_ref.block_ref), channel_id=1, source_target_pairs={{2,0},{4,2},{6,4},{8,6},{10,8},{12,10},{14,12},{0,14},{3,1},{5,3},... | collective-permute-start | bytes 1179656 | tf_op jit(solution)/shard_map/ppermute | solution.py:36
  65.8 1.4 %collective-permute-start.7 = (f32[8,2,4,384]{3,2,1,0:T(4,128)S(1)}, f32[8,2,4,384]{3,2,1,0:T(4,128)S(1)}, u32[]{:S(2)}, u32[]{:S(2)}) collective-permute-start(f32[8,2,4,384]{3,2,1,0:T(4,128)S(1)} %pad_maximum_fusion.2), channel_id=1, source_target_pairs={{0,1},{1,0},{2,3},{3,2},{4,5},{5,4},{6,7},{7,6},{8,9},{9,8},{10,11... | collective-permute-start | bytes 294920 | tf_op jit(solution)/shard_map/ppermute | solution.py:55
  87.2 13.3 %collective-permute-start.8 = (f32[8,2,16,384]{3,2,1,0:T(8,128)S(1)}, f32[8,2,16,384]{3,2,1,0:T(8,128)S(1)}, u32[]{:S(2)}, u32[]{:S(2)}) collective-permute-start(f32[8,2,16,384]{3,2,1,0:T(8,128)S(1)} %get-tuple-element.52.corrections_ref.block_ref), channel_id=1, source_target_pairs={{0,2},{2,4},{4,6},{6,8},{8,10},{10,12},{12,14},{14,0},{1,3},{3,5},... | collective-permute-start | bytes 1179656 | tf_op jit(solution)/shard_map/ppermute | solution.py:41

commit v4 on v3

v4 whole, which is shorter than its diff:
```python
import functools

import jax
import jax.numpy as jnp
from jax import lax
from jax.experimental import pallas as pl
from jax.experimental.pallas import tpu as pltpu
from jax.sharding import PartitionSpec as P

BLOCK = 16
MODES = 8
HALF = BLOCK // 2
LANES = 128
MAX_SWEEPS = 14
HIGHEST = lax.Precision.HIGHEST
VMEM = pl.BlockSpec(memory_space=pltpu.VMEM)


def call(kernel, out_shapes, args, scratch=(), flops=1000000, name=None):
    out_shape = tuple(jax.ShapeDtypeStruct(s, jnp.float32) for s in out_shapes)
    moved = 4 * sum(x.size for x in list(args) + list(out_shape))
    return pl.pallas_call(
        kernel,
        out_shape=out_shape,
        in_specs=[VMEM] * len(args),
        out_specs=[VMEM] * len(out_shape),
        scratch_shapes=list(scratch),
        compiler_params=pltpu.CompilerParams(vmem_limit_bytes=40 * 1024 * 1024),
        cost_estimate=pl.CostEstimate(flops=flops, bytes_accessed=moved, transcendentals=0),
        name=name,
    )(*args)


def pair_swap(x):
    return lax.ppermute(x, "gz", [(i, i ^ 1) for i in range(lax.axis_size("gz"))])


def core_swap(x):
    return lax.ppermute(x, "gy", [(0, 1), (1, 0)])


def from_beyond(x):
    size = lax.axis_size("gz")
    return lax.ppermute(x, "gz", [((i + (2 if i % 2 == 0 else size - 2)) % size, i) for i in range(size)])


def from_behind(x):
    size = lax.axis_size("gz")
    return lax.ppermute(x, "gz", [((i + (size - 2 if i % 2 == 0 else 2)) % size, i) for i in range(size)])


def grid_sum(x):
    axes = ("gz", "gy")
    total = lax.axis_size("gz") * lax.axis_size("gy")
    if total & (total - 1):
        return lax.psum(x, axes)
    mask = 1
    while mask < total:
        x = x + lax.ppermute(x, axes, [(i, i ^ mask) for i in range(total)])
        mask *= 2
    return x


def spread_rows(x, k):
    return jnp.broadcast_to(x[k : k + 1, :], (8, LANES))


def every_row(x):
    x = x + pltpu.roll(x, 4, 0)
    x = x + pltpu.roll(x, 2, 0)
    return x + pltpu.roll(x, 1, 0)


def packed_sums(tiles, row):
    low4, low2, low1 = row < 4, (row & 2) == 0, (row & 1) == 0
    tiles = [
        jnp.where(low4, tiles[k], tiles[k + 4])
        + pltpu.roll(jnp.where(low4, tiles[k + 4], tiles[k]), 4, 0)
        for k in range(4)
    ]

    def fold(a, b, low, step):
        other = jnp.where(low, b, a)
        moved = jnp.where(low, pltpu.roll(other, 8 - step, 0), pltpu.roll(other, step, 0))
        return jnp.where(low, a, b) + moved

    tiles = [fold(tiles[k], tiles[k + 2], low2, 2) for k in range(2)]
    return fold(tiles[0], tiles[1], low1, 1)


def tournament():
    players = list(range(BLOCK))
    rounds = []
    for _ in range(BLOCK - 1):
        rounds.append([(players[k], players[BLOCK - 1 - k]) for k in range(HALF)])
        players = [players[0], players[-1]] + players[1:-1]
    return rounds


def ritz_kernel(pencil_ref, theta_ref, theta_rows_ref, mix_ref):
    total = pencil_ref[...]
    row = lax.broadcasted_iota(jnp.int32, (8, LANES), 0)
    lane = lax.broadcasted_iota(jnp.int32, (8, LANES), 1)

    def columns(upper, lower):
        return (
            [jnp.broadcast_to(upper[:, k : k + 1], (8, LANES)) for k in range(BLOCK)],
            [jnp.broadcast_to(lower[:, k : k + 1], (8, LANES)) for k in range(BLOCK)],
        )

    def entry(upper, lower, k):
        return spread_rows(upper, k) if k < 8 else spread_rows(lower, k - 8)

    gram_u, gram_l = columns(total[:, :BLOCK], total[:, BLOCK : 2 * BLOCK])
    zero = jnp.zeros((8, LANES), jnp.float32)
    inverse_u = [jnp.where(row == k, 1.0, 0.0).astype(jnp.float32) for k in range(8)] + [zero] * 8
    inverse_l = [zero] * 8 + [
        jnp.where(row == k, 1.0, 0.0).astype(jnp.float32) for k in range(8)
    ]
    for k in range(BLOCK):
        root = lax.rsqrt(entry(gram_u[k], gram_l[k], k))
        gram_u[k] = gram_u[k] * root
        gram_l[k] = gram_l[k] * root
        inverse_u[k] = inverse_u[k] * root
        inverse_l[k] = inverse_l[k] * root
        for i in range(k + 1, BLOCK):
            factor = entry(gram_u[k], gram_l[k], i)
            if i < 8:
                gram_u[i] = gram_u[i] - factor * gram_u[k]
            gram_l[i] = gram_l[i] - factor * gram_l[k]
            inverse_u[i] = inverse_u[i] - factor * inverse_u[k]
            if k >= 8:
                inverse_l[i] = inverse_l[i] - factor * inverse_l[k]
    transposed_u, transposed_l = zero, zero
    for k in range(BLOCK):
        transposed_u = jnp.where(lane == k, inverse_u[k], transposed_u)
        transposed_l = jnp.where(lane == k, inverse_l[k], transposed_l)
    transposed = jnp.concatenate([transposed_u, transposed_l], axis=0)[:, :BLOCK]

    dot = functools.partial(
        lax.dot_general, precision=HIGHEST, preferred_element_type=jnp.float32
    )
    stiff = jnp.concatenate(
        [total[:, 2 * BLOCK : 3 * BLOCK], total[:, 3 * BLOCK : 4 * BLOCK]], axis=0
    )
    half_way = dot(stiff, transposed, (((1,), (0,)), ((), ())))
    projected = dot(transposed, half_way, (((0,), (0,)), ((), ())))

    upper, lower = columns(projected[:8], projected[8:])
    diagonal = zero
    for k in range(8):
        diagonal = diagonal + jnp.where(row == k, upper[k] + lower[k + 8], 0.0)
    mean = every_row(diagonal) * (1.0 / BLOCK)
    size = zero
    for k in range(8):
        upper[k] = upper[k] - jnp.where(row == k, mean, 0.0)
        lower[k + 8] = lower[k + 8] - jnp.where(row == k, mean, 0.0)
    for k in range(BLOCK):
        size = size + (upper[k] * upper[k] + lower[k] * lower[k])
    scale = 1.25 * jnp.sqrt(every_row(size)) + 1e-30
    shrink = 1.0 / scale
    for k in range(BLOCK):
        upper[k] = upper[k] * shrink
        lower[k] = lower[k] * shrink
    for k in range(8):
        upper[k] = upper[k] + jnp.where(row == k, 1.0, 0.0)
        lower[k + 8] = lower[k + 8] + jnp.where(row == k, 1.0, 0.0)

    def squares(upper, lower):
        top = packed_sums([upper[k] * upper[k] + lower[k] * lower[k] for k in range(8)], row)
        bottom = packed_sums(
            [upper[15 - k] * upper[15 - k] + lower[15 - k] * lower[15 - k] for k in range(8)], row
        )
        return top, bottom

    def sweep(carry):
        count, _, upper, lower = carry
        upper, lower = list(upper), list(lower)
        top, bottom = squares(upper, lower)
        worst = zero
        for pairs in tournament():
            g = packed_sums([upper[i] * upper[j] + lower[i] * lower[j] for i, j in pairs], row)
            d = bottom - top
            g2 = g * g
            worst = jnp.maximum(worst, g2)
            dd = jnp.maximum(jnp.abs(d), 1e-18)
            ih = lax.rsqrt(dd * dd + 4.0 * g2)
            c2 = 0.5 + (0.5 * dd) * ih
            ic = lax.rsqrt(c2)
            c = c2 * ic
            s = jnp.where(d >= 0.0, g, -g) * (ih * ic)
            move = (s * ic) * g
            top = top - move
            bottom = bottom + move
            for k, (i, j) in enumerate(pairs):
                ck, sk = spread_rows(c, k), spread_rows(s, k)
                ui, uj, li, lj = upper[i], upper[j], lower[i], lower[j]
                upper[i] = ck * ui - sk * uj
                lower[i] = ck * li - sk * lj
                upper[j] = sk * ui + ck * uj
                lower[j] = sk * li + ck * lj
            next_top = jnp.where(
                row == 0, top, jnp.where(row == 1, pltpu.roll(bottom, 1, 0), pltpu.roll(top, 1, 0))
            )
            bottom = jnp.where(row == 7, top, pltpu.roll(bottom, 7, 0))
            top = next_top
        return count + 1, jnp.max(worst), tuple(upper), tuple(lower)

    def unfinished(carry):
        count, worst, _, _ = carry
        return jnp.logical_and(count < MAX_SWEEPS, worst > 1e-8)

    _, _, upper, lower = lax.while_loop(
        unfinished, sweep, (jnp.int32(0), jnp.float32(1.0), tuple(upper), tuple(lower))
    )

    top, bottom = squares(upper, lower)
    rank_top, rank_bottom = zero, zero
    for k in range(BLOCK):
        mine = spread_rows(top, k) if k < 8 else spread_rows(bottom, 15 - k)
        before_top = (mine < top) | ((mine == top) & (k < row))
        before_bottom = (mine < bottom) | ((mine == bottom) & (k < 15 - row))
        rank_top = rank_top + jnp.where(before_top, 1.0, 0.0)
        rank_bottom = rank_bottom + jnp.where(before_bottom, 1.0, 0.0)
    inverse_top, inverse_bottom = lax.rsqrt(top), lax.rsqrt(bottom)
    value_top, value_bottom = top * inverse_top, bottom * inverse_bottom
    lane_float = lane.astype(jnp.float32)
    theta = zero
    vectors_u, vectors_l = zero, zero
    for k in range(BLOCK):

        def of(first, second):
            return spread_rows(first, k) if k < 8 else spread_rows(second, 15 - k)

        here = lane_float == of(rank_top, rank_bottom)
        inverse_norm = of(inverse_top, inverse_bottom)
        theta = jnp.where(here, of(value_top, value_bottom), theta)
        vectors_u = jnp.where(here, upper[k] * inverse_norm, vectors_u)
        vectors_l = jnp.where(here, lower[k] * inverse_norm, vectors_l)
    theta = mean + scale * (theta - 1.0)
    theta_ref[...] = theta[0, :MODES]
    on_row = jnp.sum(jnp.where(row == lane, theta, 0.0), axis=1, keepdims=True)
    theta_rows_ref[...] = jnp.broadcast_to(on_row, (8, LANES))
    vectors = jnp.concatenate([vectors_u, vectors_l], axis=0)
    mix = dot(transposed, vectors, (((1,), (0,)), ((), ())))
    for j in range(MODES):
        mix_ref[j] = jnp.broadcast_to(mix[:, j : j + 1], (BLOCK, LANES))


def ritz_pairs(pencil):
    return call(
        ritz_kernel,
        [(MODES,), (8, LANES), (MODES, BLOCK, LANES)],
        [pencil],
        flops=10000000,
        name="ritz_pairs",
    )


def inner(a, b):
    return lax.dot_general(
        a, b, (((1,), (1,)), ((), ())), precision=HIGHEST, preferred_element_type=jnp.float32
    )


def folded(products, offset):
    height, width = products.shape
    row = lax.broadcasted_iota(jnp.int32, (height, width), 0)
    column = lax.broadcasted_iota(jnp.int32, (height, width), 1)
    same = jnp.where((row & 7) == (column & 7), products, 0.0)
    sums = jnp.sum(same.reshape(height // 8, 8, width), axis=1)
    row = lax.broadcasted_iota(jnp.int32, (width, LANES), 0)
    lane = lax.broadcasted_iota(jnp.int32, (width, LANES), 1)
    place = jnp.where((row >> 3) + offset == lane, 1.0, 0.0).astype(jnp.float32)
    return jnp.dot(sums, place, precision=HIGHEST, preferred_element_type=jnp.float32)


def rows_of(x):
    return x.reshape(x.shape[0] * x.shape[1], x.shape[2])


def roll(x, shift, axis):
    return pltpu.roll(x, shift % x.shape[axis], axis)


def store_y_differences(source_ref, beside_ref, wide_ref, change_ref, z):
    count, _, ny, _ = source_ref.shape

    @pl.loop(0, count)
    def _(a):
        wide_ref[6:8, :] = beside_ref[a, z, :2]
        wide_ref[8 : 8 + ny, :] = source_ref[a, z]
        wide_ref[8 + ny : 10 + ny, :] = beside_ref[a, z, 2:]
        wide = wide_ref[...]
        change = roll(wide, -1, 0) + roll(wide, 1, 0) - 2.0 * wide
        change_ref[a] = change[8 : 8 + ny]


def second_x(rows):
    return roll(rows, -1, 1) + roll(rows, 1, 1) - 2.0 * rows


def prepare_kernel(flags_ref, block_ref, stiffness_ref, concentration_ref, mine_ref, other_ref):
    nz, ny, _ = concentration_ref.shape
    half = ny // 2
    odd = flags_ref[0] > 0.5
    high = flags_ref[1] > 0.5

    def split(source, a):
        for z in range(nz):
            layer = [
                jnp.where(odd, source(nz - 1 - z)[part], source(z)[part])
                for part in (slice(0, half), slice(half, ny))
            ]
            mine_ref[a, z] = jnp.where(high, layer[1], layer[0])
            other_ref[a, nz - 1 - z] = jnp.where(high, layer[0], layer[1])

    @pl.loop(0, BLOCK)
    def _(a):
        split(lambda z: block_ref[a, z], a)

    split(lambda z: stiffness_ref[z], BLOCK)
    split(lambda z: concentration_ref[z], BLOCK + 1)


def first_local_kernel(block_ref, beside_ref, curvature_ref, stiffness_ref, tile_ref, wide_ref, change_ref):
    nz, ny, nx = curvature_ref.shape
    wide_ref[...] = jnp.zeros(wide_ref.shape, jnp.float32)
    gram = jnp.zeros((8 * BLOCK, 8 * BLOCK), jnp.float32)
    stiff = jnp.zeros((8 * BLOCK, 8 * BLOCK), jnp.float32)
    for z in range(nz):
        store_y_differences(block_ref, beside_ref, wide_ref, change_ref, z)
        for start in range(0, ny, 8):
            part = slice(start, start + 8)
            field = block_ref[:, z, part, :]
            weight = stiffness_ref[z, part, :][None]
            rows = rows_of(field)
            along_x = second_x(rows)
            along_y = change_ref[:, part, :]
            gram = gram + inner(rows, rows)
            stiff = stiff + inner(rows_of(field * curvature_ref[z, part, :][None]), rows)
            stiff = stiff + inner(rows_of(along_x.reshape(field.shape) * weight), along_x)
            stiff = stiff + inner(rows_of(along_y * weight), rows_of(along_y))
    half = 8 * HALF
    tile_ref[...] = (
        folded(gram[:half], 0)
        + folded(gram[half:], BLOCK)
        + folded(stiff[:half], 2 * BLOCK)
        + folded(stiff[half:], 3 * BLOCK)
    )


def edges(flags_ref, field, layers):
    high = flags_ref[1][:2] > 0.5
    to_pair, to_core = [], []
    for u in range(layers):
        first, last = field(u)[:2], field(u)[-2:]
        to_pair.append(jnp.where(high, first, last))
        to_core.append(jnp.where(high, last, first))
    return to_pair[::-1], to_core


def first_across_kernel(flags_ref, mine_ref, theirs_ref, beyond_ref, tile_ref, sum_ref, pair_ref, core_ref):
    nz, ny = mine_ref.shape[1:3]
    half = 8 * HALF
    stiff = jnp.zeros((8 * BLOCK, 8 * BLOCK), jnp.float32)
    sources = [(mine_ref, z) for z in range(nz)] + [(theirs_ref, z) for z in range(nz)]
    sources = sources + [(beyond_ref, z) for z in range(2)]
    for u in range(1, 2 * nz + 1):
        for start in range(0, ny, 8):
            part = slice(start, start + 8)

            def layer(k):
                source, z = sources[k]
                return source[:BLOCK, z, part, :]

            source, z = sources[u]
            change = (layer(u + 1) + layer(u - 1)) - 2.0 * layer(u)
            weight = source[BLOCK, z, part, :]
            stiff = stiff + inner(rows_of(change * weight[None]), rows_of(change))
    sum_ref[...] = (
        tile_ref[...] + folded(stiff[:half], 2 * BLOCK) + folded(stiff[half:], 3 * BLOCK)
    )

    @pl.loop(0, BLOCK + 1)
    def _(a):
        field = lambda u: sources[u][0][a, sources[u][1]]
        to_pair, to_core = edges(flags_ref, field, 2 * nz)
        for u in range(2 * nz):
            pair_ref[a, 2 * u : 2 * u + 2, :] = to_pair[u]
            core_ref[a, 2 * u : 2 * u + 2, :] = to_core[u]


def apply_hessian(field, layers, stiff_layers, u, curvature, wide, stiff_wide):
    def flux(k):
        return stiff_layers(k) * ((layers(k + 1) + layers(k - 1)) - 2.0 * layers(k))

    total = curvature * field + (flux(u + 1) + flux(u - 1) - 2.0 * flux(u))
    change = second_x(stiff_layers(u) * second_x(field))
    total = total + change
    change = stiff_wide * (roll(wide, -1, 0) + roll(wide, 1, 0) - 2.0 * wide)
    change = roll(change, -1, 0) + roll(change, 1, 0) - 2.0 * change
    return total + change[8 : 8 + field.shape[0]]


def store_wide(wide_ref, index, flags_ref, field, pair_rows, core_rows):
    ny = field.shape[0]
    high = flags_ref[1][:2] > 0.5
    wide_ref[index, 6:8, :] = jnp.where(high, pair_rows, core_rows)
    wide_ref[index, 8 : 8 + ny, :] = field
    wide_ref[index, 8 + ny : 10 + ny, :] = jnp.where(high, core_rows, pair_rows)


def update_kernel(
    flags_ref, mix_ref, theta_ref, mine_ref, theirs_ref, behind_ref, beyond_ref, pair_ref, core_ref,
    modes_ref, images_ref, near_ref, far_ref, to_pair_ref, to_core_ref,
    curvature_ref, stiff_layers_ref, stiff_wide_ref,
    mixed_ref, mixed_pair_ref, mixed_core_ref, wide_ref, inverse_ref,
):
    depth, ny, nx = curvature_ref.shape
    nz = depth // 2
    wide_ref[...] = jnp.zeros(wide_ref.shape, jnp.float32)
    stiff_wide_ref[...] = jnp.zeros(stiff_wide_ref.shape, jnp.float32)
    sources = [(behind_ref, nz - 2), (behind_ref, nz - 1)]
    sources = sources + [(mine_ref, z) for z in range(nz)] + [(theirs_ref, z) for z in range(nz)]
    sources = sources + [(beyond_ref, 0), (beyond_ref, 1)]
    tiles = [(source, z, mixed_ref, k) for k, (source, z) in enumerate(sources)]
    tiles = tiles + [(pair_ref, None, mixed_pair_ref, None), (core_ref, None, mixed_core_ref, None)]
    for source, z, target, k in tiles:
        for start in range(0, nx, LANES):
            lanes = slice(start, start + LANES)
            if z is None:
                parts = [source[a, :, lanes] for a in range(BLOCK)]
            else:
                parts = [source[a, z, :, lanes] for a in range(BLOCK)]
            for j in range(MODES):
                mixed = mix_ref[j, 0:1, :] * parts[0]
                for a in range(1, BLOCK):
                    mixed = mixed + mix_ref[j, a : a + 1, :] * parts[a]
                if z is None:
                    target[j, :, lanes] = mixed
                else:
                    target[j, k, :, lanes] = mixed

    for k in range(depth + 2):
        source, z = sources[k + 1]
        stiff_layers_ref[k] = source[BLOCK, z]
    for u in range(depth):
        rows = slice(2 * u, 2 * u + 2)
        stiff = stiff_layers_ref[u + 1]
        store_wide(stiff_wide_ref, u, flags_ref, stiff, pair_ref[BLOCK, rows, :], core_ref[BLOCK, rows, :])
        source, z = sources[u + 2]
        concentration = source[BLOCK + 1, z]
        curvature = 3.0 * concentration * concentration - 1.0
        curvature_ref[u] = curvature
        total = (curvature + 2.0) + 12.0 * stiff
        total = total + (stiff_layers_ref[u] + stiff_layers_ref[u + 2])
        total = total + (stiff_wide_ref[u, 7 : 7 + ny, :] + stiff_wide_ref[u, 9 : 9 + ny, :])
        total = total + (roll(stiff, -1, 1) + roll(stiff, 1, 1))
        inverse_ref[u] = 1.0 / total

    @pl.loop(0, MODES)
    def _(j):
        theta = jnp.broadcast_to(theta_ref[pl.ds(j, 1), :1], (1, nx))
        corrections = []
        for u in range(depth):
            rows = slice(2 * u, 2 * u + 2)
            mode = mixed_ref[j, u + 2]
            store_wide(wide_ref, u, flags_ref, mode, mixed_pair_ref[j, rows, :], mixed_core_ref[j, rows, :])
            image = apply_hessian(
                mode, lambda k: mixed_ref[j, k + 2], lambda k: stiff_layers_ref[k + 1], u,
                curvature_ref[u], wide_ref[u], stiff_wide_ref[u],
            )
            images_ref[j, u] = image
            modes_ref[j, u] = mode
            correction = (image - theta * mode) * inverse_ref[u]
            corrections.append(correction)
            if u < nz:
                near_ref[j, u] = correction
            else:
                far_ref[j, u - nz] = correction
        to_pair, to_core = edges(flags_ref, lambda u: corrections[u], depth)
        for u in range(depth):
            to_pair_ref[j, 2 * u : 2 * u + 2, :] = to_pair[u]
            to_core_ref[j, 2 * u : 2 * u + 2, :] = to_core[u]


def second_local_kernel(modes_ref, images_ref, near_ref, far_ref, curvature_ref, stiff_layers_ref, tile_ref):
    depth, ny, nx = curvature_ref.shape
    nz = depth // 2
    half = 8 * HALF
    gram = jnp.zeros((2 * half, 2 * half), jnp.float32)
    cross = jnp.zeros((half, 2 * half), jnp.float32)
    back = jnp.zeros((half, half), jnp.float32)
    low = jnp.zeros((half, half), jnp.float32)
    for u in range(depth):
        for start in range(0, ny, 8):
            part = slice(start, start + 8)
            field = near_ref[:, u, part, :] if u < nz else far_ref[:, u - nz, part, :]
            weight = stiff_layers_ref[u + 1, part, :][None]
            second = rows_of(field)
            rows = jnp.concatenate([rows_of(modes_ref[:, u, part, :]), second], axis=0)
            images = rows_of(images_ref[:, u, part, :])
            along_x = second_x(second)
            gram = gram + inner(rows, rows)
            cross = cross + inner(images, rows)
            back = back + inner(second, images)
            low = low + inner(rows_of(field * curvature_ref[u, part, :][None]), second)
            low = low + inner(rows_of(along_x.reshape(field.shape) * weight), along_x)
    tile_ref[...] = (
        folded(gram[:half], 0)
        + folded(gram[half:], BLOCK)
        + folded(cross, 2 * BLOCK)
        + (folded(back, 3 * BLOCK) + folded(low, 3 * BLOCK + HALF))
    )


def second_across_kernel(
    flags_ref, near_ref, far_ref, beyond_ref, pair_ref, core_ref, stiff_layers_ref, tile_ref,
    sum_ref, wide_ref, change_ref,
):
    nz, ny = near_ref.shape[1:3]
    depth = 2 * nz
    wide_ref[...] = jnp.zeros(wide_ref.shape, jnp.float32)
    sources = [(near_ref, z) for z in range(nz)] + [(far_ref, z) for z in range(nz)]
    sources = sources + [(beyond_ref, 0), (beyond_ref, 1)]

    @pl.loop(0, MODES)
    def _(j):
        for u in range(depth):
            source, z = sources[u]
            rows = slice(2 * u, 2 * u + 2)
            store_wide(wide_ref, u, flags_ref, source[j, z], pair_ref[j, rows, :], core_ref[j, rows, :])
            wide = wide_ref[u]
            change = roll(wide, -1, 0) + roll(wide, 1, 0) - 2.0 * wide
            change_ref[j, u] = change[8 : 8 + ny]

    low = jnp.zeros((8 * MODES, 8 * MODES), jnp.float32)
    for u in range(depth):
        for start in range(0, ny, 8):
            part = slice(start, start + 8)

            def layer(k):
                source, z = sources[k]
                return source[:, z, part, :]

            change = change_ref[:, u, part, :]
            weight = stiff_layers_ref[u + 1, part, :][None]
            low = low + inner(rows_of(change * weight), rows_of(change))
            change = (layer(u + 2) + layer(u)) - 2.0 * layer(u + 1)
            weight = stiff_layers_ref[u + 2, part, :][None]
            low = low + inner(rows_of(change * weight), rows_of(change))
    sum_ref[...] = tile_ref[...] + folded(low, 3 * BLOCK + HALF)


def images_kernel(
    flags_ref, near_ref, far_ref, behind_ref, beyond_ref, pair_ref, core_ref,
    curvature_ref, stiff_layers_ref, stiff_wide_ref, images_ref, wide_ref,
):
    depth, ny, nx = curvature_ref.shape
    nz = depth // 2
    wide_ref[...] = jnp.zeros(wide_ref.shape, jnp.float32)
    sources = [(behind_ref, nz - 2), (behind_ref, nz - 1)]
    sources = sources + [(near_ref, z) for z in range(nz)] + [(far_ref, z) for z in range(nz)]
    sources = sources + [(beyond_ref, 0), (beyond_ref, 1)]

    @pl.loop(0, MODES)
    def _(j):
        layers = [source[j, z] for source, z in sources]
        for u in range(depth):
            rows = slice(2 * u, 2 * u + 2)
            store_wide(wide_ref, u, flags_ref, layers[u + 2], pair_ref[j, rows, :], core_ref[j, rows, :])
            images_ref[j, u] = apply_hessian(
                layers[u + 2], lambda k: layers[k + 2], lambda k: stiff_layers_ref[k + 1], u,
                curvature_ref[u], wide_ref[u], stiff_wide_ref[u],
            )


def density_kernel(
    factor, mix_ref, theta_ref, modes_ref, near_ref, far_ref, first_ref, second_ref, mine_ref, theirs_ref,
):
    depth, ny, nx = modes_ref.shape[1:]
    nz = depth // 2
    for u in range(depth):
        for start in range(0, nx, LANES):
            lanes = slice(start, start + LANES)
            vectors = [modes_ref[a, u, :, lanes] for a in range(MODES)]
            if u < nz:
                vectors = vectors + [near_ref[a, u, :, lanes] for a in range(MODES)]
            else:
                vectors = vectors + [far_ref[a, u - nz, :, lanes] for a in range(MODES)]
            images = [first_ref[a, u, :, lanes] for a in range(MODES)]
            images = images + [second_ref[a, u, :, lanes] for a in range(MODES)]
            mode_sum = jnp.zeros((ny, LANES), jnp.float32)
            residual_sum = jnp.zeros((ny, LANES), jnp.float32)
            for j in range(MODES):
                mode = mix_ref[j, 0:1, :] * vectors[0]
                image = mix_ref[j, 0:1, :] * images[0]
                for a in range(1, BLOCK):
                    mode = mode + mix_ref[j, a : a + 1, :] * vectors[a]
                    image = image + mix_ref[j, a : a + 1, :] * images[a]
                residual = image - theta_ref[j : j + 1, :] * mode
                mode_sum = mode_sum + mode * mode
                residual_sum = residual_sum + residual * residual
            for k, total in ((0, mode_sum), (1, residual_sum)):
                if u < nz:
                    mine_ref[k, u, :, lanes] = factor * total
                else:
                    theirs_ref[k, depth - 1 - u, :, lanes] = factor * total


def merge_kernel(flags_ref, mine_ref, other_ref, modes_ref, residuals_ref):
    nz, ny, _ = modes_ref.shape
    half = ny // 2
    odd = flags_ref[0] > 0.5
    high = flags_ref[1] > 0.5
    for k, target in ((0, modes_ref), (1, residuals_ref)):
        for z in range(nz):
            mine = jnp.where(odd, mine_ref[k, nz - 1 - z], mine_ref[k, z])
            other = jnp.where(odd, other_ref[k, nz - 1 - z], other_ref[k, z])
            target[z, :half, :] = jnp.where(high, other, mine)
            target[z, half:, :] = jnp.where(high, mine, other)


def local(initial_block, concentration, stiffness):
    nz, ny, nx = concentration.shape
    half = ny // 2
    depth = 2 * nz
    cells_total = nz * ny * nx * lax.axis_size("gz") * lax.axis_size("gy")
    odd = lax.axis_index("gz") % 2
    high = 1 - (odd ^ lax.axis_index("gy"))
    flags = jnp.broadcast_to(
        jnp.stack([odd, high]).astype(jnp.float32)[:, None, None], (2, half, nx)
    )
    halves = (BLOCK + 2, nz, half, nx)
    vector_rows = (BLOCK + 1, 2 * depth, nx)
    plane = (depth, half, nx)
    wide = (depth, half + 16, nx)
    mode_plane = (MODES,) + plane
    mode_half = (MODES, nz, half, nx)
    mode_rows = (MODES, 2 * depth, nx)

    mine, other = call(
        prepare_kernel, [halves, halves], [flags, initial_block, stiffness, concentration], name="prepare"
    )
    theirs = pair_swap(other)
    beyond = from_beyond(mine[:, :2])
    edge_rows = jnp.concatenate([initial_block[:, :, ny - 2 :], initial_block[:, :, :2]], axis=2)
    beside = core_swap(edge_rows)
    curvature = 3.0 * concentration * concentration - 1.0
    (tile,) = call(
        first_local_kernel,
        [(8, LANES)],
        [initial_block, beside, curvature, stiffness],
        scratch=[pltpu.VMEM((ny + 16, nx), jnp.float32), pltpu.VMEM((BLOCK, ny, nx), jnp.float32)],
        flops=100000000,
        name="first_local",
    )
    theirs, beyond, tile = lax.optimization_barrier((theirs, beyond, tile))
    tile, to_pair, to_core = call(
        first_across_kernel,
        [(8, LANES), vector_rows, vector_rows],
        [flags, mine, theirs, beyond, tile],
        flops=25000000,
        name="first_across",
    )
    pencil = grid_sum(tile)
    pencil, held, to_pair, to_core = lax.optimization_barrier((pencil, theirs, to_pair, to_core))
    behind = from_behind(held[:, nz - 2 :])
    pair_rows = pair_swap(to_pair)
    core_rows = core_swap(to_core)
    _, theta_rows, mix = ritz_pairs(pencil)

    (
        modes, mode_images, near, far, to_pair, to_core, curvature, stiff_layers, stiff_wide,
    ) = call(
        update_kernel,
        [mode_plane, mode_plane, mode_half, mode_half, mode_rows, mode_rows]
        + [plane, (depth + 2, half, nx), wide],
        [flags, mix, theta_rows, mine, theirs, behind, beyond, pair_rows, core_rows],
        scratch=[
            pltpu.VMEM((MODES, depth + 4, half, nx), jnp.float32),
            pltpu.VMEM(mode_rows, jnp.float32),
            pltpu.VMEM(mode_rows, jnp.float32),
            pltpu.VMEM(wide, jnp.float32),
            pltpu.VMEM(plane, jnp.float32),
        ],
        name="update",
    )

    beyond = from_beyond(near[:, :2])
    pair_rows = pair_swap(to_pair)
    core_rows = core_swap(to_core)
    (tile,) = call(
        second_local_kernel,
        [(8, LANES)],
        [modes, mode_images, near, far, curvature, stiff_layers],
        flops=80000000,
        name="second_local",
    )
    beyond, pair_rows, core_rows, tile = lax.optimization_barrier((beyond, pair_rows, core_rows, tile))
    (tile,) = call(
        second_across_kernel,
        [(8, LANES)],
        [flags, near, far, beyond, pair_rows, core_rows, stiff_layers, tile],
        scratch=[pltpu.VMEM(wide, jnp.float32), pltpu.VMEM(mode_plane, jnp.float32)],
        flops=25000000,
        name="second_across",
    )
    pencil = grid_sum(tile)
    pencil, held = lax.optimization_barrier((pencil, far))
    behind = from_behind(held[:, nz - 2 :])
    theta, theta_rows, mix = ritz_pairs(pencil)
    (correction_images,) = call(
        images_kernel,
        [mode_plane],
        [flags, near, far, behind, beyond, pair_rows, core_rows, curvature, stiff_layers, stiff_wide],
        scratch=[pltpu.VMEM(wide, jnp.float32)],
        name="images",
    )
    mine, theirs = call(
        functools.partial(density_kernel, float(cells_total / MODES)),
        [(2, nz, half, nx)] * 2,
        [mix, theta_rows, modes, near, far, mode_images, correction_images],
        name="densities",
    )
    mode_density, residual_density = call(
        merge_kernel, [(nz, ny, nx)] * 2, [flags, mine, pair_swap(theirs)], name="merge"
    )
    return (theta, mode_density, residual_density)


def solution(mesh):
    return jax.shard_map(
        local,
        mesh=mesh,
        in_specs=(P("img", "gz", "gy", None), P(("img", "gz"), "gy", None), P("gz", "gy", None)),
        out_specs=(P("img"), P(("img", "gz"), "gy", None), P(("img", "gz"), "gy", None)),
        check_vma=False,
    )
```

time: 104 us -> 84 us (0.81)
  blocking collectives: 25.4 us -> 0 us
  starting transfers between devices: 12 us -> 23.4 us
  waiting for transfers between devices: 32.1 us -> 26.6 us
    all_to_all x2 -> x0, blocking collectives: 25.4 us -> none  [all_terms(): return lax.all_to_all(copies, ('gz', 'gy'), 0, 0, tiled=True)]
    ppermute x9 -> x19, starting transfers between devices: 12 us -> 23.4 us  [the longest x8 8.25 us: grid_sum(): x = x + lax.ppermute(x, axes, [(i, i ^ mask) for i in range(total)])]
    ppermute x9 -> x19, waiting for transfers between devices: 32.1 us -> 26.6 us  [the longest x8 17.6 us: grid_sum(): x = x + lax.ppermute(x, axes, [(i, i ^ mask) for i in range(total)])]
    unnamed x6 -> x8, local copies, waits for them, and re-layouts: 0.34 us -> 2.56 us
    slice x8 -> x1, local copies, waits for them, and re-layouts: 2.26 us -> 0.07 us  [local(): initial_block[:, :, ny - 2:]]
    pallas_call x9 -> x11, Pallas kernels: 30.5 us -> 30 us  [call(): pl.pallas_call(kernel, out_shape=out_shape, in_specs=[VMEM] * len(args),...]
  transfers between devices with their start and end apart: 9 -> 19, of which waited for: 7 -> 15; matrix products, arithmetic and copies ran while one was open for 3% -> 0% of each run, Pallas kernels for 21% -> 25%
where the time goes in v4:
time: 84 us; the launch traced here: 83.8 us
  Pallas kernels  30 us (36%)
  waiting for transfers between devices  26.6 us (32%)
  starting transfers between devices  23.4 us (28%)
  local copies, waits for them, and re-layouts  2.71 us (3%)
    pallas_call x11, Pallas kernels, call(): pl.pallas_call(kernel, out_shape=out_shape, in_specs=[VMEM] * len(args),...  30 us
    ppermute x8, waiting for transfers between devices, grid_sum(): x = x + lax.ppermute(x, axes, [(i, i ^ mask) for i in range(total)])  17.6 us
    ppermute x8, starting transfers between devices, grid_sum(): x = x + lax.ppermute(x, axes, [(i, i ^ mask) for i in range(total)])  8.25 us
    ppermute x4, starting transfers between devices, pair_swap(): lax.ppermute(x, 'gz', [(i, i ^ 1) for i in range(lax.axis_size('gz'))])  7.2 us
    ppermute x2, starting transfers between devices, from_beyond(): lax.ppermute(x, 'gz', [((i + (2 if i % 2 == 0 else size - 2)) % size, i)...  5.62 us
    ppermute x4, waiting for transfers between devices, pair_swap(): lax.ppermute(x, 'gz', [(i, i ^ 1) for i in range(lax.axis_size('gz'))])  3.33 us
    ppermute x2, waiting for transfers between devices, from_beyond(): lax.ppermute(x, 'gz', [((i + (2 if i % 2 == 0 else size - 2)) % size, i)...  2.6 us
    unnamed x8, local copies, waits for them, and re-layouts  2.56 us
  transfers between devices with their start and end apart: 19, of which 15 were waited for; matrix products, arithmetic and copies ran while one was open for 0% of the time, Pallas kernels for 25%

profile of v4, /device:TPU:0, one launch (start us, length us, event | category | flops | bytes accessed | tf_op | source)
XLA Modules:
  0.0 83.8 jit_solution(17408684431196035262)
XLA Ops:
  1.4 1.1 %copy-done = f32[16,2,16,384]{3,2,1,0:T(8,128)S(1)} copy-done((f32[16,2,16,384]{3,2,1,0:T(8,128)S(1)}, f32[16,2,16,384]{3,2,1,0:T(8,128)}, u32[]{:S(2)}) %copy-start) | copy-done | bytes 786456
  3.5 3.0 %collective-permute-start = (f32[18,2,8,384]{3,2,1,0:T(8,128)S(1)}, f32[18,2,8,384]{3,2,1,0:T(8,128)S(1)}, u32[]{:S(2)}, u32[]{:S(2)}) collective-permute-start(f32[18,2,8,384]{3,2,1,0:T(8,128)S(1)} %get-tuple-element.40), channel_id=1, source_target_pairs={{0,2},{2,0},{4,6},{6,4},{8,10},{10,8},{12,14},{14,12},{1,3},{3,1},... | collective-permute-start | bytes 1327112 | tf_op jit(solution)/shard_map/ppermute | solution.py:35
  6.5 3.6 %collective-permute-start.1 = (f32[18,2,8,384]{3,2,1,0:T(8,128)S(1)}, f32[18,2,8,384]{3,2,1,0:T(8,128)S(1)}, u32[]{:S(2)}, u32[]{:S(2)}) collective-permute-start(f32[18,2,8,384]{3,2,1,0:T(8,128)S(1)} %get-tuple-element.39.mine_ref), channel_id=1, source_target_pairs={{4,0},{14,2},{8,4},{2,6},{12,8},{6,10},{0,12},{10,14},{5,1},{15,3}... | collective-permute-start | bytes 1327112 | tf_op jit(solution)/shard_map/ppermute | solution.py:44
  10.4 1.4 %collective-permute-done.2.beside_ref = f32[16,2,4,384]{3,2,1,0:T(4,128)S(1)} collective-permute-done((f32[16,2,4,384]{3,2,1,0:T(4,128)S(1)}, f32[16,2,4,384]{3,2,1,0:T(4,128)S(1)}, u32[]{:S(2)}, u32[]{:S(2)}) %collective-permute-start.2) | collective-permute-done | bytes 196640 | tf_op jit(solution)/shard_map/ppermute | solution.py:39
  11.8 5.0 %first_local.1.tile_ref = f32[8,128]{1,0:T(8,128)S(1)} custom-call(f32[16,2,16,384]{3,2,1,0:T(8,128)S(1)} %copy-done.1, f32[16,2,4,384]{3,2,1,0:T(4,128)S(1)} %collective-permute-done.2.beside_ref, f32[2,16,384]{2,1,0:T(8,128)S(1)} %fusion.curvature_ref, f32[2,16,384]{2,1,0:T(8,128)S(1)} %copy-done.2), custom_call_target="tpu_custom_call" | custom-call | flops 100000000 | bytes 1085440 | tf_op jit(solution)/shard_map/first_local/pallas_call | solution.py:22
  16.8 2.5 %collective-permute-done.1.beyond_ref = f32[18,2,8,384]{3,2,1,0:T(8,128)S(1)} collective-permute-done((f32[18,2,8,384]{3,2,1,0:T(8,128)S(1)}, f32[18,2,8,384]{3,2,1,0:T(8,128)S(1)}, u32[]{:S(2)}, u32[]{:S(2)}) %collective-permute-start.1) | collective-permute-done | bytes 442400 | tf_op jit(solution)/shard_map/ppermute | solution.py:44
  19.3 1.6 %first_across.1 = (f32[8,128]{1,0:T(8,128)S(1)}, f32[17,8,384]{2,1,0:T(8,128)S(1)}, f32[17,8,384]{2,1,0:T(8,128)S(1)}) custom-call(f32[2,8,384]{2,1,0:T(8,128)S(1)} %broadcast_in_dim.2.flags_ref, f32[18,2,8,384]{3,2,1,0:T(8,128)S(1)} %get-tuple-element.39.mine_ref, f32[18,2,8,384]{3,2,1,0:T(8,128)S(1)} %collective-permute-done.theirs_ref, ...), custom_call_target="tpu_custom_call" | custom-call | flops 25000000 | bytes 1777664 | tf_op jit(solution)/shard_map/first_across/pallas_call | solution.py:22
  21.0 1.2 %collective-permute-done.3 = f32[8,128]{1,0:T(8,128)S(1)} collective-permute-done((f32[8,128]{1,0:T(8,128)S(1)}, f32[8,128]{1,0:T(8,128)S(1)}, u32[]{:S(2)}, u32[]{:S(2)}) %collective-permute-start.3) | collective-permute-done | bytes 4128 | tf_op jit(solution)/shard_map/ppermute | solution.py:59
  22.2 1.2 %collective-permute-start.4 = (f32[8,128]{1,0:T(8,128)S(1)}, f32[8,128]{1,0:T(8,128)S(1)}, u32[]{:S(2)}, u32[]{:S(2)}) collective-permute-start(f32[8,128]{1,0:T(8,128)S(1)} %add.30), channel_id=1, source_target_pairs={{0,2},{1,3},{2,0},{3,1},{4,6},{5,7},{6,4},{7,5},{8,10},{9,11},{10,... | collective-permute-start | bytes 12296 | tf_op jit(solution)/shard_map/ppermute | solution.py:59
  23.4 2.4 %collective-permute-done.4 = f32[8,128]{1,0:T(8,128)S(1)} collective-permute-done((f32[8,128]{1,0:T(8,128)S(1)}, f32[8,128]{1,0:T(8,128)S(1)}, u32[]{:S(2)}, u32[]{:S(2)}) %collective-permute-start.4) | collective-permute-done | bytes 4128 | tf_op jit(solution)/shard_map/ppermute | solution.py:59
  26.2 3.1 %collective-permute-done.5 = f32[8,128]{1,0:T(8,128)S(1)} collective-permute-done((f32[8,128]{1,0:T(8,128)S(1)}, f32[8,128]{1,0:T(8,128)S(1)}, u32[]{:S(2)}, u32[]{:S(2)}) %collective-permute-start.5) | collective-permute-done | bytes 4128 | tf_op jit(solution)/shard_map/ppermute | solution.py:59
  29.4 2.8 %collective-permute-start.6 = (f32[8,128]{1,0:T(8,128)S(1)}, f32[8,128]{1,0:T(8,128)S(1)}, u32[]{:S(2)}, u32[]{:S(2)}) collective-permute-start(f32[8,128]{1,0:T(8,128)S(1)} %add.32), channel_id=1, source_target_pairs={{0,8},{1,9},{2,10},{3,11},{4,12},{5,13},{6,14},{7,15},{8,0},{9,1},... | collective-permute-start | bytes 12296 | tf_op jit(solution)/shard_map/ppermute | solution.py:59
  32.2 1.7 %collective-permute-done.6 = f32[8,128]{1,0:T(8,128)S(1)} collective-permute-done((f32[8,128]{1,0:T(8,128)S(1)}, f32[8,128]{1,0:T(8,128)S(1)}, u32[]{:S(2)}, u32[]{:S(2)}) %collective-permute-start.6) | collective-permute-done | bytes 4128 | tf_op jit(solution)/shard_map/ppermute | solution.py:59
  33.9 1.9 %collective-permute-start.7 = (f32[18,2,8,384]{3,2,1,0:T(8,128)S(1)}, f32[18,2,8,384]{3,2,1,0:T(8,128)S(1)}, u32[]{:S(2)}, u32[]{:S(2)}) collective-permute-start(f32[18,2,8,384]{3,2,1,0:T(8,128)S(1)} %collective-permute-done.theirs_ref), channel_id=1, source_target_pairs={{12,0},{6,2},{0,4},{10,6},{4,8},{14,10},{8,12},{2,14},{13,1},{7,3}... | collective-permute-start | bytes 1327112 | tf_op jit(solution)/shard_map/ppermute | solution.py:49
  35.8 2.4 %collective-permute-start.8 = (f32[17,8,384]{2,1,0:T(8,128)S(1)}, f32[17,8,384]{2,1,0:T(8,128)S(1)}, u32[]{:S(2)}, u32[]{:S(2)}) collective-permute-start(f32[17,8,384]{2,1,0:T(8,128)S(1)} %get-tuple-element.51), channel_id=1, source_target_pairs={{0,2},{2,0},{4,6},{6,4},{8,10},{10,8},{12,14},{14,12},{1,3},{3,1},... | collective-permute-start | bytes 626696 | tf_op jit(solution)/shard_map/ppermute | solution.py:35
  38.2 6.2 %ritz_pairs.2 = (f32[8]{0:T(128)}, f32[8,128]{1,0:T(8,128)S(1)}, f32[8,16,128]{2,1,0:T(8,128)S(1)}) custom-call(f32[8,128]{1,0:T(8,128)S(1)} %add.33.pencil_ref), custom_call_target="tpu_custom_call" | custom-call | flops 10000000 | bytes 73760 | tf_op jit(solution)/shard_map/ritz_pairs/pallas_call | solution.py:22
  45.2 2.7 %update.1 = (f32[8,4,8,384]{3,2,1,0:T(8,128)S(1)}, f32[8,4,8,384]{3,2,1,0:T(8,128)S(1)}, f32[8,2,8,384]{3,2,1,0:T(8,128)S(1)}, f32[8,2,8,384]{3,2,1,0:T(8,128)S(...) custom-call(f32[2,8,384]{2,1,0:T(8,128)S(1)} %broadcast_in_dim.2.fla, ...), custom_call_target="tpu_custom_call" | custom-call | flops 1000000 | bytes 3928064 | tf_op jit(solution)/shard_map/update/pallas_call | solution.py:22
  47.9 2.0 %collective-permute-start.10 = (f32[8,2,8,384]{3,2,1,0:T(8,128)S(1)}, f32[8,2,8,384]{3,2,1,0:T(8,128)S(1)}, u32[]{:S(2)}, u32[]{:S(2)}) collective-permute-start(f32[8,2,8,384]{3,2,1,0:T(8,128)S(1)} %get-tuple-element.53.near_ref), channel_id=1, source_target_pairs={{4,0},{14,2},{8,4},{2,6},{12,8},{6,10},{0,12},{10,14},{5,1},{15,3}... | collective-permute-start | bytes 589832 | tf_op jit(solution)/shard_map/ppermute | solution.py:44
  49.9 3.6 %second_local.1.tile_ref = f32[8,128]{1,0:T(8,128)S(1)} custom-call(f32[8,4,8,384]{3,2,1,0:T(8,128)S(1)} %get-tuple-element.57.modes_ref, f32[8,4,8,384]{3,2,1,0:T(8,128)S(1)} %get-tuple-element.58.images_ref.first_ref, f32[8,2,8,384]{3,2,1,0:T(8,128)S(1)} %get-tuple-element.53.near_ref, f32[8,2,8,384]{3,2,1,0:T(8,128)S(1)} %get-tuple-element.69.far_ref, ...), custom_call_target="tpu_custom_call" | custom-call | flops 80000000 | bytes 1306624 | tf_op jit(solution)/shard_map/second_local/pallas_call | solution.py:22
  53.6 1.0 %collective-permute-done.11.pair_ref = f32[8,8,384]{2,1,0:T(8,128)S(1)} collective-permute-done((f32[8,8,384]{2,1,0:T(8,128)S(1)}, f32[8,8,384]{2,1,0:T(8,128)S(1)}, u32[]{:S(2)}, u32[]{:S(2)}) %collective-permute-start.11) | collective-permute-done | bytes 98336 | tf_op jit(solution)/shard_map/ppermute | solution.py:35
  54.7 1.4 %second_across.1 = f32[8,128]{1,0:T(8,128)S(1)} custom-call(f32[2,8,384]{2,1,0:T(8,128)S(1)} %broadcast_in_dim.2.flags_ref, f32[8,2,8,384]{3,2,1,0:T(8,128)S(1)} %get-tuple-element.53.near_ref, f32[8,2,8,384]{3,2,1,0:T(8,128)S(1)} %get-tuple-element.69.far_ref, f32[8,2,8,384]{3,2,1,0:T(8,128)S(1)} %collective-permute-done.10.beyond_ref, ...), custom_call_target="tpu_custom_call" | custom-call | flops 25000000 | bytes 892928 | tf_op jit(solution)/shard_map/second_across/pallas_call | solution.py:22
  56.1 1.2 %collective-permute-done.13 = f32[8,128]{1,0:T(8,128)S(1)} collective-permute-done((f32[8,128]{1,0:T(8,128)S(1)}, f32[8,128]{1,0:T(8,128)S(1)}, u32[]{:S(2)}, u32[]{:S(2)}) %collective-permute-start.13) | collective-permute-done | bytes 4128 | tf_op jit(solution)/shard_map/ppermute | solution.py:59
  57.3 1.8 %collective-permute-start.14 = (f32[8,128]{1,0:T(8,128)S(1)}, f32[8,128]{1,0:T(8,128)S(1)}, u32[]{:S(2)}, u32[]{:S(2)}) collective-permute-start(f32[8,128]{1,0:T(8,128)S(1)} %add.34), channel_id=1, source_target_pairs={{0,2},{1,3},{2,0},{3,1},{4,6},{5,7},{6,4},{7,5},{8,10},{9,11},{10,... | collective-permute-start | bytes 12296 | tf_op jit(solution)/shard_map/ppermute | solution.py:59
  59.1 1.8 %collective-permute-done.14 = f32[8,128]{1,0:T(8,128)S(1)} collective-permute-done((f32[8,128]{1,0:T(8,128)S(1)}, f32[8,128]{1,0:T(8,128)S(1)}, u32[]{:S(2)}, u32[]{:S(2)}) %collective-permute-start.14) | collective-permute-done | bytes 4128 | tf_op jit(solution)/shard_map/ppermute | solution.py:59
  61.0 3.5 %collective-permute-done.15 = f32[8,128]{1,0:T(8,128)S(1)} collective-permute-done((f32[8,128]{1,0:T(8,128)S(1)}, f32[8,128]{1,0:T(8,128)S(1)}, u32[]{:S(2)}, u32[]{:S(2)}) %collective-permute-start.15) | collective-permute-done | bytes 4128 | tf_op jit(solution)/shard_map/ppermute | solution.py:59
  64.5 1.7 %collective-permute-start.16 = (f32[8,128]{1,0:T(8,128)S(1)}, f32[8,128]{1,0:T(8,128)S(1)}, u32[]{:S(2)}, u32[]{:S(2)}) collective-permute-start(f32[8,128]{1,0:T(8,128)S(1)} %add.36), channel_id=1, source_target_pairs={{0,8},{1,9},{2,10},{3,11},{4,12},{5,13},{6,14},{7,15},{8,0},{9,1},... | collective-permute-start | bytes 12296 | tf_op jit(solution)/shard_map/ppermute | solution.py:59
  66.2 2.8 %collective-permute-done.16 = f32[8,128]{1,0:T(8,128)S(1)} collective-permute-done((f32[8,128]{1,0:T(8,128)S(1)}, f32[8,128]{1,0:T(8,128)S(1)}, u32[]{:S(2)}, u32[]{:S(2)}) %collective-permute-start.16) | collective-permute-done | bytes 4128 | tf_op jit(solution)/shard_map/ppermute | solution.py:59
  69.4 6.2 %ritz_pairs.3 = (f32[8]{0:T(128)}, f32[8,128]{1,0:T(8,128)S(1)}, f32[8,16,128]{2,1,0:T(8,128)S(1)}) custom-call(f32[8,128]{1,0:T(8,128)S(1)} %add.37.pencil_ref), custom_call_target="tpu_custom_call" | custom-call | flops 10000000 | bytes 73760 | tf_op jit(solution)/shard_map/ritz_pairs/pallas_call | solution.py:22
  76.5 1.4 %images.1.second_ref = f32[8,4,8,384]{3,2,1,0:T(8,128)S(1)} custom-call(f32[2,8,384]{2,1,0:T(8,128)S(1)} %broadcast_in_dim.2.flags_ref, f32[8,2,8,384]{3,2,1,0:T(8,128)S(1)} %get-tuple-element.53.near_ref, f32[8,2,8,384]{3,2,1,0:T(8,128)S(1)} %get-tuple-element.69.far_ref, f32[8,2,8,384]{3,2,1,0:T(8,128)S(1)} %collective-permute-done.17.behind_ref, ...), custom_call_target="tpu_custom_call" | custom-call | flops 1000000 | bytes 1671168 | tf_op jit(solution)/shard_map/images/pallas_call | solution.py:22
  78.0 1.0 %densities.1 = (f32[2,2,8,384]{3,2,1,0:T(8,128)S(1)}, f32[2,2,8,384]{3,2,1,0:T(8,128)S(1)}) custom-call(f32[8,16,128]{2,1,0:T(8,128)S(1)} %get-tuple-element.67.mix_ref, f32[8,128]{1,0:T(8,128)S(1)} %get-tuple-element.68.theta_ref, f32[8,4,8,384]{3,2,1,0:T(8,128)S(1)} %get-tuple-element.57.modes_ref, f32[8,2,8,384]{3,2,1,0:T(8,128)S(1)} %get-tuple-element.53.near_ref, ...), custom_call_target="tpu_custom_call" | custom-call | flops 1000000 | bytes 1740800 | tf_op jit(solution)/shard_map/densities/pallas_call | solution.py:22
  78.9 1.8 %collective-permute-start.18 = (f32[2,2,8,384]{3,2,1,0:T(8,128)S(1)}, f32[2,2,8,384]{3,2,1,0:T(8,128)S(1)}, u32[]{:S(2)}, u32[]{:S(2)}) collective-permute-start(f32[2,2,8,384]{3,2,1,0:T(8,128)S(1)} %get-tuple-element.72), channel_id=1, source_target_pairs={{0,2},{2,0},{4,6},{6,4},{8,10},{10,8},{12,14},{14,12},{1,3},{3,1},... | collective-permute-start | bytes 147464 | tf_op jit(solution)/shard_map/ppermute | solution.py:35
  80.8 2.3 %collective-permute-done.18.other_ref = f32[2,2,8,384]{3,2,1,0:T(8,128)S(1)} collective-permute-done((f32[2,2,8,384]{3,2,1,0:T(8,128)S(1)}, f32[2,2,8,384]{3,2,1,0:T(8,128)S(1)}, u32[]{:S(2)}, u32[]{:S(2)}) %collective-permute-start.18) | collective-permute-done | bytes 49184 | tf_op jit(solution)/shard_map/ppermute | solution.py:35
  (38 shorter events, 5.5 us)
Async XLA Ops:
  0.6 0.8 copy-start.2
  1.4 1.1 %copy-start = (f32[16,2,16,384]{3,2,1,0:T(8,128)S(1)}, f32[16,2,16,384]{3,2,1,0:T(8,128)}, u32[]{:S(2)}) copy-start(f32[16,2,16,384]{3,2,1,0:T(8,128)} %block_ref.3) | copy-start | bytes 2359300
  2.6 0.8 copy-start.3
  3.4 8.4 %copy-start.1 = (f32[16,2,16,384]{3,2,1,0:T(8,128)S(1)}, f32[16,2,16,384]{3,2,1,0:T(8,128)}, u32[]{:S(2)}) copy-start(f32[16,2,16,384]{3,2,1,0:T(8,128)} %block_ref.3) | copy-start | bytes 2359300
  3.5 13.3 %collective-permute-start = (f32[18,2,8,384]{3,2,1,0:T(8,128)S(1)}, f32[18,2,8,384]{3,2,1,0:T(8,128)S(1)}, u32[]{:S(2)}, u32[]{:S(2)}) collective-permute-start(f32[18,2,8,384]{3,2,1,0:T(8,128)S(1)} %get-tuple-element.40), channel_id=1, source_target_pairs={{0,2},{2,0},{4,6},{6,4},{8,10},{10,8},{12,14},{14,12},{1,3},{3,1},... | collective-permute-start | bytes 1327112 | tf_op jit(solution)/shard_map/ppermute | solution.py:35
  6.5 12.7 %collective-permute-start.1 = (f32[18,2,8,384]{3,2,1,0:T(8,128)S(1)}, f32[18,2,8,384]{3,2,1,0:T(8,128)S(1)}, u32[]{:S(2)}, u32[]{:S(2)}) collective-permute-start(f32[18,2,8,384]{3,2,1,0:T(8,128)S(1)} %get-tuple-element.39.mine_ref), channel_id=1, source_target_pairs={{4,0},{14,2},{8,4},{2,6},{12,8},{6,10},{0,12},{10,14},{5,1},{15,3}... | collective-permute-start | bytes 1327112 | tf_op jit(solution)/shard_map/ppermute | solution.py:44
  10.3 1.5 %collective-permute-start.2 = (f32[16,2,4,384]{3,2,1,0:T(4,128)S(1)}, f32[16,2,4,384]{3,2,1,0:T(4,128)S(1)}, u32[]{:S(2)}, u32[]{:S(2)}) collective-permute-start(f32[16,2,4,384]{3,2,1,0:T(4,128)S(1)} %pad_maximum_fusion), channel_id=1, source_target_pairs={{0,1},{1,0},{2,3},{3,2},{4,5},{5,4},{6,7},{7,6},{8,9},{9,8},{10,11... | collective-permute-start | bytes 589832 | tf_op jit(solution)/shard_map/ppermute | solution.py:39
  20.9 1.2 %collective-permute-start.3 = (f32[8,128]{1,0:T(8,128)S(1)}, f32[8,128]{1,0:T(8,128)S(1)}, u32[]{:S(2)}, u32[]{:S(2)}) collective-permute-start(f32[8,128]{1,0:T(8,128)S(1)} %get-tuple-element.44), channel_id=1, source_target_pairs={{0,1},{1,0},{2,3},{3,2},{4,5},{5,4},{6,7},{7,6},{8,9},{9,8},{10,11... | collective-permute-start | bytes 12296 | tf_op jit(solution)/shard_map/ppermute | solution.py:59
  22.2 3.6 %collective-permute-start.4 = (f32[8,128]{1,0:T(8,128)S(1)}, f32[8,128]{1,0:T(8,128)S(1)}, u32[]{:S(2)}, u32[]{:S(2)}) collective-permute-start(f32[8,128]{1,0:T(8,128)S(1)} %add.30), channel_id=1, source_target_pairs={{0,2},{1,3},{2,0},{3,1},{4,6},{5,7},{6,4},{7,5},{8,10},{9,11},{10,... | collective-permute-start | bytes 12296 | tf_op jit(solution)/shard_map/ppermute | solution.py:59
  25.8 3.6 %collective-permute-start.5 = (f32[8,128]{1,0:T(8,128)S(1)}, f32[8,128]{1,0:T(8,128)S(1)}, u32[]{:S(2)}, u32[]{:S(2)}) collective-permute-start(f32[8,128]{1,0:T(8,128)S(1)} %add.31), channel_id=1, source_target_pairs={{0,4},{1,5},{2,6},{3,7},{4,0},{5,1},{6,2},{7,3},{8,12},{9,13},{10,... | collective-permute-start | bytes 12296 | tf_op jit(solution)/shard_map/ppermute | solution.py:59
  29.4 4.5 %collective-permute-start.6 = (f32[8,128]{1,0:T(8,128)S(1)}, f32[8,128]{1,0:T(8,128)S(1)}, u32[]{:S(2)}, u32[]{:S(2)}) collective-permute-start(f32[8,128]{1,0:T(8,128)S(1)} %add.32), channel_id=1, source_target_pairs={{0,8},{1,9},{2,10},{3,11},{4,12},{5,13},{6,14},{7,15},{8,0},{9,1},... | collective-permute-start | bytes 12296 | tf_op jit(solution)/shard_map/ppermute | solution.py:59
  33.9 11.3 %collective-permute-start.7 = (f32[18,2,8,384]{3,2,1,0:T(8,128)S(1)}, f32[18,2,8,384]{3,2,1,0:T(8,128)S(1)}, u32[]{:S(2)}, u32[]{:S(2)}) collective-permute-start(f32[18,2,8,384]{3,2,1,0:T(8,128)S(1)} %collective-permute-done.theirs_ref), channel_id=1, source_target_pairs={{12,0},{6,2},{0,4},{10,6},{4,8},{14,10},{8,12},{2,14},{13,1},{7,3}... | collective-permute-start | bytes 1327112 | tf_op jit(solution)/shard_map/ppermute | solution.py:49
  35.8 8.6 %collective-permute-start.8 = (f32[17,8,384]{2,1,0:T(8,128)S(1)}, f32[17,8,384]{2,1,0:T(8,128)S(1)}, u32[]{:S(2)}, u32[]{:S(2)}) collective-permute-start(f32[17,8,384]{2,1,0:T(8,128)S(1)} %get-tuple-element.51), channel_id=1, source_target_pairs={{0,2},{2,0},{4,6},{6,4},{8,10},{10,8},{12,14},{14,12},{1,3},{3,1},... | collective-permute-start | bytes 626696 | tf_op jit(solution)/shard_map/ppermute | solution.py:35
  38.2 6.2 %collective-permute-start.9 = (f32[17,8,384]{2,1,0:T(8,128)S(1)}, f32[17,8,384]{2,1,0:T(8,128)S(1)}, u32[]{:S(2)}, u32[]{:S(2)}) collective-permute-start(f32[17,8,384]{2,1,0:T(8,128)S(1)} %get-tuple-element.52), channel_id=1, source_target_pairs={{0,1},{1,0},{2,3},{3,2},{4,5},{5,4},{6,7},{7,6},{8,9},{9,8},{10,11... | collective-permute-start | bytes 626696 | tf_op jit(solution)/shard_map/ppermute | solution.py:39
  47.9 6.8 %collective-permute-start.10 = (f32[8,2,8,384]{3,2,1,0:T(8,128)S(1)}, f32[8,2,8,384]{3,2,1,0:T(8,128)S(1)}, u32[]{:S(2)}, u32[]{:S(2)}) collective-permute-start(f32[8,2,8,384]{3,2,1,0:T(8,128)S(1)} %get-tuple-element.53.near_ref), channel_id=1, source_target_pairs={{4,0},{14,2},{8,4},{2,6},{12,8},{6,10},{0,12},{10,14},{5,1},{15,3}... | collective-permute-start | bytes 589832 | tf_op jit(solution)/shard_map/ppermute | solution.py:44
  49.9 4.6 %collective-permute-start.11 = (f32[8,8,384]{2,1,0:T(8,128)S(1)}, f32[8,8,384]{2,1,0:T(8,128)S(1)}, u32[]{:S(2)}, u32[]{:S(2)}) collective-permute-start(f32[8,8,384]{2,1,0:T(8,128)S(1)} %get-tuple-element.55), channel_id=1, source_target_pairs={{0,2},{2,0},{4,6},{6,4},{8,10},{10,8},{12,14},{14,12},{1,3},{3,1},... | collective-permute-start | bytes 294920 | tf_op jit(solution)/shard_map/ppermute | solution.py:35
  49.9 4.6 %collective-permute-start.12 = (f32[8,8,384]{2,1,0:T(8,128)S(1)}, f32[8,8,384]{2,1,0:T(8,128)S(1)}, u32[]{:S(2)}, u32[]{:S(2)}) collective-permute-start(f32[8,8,384]{2,1,0:T(8,128)S(1)} %get-tuple-element.56), channel_id=1, source_target_pairs={{0,1},{1,0},{2,3},{3,2},{4,5},{5,4},{6,7},{7,6},{8,9},{9,8},{10,11... | collective-permute-start | bytes 294920 | tf_op jit(solution)/shard_map/ppermute | solution.py:39
  56.1 1.2 %collective-permute-start.13 = (f32[8,128]{1,0:T(8,128)S(1)}, f32[8,128]{1,0:T(8,128)S(1)}, u32[]{:S(2)}, u32[]{:S(2)}) collective-permute-start(f32[8,128]{1,0:T(8,128)S(1)} %second_across.1), channel_id=1, source_target_pairs={{0,1},{1,0},{2,3},{3,2},{4,5},{5,4},{6,7},{7,6},{8,9},{9,8},{10,11... | collective-permute-start | bytes 12296 | tf_op jit(solution)/shard_map/ppermute | solution.py:59
  57.3 3.6 %collective-permute-start.14 = (f32[8,128]{1,0:T(8,128)S(1)}, f32[8,128]{1,0:T(8,128)S(1)}, u32[]{:S(2)}, u32[]{:S(2)}) collective-permute-start(f32[8,128]{1,0:T(8,128)S(1)} %add.34), channel_id=1, source_target_pairs={{0,2},{1,3},{2,0},{3,1},{4,6},{5,7},{6,4},{7,5},{8,10},{9,11},{10,... | collective-permute-start | bytes 12296 | tf_op jit(solution)/shard_map/ppermute | solution.py:59
  60.9 3.6 %collective-permute-start.15 = (f32[8,128]{1,0:T(8,128)S(1)}, f32[8,128]{1,0:T(8,128)S(1)}, u32[]{:S(2)}, u32[]{:S(2)}) collective-permute-start(f32[8,128]{1,0:T(8,128)S(1)} %add.35), channel_id=1, source_target_pairs={{0,4},{1,5},{2,6},{3,7},{4,0},{5,1},{6,2},{7,3},{8,12},{9,13},{10,... | collective-permute-start | bytes 12296 | tf_op jit(solution)/shard_map/ppermute | solution.py:59
  64.5 4.5 %collective-permute-start.16 = (f32[8,128]{1,0:T(8,128)S(1)}, f32[8,128]{1,0:T(8,128)S(1)}, u32[]{:S(2)}, u32[]{:S(2)}) collective-permute-start(f32[8,128]{1,0:T(8,128)S(1)} %add.36), channel_id=1, source_target_pairs={{0,8},{1,9},{2,10},{3,11},{4,12},{5,13},{6,14},{7,15},{8,0},{9,1},... | collective-permute-start | bytes 12296 | tf_op jit(solution)/shard_map/ppermute | solution.py:59
  69.0 7.5 %collective-permute-start.17 = (f32[8,2,8,384]{3,2,1,0:T(8,128)S(1)}, f32[8,2,8,384]{3,2,1,0:T(8,128)S(1)}, u32[]{:S(2)}, u32[]{:S(2)}) collective-permute-start(f32[8,2,8,384]{3,2,1,0:T(8,128)S(1)} %get-tuple-element.69.far_ref), channel_id=1, source_target_pairs={{12,0},{6,2},{0,4},{10,6},{4,8},{14,10},{8,12},{2,14},{13,1},{7,3}... | collective-permute-start | bytes 589832 | tf_op jit(solution)/shard_map/ppermute | solution.py:49
  78.9 4.2 %collective-permute-start.18 = (f32[2,2,8,384]{3,2,1,0:T(8,128)S(1)}, f32[2,2,8,384]{3,2,1,0:T(8,128)S(1)}, u32[]{:S(2)}, u32[]{:S(2)}) collective-permute-start(f32[2,2,8,384]{3,2,1,0:T(8,128)S(1)} %get-tuple-element.72), channel_id=1, source_target_pairs={{0,2},{2,0},{4,6},{6,4},{8,10},{10,8},{12,14},{14,12},{1,3},{3,1},... | collective-permute-start | bytes 147464 | tf_op jit(solution)/shard_map/ppermute | solution.py:35

commit v5 on v4

--- a/solution.py
+++ b/solution.py
@@ -49,16 +49,18 @@
     return lax.ppermute(x, "gz", [((i + (size - 2 if i % 2 == 0 else 2)) % size, i) for i in range(size)])
 
 
-def grid_sum(x):
+def grid_sum(x, later=()):
     axes = ("gz", "gy")
     total = lax.axis_size("gz") * lax.axis_size("gy")
     if total & (total - 1):
-        return lax.psum(x, axes)
+        return lax.psum(x, axes), later
     mask = 1
     while mask < total:
+        if 2 * mask == total:
+            x, later = lax.optimization_barrier((x, later))
         x = x + lax.ppermute(x, axes, [(i, i ^ mask) for i in range(total)])
         mask *= 2
-    return x
+    return x, later
 
 
 def spread_rows(x, k):
@@ -208,7 +210,7 @@
 
     def unfinished(carry):
         count, worst, _, _ = carry
-        return jnp.logical_and(count < MAX_SWEEPS, worst > 1e-8)
+        return jnp.logical_and(count < MAX_SWEEPS, worst > 1.6e-7)
 
     _, _, upper, lower = lax.while_loop(
         unfinished, sweep, (jnp.int32(0), jnp.float32(1.0), tuple(upper), tuple(lower))
@@ -300,27 +302,50 @@
     return roll(rows, -1, 1) + roll(rows, 1, 1) - 2.0 * rows
 
 
-def prepare_kernel(flags_ref, block_ref, stiffness_ref, concentration_ref, mine_ref, other_ref):
+def is_odd():
+    return lax.rem(lax.axis_index("gz"), 2)
+
+
+def is_high():
+    return lax.rem(1 + is_odd() + lax.axis_index("gy"), 2)
+
+
+def prepare_kernel(block_ref, stiffness_ref, concentration_ref, mine_ref, other_ref, arrived):
     nz, ny, _ = concentration_ref.shape
     half = ny // 2
-    odd = flags_ref[0] > 0.5
-    high = flags_ref[1] > 0.5
-
-    def split(source, a):
-        for z in range(nz):
-            layer = [
-                jnp.where(odd, source(nz - 1 - z)[part], source(z)[part])
-                for part in (slice(0, half), slice(half, ny))
-            ]
-            mine_ref[a, z] = jnp.where(high, layer[1], layer[0])
-            other_ref[a, nz - 1 - z] = jnp.where(high, layer[0], layer[1])
-
-    @pl.loop(0, BLOCK)
-    def _(a):
-        split(lambda z: block_ref[a, z], a)
-
-    split(lambda z: stiffness_ref[z], BLOCK)
-    split(lambda z: concentration_ref[z], BLOCK + 1)
+    odd, high = is_odd(), is_high()
+    upper = pl.ds(pl.multiple_of(half * high, half), half)
+    lower = pl.ds(pl.multiple_of(half * (1 - high), half), half)
+    copies = []
+    for z in range(nz):
+        inward = z + odd * (nz - 1 - 2 * z)
+        outward = nz - 1 - inward
+        for layer, rows, target in ((inward, upper, mine_ref), (outward, lower, other_ref)):
+            moves = (
+                (block_ref.at[:, layer, rows, :], target.at[0:BLOCK, z]),
+                (stiffness_ref.at[layer, rows, :], target.at[BLOCK, z]),
+                (concentration_ref.at[layer, rows, :], target.at[BLOCK + 1, z]),
+            )
+            for source, place in moves:
+                copies.append(pltpu.make_async_copy(source, place, arrived.at[len(copies)]))
+    for copy in copies:
+        copy.start()
+    for copy in copies:
+        copy.wait()
+
+
+def prepare(block, stiffness, concentration):
+    nz, ny, nx = concentration.shape
+    shape = jax.ShapeDtypeStruct((BLOCK + 2, nz, ny // 2, nx), jnp.float32)
+    return pl.pallas_call(
+        prepare_kernel,
+        out_shape=(shape, shape),
+        in_specs=[pl.BlockSpec(memory_space=pltpu.HBM)] * 3,
+        out_specs=[VMEM] * 2,
+        scratch_shapes=[pltpu.SemaphoreType.DMA((6 * nz,))],
+        compiler_params=pltpu.CompilerParams(vmem_limit_bytes=62 * 1024 * 1024),
+        name="prepare",
+    )(block, stiffness, concentration)
 
 
 def first_local_kernel(block_ref, beside_ref, curvature_ref, stiffness_ref, tile_ref, wide_ref, change_ref):
@@ -350,8 +375,8 @@
     )
 
 
-def edges(flags_ref, field, layers):
-    high = flags_ref[1][:2] > 0.5
+def edges(field, layers):
+    high = is_high() == 1
     to_pair, to_core = [], []
     for u in range(layers):
         first, last = field(u)[:2], field(u)[-2:]
@@ -360,7 +385,19 @@
     return to_pair[::-1], to_core
 
 
-def first_across_kernel(flags_ref, mine_ref, theirs_ref, beyond_ref, tile_ref, sum_ref, pair_ref, core_ref):
+def edges_kernel(mine_ref, theirs_ref, pair_ref, core_ref):
+    nz = mine_ref.shape[1]
+
+    @pl.loop(0, BLOCK + 1)
+    def _(a):
+        field = lambda u: mine_ref[a, u] if u < nz else theirs_ref[a, u - nz]
+        to_pair, to_core = edges(field, 2 * nz)
+        for u in range(2 * nz):
+            pair_ref[a, 2 * u : 2 * u + 2, :] = to_pair[u]
+            core_ref[a, 2 * u : 2 * u + 2, :] = to_core[u]
+
+
+def first_across_kernel(mine_ref, theirs_ref, beyond_ref, tile_ref, sum_ref):
     nz, ny = mine_ref.shape[1:3]
     half = 8 * HALF
     stiff = jnp.zeros((8 * BLOCK, 8 * BLOCK), jnp.float32)
@@ -382,14 +419,6 @@
         tile_ref[...] + folded(stiff[:half], 2 * BLOCK) + folded(stiff[half:], 3 * BLOCK)
     )
 
-    @pl.loop(0, BLOCK + 1)
-    def _(a):
-        field = lambda u: sources[u][0][a, sources[u][1]]
-        to_pair, to_core = edges(flags_ref, field, 2 * nz)
-        for u in range(2 * nz):
-            pair_ref[a, 2 * u : 2 * u + 2, :] = to_pair[u]
-            core_ref[a, 2 * u : 2 * u + 2, :] = to_core[u]
-
 
 def apply_hessian(field, layers, stiff_layers, u, curvature, wide, stiff_wide):
     def flux(k):
@@ -403,19 +432,17 @@
     return total + change[8 : 8 + field.shape[0]]
 
 
-def store_wide(wide_ref, index, flags_ref, field, pair_rows, core_rows):
+def store_wide(wide_ref, index, field, pair_rows, core_rows):
     ny = field.shape[0]
-    high = flags_ref[1][:2] > 0.5
+    high = is_high() == 1
     wide_ref[index, 6:8, :] = jnp.where(high, pair_rows, core_rows)
     wide_ref[index, 8 : 8 + ny, :] = field
     wide_ref[index, 8 + ny : 10 + ny, :] = jnp.where(high, core_rows, pair_rows)
 
 
-def update_kernel(
-    flags_ref, mix_ref, theta_ref, mine_ref, theirs_ref, behind_ref, beyond_ref, pair_ref, core_ref,
-    modes_ref, images_ref, near_ref, far_ref, to_pair_ref, to_core_ref,
-    curvature_ref, stiff_layers_ref, stiff_wide_ref,
-    mixed_ref, mixed_pair_ref, mixed_core_ref, wide_ref, inverse_ref,
+def first_images_kernel(
+    mine_ref, theirs_ref, behind_ref, beyond_ref, pair_ref, core_ref,
+    images_ref, inverse_ref, curvature_ref, stiff_layers_ref, stiff_wide_ref, wide_ref,
 ):
     depth, ny, nx = curvature_ref.shape
     nz = depth // 2
@@ -424,31 +451,13 @@
     sources = [(behind_ref, nz - 2), (behind_ref, nz - 1)]
     sources = sources + [(mine_ref, z) for z in range(nz)] + [(theirs_ref, z) for z in range(nz)]
     sources = sources + [(beyond_ref, 0), (beyond_ref, 1)]
-    tiles = [(source, z, mixed_ref, k) for k, (source, z) in enumerate(sources)]
-    tiles = tiles + [(pair_ref, None, mixed_pair_ref, None), (core_ref, None, mixed_core_ref, None)]
-    for source, z, target, k in tiles:
-        for start in range(0, nx, LANES):
-            lanes = slice(start, start + LANES)
-            if z is None:
-                parts = [source[a, :, lanes] for a in range(BLOCK)]
-            else:
-                parts = [source[a, z, :, lanes] for a in range(BLOCK)]
-            for j in range(MODES):
-                mixed = mix_ref[j, 0:1, :] * parts[0]
-                for a in range(1, BLOCK):
-                    mixed = mixed + mix_ref[j, a : a + 1, :] * parts[a]
-                if z is None:
-                    target[j, :, lanes] = mixed
-                else:
-                    target[j, k, :, lanes] = mixed
-
     for k in range(depth + 2):
         source, z = sources[k + 1]
         stiff_layers_ref[k] = source[BLOCK, z]
     for u in range(depth):
         rows = slice(2 * u, 2 * u + 2)
         stiff = stiff_layers_ref[u + 1]
-        store_wide(stiff_wide_ref, u, flags_ref, stiff, pair_ref[BLOCK, rows, :], core_ref[BLOCK, rows, :])
+        store_wide(stiff_wide_ref, u, stiff, pair_ref[BLOCK, rows, :], core_ref[BLOCK, rows, :])
         source, z = sources[u + 2]
         concentration = source[BLOCK + 1, z]
         curvature = 3.0 * concentration * concentration - 1.0
@@ -459,27 +468,49 @@
         total = total + (roll(stiff, -1, 1) + roll(stiff, 1, 1))
         inverse_ref[u] = 1.0 / total
 
+    @pl.loop(0, BLOCK)
+    def _(a):
+        layers = [source[a, z] for source, z in sources]
+        for u in range(depth):
+            rows = slice(2 * u, 2 * u + 2)
+            store_wide(wide_ref, u, layers[u + 2], pair_ref[a, rows, :], core_ref[a, rows, :])
+            images_ref[a, u] = apply_hessian(
+                layers[u + 2], lambda k: layers[k + 2], lambda k: stiff_layers_ref[k + 1], u,
+                curvature_ref[u], wide_ref[u], stiff_wide_ref[u],
+            )
+
+
+def update_kernel(
+    mix_ref, theta_ref, mine_ref, theirs_ref, search_images_ref, inverse_ref,
+    modes_ref, images_ref, near_ref, far_ref, to_pair_ref, to_core_ref,
+):
+    depth, ny, nx = inverse_ref.shape
+    nz = depth // 2
+    for start in range(0, nx, LANES):
+        lanes = slice(start, start + LANES)
+        for u in range(depth):
+            source, z = (mine_ref, u) if u < nz else (theirs_ref, u - nz)
+            vectors = [source[a, z, :, lanes] for a in range(BLOCK)]
+            images = [search_images_ref[a, u, :, lanes] for a in range(BLOCK)]
+            inverse = inverse_ref[u, :, lanes]
+            for j in range(MODES):
+                mode = mix_ref[j, 0:1, :] * vectors[0]
+                image = mix_ref[j, 0:1, :] * images[0]
+                for a in range(1, BLOCK):
+                    mode = mode + mix_ref[j, a : a + 1, :] * vectors[a]
+                    image = image + mix_ref[j, a : a + 1, :] * images[a]
+                modes_ref[j, u, :, lanes] = mode
+                images_ref[j, u, :, lanes] = image
+                correction = (image - theta_ref[j : j + 1, :] * mode) * inverse
+                if u < nz:
+                    near_ref[j, u, :, lanes] = correction
+                else:
+                    far_ref[j, u - nz, :, lanes] = correction
+
     @pl.loop(0, MODES)
     def _(j):
-        theta = jnp.broadcast_to(theta_ref[pl.ds(j, 1), :1], (1, nx))
-        corrections = []
-        for u in range(depth):
-            rows = slice(2 * u, 2 * u + 2)
-            mode = mixed_ref[j, u + 2]
-            store_wide(wide_ref, u, flags_ref, mode, mixed_pair_ref[j, rows, :], mixed_core_ref[j, rows, :])
-            image = apply_hessian(
-                mode, lambda k: mixed_ref[j, k + 2], lambda k: stiff_layers_ref[k + 1], u,
-                curvature_ref[u], wide_ref[u], stiff_wide_ref[u],
-            )
-            images_ref[j, u] = image
-            modes_ref[j, u] = mode
-            correction = (image - theta * mode) * inverse_ref[u]
-            corrections.append(correction)
-            if u < nz:
-                near_ref[j, u] = correction
-            else:
-                far_ref[j, u - nz] = correction
-        to_pair, to_core = edges(flags_ref, lambda u: corrections[u], depth)
+        field = lambda u: near_ref[j, u] if u < nz else far_ref[j, u - nz]
+        to_pair, to_core = edges(field, depth)
         for u in range(depth):
             to_pair_ref[j, 2 * u : 2 * u + 2, :] = to_pair[u]
             to_core_ref[j, 2 * u : 2 * u + 2, :] = to_core[u]
@@ -516,7 +547,7 @@
 
 
 def second_across_kernel(
-    flags_ref, near_ref, far_ref, beyond_ref, pair_ref, core_ref, stiff_layers_ref, tile_ref,
+    near_ref, far_ref, beyond_ref, pair_ref, core_ref, stiff_layers_ref, tile_ref,
     sum_ref, wide_ref, change_ref,
 ):
     nz, ny = near_ref.shape[1:3]
@@ -530,7 +561,7 @@
         for u in range(depth):
             source, z = sources[u]
             rows = slice(2 * u, 2 * u + 2)
-            store_wide(wide_ref, u, flags_ref, source[j, z], pair_ref[j, rows, :], core_ref[j, rows, :])
+            store_wide(wide_ref, u, source[j, z], pair_ref[j, rows, :], core_ref[j, rows, :])
             wide = wide_ref[u]
             change = roll(wide, -1, 0) + roll(wide, 1, 0) - 2.0 * wide
             change_ref[j, u] = change[8 : 8 + ny]
@@ -554,7 +585,7 @@
 
 
 def images_kernel(
-    flags_ref, near_ref, far_ref, behind_ref, beyond_ref, pair_ref, core_ref,
+    near_ref, far_ref, behind_ref, beyond_ref, pair_ref, core_ref,
     curvature_ref, stiff_layers_ref, stiff_wide_ref, images_ref, wide_ref,
 ):
     depth, ny, nx = curvature_ref.shape
@@ -569,7 +600,7 @@
         layers = [source[j, z] for source, z in sources]
         for u in range(depth):
             rows = slice(2 * u, 2 * u + 2)
-            store_wide(wide_ref, u, flags_ref, layers[u + 2], pair_ref[j, rows, :], core_ref[j, rows, :])
+            store_wide(wide_ref, u, layers[u + 2], pair_ref[j, rows, :], core_ref[j, rows, :])
             images_ref[j, u] = apply_hessian(
                 layers[u + 2], lambda k: layers[k + 2], lambda k: stiff_layers_ref[k + 1], u,
                 curvature_ref[u], wide_ref[u], stiff_wide_ref[u],
@@ -577,18 +608,16 @@
 
 
 def density_kernel(
-    factor, mix_ref, theta_ref, modes_ref, near_ref, far_ref, first_ref, second_ref, mine_ref, theirs_ref,
+    factor, offset, mix_ref, theta_ref, modes_ref, corrections_ref, first_ref, second_ref, density_ref,
 ):
-    depth, ny, nx = modes_ref.shape[1:]
-    nz = depth // 2
-    for u in range(depth):
+    nz, ny, nx = density_ref.shape[1:]
+    for layer in range(nz):
+        u = offset + layer
+        place = layer if offset == 0 else nz - 1 - layer
         for start in range(0, nx, LANES):
             lanes = slice(start, start + LANES)
             vectors = [modes_ref[a, u, :, lanes] for a in range(MODES)]
-            if u < nz:
-                vectors = vectors + [near_ref[a, u, :, lanes] for a in range(MODES)]
-            else:
-                vectors = vectors + [far_ref[a, u - nz, :, lanes] for a in range(MODES)]
+            vectors = vectors + [corrections_ref[a, layer, :, lanes] for a in range(MODES)]
             images = [first_ref[a, u, :, lanes] for a in range(MODES)]
             images = images + [second_ref[a, u, :, lanes] for a in range(MODES)]
             mode_sum = jnp.zeros((ny, LANES), jnp.float32)
@@ -602,18 +631,14 @@
                 residual = image - theta_ref[j : j + 1, :] * mode
                 mode_sum = mode_sum + mode * mode
                 residual_sum = residual_sum + residual * residual
-            for k, total in ((0, mode_sum), (1, residual_sum)):
-                if u < nz:
-                    mine_ref[k, u, :, lanes] = factor * total
-                else:
-                    theirs_ref[k, depth - 1 - u, :, lanes] = factor * total
-
-
-def merge_kernel(flags_ref, mine_ref, other_ref, modes_ref, residuals_ref):
+            density_ref[0, place, :, lanes] = factor * mode_sum
+            density_ref[1, place, :, lanes] = factor * residual_sum
+
+
+def merge_kernel(mine_ref, other_ref, modes_ref, residuals_ref):
     nz, ny, _ = modes_ref.shape
     half = ny // 2
-    odd = flags_ref[0] > 0.5
-    high = flags_ref[1] > 0.5
+    odd, high = is_odd() == 1, is_high() == 1
     for k, target in ((0, modes_ref), (1, residuals_ref)):
         for z in range(nz):
             mine = jnp.where(odd, mine_ref[k, nz - 1 - z], mine_ref[k, z])
@@ -627,12 +652,6 @@
     half = ny // 2
     depth = 2 * nz
     cells_total = nz * ny * nx * lax.axis_size("gz") * lax.axis_size("gy")
-    odd = lax.axis_index("gz") % 2
-    high = 1 - (odd ^ lax.axis_index("gy"))
-    flags = jnp.broadcast_to(
-        jnp.stack([odd, high]).astype(jnp.float32)[:, None, None], (2, half, nx)
-    )
-    halves = (BLOCK + 2, nz, half, nx)
     vector_rows = (BLOCK + 1, 2 * depth, nx)
     plane = (depth, half, nx)
     wide = (depth, half + 16, nx)
@@ -640,9 +659,7 @@
     mode_half = (MODES, nz, half, nx)
     mode_rows = (MODES, 2 * depth, nx)
 
-    mine, other = call(
-        prepare_kernel, [halves, halves], [flags, initial_block, stiffness, concentration], name="prepare"
-    )
+    mine, other = prepare(initial_block, stiffness, concentration)
     theirs = pair_swap(other)
     beyond = from_beyond(mine[:, :2])
     edge_rows = jnp.concatenate([initial_block[:, :, ny - 2 :], initial_block[:, :, :2]], axis=2)
@@ -656,35 +673,35 @@
         flops=100000000,
         name="first_local",
     )
-    theirs, beyond, tile = lax.optimization_barrier((theirs, beyond, tile))
-    tile, to_pair, to_core = call(
+    theirs, tile = lax.optimization_barrier((theirs, tile))
+    to_pair, to_core = call(
+        edges_kernel, [vector_rows, vector_rows], [mine, theirs], name="edges"
+    )
+    core_rows = core_swap(to_core)
+    pair_rows = pair_swap(to_pair)
+    held, beyond, to_pair, to_core = lax.optimization_barrier((theirs, beyond, to_pair, to_core))
+    behind = from_behind(held[:, nz - 2 :])
+    (tile,) = call(
         first_across_kernel,
-        [(8, LANES), vector_rows, vector_rows],
-        [flags, mine, theirs, beyond, tile],
+        [(8, LANES)],
+        [mine, theirs, beyond, tile],
         flops=25000000,
         name="first_across",
     )
-    pencil = grid_sum(tile)
-    pencil, held, to_pair, to_core = lax.optimization_barrier((pencil, theirs, to_pair, to_core))
-    behind = from_behind(held[:, nz - 2 :])
-    pair_rows = pair_swap(to_pair)
-    core_rows = core_swap(to_core)
+    pencil, (behind, pair_rows, core_rows) = grid_sum(tile, (behind, pair_rows, core_rows))
+    search_images, inverse, curvature, stiff_layers, stiff_wide = call(
+        first_images_kernel,
+        [(BLOCK,) + plane, plane, plane, (depth + 2, half, nx), wide],
+        [mine, theirs, behind, beyond, pair_rows, core_rows],
+        scratch=[pltpu.VMEM(wide, jnp.float32)],
+        flops=6000000,
+        name="first_images",
+    )
     _, theta_rows, mix = ritz_pairs(pencil)
-
-    (
-        modes, mode_images, near, far, to_pair, to_core, curvature, stiff_layers, stiff_wide,
-    ) = call(
+    modes, mode_images, near, far, to_pair, to_core = call(
         update_kernel,
-        [mode_plane, mode_plane, mode_half, mode_half, mode_rows, mode_rows]
-        + [plane, (depth + 2, half, nx), wide],
-        [flags, mix, theta_rows, mine, theirs, behind, beyond, pair_rows, core_rows],
-        scratch=[
-            pltpu.VMEM((MODES, depth + 4, half, nx), jnp.float32),
-            pltpu.VMEM(mode_rows, jnp.float32),
-            pltpu.VMEM(mode_rows, jnp.float32),
-            pltpu.VMEM(wide, jnp.float32),
-            pltpu.VMEM(plane, jnp.float32),
-        ],
+        [mode_plane, mode_plane, mode_half, mode_half, mode_rows, mode_rows],
+        [mix, theta_rows, mine, theirs, search_images, inverse],
         name="update",
     )
 
@@ -698,34 +715,39 @@
         flops=80000000,
         name="second_local",
     )
-    beyond, pair_rows, core_rows, tile = lax.optimization_barrier((beyond, pair_rows, core_rows, tile))
+    held, beyond, pair_rows, core_rows, tile = lax.optimization_barrier(
+        (far, beyond, pair_rows, core_rows, tile)
+    )
+    behind = from_behind(held[:, nz - 2 :])
     (tile,) = call(
         second_across_kernel,
         [(8, LANES)],
-        [flags, near, far, beyond, pair_rows, core_rows, stiff_layers, tile],
+        [near, far, beyond, pair_rows, core_rows, stiff_layers, tile],
         scratch=[pltpu.VMEM(wide, jnp.float32), pltpu.VMEM(mode_plane, jnp.float32)],
         flops=25000000,
         name="second_across",
     )
-    pencil = grid_sum(tile)
-    pencil, held = lax.optimization_barrier((pencil, far))
-    behind = from_behind(held[:, nz - 2 :])
-    theta, theta_rows, mix = ritz_pairs(pencil)
+    pencil, behind = grid_sum(tile, behind)
     (correction_images,) = call(
         images_kernel,
         [mode_plane],
-        [flags, near, far, behind, beyond, pair_rows, core_rows, curvature, stiff_layers, stiff_wide],
+        [near, far, behind, beyond, pair_rows, core_rows, curvature, stiff_layers, stiff_wide],
         scratch=[pltpu.VMEM(wide, jnp.float32)],
         name="images",
     )
-    mine, theirs = call(
-        functools.partial(density_kernel, float(cells_total / MODES)),
-        [(2, nz, half, nx)] * 2,
-        [mix, theta_rows, modes, near, far, mode_images, correction_images],
-        name="densities",
-    )
+    theta, theta_rows, mix = ritz_pairs(pencil)
+    shares = []
+    for offset, corrections in ((nz, far), (0, near)):
+        (share,) = call(
+            functools.partial(density_kernel, float(cells_total / MODES), offset),
+            [(2, nz, half, nx)],
+            [mix, theta_rows, modes, corrections, mode_images, correction_images],
+            name="densities",
+        )
+        shares.append(share)
+    other = pair_swap(shares[0])
     mode_density, residual_density = call(
-        merge_kernel, [(nz, ny, nx)] * 2, [flags, mine, pair_swap(theirs)], name="merge"
+        merge_kernel, [(nz, ny, nx)] * 2, [shares[1], other], name="merge"
     )
     return (theta, mode_density, residual_density)
 

time: 84 us -> 79.6 us (0.948)
  waiting for transfers between devices: 26.6 us -> 20.1 us
  Pallas kernels: 30 us -> 33.2 us
  local copies, waits for them, and re-layouts: 2.71 us -> 0.69 us
    ppermute x8, waiting for transfers between devices: 17.6 us -> 14.6 us  [grid_sum(): x = x + lax.ppermute(x, axes, [(i, i ^ mask) for i in range(total)])]
    pallas_call x0 -> x1, Pallas kernels: none -> 2.43 us  [prepare(): pl.pallas_call(prepare_kernel, out_shape=(shape, shape), in_specs=[pl.Blo...]
    unnamed x8, local copies, waits for them, and re-layouts: 2.56 us -> 0.62 us
    ppermute x2, waiting for transfers between devices: 1.66 us -> 0.01 us  [from_behind(): lax.ppermute(x, 'gz', [((i + (size - 2 if i % 2 == 0 else 2)) % size, i)...]
    ppermute x4, waiting for transfers between devices: 3.33 us -> 1.71 us  [pair_swap(): lax.ppermute(x, 'gz', [(i, i ^ 1) for i in range(lax.axis_size('gz'))])]
    ppermute x4, starting transfers between devices: 7.2 us -> 8.65 us  [pair_swap(): lax.ppermute(x, 'gz', [(i, i ^ 1) for i in range(lax.axis_size('gz'))])]
    pallas_call x11 -> x13, Pallas kernels: 30 us -> 30.8 us  [call(): pl.pallas_call(kernel, out_shape=out_shape, in_specs=[VMEM] * len(args),...]
  transfers between devices with their start and end apart: 19 -> 19, of which waited for: 15 -> 11; matrix products, arithmetic and copies ran while one was open for 0% -> 0% of each run, Pallas kernels for 25% -> 21%
where the time goes in v5:
time: 79.6 us; the launch traced here: 79 us
  Pallas kernels  33.2 us (42%)
  starting transfers between devices  24.1 us (30%)
  waiting for transfers between devices  20.1 us (25%)
    pallas_call x13, Pallas kernels, call(): pl.pallas_call(kernel, out_shape=out_shape, in_specs=[VMEM] * len(args),...  30.8 us
    ppermute x8, waiting for transfers between devices, grid_sum(): x = x + lax.ppermute(x, axes, [(i, i ^ mask) for i in range(total)])  14.6 us
    ppermute x4, starting transfers between devices, pair_swap(): lax.ppermute(x, 'gz', [(i, i ^ 1) for i in range(lax.axis_size('gz'))])  8.65 us
    ppermute x8, starting transfers between devices, grid_sum(): x = x + lax.ppermute(x, axes, [(i, i ^ mask) for i in range(total)])  8.47 us
    ppermute x2, starting transfers between devices, from_beyond(): lax.ppermute(x, 'gz', [((i + (2 if i % 2 == 0 else size - 2)) % size, i)...  4.84 us
    ppermute x2, waiting for transfers between devices, from_beyond(): lax.ppermute(x, 'gz', [((i + (2 if i % 2 == 0 else size - 2)) % size, i)...  2.97 us
    pallas_call x1, Pallas kernels, prepare(): pl.pallas_call(prepare_kernel, out_shape=(shape, shape), in_specs=[pl.Blo...  2.43 us
    ppermute x2, starting transfers between devices, from_behind(): lax.ppermute(x, 'gz', [((i + (size - 2 if i % 2 == 0 else 2)) % size, i)...  2.05 us
  transfers between devices with their start and end apart: 19, of which 11 were waited for; matrix products, arithmetic and copies ran while one was open for 0% of the time, Pallas kernels for 21%

profile of v5, /device:TPU:0, one launch (start us, length us, event | category | flops | bytes accessed | tf_op | source)
XLA Modules:
  0.0 79.0 jit_solution(6404666441160594970)
XLA Ops:
  0.6 2.4 %prepare.1 = (f32[18,2,8,384]{3,2,1,0:T(8,128)}, f32[18,2,8,384]{3,2,1,0:T(8,128)}) custom-call(f32[16,2,16,384]{3,2,1,0:T(8,128)} %block_ref.3, f32[2,16,384]{2,1,0:T(8,128)} %stiffness_ref.3, f32[2,16,384]{2,1,0:T(8,128)} %concentration_ref.1), custom_call_target="tpu_custom_call" | custom-call | tf_op jit(solution)/shard_map/prepare/pallas_call | solution.py:340
  3.1 3.0 %collective-permute-start = (f32[18,2,8,384]{3,2,1,0:T(8,128)}, f32[18,2,8,384]{3,2,1,0:T(8,128)S(1)}, u32[]{:S(2)}, u32[]{:S(2)}) collective-permute-start(f32[18,2,8,384]{3,2,1,0:T(8,128)} %get-tuple-element.41), channel_id=1, source_target_pairs={{0,2},{2,0},{4,6},{6,4},{8,10},{10,8},{12,14},{14,12},{1,3},{3,1},... | collective-permute-start | bytes 1327112 | tf_op jit(solution)/shard_map/ppermute | solution.py:35
  6.1 3.6 %collective-permute-start.2 = (f32[18,2,8,384]{3,2,1,0:T(8,128)}, f32[18,2,8,384]{3,2,1,0:T(8,128)S(1)}, u32[]{:S(2)}, u32[]{:S(2)}) collective-permute-start(f32[18,2,8,384]{3,2,1,0:T(8,128)} %get-tuple-element.40.mine_ref), channel_id=1, source_target_pairs={{4,0},{14,2},{8,4},{2,6},{12,8},{6,10},{0,12},{10,14},{5,1},{15,3}... | collective-permute-start | bytes 1327112 | tf_op jit(solution)/shard_map/ppermute | solution.py:44
  10.6 0.8 %collective-permute-done.1.beside_ref = f32[16,2,4,384]{3,2,1,0:T(4,128)S(1)} collective-permute-done((f32[16,2,4,384]{3,2,1,0:T(4,128)S(1)}, f32[16,2,4,384]{3,2,1,0:T(4,128)S(1)}, u32[]{:S(2)}, u32[]{:S(2)}) %collective-permute-start.1) | collective-permute-done | bytes 196640 | tf_op jit(solution)/shard_map/ppermute | solution.py:39
  11.4 4.9 %first_local.1.tile_ref = f32[8,128]{1,0:T(8,128)S(1)} custom-call(f32[16,2,16,384]{3,2,1,0:T(8,128)S(1)} %copy-done.1, f32[16,2,4,384]{3,2,1,0:T(4,128)S(1)} %collective-permute-done.1.beside_ref, f32[2,16,384]{2,1,0:T(8,128)S(1)} %fusion.curvature_ref, f32[2,16,384]{2,1,0:T(8,128)S(1)} %copy-done.2), custom_call_target="tpu_custom_call" | custom-call | flops 100000000 | bytes 1085440 | tf_op jit(solution)/shard_map/first_local/pallas_call | solution.py:22
  16.9 3.0 %collective-permute-done.2.beyond_ref = f32[18,2,8,384]{3,2,1,0:T(8,128)S(1)} collective-permute-done((f32[18,2,8,384]{3,2,1,0:T(8,128)}, f32[18,2,8,384]{3,2,1,0:T(8,128)S(1)}, u32[]{:S(2)}, u32[]{:S(2)}) %collective-permute-start.2) | collective-permute-done | bytes 442400 | tf_op jit(solution)/shard_map/ppermute | solution.py:44
  19.9 2.4 %collective-permute-start.7 = (f32[17,8,384]{2,1,0:T(8,128)S(1)}, f32[17,8,384]{2,1,0:T(8,128)S(1)}, u32[]{:S(2)}, u32[]{:S(2)}) collective-permute-start(f32[17,8,384]{2,1,0:T(8,128)S(1)} %get-tuple-element.43), channel_id=1, source_target_pairs={{0,2},{2,0},{4,6},{6,4},{8,10},{10,8},{12,14},{14,12},{1,3},{3,1},... | collective-permute-start | bytes 626696 | tf_op jit(solution)/shard_map/ppermute | solution.py:35
  22.3 1.4 %first_across.1 = f32[8,128]{1,0:T(8,128)S(1)} custom-call(f32[18,2,8,384]{3,2,1,0:T(8,128)S(1)} %copy-done, f32[18,2,8,384]{3,2,1,0:T(8,128)S(1)} %collective-permute-done.theirs_ref, f32[18,2,8,384]{3,2,1,0:T(8,128)S(1)} %collective-permute-done.2.beyond_ref, f32[8,128]{1,0:T(8,128)S(1)} %first_local.1.tile_ref), custom_call_target="tpu_custom_call" | custom-call | flops 25000000 | bytes 1335296 | tf_op jit(solution)/shard_map/first_across/pallas_call | solution.py:22
  24.3 0.8 %collective-permute-done.3 = f32[8,128]{1,0:T(8,128)S(1)} collective-permute-done((f32[8,128]{1,0:T(8,128)S(1)}, f32[8,128]{1,0:T(8,128)S(1)}, u32[]{:S(2)}, u32[]{:S(2)}) %collective-permute-start.3) | collective-permute-done | bytes 4128 | tf_op jit(solution)/shard_map/ppermute | solution.py:61
  25.1 3.6 %collective-permute-done.4 = f32[8,128]{1,0:T(8,128)S(1)} collective-permute-done((f32[8,128]{1,0:T(8,128)S(1)}, f32[8,128]{1,0:T(8,128)S(1)}, u32[]{:S(2)}, u32[]{:S(2)}) %collective-permute-start.4) | collective-permute-done | bytes 4128 | tf_op jit(solution)/shard_map/ppermute | solution.py:61
  28.7 3.7 %collective-permute-done.5 = f32[8,128]{1,0:T(8,128)S(1)} collective-permute-done((f32[8,128]{1,0:T(8,128)S(1)}, f32[8,128]{1,0:T(8,128)S(1)}, u32[]{:S(2)}, u32[]{:S(2)}) %collective-permute-start.5) | collective-permute-done | bytes 4128 | tf_op jit(solution)/shard_map/ppermute | solution.py:61
  32.4 2.3 %collective-permute-start.9 = (f32[8,128]{1,0:T(8,128)S(1)}, f32[8,128]{1,0:T(8,128)S(1)}, u32[]{:S(2)}, u32[]{:S(2)}) collective-permute-start(f32[8,128]{1,0:T(8,128)S(1)} %add.27), channel_id=1, source_target_pairs={{0,8},{1,9},{2,10},{3,11},{4,12},{5,13},{6,14},{7,15},{8,0},{9,1},... | collective-permute-start | bytes 12296 | tf_op jit(solution)/shard_map/ppermute | solution.py:61
  34.7 3.0 %first_images.1 = (f32[16,4,8,384]{3,2,1,0:T(8,128)S(1)}, f32[4,8,384]{2,1,0:T(8,128)S(1)}, f32[4,8,384]{2,1,0:T(8,128)S(1)}, f32[6,8,384]{2,1,0:T(8,128)S(1)}, f32[4,24,384]{2,1,0:T(8,128)S(1)}) custom-call(f32[18,2,8,384]{3,2,1,0:T(8,128)S(1)} %copy-done, f32[18,2,8,384]{3,2,1,0:T(8,128)S(1)} %collective-permute-done.theirs_ref, ...), custom_call_target="tpu_custom_call" | custom-call | flops 6000000 | bytes 3293184 | tf_op jit(solution)/shard_map/first_images/pallas_call | solution.py:22
  37.7 6.2 %ritz_pairs.2 = (f32[8]{0:T(128)}, f32[8,128]{1,0:T(8,128)S(1)}, f32[8,16,128]{2,1,0:T(8,128)S(1)}) custom-call(f32[8,128]{1,0:T(8,128)S(1)} %add.28.pencil_ref), custom_call_target="tpu_custom_call" | custom-call | flops 10000000 | bytes 73760 | tf_op jit(solution)/shard_map/ritz_pairs/pallas_call | solution.py:22
  44.0 1.2 %update.1 = (f32[8,4,8,384]{3,2,1,0:T(8,128)S(1)}, f32[8,4,8,384]{3,2,1,0:T(8,128)S(1)}, f32[8,2,8,384]{3,2,1,0:T(8,128)S(1)}, f32[8,2,8,384]{3,2,1,0:T(8,128)S(...) custom-call(f32[8,16,128]{2,1,0:T(8,128)S(1)} %get-tuple-element.49.mix_ref, ...), custom_call_target="tpu_custom_call" | custom-call | flops 1000000 | bytes 3166208 | tf_op jit(solution)/shard_map/update/pallas_call | solution.py:22
  45.2 1.2 %collective-permute-start.10 = (f32[8,2,8,384]{3,2,1,0:T(8,128)S(1)}, f32[8,2,8,384]{3,2,1,0:T(8,128)S(1)}, u32[]{:S(2)}, u32[]{:S(2)}) collective-permute-start(f32[8,2,8,384]{3,2,1,0:T(8,128)S(1)} %get-tuple-element.56.near_ref.corrections_ref), channel_id=1, source_target_pairs={{4,0},{14,2},{8,4},{2,6},{12,8},{6,10},{0,12},{10,14},{5,1},{15,3}... | collective-permute-start | bytes 589832 | tf_op jit(solution)/shard_map/ppermute | solution.py:44
  46.4 1.1 %collective-permute-start.11 = (f32[8,8,384]{2,1,0:T(8,128)S(1)}, f32[8,8,384]{2,1,0:T(8,128)S(1)}, u32[]{:S(2)}, u32[]{:S(2)}) collective-permute-start(f32[8,8,384]{2,1,0:T(8,128)S(1)} %get-tuple-element.58), channel_id=1, source_target_pairs={{0,2},{2,0},{4,6},{6,4},{8,10},{10,8},{12,14},{14,12},{1,3},{3,1},... | collective-permute-start | bytes 294920 | tf_op jit(solution)/shard_map/ppermute | solution.py:35
  47.5 3.6 %second_local.1.tile_ref = f32[8,128]{1,0:T(8,128)S(1)} custom-call(f32[8,4,8,384]{3,2,1,0:T(8,128)S(1)} %get-tuple-element.60.modes_ref, f32[8,4,8,384]{3,2,1,0:T(8,128)S(1)} %get-tuple-element.61.images_ref.first_ref, f32[8,2,8,384]{3,2,1,0:T(8,128)S(1)} %get-tuple-element.56.near_ref.corrections_ref, ...), custom_call_target="tpu_custom_call" | custom-call | flops 80000000 | bytes 1306624 | tf_op jit(solution)/shard_map/second_local/pallas_call | solution.py:22
  51.2 2.0 %collective-permute-start.16 = (f32[8,2,8,384]{3,2,1,0:T(8,128)S(1)}, f32[8,2,8,384]{3,2,1,0:T(8,128)S(1)}, u32[]{:S(2)}, u32[]{:S(2)}) collective-permute-start(f32[8,2,8,384]{3,2,1,0:T(8,128)S(1)} %get-tuple-element.68.far_ref.corrections_ref), channel_id=1, source_target_pairs={{12,0},{6,2},{0,4},{10,6},{4,8},{14,10},{8,12},{2,14},{13,1},{7,3}... | collective-permute-start | bytes 589832 | tf_op jit(solution)/shard_map/ppermute | solution.py:49
  53.2 1.4 %second_across.1 = f32[8,128]{1,0:T(8,128)S(1)} custom-call(f32[8,2,8,384]{3,2,1,0:T(8,128)S(1)} %get-tuple-element.56.near_ref.corrections_ref, f32[8,2,8,384]{3,2,1,0:T(8,128)S(1)} %get-tuple-element.68.far_ref.corrections_ref, f32[8,2,8,384]{3,2,1,0:T(8,128)S(1)} %collective-permute-done.10.beyond_ref, f32[8,8,384]{2,1,0:T(8,128)S(1)} %collective-permute-done.11.pair_ref, ...), custom_call_target="tpu_custom_call" | custom-call | flops 25000000 | bytes 868352 | tf_op jit(solution)/shard_map/second_across/pallas_call | solution.py:22
  54.9 0.9 %collective-permute-done.13 = f32[8,128]{1,0:T(8,128)S(1)} collective-permute-done((f32[8,128]{1,0:T(8,128)S(1)}, f32[8,128]{1,0:T(8,128)S(1)}, u32[]{:S(2)}, u32[]{:S(2)}) %collective-permute-start.13) | collective-permute-done | bytes 4128 | tf_op jit(solution)/shard_map/ppermute | solution.py:61
  55.8 2.7 %collective-permute-start.14 = (f32[8,128]{1,0:T(8,128)S(1)}, f32[8,128]{1,0:T(8,128)S(1)}, u32[]{:S(2)}, u32[]{:S(2)}) collective-permute-start(f32[8,128]{1,0:T(8,128)S(1)} %add.29), channel_id=1, source_target_pairs={{0,2},{1,3},{2,0},{3,1},{4,6},{5,7},{6,4},{7,5},{8,10},{9,11},{10,... | collective-permute-start | bytes 12296 | tf_op jit(solution)/shard_map/ppermute | solution.py:61
  58.5 1.6 %collective-permute-done.14 = f32[8,128]{1,0:T(8,128)S(1)} collective-permute-done((f32[8,128]{1,0:T(8,128)S(1)}, f32[8,128]{1,0:T(8,128)S(1)}, u32[]{:S(2)}, u32[]{:S(2)}) %collective-permute-start.14) | collective-permute-done | bytes 4128 | tf_op jit(solution)/shard_map/ppermute | solution.py:61
  60.1 1.0 %collective-permute-start.15 = (f32[8,128]{1,0:T(8,128)S(1)}, f32[8,128]{1,0:T(8,128)S(1)}, u32[]{:S(2)}, u32[]{:S(2)}) collective-permute-start(f32[8,128]{1,0:T(8,128)S(1)} %add.30), channel_id=1, source_target_pairs={{0,4},{1,5},{2,6},{3,7},{4,0},{5,1},{6,2},{7,3},{8,12},{9,13},{10,... | collective-permute-start | bytes 12296 | tf_op jit(solution)/shard_map/ppermute | solution.py:61
  61.1 2.6 %collective-permute-done.15 = f32[8,128]{1,0:T(8,128)S(1)} collective-permute-done((f32[8,128]{1,0:T(8,128)S(1)}, f32[8,128]{1,0:T(8,128)S(1)}, u32[]{:S(2)}, u32[]{:S(2)}) %collective-permute-start.15) | collective-permute-done | bytes 4128 | tf_op jit(solution)/shard_map/ppermute | solution.py:61
  63.7 1.7 %collective-permute-start.17 = (f32[8,128]{1,0:T(8,128)S(1)}, f32[8,128]{1,0:T(8,128)S(1)}, u32[]{:S(2)}, u32[]{:S(2)}) collective-permute-start(f32[8,128]{1,0:T(8,128)S(1)} %add.31), channel_id=1, source_target_pairs={{0,8},{1,9},{2,10},{3,11},{4,12},{5,13},{6,14},{7,15},{8,0},{9,1},... | collective-permute-start | bytes 12296 | tf_op jit(solution)/shard_map/ppermute | solution.py:61
  65.4 1.4 %images.1.second_ref = f32[8,4,8,384]{3,2,1,0:T(8,128)S(1)} custom-call(f32[8,2,8,384]{3,2,1,0:T(8,128)S(1)} %get-tuple-element.56.near_ref.corrections_ref, f32[8,2,8,384]{3,2,1,0:T(8,128)S(1)} %get-tuple-element.68.far_ref.corrections_ref, f32[8,2,8,384]{3,2,1,0:T(8,128)S(1)} %collective-permute-done.16.behind_ref, ...), custom_call_target="tpu_custom_call" | custom-call | flops 1000000 | bytes 1646592 | tf_op jit(solution)/shard_map/images/pallas_call | solution.py:22
  66.8 1.4 %collective-permute-done.17 = f32[8,128]{1,0:T(8,128)S(1)} collective-permute-done((f32[8,128]{1,0:T(8,128)S(1)}, f32[8,128]{1,0:T(8,128)S(1)}, u32[]{:S(2)}, u32[]{:S(2)}) %collective-permute-start.17) | collective-permute-done | bytes 4128 | tf_op jit(solution)/shard_map/ppermute | solution.py:61
  68.2 5.4 %ritz_pairs.3 = (f32[8]{0:T(128)}, f32[8,128]{1,0:T(8,128)S(1)}, f32[8,16,128]{2,1,0:T(8,128)S(1)}) custom-call(f32[8,128]{1,0:T(8,128)S(1)} %add.32.pencil_ref), custom_call_target="tpu_custom_call" | custom-call | flops 10000000 | bytes 73760 | tf_op jit(solution)/shard_map/ritz_pairs/pallas_call | solution.py:22
  74.1 2.1 %collective-permute-start.18 = (f32[2,2,8,384]{3,2,1,0:T(8,128)S(1)}, f32[2,2,8,384]{3,2,1,0:T(8,128)S(1)}, u32[]{:S(2)}, u32[]{:S(2)}) collective-permute-start(f32[2,2,8,384]{3,2,1,0:T(8,128)S(1)} %densities.3), channel_id=1, source_target_pairs={{0,2},{2,0},{4,6},{6,4},{8,10},{10,8},{12,14},{14,12},{1,3},{3,1},... | collective-permute-start | bytes 147464 | tf_op jit(solution)/shard_map/ppermute | solution.py:35
  76.7 1.6 %collective-permute-done.18.other_ref = f32[2,2,8,384]{3,2,1,0:T(8,128)S(1)} collective-permute-done((f32[2,2,8,384]{3,2,1,0:T(8,128)S(1)}, f32[2,2,8,384]{3,2,1,0:T(8,128)S(1)}, u32[]{:S(2)}, u32[]{:S(2)}) %collective-permute-start.18) | collective-permute-done | bytes 49184 | tf_op jit(solution)/shard_map/ppermute | solution.py:35
  78.3 0.7 merge.1
  (39 shorter events, 3.3 us)
Async XLA Ops:
  0.6 9.1 %copy-start.1 = (f32[16,2,16,384]{3,2,1,0:T(8,128)S(1)}, f32[16,2,16,384]{3,2,1,0:T(8,128)}, u32[]{:S(2)}) copy-start(f32[16,2,16,384]{3,2,1,0:T(8,128)} %block_ref.3) | copy-start | bytes 2359300
  3.1 13.4 %collective-permute-start = (f32[18,2,8,384]{3,2,1,0:T(8,128)}, f32[18,2,8,384]{3,2,1,0:T(8,128)S(1)}, u32[]{:S(2)}, u32[]{:S(2)}) collective-permute-start(f32[18,2,8,384]{3,2,1,0:T(8,128)} %get-tuple-element.41), channel_id=1, source_target_pairs={{0,2},{2,0},{4,6},{6,4},{8,10},{10,8},{12,14},{14,12},{1,3},{3,1},... | collective-permute-start | bytes 1327112 | tf_op jit(solution)/shard_map/ppermute | solution.py:35
  6.1 13.8 %collective-permute-start.2 = (f32[18,2,8,384]{3,2,1,0:T(8,128)}, f32[18,2,8,384]{3,2,1,0:T(8,128)S(1)}, u32[]{:S(2)}, u32[]{:S(2)}) collective-permute-start(f32[18,2,8,384]{3,2,1,0:T(8,128)} %get-tuple-element.40.mine_ref), channel_id=1, source_target_pairs={{4,0},{14,2},{8,4},{2,6},{12,8},{6,10},{0,12},{10,14},{5,1},{15,3}... | collective-permute-start | bytes 1327112 | tf_op jit(solution)/shard_map/ppermute | solution.py:44
  9.8 0.8 %copy-start.3 = (f32[2,16,384]{2,1,0:T(8,128)S(1)}, f32[2,16,384]{2,1,0:T(8,128)}, u32[]{:S(2)}) copy-start(f32[2,16,384]{2,1,0:T(8,128)} %concentration_ref.1) | copy-start | bytes 147460
  9.9 1.5 %copy-start.2 = (f32[2,16,384]{2,1,0:T(8,128)S(1)}, f32[2,16,384]{2,1,0:T(8,128)}, u32[]{:S(2)}) copy-start(f32[2,16,384]{2,1,0:T(8,128)} %stiffness_ref.3) | copy-start | bytes 147460
  9.9 1.5 %collective-permute-start.1 = (f32[16,2,4,384]{3,2,1,0:T(4,128)S(1)}, f32[16,2,4,384]{3,2,1,0:T(4,128)S(1)}, u32[]{:S(2)}, u32[]{:S(2)}) collective-permute-start(f32[16,2,4,384]{3,2,1,0:T(4,128)S(1)} %pad_maximum_fusion), channel_id=1, source_target_pairs={{0,1},{1,0},{2,3},{3,2},{4,5},{5,4},{6,7},{7,6},{8,9},{9,8},{10,11... | collective-permute-start | bytes 589832 | tf_op jit(solution)/shard_map/ppermute | solution.py:39
  10.6 5.9 %copy-start = (f32[18,2,8,384]{3,2,1,0:T(8,128)S(1)}, f32[18,2,8,384]{3,2,1,0:T(8,128)}, u32[]{:S(2)}) copy-start(f32[18,2,8,384]{3,2,1,0:T(8,128)} %get-tuple-element.40.mine_ref) | copy-start | bytes 1327108
  19.9 12.5 %collective-permute-start.6 = (f32[18,2,8,384]{3,2,1,0:T(8,128)S(1)}, f32[18,2,8,384]{3,2,1,0:T(8,128)S(1)}, u32[]{:S(2)}, u32[]{:S(2)}) collective-permute-start(f32[18,2,8,384]{3,2,1,0:T(8,128)S(1)} %collective-permute-done.theirs_ref), channel_id=1, source_target_pairs={{12,0},{6,2},{0,4},{10,6},{4,8},{14,10},{8,12},{2,14},{13,1},{7,3}... | collective-permute-start | bytes 1327112 | tf_op jit(solution)/shard_map/ppermute | solution.py:49
  19.9 12.5 %collective-permute-start.7 = (f32[17,8,384]{2,1,0:T(8,128)S(1)}, f32[17,8,384]{2,1,0:T(8,128)S(1)}, u32[]{:S(2)}, u32[]{:S(2)}) collective-permute-start(f32[17,8,384]{2,1,0:T(8,128)S(1)} %get-tuple-element.43), channel_id=1, source_target_pairs={{0,2},{2,0},{4,6},{6,4},{8,10},{10,8},{12,14},{14,12},{1,3},{3,1},... | collective-permute-start | bytes 626696 | tf_op jit(solution)/shard_map/ppermute | solution.py:35
  22.3 10.1 %collective-permute-start.8 = (f32[17,8,384]{2,1,0:T(8,128)S(1)}, f32[17,8,384]{2,1,0:T(8,128)S(1)}, u32[]{:S(2)}, u32[]{:S(2)}) collective-permute-start(f32[17,8,384]{2,1,0:T(8,128)S(1)} %get-tuple-element.44), channel_id=1, source_target_pairs={{0,1},{1,0},{2,3},{3,2},{4,5},{5,4},{6,7},{7,6},{8,9},{9,8},{10,11... | collective-permute-start | bytes 626696 | tf_op jit(solution)/shard_map/ppermute | solution.py:39
  23.8 1.3 %collective-permute-start.3 = (f32[8,128]{1,0:T(8,128)S(1)}, f32[8,128]{1,0:T(8,128)S(1)}, u32[]{:S(2)}, u32[]{:S(2)}) collective-permute-start(f32[8,128]{1,0:T(8,128)S(1)} %first_across.1), channel_id=1, source_target_pairs={{0,1},{1,0},{2,3},{3,2},{4,5},{5,4},{6,7},{7,6},{8,9},{9,8},{10,11... | collective-permute-start | bytes 12296 | tf_op jit(solution)/shard_map/ppermute | solution.py:61
  25.1 3.6 %collective-permute-start.4 = (f32[8,128]{1,0:T(8,128)S(1)}, f32[8,128]{1,0:T(8,128)S(1)}, u32[]{:S(2)}, u32[]{:S(2)}) collective-permute-start(f32[8,128]{1,0:T(8,128)S(1)} %add.25), channel_id=1, source_target_pairs={{0,2},{1,3},{2,0},{3,1},{4,6},{5,7},{6,4},{7,5},{8,10},{9,11},{10,... | collective-permute-start | bytes 12296 | tf_op jit(solution)/shard_map/ppermute | solution.py:61
  28.7 3.7 %collective-permute-start.5 = (f32[8,128]{1,0:T(8,128)S(1)}, f32[8,128]{1,0:T(8,128)S(1)}, u32[]{:S(2)}, u32[]{:S(2)}) collective-permute-start(f32[8,128]{1,0:T(8,128)S(1)} %add.26), channel_id=1, source_target_pairs={{0,4},{1,5},{2,6},{3,7},{4,0},{5,1},{6,2},{7,3},{8,12},{9,13},{10,... | collective-permute-start | bytes 12296 | tf_op jit(solution)/shard_map/ppermute | solution.py:61
  32.4 5.3 %collective-permute-start.9 = (f32[8,128]{1,0:T(8,128)S(1)}, f32[8,128]{1,0:T(8,128)S(1)}, u32[]{:S(2)}, u32[]{:S(2)}) collective-permute-start(f32[8,128]{1,0:T(8,128)S(1)} %add.27), channel_id=1, source_target_pairs={{0,8},{1,9},{2,10},{3,11},{4,12},{5,13},{6,14},{7,15},{8,0},{9,1},... | collective-permute-start | bytes 12296 | tf_op jit(solution)/shard_map/ppermute | solution.py:61
  45.2 6.0 %collective-permute-start.10 = (f32[8,2,8,384]{3,2,1,0:T(8,128)S(1)}, f32[8,2,8,384]{3,2,1,0:T(8,128)S(1)}, u32[]{:S(2)}, u32[]{:S(2)}) collective-permute-start(f32[8,2,8,384]{3,2,1,0:T(8,128)S(1)} %get-tuple-element.56.near_ref.corrections_ref), channel_id=1, source_target_pairs={{4,0},{14,2},{8,4},{2,6},{12,8},{6,10},{0,12},{10,14},{5,1},{15,3}... | collective-permute-start | bytes 589832 | tf_op jit(solution)/shard_map/ppermute | solution.py:44
  46.4 4.7 %collective-permute-start.11 = (f32[8,8,384]{2,1,0:T(8,128)S(1)}, f32[8,8,384]{2,1,0:T(8,128)S(1)}, u32[]{:S(2)}, u32[]{:S(2)}) collective-permute-start(f32[8,8,384]{2,1,0:T(8,128)S(1)} %get-tuple-element.58), channel_id=1, source_target_pairs={{0,2},{2,0},{4,6},{6,4},{8,10},{10,8},{12,14},{14,12},{1,3},{3,1},... | collective-permute-start | bytes 294920 | tf_op jit(solution)/shard_map/ppermute | solution.py:35
  47.5 3.6 %collective-permute-start.12 = (f32[8,8,384]{2,1,0:T(8,128)S(1)}, f32[8,8,384]{2,1,0:T(8,128)S(1)}, u32[]{:S(2)}, u32[]{:S(2)}) collective-permute-start(f32[8,8,384]{2,1,0:T(8,128)S(1)} %get-tuple-element.59), channel_id=1, source_target_pairs={{0,1},{1,0},{2,3},{3,2},{4,5},{5,4},{6,7},{7,6},{8,9},{9,8},{10,11... | collective-permute-start | bytes 294920 | tf_op jit(solution)/shard_map/ppermute | solution.py:39
  51.2 12.5 %collective-permute-start.16 = (f32[8,2,8,384]{3,2,1,0:T(8,128)S(1)}, f32[8,2,8,384]{3,2,1,0:T(8,128)S(1)}, u32[]{:S(2)}, u32[]{:S(2)}) collective-permute-start(f32[8,2,8,384]{3,2,1,0:T(8,128)S(1)} %get-tuple-element.68.far_ref.corrections_ref), channel_id=1, source_target_pairs={{12,0},{6,2},{0,4},{10,6},{4,8},{14,10},{8,12},{2,14},{13,1},{7,3}... | collective-permute-start | bytes 589832 | tf_op jit(solution)/shard_map/ppermute | solution.py:49
  54.6 1.2 %collective-permute-start.13 = (f32[8,128]{1,0:T(8,128)S(1)}, f32[8,128]{1,0:T(8,128)S(1)}, u32[]{:S(2)}, u32[]{:S(2)}) collective-permute-start(f32[8,128]{1,0:T(8,128)S(1)} %second_across.1), channel_id=1, source_target_pairs={{0,1},{1,0},{2,3},{3,2},{4,5},{5,4},{6,7},{7,6},{8,9},{9,8},{10,11... | collective-permute-start | bytes 12296 | tf_op jit(solution)/shard_map/ppermute | solution.py:61
  55.8 4.3 %collective-permute-start.14 = (f32[8,128]{1,0:T(8,128)S(1)}, f32[8,128]{1,0:T(8,128)S(1)}, u32[]{:S(2)}, u32[]{:S(2)}) collective-permute-start(f32[8,128]{1,0:T(8,128)S(1)} %add.29), channel_id=1, source_target_pairs={{0,2},{1,3},{2,0},{3,1},{4,6},{5,7},{6,4},{7,5},{8,10},{9,11},{10,... | collective-permute-start | bytes 12296 | tf_op jit(solution)/shard_map/ppermute | solution.py:61
  60.1 3.6 %collective-permute-start.15 = (f32[8,128]{1,0:T(8,128)S(1)}, f32[8,128]{1,0:T(8,128)S(1)}, u32[]{:S(2)}, u32[]{:S(2)}) collective-permute-start(f32[8,128]{1,0:T(8,128)S(1)} %add.30), channel_id=1, source_target_pairs={{0,4},{1,5},{2,6},{3,7},{4,0},{5,1},{6,2},{7,3},{8,12},{9,13},{10,... | collective-permute-start | bytes 12296 | tf_op jit(solution)/shard_map/ppermute | solution.py:61
  63.7 4.5 %collective-permute-start.17 = (f32[8,128]{1,0:T(8,128)S(1)}, f32[8,128]{1,0:T(8,128)S(1)}, u32[]{:S(2)}, u32[]{:S(2)}) collective-permute-start(f32[8,128]{1,0:T(8,128)S(1)} %add.31), channel_id=1, source_target_pairs={{0,8},{1,9},{2,10},{3,11},{4,12},{5,13},{6,14},{7,15},{8,0},{9,1},... | collective-permute-start | bytes 12296 | tf_op jit(solution)/shard_map/ppermute | solution.py:61
  74.1 4.2 %collective-permute-start.18 = (f32[2,2,8,384]{3,2,1,0:T(8,128)S(1)}, f32[2,2,8,384]{3,2,1,0:T(8,128)S(1)}, u32[]{:S(2)}, u32[]{:S(2)}) collective-permute-start(f32[2,2,8,384]{3,2,1,0:T(8,128)S(1)} %densities.3), channel_id=1, source_target_pairs={{0,2},{2,0},{4,6},{6,4},{8,10},{10,8},{12,14},{14,12},{1,3},{3,1},... | collective-permute-start | bytes 147464 | tf_op jit(solution)/shard_map/ppermute | solution.py:35

commit v6 on v5

--- a/solution.py
+++ b/solution.py
@@ -54,12 +54,21 @@
     total = lax.axis_size("gz") * lax.axis_size("gy")
     if total & (total - 1):
         return lax.psum(x, axes), later
+
+    def other(mask):
+        return lax.ppermute(x, axes, [(i, i ^ mask) for i in range(total)])
+
     mask = 1
     while mask < total:
-        if 2 * mask == total:
+        wide = mask >= 4 and 4 * mask <= total
+        if mask * (4 if wide else 2) == total:
             x, later = lax.optimization_barrier((x, later))
-        x = x + lax.ppermute(x, axes, [(i, i ^ mask) for i in range(total)])
-        mask *= 2
+        if wide:
+            x = (x + other(mask)) + (other(2 * mask) + other(3 * mask))
+            mask *= 4
+        else:
+            x = x + other(mask)
+            mask *= 2
     return x, later
 
 
@@ -186,11 +195,11 @@
             g2 = g * g
             worst = jnp.maximum(worst, g2)
             dd = jnp.maximum(jnp.abs(d), 1e-18)
-            ih = lax.rsqrt(dd * dd + 4.0 * g2)
-            c2 = 0.5 + (0.5 * dd) * ih
+            ih = lax.rsqrt(g2 + 0.25 * (dd * dd))
+            c2 = 0.5 + (0.25 * dd) * ih
             ic = lax.rsqrt(c2)
             c = c2 * ic
-            s = jnp.where(d >= 0.0, g, -g) * (ih * ic)
+            s = (jnp.where(d >= 0.0, 0.5, -0.5) * g) * (ih * ic)
             move = (s * ic) * g
             top = top - move
             bottom = bottom + move
@@ -341,7 +350,7 @@
         prepare_kernel,
         out_shape=(shape, shape),
         in_specs=[pl.BlockSpec(memory_space=pltpu.HBM)] * 3,
-        out_specs=[VMEM] * 2,
+        out_specs=[pl.BlockSpec(memory_space=pltpu.HBM)] * 2,
         scratch_shapes=[pltpu.SemaphoreType.DMA((6 * nz,))],
         compiler_params=pltpu.CompilerParams(vmem_limit_bytes=62 * 1024 * 1024),
         name="prepare",
@@ -520,9 +529,7 @@
     depth, ny, nx = curvature_ref.shape
     nz = depth // 2
     half = 8 * HALF
-    gram = jnp.zeros((2 * half, 2 * half), jnp.float32)
-    cross = jnp.zeros((half, 2 * half), jnp.float32)
-    back = jnp.zeros((half, half), jnp.float32)
+    products = jnp.zeros((4 * half, 3 * half), jnp.float32)
     low = jnp.zeros((half, half), jnp.float32)
     for u in range(depth):
         for start in range(0, ny, 8):
@@ -533,11 +540,15 @@
             rows = jnp.concatenate([rows_of(modes_ref[:, u, part, :]), second], axis=0)
             images = rows_of(images_ref[:, u, part, :])
             along_x = second_x(second)
-            gram = gram + inner(rows, rows)
-            cross = cross + inner(images, rows)
-            back = back + inner(second, images)
-            low = low + inner(rows_of(field * curvature_ref[u, part, :][None]), second)
+            bent = rows_of(field * curvature_ref[u, part, :][None])
+            products = products + inner(
+                jnp.concatenate([rows, bent, images], axis=0), jnp.concatenate([rows, images], axis=0)
+            )
             low = low + inner(rows_of(along_x.reshape(field.shape) * weight), along_x)
+    gram = products[: 2 * half, : 2 * half]
+    back = products[half : 2 * half, 2 * half :]
+    low = low + products[2 * half : 3 * half, half : 2 * half]
+    cross = products[3 * half :, : 2 * half]
     tile_ref[...] = (
         folded(gram[:half], 0)
         + folded(gram[half:], BLOCK)

time: 79.6 us -> 104 us (1.31)
  Pallas kernels: 33.2 us -> 58 us
  waiting for transfers between devices: 20.1 us -> 22.1 us
  starting transfers between devices: 24.1 us -> 22.7 us
    pallas_call x1, Pallas kernels: 2.43 us -> 28 us  [prepare(): pl.pallas_call(prepare_kernel, out_shape=(shape, shape), in_specs=[pl.Blo...]
    ppermute x8 -> x10, waiting for transfers between devices: 14.6 us -> 8.43 us  [other(): return lax.ppermute(x, axes, [(i, i ^ mask) for i in range(total)])]
    ppermute x2, waiting for transfers between devices: 0.01 us -> 4.74 us  [from_behind(): lax.ppermute(x, 'gz', [((i + (size - 2 if i % 2 == 0 else 2)) % size, i)...]
    ppermute x4, waiting for transfers between devices: 1.71 us -> 5.16 us  [pair_swap(): lax.ppermute(x, 'gz', [(i, i ^ 1) for i in range(lax.axis_size('gz'))])]
    ppermute x4, starting transfers between devices: 8.65 us -> 5.77 us  [pair_swap(): lax.ppermute(x, 'gz', [(i, i ^ 1) for i in range(lax.axis_size('gz'))])]
    ppermute x8 -> x10, starting transfers between devices: 8.47 us -> 11.1 us  [other(): return lax.ppermute(x, axes, [(i, i ^ mask) for i in range(total)])]
    ppermute x2, starting transfers between devices: 2.05 us -> 0.33 us  [from_behind(): lax.ppermute(x, 'gz', [((i + (size - 2 if i % 2 == 0 else 2)) % size, i)...]
  transfers between devices with their start and end apart: 19 -> 21, of which waited for: 11 -> 12; matrix products, arithmetic and copies ran while one was open for 0% -> 0% of each run, Pallas kernels for 21% -> 15%
where the time goes in v6:
time: 104 us
  Pallas kernels  58 us (56%)
  starting transfers between devices  22.7 us (22%)
  waiting for transfers between devices  22.1 us (21%)
    pallas_call x13, Pallas kernels, call(): pl.pallas_call(kernel, out_shape=out_shape, in_specs=[VMEM] * len(args),...  29.9 us
    pallas_call x1, Pallas kernels, prepare(): pl.pallas_call(prepare_kernel, out_shape=(shape, shape), in_specs=[pl.Blo...  28 us
    ppermute x10, starting transfers between devices, other(): return lax.ppermute(x, axes, [(i, i ^ mask) for i in range(total)])  11.1 us
    ppermute x10, waiting for transfers between devices, other(): return lax.ppermute(x, axes, [(i, i ^ mask) for i in range(total)])  8.43 us
    ppermute x4, starting transfers between devices, pair_swap(): lax.ppermute(x, 'gz', [(i, i ^ 1) for i in range(lax.axis_size('gz'))])  5.77 us
    ppermute x2, starting transfers between devices, from_beyond(): lax.ppermute(x, 'gz', [((i + (2 if i % 2 == 0 else size - 2)) % size, i)...  5.35 us
    ppermute x4, waiting for transfers between devices, pair_swap(): lax.ppermute(x, 'gz', [(i, i ^ 1) for i in range(lax.axis_size('gz'))])  5.16 us
    ppermute x2, waiting for transfers between devices, from_behind(): lax.ppermute(x, 'gz', [((i + (size - 2 if i % 2 == 0 else 2)) % size, i)...  4.74 us
  transfers between devices with their start and end apart: 21, of which 12 were waited for; matrix products, arithmetic and copies ran while one was open for 0% of the time, Pallas kernels for 15%

profile of v6, /device:TPU:0, one launch (start us, length us, event | category | flops | bytes accessed | tf_op | source)
XLA Modules:
  0.0 104.3 jit_solution(11552929280162478050)
XLA Ops:
  0.6 28.0 %prepare.1 = (f32[18,2,8,384]{3,2,1,0:T(8,128)}, f32[18,2,8,384]{3,2,1,0:T(8,128)}) custom-call(f32[16,2,16,384]{3,2,1,0:T(8,128)} %block_ref.3, f32[2,16,384]{2,1,0:T(8,128)} %stiffness_ref.3, f32[2,16,384]{2,1,0:T(8,128)} %concentration_ref.1), custom_call_target="tpu_custom_call" | custom-call | tf_op jit(solution)/shard_map/prepare/pallas_call | solution.py:349
  28.7 3.0 %collective-permute-start = (f32[18,2,8,384]{3,2,1,0:T(8,128)}, f32[18,2,8,384]{3,2,1,0:T(8,128)S(1)}, u32[]{:S(2)}, u32[]{:S(2)}) collective-permute-start(f32[18,2,8,384]{3,2,1,0:T(8,128)} %get-tuple-element.41), channel_id=1, source_target_pairs={{0,2},{2,0},{4,6},{6,4},{8,10},{10,8},{12,14},{14,12},{1,3},{3,1},... | collective-permute-start | bytes 1327112 | tf_op jit(solution)/shard_map/ppermute | solution.py:35
  31.7 3.6 %collective-permute-start.2 = (f32[18,2,8,384]{3,2,1,0:T(8,128)}, f32[18,2,8,384]{3,2,1,0:T(8,128)S(1)}, u32[]{:S(2)}, u32[]{:S(2)}) collective-permute-start(f32[18,2,8,384]{3,2,1,0:T(8,128)} %get-tuple-element.40.mine_ref), channel_id=1, source_target_pairs={{4,0},{14,2},{8,4},{2,6},{12,8},{6,10},{0,12},{10,14},{5,1},{15,3}... | collective-permute-start | bytes 1327112 | tf_op jit(solution)/shard_map/ppermute | solution.py:44
  35.6 0.6 copy-done.3
  36.2 0.8 collective-permute-done.1.beside_ref
  37.0 4.9 %first_local.1.tile_ref = f32[8,128]{1,0:T(8,128)S(1)} custom-call(f32[16,2,16,384]{3,2,1,0:T(8,128)S(1)} %copy-done.1, f32[16,2,4,384]{3,2,1,0:T(4,128)S(1)} %collective-permute-done.1.beside_ref, f32[2,16,384]{2,1,0:T(8,128)S(1)} %fusion.curvature_ref, f32[2,16,384]{2,1,0:T(8,128)S(1)} %copy-done.2), custom_call_target="tpu_custom_call" | custom-call | flops 100000000 | bytes 1085440 | tf_op jit(solution)/shard_map/first_local/pallas_call | solution.py:22
  42.5 3.0 %collective-permute-done.2.beyond_ref = f32[18,2,8,384]{3,2,1,0:T(8,128)S(1)} collective-permute-done((f32[18,2,8,384]{3,2,1,0:T(8,128)}, f32[18,2,8,384]{3,2,1,0:T(8,128)S(1)}, u32[]{:S(2)}, u32[]{:S(2)}) %collective-permute-start.2) | collective-permute-done | bytes 442400 | tf_op jit(solution)/shard_map/ppermute | solution.py:44
  45.5 2.4 %collective-permute-start.6 = (f32[17,8,384]{2,1,0:T(8,128)S(1)}, f32[17,8,384]{2,1,0:T(8,128)S(1)}, u32[]{:S(2)}, u32[]{:S(2)}) collective-permute-start(f32[17,8,384]{2,1,0:T(8,128)S(1)} %get-tuple-element.43), channel_id=1, source_target_pairs={{0,2},{2,0},{4,6},{6,4},{8,10},{10,8},{12,14},{14,12},{1,3},{3,1},... | collective-permute-start | bytes 626696 | tf_op jit(solution)/shard_map/ppermute | solution.py:35
  47.9 1.4 %first_across.1 = f32[8,128]{1,0:T(8,128)S(1)} custom-call(f32[18,2,8,384]{3,2,1,0:T(8,128)S(1)} %copy-done, f32[18,2,8,384]{3,2,1,0:T(8,128)S(1)} %collective-permute-done.theirs_ref, f32[18,2,8,384]{3,2,1,0:T(8,128)S(1)} %collective-permute-done.2.beyond_ref, f32[8,128]{1,0:T(8,128)S(1)} %first_local.1.tile_ref), custom_call_target="tpu_custom_call" | custom-call | flops 25000000 | bytes 1335296 | tf_op jit(solution)/shard_map/first_across/pallas_call | solution.py:22
  49.9 0.8 collective-permute-done.3
  50.7 3.6 %collective-permute-done.4 = f32[8,128]{1,0:T(8,128)S(1)} collective-permute-done((f32[8,128]{1,0:T(8,128)S(1)}, f32[8,128]{1,0:T(8,128)S(1)}, u32[]{:S(2)}, u32[]{:S(2)}) %collective-permute-start.4) | collective-permute-done | bytes 4128 | tf_op jit(solution)/shard_map/ppermute | solution.py:59
  54.4 3.6 %collective-permute-done.5.behind_ref = f32[18,2,8,384]{3,2,1,0:T(8,128)S(1)} collective-permute-done((f32[18,2,8,384]{3,2,1,0:T(8,128)S(1)}, f32[18,2,8,384]{3,2,1,0:T(8,128)S(1)}, u32[]{:S(2)}, u32[]{:S(2)}) %collective-permute-start.5) | collective-permute-done | bytes 442400 | tf_op jit(solution)/shard_map/ppermute | solution.py:49
  58.0 1.7 %collective-permute-start.10 = (f32[8,128]{1,0:T(8,128)S(1)}, f32[8,128]{1,0:T(8,128)S(1)}, u32[]{:S(2)}, u32[]{:S(2)}) collective-permute-start(f32[8,128]{1,0:T(8,128)S(1)} %add.32), channel_id=1, source_target_pairs={{0,12},{1,13},{2,14},{3,15},{4,8},{5,9},{6,10},{7,11},{8,4},{9,5},... | collective-permute-start | bytes 12296 | tf_op jit(solution)/shard_map/ppermute | solution.py:59
  59.7 2.7 %collective-permute-start.8 = (f32[8,128]{1,0:T(8,128)S(1)}, f32[8,128]{1,0:T(8,128)S(1)}, u32[]{:S(2)}, u32[]{:S(2)}) collective-permute-start(f32[8,128]{1,0:T(8,128)S(1)} %add.32), channel_id=1, source_target_pairs={{0,4},{1,5},{2,6},{3,7},{4,0},{5,1},{6,2},{7,3},{8,12},{9,13},{10,... | collective-permute-start | bytes 12296 | tf_op jit(solution)/shard_map/ppermute | solution.py:59
  62.4 3.0 %first_images.1 = (f32[16,4,8,384]{3,2,1,0:T(8,128)S(1)}, f32[4,8,384]{2,1,0:T(8,128)S(1)}, f32[4,8,384]{2,1,0:T(8,128)S(1)}, f32[6,8,384]{2,1,0:T(8,128)S(1)}, f32[4,24,384]{2,1,0:T(8,128)S(1)}) custom-call(f32[18,2,8,384]{3,2,1,0:T(8,128)S(1)} %copy-done, f32[18,2,8,384]{3,2,1,0:T(8,128)S(1)} %collective-permute-done.theirs_ref, ...), custom_call_target="tpu_custom_call" | custom-call | flops 6000000 | bytes 3293184 | tf_op jit(solution)/shard_map/first_images/pallas_call | solution.py:22
  65.4 6.2 %ritz_pairs.2 = (f32[8]{0:T(128)}, f32[8,128]{1,0:T(8,128)S(1)}, f32[8,16,128]{2,1,0:T(8,128)S(1)}) custom-call(f32[8,128]{1,0:T(8,128)S(1)} %add_add_fusion.1.pencil_ref), custom_call_target="tpu_custom_call" | custom-call | flops 10000000 | bytes 73760 | tf_op jit(solution)/shard_map/ritz_pairs/pallas_call | solution.py:22
  71.5 1.2 %update.1 = (f32[8,4,8,384]{3,2,1,0:T(8,128)S(1)}, f32[8,4,8,384]{3,2,1,0:T(8,128)S(1)}, f32[8,2,8,384]{3,2,1,0:T(8,128)S(1)}, f32[8,2,8,384]{3,2,1,0:T(8,128)S(...) custom-call(f32[8,16,128]{2,1,0:T(8,128)S(1)} %get-tuple-element.49.mix_ref, ...), custom_call_target="tpu_custom_call" | custom-call | flops 1000000 | bytes 3166208 | tf_op jit(solution)/shard_map/update/pallas_call | solution.py:22
  72.7 1.8 %collective-permute-start.11 = (f32[8,2,8,384]{3,2,1,0:T(8,128)S(1)}, f32[8,2,8,384]{3,2,1,0:T(8,128)S(1)}, u32[]{:S(2)}, u32[]{:S(2)}) collective-permute-start(f32[8,2,8,384]{3,2,1,0:T(8,128)S(1)} %get-tuple-element.56.near_ref.corrections_ref), channel_id=1, source_target_pairs={{4,0},{14,2},{8,4},{2,6},{12,8},{6,10},{0,12},{10,14},{5,1},{15,3}... | collective-permute-start | bytes 589832 | tf_op jit(solution)/shard_map/ppermute | solution.py:44
  74.5 2.9 %second_local.1.tile_ref = f32[8,128]{1,0:T(8,128)S(1)} custom-call(f32[8,4,8,384]{3,2,1,0:T(8,128)S(1)} %get-tuple-element.60.modes_ref, f32[8,4,8,384]{3,2,1,0:T(8,128)S(1)} %get-tuple-element.61.images_ref.first_ref, f32[8,2,8,384]{3,2,1,0:T(8,128)S(1)} %get-tuple-element.56.near_ref.corrections_ref, ...), custom_call_target="tpu_custom_call" | custom-call | flops 80000000 | bytes 1306624 | tf_op jit(solution)/shard_map/second_local/pallas_call | solution.py:22
  77.4 1.7 %collective-permute-done.12.pair_ref = f32[8,8,384]{2,1,0:T(8,128)S(1)} collective-permute-done((f32[8,8,384]{2,1,0:T(8,128)S(1)}, f32[8,8,384]{2,1,0:T(8,128)S(1)}, u32[]{:S(2)}, u32[]{:S(2)}) %collective-permute-start.12) | collective-permute-done | bytes 98336 | tf_op jit(solution)/shard_map/ppermute | solution.py:35
  79.4 1.4 %second_across.1 = f32[8,128]{1,0:T(8,128)S(1)} custom-call(f32[8,2,8,384]{3,2,1,0:T(8,128)S(1)} %get-tuple-element.56.near_ref.corrections_ref, f32[8,2,8,384]{3,2,1,0:T(8,128)S(1)} %get-tuple-element.68.far_ref.corrections_ref, f32[8,2,8,384]{3,2,1,0:T(8,128)S(1)} %collective-permute-done.11.beyond_ref, f32[8,8,384]{2,1,0:T(8,128)S(1)} %collective-permute-done.12.pair_ref, ...), custom_call_target="tpu_custom_call" | custom-call | flops 25000000 | bytes 868352 | tf_op jit(solution)/shard_map/second_across/pallas_call | solution.py:22
  80.9 1.2 %collective-permute-done.14 = f32[8,128]{1,0:T(8,128)S(1)} collective-permute-done((f32[8,128]{1,0:T(8,128)S(1)}, f32[8,128]{1,0:T(8,128)S(1)}, u32[]{:S(2)}, u32[]{:S(2)}) %collective-permute-start.14) | collective-permute-done | bytes 4128 | tf_op jit(solution)/shard_map/ppermute | solution.py:59
  82.1 1.8 %collective-permute-start.15 = (f32[8,128]{1,0:T(8,128)S(1)}, f32[8,128]{1,0:T(8,128)S(1)}, u32[]{:S(2)}, u32[]{:S(2)}) collective-permute-start(f32[8,128]{1,0:T(8,128)S(1)} %add.36), channel_id=1, source_target_pairs={{0,2},{1,3},{2,0},{3,1},{4,6},{5,7},{6,4},{7,5},{8,10},{9,11},{10,... | collective-permute-start | bytes 12296 | tf_op jit(solution)/shard_map/ppermute | solution.py:59
  83.9 1.8 %collective-permute-done.15 = f32[8,128]{1,0:T(8,128)S(1)} collective-permute-done((f32[8,128]{1,0:T(8,128)S(1)}, f32[8,128]{1,0:T(8,128)S(1)}, u32[]{:S(2)}, u32[]{:S(2)}) %collective-permute-start.15) | collective-permute-done | bytes 4128 | tf_op jit(solution)/shard_map/ppermute | solution.py:59
  85.7 1.1 %collective-permute-done.16.behind_ref = f32[8,2,8,384]{3,2,1,0:T(8,128)S(1)} collective-permute-done((f32[8,2,8,384]{3,2,1,0:T(8,128)S(1)}, f32[8,2,8,384]{3,2,1,0:T(8,128)S(1)}, u32[]{:S(2)}, u32[]{:S(2)}) %collective-permute-start.16) | collective-permute-done | bytes 196640 | tf_op jit(solution)/shard_map/ppermute | solution.py:49
  86.8 2.4 %collective-permute-start.19 = (f32[8,128]{1,0:T(8,128)S(1)}, f32[8,128]{1,0:T(8,128)S(1)}, u32[]{:S(2)}, u32[]{:S(2)}) collective-permute-start(f32[8,128]{1,0:T(8,128)S(1)} %add.37), channel_id=1, source_target_pairs={{0,12},{1,13},{2,14},{3,15},{4,8},{5,9},{6,10},{7,11},{8,4},{9,5},... | collective-permute-start | bytes 12296 | tf_op jit(solution)/shard_map/ppermute | solution.py:59
  89.2 2.0 %collective-permute-start.17 = (f32[8,128]{1,0:T(8,128)S(1)}, f32[8,128]{1,0:T(8,128)S(1)}, u32[]{:S(2)}, u32[]{:S(2)}) collective-permute-start(f32[8,128]{1,0:T(8,128)S(1)} %add.37), channel_id=1, source_target_pairs={{0,4},{1,5},{2,6},{3,7},{4,0},{5,1},{6,2},{7,3},{8,12},{9,13},{10,... | collective-permute-start | bytes 12296 | tf_op jit(solution)/shard_map/ppermute | solution.py:59
  91.2 1.4 %images.1.second_ref = f32[8,4,8,384]{3,2,1,0:T(8,128)S(1)} custom-call(f32[8,2,8,384]{3,2,1,0:T(8,128)S(1)} %get-tuple-element.56.near_ref.corrections_ref, f32[8,2,8,384]{3,2,1,0:T(8,128)S(1)} %get-tuple-element.68.far_ref.corrections_ref, f32[8,2,8,384]{3,2,1,0:T(8,128)S(1)} %collective-permute-done.16.behind_ref, ...), custom_call_target="tpu_custom_call" | custom-call | flops 1000000 | bytes 1646592 | tf_op jit(solution)/shard_map/images/pallas_call | solution.py:22
  92.6 1.1 %collective-permute-done.18 = f32[8,128]{1,0:T(8,128)S(1)} collective-permute-done((f32[8,128]{1,0:T(8,128)S(1)}, f32[8,128]{1,0:T(8,128)S(1)}, u32[]{:S(2)}, u32[]{:S(2)}) %collective-permute-start.18) | collective-permute-done | bytes 4128 | tf_op jit(solution)/shard_map/ppermute | solution.py:59
  93.7 5.3 %ritz_pairs.3 = (f32[8]{0:T(128)}, f32[8,128]{1,0:T(8,128)S(1)}, f32[8,16,128]{2,1,0:T(8,128)S(1)}) custom-call(f32[8,128]{1,0:T(8,128)S(1)} %add_add_fusion.pencil_ref), custom_call_target="tpu_custom_call" | custom-call | flops 10000000 | bytes 73760 | tf_op jit(solution)/shard_map/ritz_pairs/pallas_call | solution.py:22
  100.3 3.4 %collective-permute-done.20.other_ref = f32[2,2,8,384]{3,2,1,0:T(8,128)S(1)} collective-permute-done((f32[2,2,8,384]{3,2,1,0:T(8,128)S(1)}, f32[2,2,8,384]{3,2,1,0:T(8,128)S(1)}, u32[]{:S(2)}, u32[]{:S(2)}) %collective-permute-start.20) | collective-permute-done | bytes 49184 | tf_op jit(solution)/shard_map/ppermute | solution.py:35
  103.7 0.7 merge.1
  (41 shorter events, 3.1 us)
Async XLA Ops:
  0.6 34.7 %copy-start.1 = (f32[16,2,16,384]{3,2,1,0:T(8,128)S(1)}, f32[16,2,16,384]{3,2,1,0:T(8,128)}, u32[]{:S(2)}) copy-start(f32[16,2,16,384]{3,2,1,0:T(8,128)} %block_ref.3) | copy-start | bytes 2359300
  28.7 13.4 %collective-permute-start = (f32[18,2,8,384]{3,2,1,0:T(8,128)}, f32[18,2,8,384]{3,2,1,0:T(8,128)S(1)}, u32[]{:S(2)}, u32[]{:S(2)}) collective-permute-start(f32[18,2,8,384]{3,2,1,0:T(8,128)} %get-tuple-element.41), channel_id=1, source_target_pairs={{0,2},{2,0},{4,6},{6,4},{8,10},{10,8},{12,14},{14,12},{1,3},{3,1},... | collective-permute-start | bytes 1327112 | tf_op jit(solution)/shard_map/ppermute | solution.py:35
  31.7 13.8 %collective-permute-start.2 = (f32[18,2,8,384]{3,2,1,0:T(8,128)}, f32[18,2,8,384]{3,2,1,0:T(8,128)S(1)}, u32[]{:S(2)}, u32[]{:S(2)}) collective-permute-start(f32[18,2,8,384]{3,2,1,0:T(8,128)} %get-tuple-element.40.mine_ref), channel_id=1, source_target_pairs={{4,0},{14,2},{8,4},{2,6},{12,8},{6,10},{0,12},{10,14},{5,1},{15,3}... | collective-permute-start | bytes 1327112 | tf_op jit(solution)/shard_map/ppermute | solution.py:44
  35.4 0.8 copy-start.3
  35.5 1.5 %copy-start.2 = (f32[2,16,384]{2,1,0:T(8,128)S(1)}, f32[2,16,384]{2,1,0:T(8,128)}, u32[]{:S(2)}) copy-start(f32[2,16,384]{2,1,0:T(8,128)} %stiffness_ref.3) | copy-start | bytes 147460
  35.5 1.5 %collective-permute-start.1 = (f32[16,2,4,384]{3,2,1,0:T(4,128)S(1)}, f32[16,2,4,384]{3,2,1,0:T(4,128)S(1)}, u32[]{:S(2)}, u32[]{:S(2)}) collective-permute-start(f32[16,2,4,384]{3,2,1,0:T(4,128)S(1)} %pad_maximum_fusion), channel_id=1, source_target_pairs={{0,1},{1,0},{2,3},{3,2},{4,5},{5,4},{6,7},{7,6},{8,9},{9,8},{10,11... | collective-permute-start | bytes 589832 | tf_op jit(solution)/shard_map/ppermute | solution.py:39
  36.2 5.9 %copy-start = (f32[18,2,8,384]{3,2,1,0:T(8,128)S(1)}, f32[18,2,8,384]{3,2,1,0:T(8,128)}, u32[]{:S(2)}) copy-start(f32[18,2,8,384]{3,2,1,0:T(8,128)} %get-tuple-element.40.mine_ref) | copy-start | bytes 1327108
  45.5 12.5 %collective-permute-start.5 = (f32[18,2,8,384]{3,2,1,0:T(8,128)S(1)}, f32[18,2,8,384]{3,2,1,0:T(8,128)S(1)}, u32[]{:S(2)}, u32[]{:S(2)}) collective-permute-start(f32[18,2,8,384]{3,2,1,0:T(8,128)S(1)} %collective-permute-done.theirs_ref), channel_id=1, source_target_pairs={{12,0},{6,2},{0,4},{10,6},{4,8},{14,10},{8,12},{2,14},{13,1},{7,3}... | collective-permute-start | bytes 1327112 | tf_op jit(solution)/shard_map/ppermute | solution.py:49
  45.5 8.8 %collective-permute-start.6 = (f32[17,8,384]{2,1,0:T(8,128)S(1)}, f32[17,8,384]{2,1,0:T(8,128)S(1)}, u32[]{:S(2)}, u32[]{:S(2)}) collective-permute-start(f32[17,8,384]{2,1,0:T(8,128)S(1)} %get-tuple-element.43), channel_id=1, source_target_pairs={{0,2},{2,0},{4,6},{6,4},{8,10},{10,8},{12,14},{14,12},{1,3},{3,1},... | collective-permute-start | bytes 626696 | tf_op jit(solution)/shard_map/ppermute | solution.py:35
  47.9 6.4 %collective-permute-start.7 = (f32[17,8,384]{2,1,0:T(8,128)S(1)}, f32[17,8,384]{2,1,0:T(8,128)S(1)}, u32[]{:S(2)}, u32[]{:S(2)}) collective-permute-start(f32[17,8,384]{2,1,0:T(8,128)S(1)} %get-tuple-element.44), channel_id=1, source_target_pairs={{0,1},{1,0},{2,3},{3,2},{4,5},{5,4},{6,7},{7,6},{8,9},{9,8},{10,11... | collective-permute-start | bytes 626696 | tf_op jit(solution)/shard_map/ppermute | solution.py:39
  49.4 1.3 %collective-permute-start.3 = (f32[8,128]{1,0:T(8,128)S(1)}, f32[8,128]{1,0:T(8,128)S(1)}, u32[]{:S(2)}, u32[]{:S(2)}) collective-permute-start(f32[8,128]{1,0:T(8,128)S(1)} %first_across.1), channel_id=1, source_target_pairs={{0,1},{1,0},{2,3},{3,2},{4,5},{5,4},{6,7},{7,6},{8,9},{9,8},{10,11... | collective-permute-start | bytes 12296 | tf_op jit(solution)/shard_map/ppermute | solution.py:59
  50.7 3.6 %collective-permute-start.4 = (f32[8,128]{1,0:T(8,128)S(1)}, f32[8,128]{1,0:T(8,128)S(1)}, u32[]{:S(2)}, u32[]{:S(2)}) collective-permute-start(f32[8,128]{1,0:T(8,128)S(1)} %add.31), channel_id=1, source_target_pairs={{0,2},{1,3},{2,0},{3,1},{4,6},{5,7},{6,4},{7,5},{8,10},{9,11},{10,... | collective-permute-start | bytes 12296 | tf_op jit(solution)/shard_map/ppermute | solution.py:59
  58.0 7.4 %collective-permute-start.10 = (f32[8,128]{1,0:T(8,128)S(1)}, f32[8,128]{1,0:T(8,128)S(1)}, u32[]{:S(2)}, u32[]{:S(2)}) collective-permute-start(f32[8,128]{1,0:T(8,128)S(1)} %add.32), channel_id=1, source_target_pairs={{0,12},{1,13},{2,14},{3,15},{4,8},{5,9},{6,10},{7,11},{8,4},{9,5},... | collective-permute-start | bytes 12296 | tf_op jit(solution)/shard_map/ppermute | solution.py:59
  59.7 5.7 %collective-permute-start.9 = (f32[8,128]{1,0:T(8,128)S(1)}, f32[8,128]{1,0:T(8,128)S(1)}, u32[]{:S(2)}, u32[]{:S(2)}) collective-permute-start(f32[8,128]{1,0:T(8,128)S(1)} %add.32), channel_id=1, source_target_pairs={{0,8},{1,9},{2,10},{3,11},{4,12},{5,13},{6,14},{7,15},{8,0},{9,1},... | collective-permute-start | bytes 12296 | tf_op jit(solution)/shard_map/ppermute | solution.py:59
  59.7 5.7 %collective-permute-start.8 = (f32[8,128]{1,0:T(8,128)S(1)}, f32[8,128]{1,0:T(8,128)S(1)}, u32[]{:S(2)}, u32[]{:S(2)}) collective-permute-start(f32[8,128]{1,0:T(8,128)S(1)} %add.32), channel_id=1, source_target_pairs={{0,4},{1,5},{2,6},{3,7},{4,0},{5,1},{6,2},{7,3},{8,12},{9,13},{10,... | collective-permute-start | bytes 12296 | tf_op jit(solution)/shard_map/ppermute | solution.py:59
  72.7 6.4 %collective-permute-start.11 = (f32[8,2,8,384]{3,2,1,0:T(8,128)S(1)}, f32[8,2,8,384]{3,2,1,0:T(8,128)S(1)}, u32[]{:S(2)}, u32[]{:S(2)}) collective-permute-start(f32[8,2,8,384]{3,2,1,0:T(8,128)S(1)} %get-tuple-element.56.near_ref.corrections_ref), channel_id=1, source_target_pairs={{4,0},{14,2},{8,4},{2,6},{12,8},{6,10},{0,12},{10,14},{5,1},{15,3}... | collective-permute-start | bytes 589832 | tf_op jit(solution)/shard_map/ppermute | solution.py:44
  74.5 4.6 %collective-permute-start.12 = (f32[8,8,384]{2,1,0:T(8,128)S(1)}, f32[8,8,384]{2,1,0:T(8,128)S(1)}, u32[]{:S(2)}, u32[]{:S(2)}) collective-permute-start(f32[8,8,384]{2,1,0:T(8,128)S(1)} %get-tuple-element.58), channel_id=1, source_target_pairs={{0,2},{2,0},{4,6},{6,4},{8,10},{10,8},{12,14},{14,12},{1,3},{3,1},... | collective-permute-start | bytes 294920 | tf_op jit(solution)/shard_map/ppermute | solution.py:35
  74.5 4.6 %collective-permute-start.13 = (f32[8,8,384]{2,1,0:T(8,128)S(1)}, f32[8,8,384]{2,1,0:T(8,128)S(1)}, u32[]{:S(2)}, u32[]{:S(2)}) collective-permute-start(f32[8,8,384]{2,1,0:T(8,128)S(1)} %get-tuple-element.59), channel_id=1, source_target_pairs={{0,1},{1,0},{2,3},{3,2},{4,5},{5,4},{6,7},{7,6},{8,9},{9,8},{10,11... | collective-permute-start | bytes 294920 | tf_op jit(solution)/shard_map/ppermute | solution.py:39
  79.1 7.7 %collective-permute-start.16 = (f32[8,2,8,384]{3,2,1,0:T(8,128)S(1)}, f32[8,2,8,384]{3,2,1,0:T(8,128)S(1)}, u32[]{:S(2)}, u32[]{:S(2)}) collective-permute-start(f32[8,2,8,384]{3,2,1,0:T(8,128)S(1)} %get-tuple-element.68.far_ref.corrections_ref), channel_id=1, source_target_pairs={{12,0},{6,2},{0,4},{10,6},{4,8},{14,10},{8,12},{2,14},{13,1},{7,3}... | collective-permute-start | bytes 589832 | tf_op jit(solution)/shard_map/ppermute | solution.py:49
  80.9 1.2 %collective-permute-start.14 = (f32[8,128]{1,0:T(8,128)S(1)}, f32[8,128]{1,0:T(8,128)S(1)}, u32[]{:S(2)}, u32[]{:S(2)}) collective-permute-start(f32[8,128]{1,0:T(8,128)S(1)} %second_across.1), channel_id=1, source_target_pairs={{0,1},{1,0},{2,3},{3,2},{4,5},{5,4},{6,7},{7,6},{8,9},{9,8},{10,11... | collective-permute-start | bytes 12296 | tf_op jit(solution)/shard_map/ppermute | solution.py:59
  82.1 3.6 %collective-permute-start.15 = (f32[8,128]{1,0:T(8,128)S(1)}, f32[8,128]{1,0:T(8,128)S(1)}, u32[]{:S(2)}, u32[]{:S(2)}) collective-permute-start(f32[8,128]{1,0:T(8,128)S(1)} %add.36), channel_id=1, source_target_pairs={{0,2},{1,3},{2,0},{3,1},{4,6},{5,7},{6,4},{7,5},{8,10},{9,11},{10,... | collective-permute-start | bytes 12296 | tf_op jit(solution)/shard_map/ppermute | solution.py:59
  86.8 5.8 %collective-permute-start.19 = (f32[8,128]{1,0:T(8,128)S(1)}, f32[8,128]{1,0:T(8,128)S(1)}, u32[]{:S(2)}, u32[]{:S(2)}) collective-permute-start(f32[8,128]{1,0:T(8,128)S(1)} %add.37), channel_id=1, source_target_pairs={{0,12},{1,13},{2,14},{3,15},{4,8},{5,9},{6,10},{7,11},{8,4},{9,5},... | collective-permute-start | bytes 12296 | tf_op jit(solution)/shard_map/ppermute | solution.py:59
  89.2 4.5 %collective-permute-start.18 = (f32[8,128]{1,0:T(8,128)S(1)}, f32[8,128]{1,0:T(8,128)S(1)}, u32[]{:S(2)}, u32[]{:S(2)}) collective-permute-start(f32[8,128]{1,0:T(8,128)S(1)} %add.37), channel_id=1, source_target_pairs={{0,8},{1,9},{2,10},{3,11},{4,12},{5,13},{6,14},{7,15},{8,0},{9,1},... | collective-permute-start | bytes 12296 | tf_op jit(solution)/shard_map/ppermute | solution.py:59
  89.2 4.5 %collective-permute-start.17 = (f32[8,128]{1,0:T(8,128)S(1)}, f32[8,128]{1,0:T(8,128)S(1)}, u32[]{:S(2)}, u32[]{:S(2)}) collective-permute-start(f32[8,128]{1,0:T(8,128)S(1)} %add.37), channel_id=1, source_target_pairs={{0,4},{1,5},{2,6},{3,7},{4,0},{5,1},{6,2},{7,3},{8,12},{9,13},{10,... | collective-permute-start | bytes 12296 | tf_op jit(solution)/shard_map/ppermute | solution.py:59
  99.5 4.2 %collective-permute-start.20 = (f32[2,2,8,384]{3,2,1,0:T(8,128)S(1)}, f32[2,2,8,384]{3,2,1,0:T(8,128)S(1)}, u32[]{:S(2)}, u32[]{:S(2)}) collective-permute-start(f32[2,2,8,384]{3,2,1,0:T(8,128)S(1)} %densities.3), channel_id=1, source_target_pairs={{0,2},{2,0},{4,6},{6,4},{8,10},{10,8},{12,14},{14,12},{1,3},{3,1},... | collective-permute-start | bytes 147464 | tf_op jit(solution)/shard_map/ppermute | solution.py:35

commit v7 on v6

--- a/solution.py
+++ b/solution.py
@@ -49,7 +49,7 @@
     return lax.ppermute(x, "gz", [((i + (size - 2 if i % 2 == 0 else 2)) % size, i) for i in range(size)])
 
 
-def grid_sum(x, later=()):
+def grid_sum(x, later, by_four):
     axes = ("gz", "gy")
     total = lax.axis_size("gz") * lax.axis_size("gy")
     if total & (total - 1):
@@ -60,7 +60,7 @@
 
     mask = 1
     while mask < total:
-        wide = mask >= 4 and 4 * mask <= total
+        wide = by_four and mask >= 4 and 4 * mask <= total
         if mask * (4 if wide else 2) == total:
             x, later = lax.optimization_barrier((x, later))
         if wide:
@@ -350,7 +350,7 @@
         prepare_kernel,
         out_shape=(shape, shape),
         in_specs=[pl.BlockSpec(memory_space=pltpu.HBM)] * 3,
-        out_specs=[pl.BlockSpec(memory_space=pltpu.HBM)] * 2,
+        out_specs=[VMEM] * 2,
         scratch_shapes=[pltpu.SemaphoreType.DMA((6 * nz,))],
         compiler_params=pltpu.CompilerParams(vmem_limit_bytes=62 * 1024 * 1024),
         name="prepare",
@@ -699,7 +699,9 @@
         flops=25000000,
         name="first_across",
     )
-    pencil, (behind, pair_rows, core_rows) = grid_sum(tile, (behind, pair_rows, core_rows))
+    pencil, (behind, pair_rows, core_rows) = grid_sum(
+        tile, (behind, pair_rows, core_rows), by_four=False
+    )
     search_images, inverse, curvature, stiff_layers, stiff_wide = call(
         first_images_kernel,
         [(BLOCK,) + plane, plane, plane, (depth + 2, half, nx), wide],
@@ -738,7 +740,7 @@
         flops=25000000,
         name="second_across",
     )
-    pencil, behind = grid_sum(tile, behind)
+    pencil, behind = grid_sum(tile, behind, by_four=True)
     (correction_images,) = call(
         images_kernel,
         [mode_plane],

time: 104 us -> 77.3 us (0.74)
  Pallas kernels: 58 us -> 33.1 us
  waiting for transfers between devices: 22.1 us -> 17.1 us
  starting transfers between devices: 22.7 us -> 25.6 us
    pallas_call x1, Pallas kernels: 28 us -> 2.41 us  [prepare(): pl.pallas_call(prepare_kernel, out_shape=(shape, shape), in_specs=[pl.Blo...]
    ppermute x2, waiting for transfers between devices: 4.74 us -> 0.01 us  [from_behind(): lax.ppermute(x, 'gz', [((i + (size - 2 if i % 2 == 0 else 2)) % size, i)...]
    ppermute x4, starting transfers between devices: 5.77 us -> 8.59 us  [pair_swap(): lax.ppermute(x, 'gz', [(i, i ^ 1) for i in range(lax.axis_size('gz'))])]
    ppermute x4, waiting for transfers between devices: 5.16 us -> 2.34 us  [pair_swap(): lax.ppermute(x, 'gz', [(i, i ^ 1) for i in range(lax.axis_size('gz'))])]
    ppermute x10 -> x9, waiting for transfers between devices: 8.43 us -> 11 us  [other(): return lax.ppermute(x, axes, [(i, i ^ mask) for i in range(total)])]
    ppermute x2, starting transfers between devices: 0.33 us -> 1.63 us  [from_behind(): lax.ppermute(x, 'gz', [((i + (size - 2 if i % 2 == 0 else 2)) % size, i)...]
    ppermute x10 -> x9, starting transfers between devices: 11.1 us -> 10.6 us  [other(): return lax.ppermute(x, axes, [(i, i ^ mask) for i in range(total)])]
  transfers between devices with their start and end apart: 21 -> 20, of which waited for: 12 -> 11; matrix products, arithmetic and copies ran while one was open for 0% -> 0% of each run, Pallas kernels for 15% -> 21%
where the time goes in v7:
time: 77.3 us; the launch traced here: 77.5 us
  Pallas kernels  33.1 us (43%)
  starting transfers between devices  25.6 us (33%)
  waiting for transfers between devices  17.1 us (22%)
  between operations  0.79 us (1%)
    pallas_call x13, Pallas kernels, call(): pl.pallas_call(kernel, out_shape=out_shape, in_specs=[VMEM] * len(args),...  30.7 us
    ppermute x9, waiting for transfers between devices, other(): return lax.ppermute(x, axes, [(i, i ^ mask) for i in range(total)])  11 us
    ppermute x9, starting transfers between devices, other(): return lax.ppermute(x, axes, [(i, i ^ mask) for i in range(total)])  10.6 us
    ppermute x4, starting transfers between devices, pair_swap(): lax.ppermute(x, 'gz', [(i, i ^ 1) for i in range(lax.axis_size('gz'))])  8.59 us
    ppermute x2, starting transfers between devices, from_beyond(): lax.ppermute(x, 'gz', [((i + (2 if i % 2 == 0 else size - 2)) % size, i)...  4.67 us
    ppermute x2, waiting for transfers between devices, from_beyond(): lax.ppermute(x, 'gz', [((i + (2 if i % 2 == 0 else size - 2)) % size, i)...  3 us
    pallas_call x1, Pallas kernels, prepare(): pl.pallas_call(prepare_kernel, out_shape=(shape, shape), in_specs=[pl.Blo...  2.41 us
    ppermute x4, waiting for transfers between devices, pair_swap(): lax.ppermute(x, 'gz', [(i, i ^ 1) for i in range(lax.axis_size('gz'))])  2.34 us
  transfers between devices with their start and end apart: 20, of which 11 were waited for; matrix products, arithmetic and copies ran while one was open for 0% of the time, Pallas kernels for 21%

profile of v7, /device:TPU:0, one launch (start us, length us, event | category | flops | bytes accessed | tf_op | source)
XLA Modules:
  0.0 77.5 jit_solution(3023627772306168360)
XLA Ops:
  0.6 2.4 %prepare.1 = (f32[18,2,8,384]{3,2,1,0:T(8,128)}, f32[18,2,8,384]{3,2,1,0:T(8,128)}) custom-call(f32[16,2,16,384]{3,2,1,0:T(8,128)} %block_ref.3, f32[2,16,384]{2,1,0:T(8,128)} %stiffness_ref.3, f32[2,16,384]{2,1,0:T(8,128)} %concentration_ref.1), custom_call_target="tpu_custom_call" | custom-call | tf_op jit(solution)/shard_map/prepare/pallas_call | solution.py:349
  3.1 3.0 %collective-permute-start = (f32[18,2,8,384]{3,2,1,0:T(8,128)}, f32[18,2,8,384]{3,2,1,0:T(8,128)S(1)}, u32[]{:S(2)}, u32[]{:S(2)}) collective-permute-start(f32[18,2,8,384]{3,2,1,0:T(8,128)} %get-tuple-element.41), channel_id=1, source_target_pairs={{0,2},{2,0},{4,6},{6,4},{8,10},{10,8},{12,14},{14,12},{1,3},{3,1},... | collective-permute-start | bytes 1327112 | tf_op jit(solution)/shard_map/ppermute | solution.py:35
  6.1 3.6 %collective-permute-start.2 = (f32[18,2,8,384]{3,2,1,0:T(8,128)}, f32[18,2,8,384]{3,2,1,0:T(8,128)S(1)}, u32[]{:S(2)}, u32[]{:S(2)}) collective-permute-start(f32[18,2,8,384]{3,2,1,0:T(8,128)} %get-tuple-element.40.mine_ref), channel_id=1, source_target_pairs={{4,0},{14,2},{8,4},{2,6},{12,8},{6,10},{0,12},{10,14},{5,1},{15,3}... | collective-permute-start | bytes 1327112 | tf_op jit(solution)/shard_map/ppermute | solution.py:44
  10.0 0.6 copy-done.3
  10.6 0.8 %collective-permute-done.1.beside_ref = f32[16,2,4,384]{3,2,1,0:T(4,128)S(1)} collective-permute-done((f32[16,2,4,384]{3,2,1,0:T(4,128)S(1)}, f32[16,2,4,384]{3,2,1,0:T(4,128)S(1)}, u32[]{:S(2)}, u32[]{:S(2)}) %collective-permute-start.1) | collective-permute-done | bytes 196640 | tf_op jit(solution)/shard_map/ppermute | solution.py:39
  11.4 4.9 %first_local.1.tile_ref = f32[8,128]{1,0:T(8,128)S(1)} custom-call(f32[16,2,16,384]{3,2,1,0:T(8,128)S(1)} %copy-done.1, f32[16,2,4,384]{3,2,1,0:T(4,128)S(1)} %collective-permute-done.1.beside_ref, f32[2,16,384]{2,1,0:T(8,128)S(1)} %fusion.curvature_ref, f32[2,16,384]{2,1,0:T(8,128)S(1)} %copy-done.2), custom_call_target="tpu_custom_call" | custom-call | flops 100000000 | bytes 1085440 | tf_op jit(solution)/shard_map/first_local/pallas_call | solution.py:22
  16.9 3.0 %collective-permute-done.2.beyond_ref = f32[18,2,8,384]{3,2,1,0:T(8,128)S(1)} collective-permute-done((f32[18,2,8,384]{3,2,1,0:T(8,128)}, f32[18,2,8,384]{3,2,1,0:T(8,128)S(1)}, u32[]{:S(2)}, u32[]{:S(2)}) %collective-permute-start.2) | collective-permute-done | bytes 442400 | tf_op jit(solution)/shard_map/ppermute | solution.py:44
  19.9 2.4 %collective-permute-start.7 = (f32[17,8,384]{2,1,0:T(8,128)S(1)}, f32[17,8,384]{2,1,0:T(8,128)S(1)}, u32[]{:S(2)}, u32[]{:S(2)}) collective-permute-start(f32[17,8,384]{2,1,0:T(8,128)S(1)} %get-tuple-element.43), channel_id=1, source_target_pairs={{0,2},{2,0},{4,6},{6,4},{8,10},{10,8},{12,14},{14,12},{1,3},{3,1},... | collective-permute-start | bytes 626696 | tf_op jit(solution)/shard_map/ppermute | solution.py:35
  22.3 1.4 %first_across.1 = f32[8,128]{1,0:T(8,128)S(1)} custom-call(f32[18,2,8,384]{3,2,1,0:T(8,128)S(1)} %copy-done, f32[18,2,8,384]{3,2,1,0:T(8,128)S(1)} %collective-permute-done.theirs_ref, f32[18,2,8,384]{3,2,1,0:T(8,128)S(1)} %collective-permute-done.2.beyond_ref, f32[8,128]{1,0:T(8,128)S(1)} %first_local.1.tile_ref), custom_call_target="tpu_custom_call" | custom-call | flops 25000000 | bytes 1335296 | tf_op jit(solution)/shard_map/first_across/pallas_call | solution.py:22
  24.3 0.8 %collective-permute-done.3 = f32[8,128]{1,0:T(8,128)S(1)} collective-permute-done((f32[8,128]{1,0:T(8,128)S(1)}, f32[8,128]{1,0:T(8,128)S(1)}, u32[]{:S(2)}, u32[]{:S(2)}) %collective-permute-start.3) | collective-permute-done | bytes 4128 | tf_op jit(solution)/shard_map/ppermute | solution.py:59
  25.1 3.6 %collective-permute-done.4 = f32[8,128]{1,0:T(8,128)S(1)} collective-permute-done((f32[8,128]{1,0:T(8,128)S(1)}, f32[8,128]{1,0:T(8,128)S(1)}, u32[]{:S(2)}, u32[]{:S(2)}) %collective-permute-start.4) | collective-permute-done | bytes 4128 | tf_op jit(solution)/shard_map/ppermute | solution.py:59
  28.7 3.7 %collective-permute-done.5 = f32[8,128]{1,0:T(8,128)S(1)} collective-permute-done((f32[8,128]{1,0:T(8,128)S(1)}, f32[8,128]{1,0:T(8,128)S(1)}, u32[]{:S(2)}, u32[]{:S(2)}) %collective-permute-start.5) | collective-permute-done | bytes 4128 | tf_op jit(solution)/shard_map/ppermute | solution.py:59
  32.4 2.3 %collective-permute-start.9 = (f32[8,128]{1,0:T(8,128)S(1)}, f32[8,128]{1,0:T(8,128)S(1)}, u32[]{:S(2)}, u32[]{:S(2)}) collective-permute-start(f32[8,128]{1,0:T(8,128)S(1)} %add.30), channel_id=1, source_target_pairs={{0,8},{1,9},{2,10},{3,11},{4,12},{5,13},{6,14},{7,15},{8,0},{9,1},... | collective-permute-start | bytes 12296 | tf_op jit(solution)/shard_map/ppermute | solution.py:59
  34.7 3.0 %first_images.1 = (f32[16,4,8,384]{3,2,1,0:T(8,128)S(1)}, f32[4,8,384]{2,1,0:T(8,128)S(1)}, f32[4,8,384]{2,1,0:T(8,128)S(1)}, f32[6,8,384]{2,1,0:T(8,128)S(1)}, f32[4,24,384]{2,1,0:T(8,128)S(1)}) custom-call(f32[18,2,8,384]{3,2,1,0:T(8,128)S(1)} %copy-done, f32[18,2,8,384]{3,2,1,0:T(8,128)S(1)} %collective-permute-done.theirs_ref, ...), custom_call_target="tpu_custom_call" | custom-call | flops 6000000 | bytes 3293184 | tf_op jit(solution)/shard_map/first_images/pallas_call | solution.py:22
  37.7 6.2 %ritz_pairs.2 = (f32[8]{0:T(128)}, f32[8,128]{1,0:T(8,128)S(1)}, f32[8,16,128]{2,1,0:T(8,128)S(1)}) custom-call(f32[8,128]{1,0:T(8,128)S(1)} %add.31.pencil_ref), custom_call_target="tpu_custom_call" | custom-call | flops 10000000 | bytes 73760 | tf_op jit(solution)/shard_map/ritz_pairs/pallas_call | solution.py:22
  43.9 1.2 %update.1 = (f32[8,4,8,384]{3,2,1,0:T(8,128)S(1)}, f32[8,4,8,384]{3,2,1,0:T(8,128)S(1)}, f32[8,2,8,384]{3,2,1,0:T(8,128)S(1)}, f32[8,2,8,384]{3,2,1,0:T(8,128)S(...) custom-call(f32[8,16,128]{2,1,0:T(8,128)S(1)} %get-tuple-element.49.mix_ref, ...), custom_call_target="tpu_custom_call" | custom-call | flops 1000000 | bytes 3166208 | tf_op jit(solution)/shard_map/update/pallas_call | solution.py:22
  45.1 1.1 %collective-permute-start.10 = (f32[8,2,8,384]{3,2,1,0:T(8,128)S(1)}, f32[8,2,8,384]{3,2,1,0:T(8,128)S(1)}, u32[]{:S(2)}, u32[]{:S(2)}) collective-permute-start(f32[8,2,8,384]{3,2,1,0:T(8,128)S(1)} %get-tuple-element.56.near_ref.corrections_ref), channel_id=1, source_target_pairs={{4,0},{14,2},{8,4},{2,6},{12,8},{6,10},{0,12},{10,14},{5,1},{15,3}... | collective-permute-start | bytes 589832 | tf_op jit(solution)/shard_map/ppermute | solution.py:44
  46.1 1.1 %collective-permute-start.11 = (f32[8,8,384]{2,1,0:T(8,128)S(1)}, f32[8,8,384]{2,1,0:T(8,128)S(1)}, u32[]{:S(2)}, u32[]{:S(2)}) collective-permute-start(f32[8,8,384]{2,1,0:T(8,128)S(1)} %get-tuple-element.58), channel_id=1, source_target_pairs={{0,2},{2,0},{4,6},{6,4},{8,10},{10,8},{12,14},{14,12},{1,3},{3,1},... | collective-permute-start | bytes 294920 | tf_op jit(solution)/shard_map/ppermute | solution.py:35
  47.2 2.9 %second_local.1.tile_ref = f32[8,128]{1,0:T(8,128)S(1)} custom-call(f32[8,4,8,384]{3,2,1,0:T(8,128)S(1)} %get-tuple-element.60.modes_ref, f32[8,4,8,384]{3,2,1,0:T(8,128)S(1)} %get-tuple-element.61.images_ref.first_ref, f32[8,2,8,384]{3,2,1,0:T(8,128)S(1)} %get-tuple-element.56.near_ref.corrections_ref, ...), custom_call_target="tpu_custom_call" | custom-call | flops 80000000 | bytes 1306624 | tf_op jit(solution)/shard_map/second_local/pallas_call | solution.py:22
  50.8 1.6 %collective-permute-start.15 = (f32[8,2,8,384]{3,2,1,0:T(8,128)S(1)}, f32[8,2,8,384]{3,2,1,0:T(8,128)S(1)}, u32[]{:S(2)}, u32[]{:S(2)}) collective-permute-start(f32[8,2,8,384]{3,2,1,0:T(8,128)S(1)} %get-tuple-element.68.far_ref.corrections_ref), channel_id=1, source_target_pairs={{12,0},{6,2},{0,4},{10,6},{4,8},{14,10},{8,12},{2,14},{13,1},{7,3}... | collective-permute-start | bytes 589832 | tf_op jit(solution)/shard_map/ppermute | solution.py:49
  52.4 1.4 %second_across.1 = f32[8,128]{1,0:T(8,128)S(1)} custom-call(f32[8,2,8,384]{3,2,1,0:T(8,128)S(1)} %get-tuple-element.56.near_ref.corrections_ref, f32[8,2,8,384]{3,2,1,0:T(8,128)S(1)} %get-tuple-element.68.far_ref.corrections_ref, f32[8,2,8,384]{3,2,1,0:T(8,128)S(1)} %collective-permute-done.10.beyond_ref, f32[8,8,384]{2,1,0:T(8,128)S(1)} %collective-permute-done.11.pair_ref, ...), custom_call_target="tpu_custom_call" | custom-call | flops 25000000 | bytes 868352 | tf_op jit(solution)/shard_map/second_across/pallas_call | solution.py:22
  54.1 0.9 %collective-permute-done.13 = f32[8,128]{1,0:T(8,128)S(1)} collective-permute-done((f32[8,128]{1,0:T(8,128)S(1)}, f32[8,128]{1,0:T(8,128)S(1)}, u32[]{:S(2)}, u32[]{:S(2)}) %collective-permute-start.13) | collective-permute-done | bytes 4128 | tf_op jit(solution)/shard_map/ppermute | solution.py:59
  55.0 3.2 %collective-permute-start.14 = (f32[8,128]{1,0:T(8,128)S(1)}, f32[8,128]{1,0:T(8,128)S(1)}, u32[]{:S(2)}, u32[]{:S(2)}) collective-permute-start(f32[8,128]{1,0:T(8,128)S(1)} %add.32), channel_id=1, source_target_pairs={{0,2},{1,3},{2,0},{3,1},{4,6},{5,7},{6,4},{7,5},{8,10},{9,11},{10,... | collective-permute-start | bytes 12296 | tf_op jit(solution)/shard_map/ppermute | solution.py:59
  58.2 1.6 %collective-permute-done.14 = f32[8,128]{1,0:T(8,128)S(1)} collective-permute-done((f32[8,128]{1,0:T(8,128)S(1)}, f32[8,128]{1,0:T(8,128)S(1)}, u32[]{:S(2)}, u32[]{:S(2)}) %collective-permute-start.14) | collective-permute-done | bytes 4128 | tf_op jit(solution)/shard_map/ppermute | solution.py:59
  59.8 1.7 %collective-permute-start.18 = (f32[8,128]{1,0:T(8,128)S(1)}, f32[8,128]{1,0:T(8,128)S(1)}, u32[]{:S(2)}, u32[]{:S(2)}) collective-permute-start(f32[8,128]{1,0:T(8,128)S(1)} %add.33), channel_id=1, source_target_pairs={{0,12},{1,13},{2,14},{3,15},{4,8},{5,9},{6,10},{7,11},{8,4},{9,5},... | collective-permute-start | bytes 12296 | tf_op jit(solution)/shard_map/ppermute | solution.py:59
  61.5 0.8 %collective-permute-start.17 = (f32[8,128]{1,0:T(8,128)S(1)}, f32[8,128]{1,0:T(8,128)S(1)}, u32[]{:S(2)}, u32[]{:S(2)}) collective-permute-start(f32[8,128]{1,0:T(8,128)S(1)} %add.33), channel_id=1, source_target_pairs={{0,8},{1,9},{2,10},{3,11},{4,12},{5,13},{6,14},{7,15},{8,0},{9,1},... | collective-permute-start | bytes 12296 | tf_op jit(solution)/shard_map/ppermute | solution.py:59
  62.3 1.9 %collective-permute-start.16 = (f32[8,128]{1,0:T(8,128)S(1)}, f32[8,128]{1,0:T(8,128)S(1)}, u32[]{:S(2)}, u32[]{:S(2)}) collective-permute-start(f32[8,128]{1,0:T(8,128)S(1)} %add.33), channel_id=1, source_target_pairs={{0,4},{1,5},{2,6},{3,7},{4,0},{5,1},{6,2},{7,3},{8,12},{9,13},{10,... | collective-permute-start | bytes 12296 | tf_op jit(solution)/shard_map/ppermute | solution.py:59
  64.2 1.4 %images.1.second_ref = f32[8,4,8,384]{3,2,1,0:T(8,128)S(1)} custom-call(f32[8,2,8,384]{3,2,1,0:T(8,128)S(1)} %get-tuple-element.56.near_ref.corrections_ref, f32[8,2,8,384]{3,2,1,0:T(8,128)S(1)} %get-tuple-element.68.far_ref.corrections_ref, f32[8,2,8,384]{3,2,1,0:T(8,128)S(1)} %collective-permute-done.15.behind_ref, ...), custom_call_target="tpu_custom_call" | custom-call | flops 1000000 | bytes 1646592 | tf_op jit(solution)/shard_map/images/pallas_call | solution.py:22
  66.0 6.2 %ritz_pairs.3 = (f32[8]{0:T(128)}, f32[8,128]{1,0:T(8,128)S(1)}, f32[8,16,128]{2,1,0:T(8,128)S(1)}) custom-call(f32[8,128]{1,0:T(8,128)S(1)} %add_add_fusion.pencil_ref), custom_call_target="tpu_custom_call" | custom-call | flops 10000000 | bytes 73760 | tf_op jit(solution)/shard_map/ritz_pairs/pallas_call | solution.py:22
  72.7 2.0 %collective-permute-start.19 = (f32[2,2,8,384]{3,2,1,0:T(8,128)S(1)}, f32[2,2,8,384]{3,2,1,0:T(8,128)S(1)}, u32[]{:S(2)}, u32[]{:S(2)}) collective-permute-start(f32[2,2,8,384]{3,2,1,0:T(8,128)S(1)} %densities.3), channel_id=1, source_target_pairs={{0,2},{2,0},{4,6},{6,4},{8,10},{10,8},{12,14},{14,12},{1,3},{3,1},... | collective-permute-start | bytes 147464 | tf_op jit(solution)/shard_map/ppermute | solution.py:35
  75.2 1.6 %collective-permute-done.19.other_ref = f32[2,2,8,384]{3,2,1,0:T(8,128)S(1)} collective-permute-done((f32[2,2,8,384]{3,2,1,0:T(8,128)S(1)}, f32[2,2,8,384]{3,2,1,0:T(8,128)S(1)}, u32[]{:S(2)}, u32[]{:S(2)}) %collective-permute-start.19) | collective-permute-done | bytes 49184 | tf_op jit(solution)/shard_map/ppermute | solution.py:35
  76.8 0.7 merge.1
  (40 shorter events, 3.6 us)
Async XLA Ops:
  0.6 9.1 %copy-start.1 = (f32[16,2,16,384]{3,2,1,0:T(8,128)S(1)}, f32[16,2,16,384]{3,2,1,0:T(8,128)}, u32[]{:S(2)}) copy-start(f32[16,2,16,384]{3,2,1,0:T(8,128)} %block_ref.3) | copy-start | bytes 2359300
  3.1 13.4 %collective-permute-start = (f32[18,2,8,384]{3,2,1,0:T(8,128)}, f32[18,2,8,384]{3,2,1,0:T(8,128)S(1)}, u32[]{:S(2)}, u32[]{:S(2)}) collective-permute-start(f32[18,2,8,384]{3,2,1,0:T(8,128)} %get-tuple-element.41), channel_id=1, source_target_pairs={{0,2},{2,0},{4,6},{6,4},{8,10},{10,8},{12,14},{14,12},{1,3},{3,1},... | collective-permute-start | bytes 1327112 | tf_op jit(solution)/shard_map/ppermute | solution.py:35
  6.1 13.8 %collective-permute-start.2 = (f32[18,2,8,384]{3,2,1,0:T(8,128)}, f32[18,2,8,384]{3,2,1,0:T(8,128)S(1)}, u32[]{:S(2)}, u32[]{:S(2)}) collective-permute-start(f32[18,2,8,384]{3,2,1,0:T(8,128)} %get-tuple-element.40.mine_ref), channel_id=1, source_target_pairs={{4,0},{14,2},{8,4},{2,6},{12,8},{6,10},{0,12},{10,14},{5,1},{15,3}... | collective-permute-start | bytes 1327112 | tf_op jit(solution)/shard_map/ppermute | solution.py:44
  9.8 0.8 %copy-start.3 = (f32[2,16,384]{2,1,0:T(8,128)S(1)}, f32[2,16,384]{2,1,0:T(8,128)}, u32[]{:S(2)}) copy-start(f32[2,16,384]{2,1,0:T(8,128)} %concentration_ref.1) | copy-start | bytes 147460
  9.9 1.5 %copy-start.2 = (f32[2,16,384]{2,1,0:T(8,128)S(1)}, f32[2,16,384]{2,1,0:T(8,128)}, u32[]{:S(2)}) copy-start(f32[2,16,384]{2,1,0:T(8,128)} %stiffness_ref.3) | copy-start | bytes 147460
  9.9 1.5 %collective-permute-start.1 = (f32[16,2,4,384]{3,2,1,0:T(4,128)S(1)}, f32[16,2,4,384]{3,2,1,0:T(4,128)S(1)}, u32[]{:S(2)}, u32[]{:S(2)}) collective-permute-start(f32[16,2,4,384]{3,2,1,0:T(4,128)S(1)} %pad_maximum_fusion), channel_id=1, source_target_pairs={{0,1},{1,0},{2,3},{3,2},{4,5},{5,4},{6,7},{7,6},{8,9},{9,8},{10,11... | collective-permute-start | bytes 589832 | tf_op jit(solution)/shard_map/ppermute | solution.py:39
  10.6 5.9 %copy-start = (f32[18,2,8,384]{3,2,1,0:T(8,128)S(1)}, f32[18,2,8,384]{3,2,1,0:T(8,128)}, u32[]{:S(2)}) copy-start(f32[18,2,8,384]{3,2,1,0:T(8,128)} %get-tuple-element.40.mine_ref) | copy-start | bytes 1327108
  19.9 12.5 %collective-permute-start.6 = (f32[18,2,8,384]{3,2,1,0:T(8,128)S(1)}, f32[18,2,8,384]{3,2,1,0:T(8,128)S(1)}, u32[]{:S(2)}, u32[]{:S(2)}) collective-permute-start(f32[18,2,8,384]{3,2,1,0:T(8,128)S(1)} %collective-permute-done.theirs_ref), channel_id=1, source_target_pairs={{12,0},{6,2},{0,4},{10,6},{4,8},{14,10},{8,12},{2,14},{13,1},{7,3}... | collective-permute-start | bytes 1327112 | tf_op jit(solution)/shard_map/ppermute | solution.py:49
  19.9 12.5 %collective-permute-start.7 = (f32[17,8,384]{2,1,0:T(8,128)S(1)}, f32[17,8,384]{2,1,0:T(8,128)S(1)}, u32[]{:S(2)}, u32[]{:S(2)}) collective-permute-start(f32[17,8,384]{2,1,0:T(8,128)S(1)} %get-tuple-element.43), channel_id=1, source_target_pairs={{0,2},{2,0},{4,6},{6,4},{8,10},{10,8},{12,14},{14,12},{1,3},{3,1},... | collective-permute-start | bytes 626696 | tf_op jit(solution)/shard_map/ppermute | solution.py:35
  22.3 10.1 %collective-permute-start.8 = (f32[17,8,384]{2,1,0:T(8,128)S(1)}, f32[17,8,384]{2,1,0:T(8,128)S(1)}, u32[]{:S(2)}, u32[]{:S(2)}) collective-permute-start(f32[17,8,384]{2,1,0:T(8,128)S(1)} %get-tuple-element.44), channel_id=1, source_target_pairs={{0,1},{1,0},{2,3},{3,2},{4,5},{5,4},{6,7},{7,6},{8,9},{9,8},{10,11... | collective-permute-start | bytes 626696 | tf_op jit(solution)/shard_map/ppermute | solution.py:39
  23.8 1.3 %collective-permute-start.3 = (f32[8,128]{1,0:T(8,128)S(1)}, f32[8,128]{1,0:T(8,128)S(1)}, u32[]{:S(2)}, u32[]{:S(2)}) collective-permute-start(f32[8,128]{1,0:T(8,128)S(1)} %first_across.1), channel_id=1, source_target_pairs={{0,1},{1,0},{2,3},{3,2},{4,5},{5,4},{6,7},{7,6},{8,9},{9,8},{10,11... | collective-permute-start | bytes 12296 | tf_op jit(solution)/shard_map/ppermute | solution.py:59
  25.1 3.6 %collective-permute-start.4 = (f32[8,128]{1,0:T(8,128)S(1)}, f32[8,128]{1,0:T(8,128)S(1)}, u32[]{:S(2)}, u32[]{:S(2)}) collective-permute-start(f32[8,128]{1,0:T(8,128)S(1)} %add.28), channel_id=1, source_target_pairs={{0,2},{1,3},{2,0},{3,1},{4,6},{5,7},{6,4},{7,5},{8,10},{9,11},{10,... | collective-permute-start | bytes 12296 | tf_op jit(solution)/shard_map/ppermute | solution.py:59
  28.7 3.7 %collective-permute-start.5 = (f32[8,128]{1,0:T(8,128)S(1)}, f32[8,128]{1,0:T(8,128)S(1)}, u32[]{:S(2)}, u32[]{:S(2)}) collective-permute-start(f32[8,128]{1,0:T(8,128)S(1)} %add.29), channel_id=1, source_target_pairs={{0,4},{1,5},{2,6},{3,7},{4,0},{5,1},{6,2},{7,3},{8,12},{9,13},{10,... | collective-permute-start | bytes 12296 | tf_op jit(solution)/shard_map/ppermute | solution.py:59
  32.4 5.3 %collective-permute-start.9 = (f32[8,128]{1,0:T(8,128)S(1)}, f32[8,128]{1,0:T(8,128)S(1)}, u32[]{:S(2)}, u32[]{:S(2)}) collective-permute-start(f32[8,128]{1,0:T(8,128)S(1)} %add.30), channel_id=1, source_target_pairs={{0,8},{1,9},{2,10},{3,11},{4,12},{5,13},{6,14},{7,15},{8,0},{9,1},... | collective-permute-start | bytes 12296 | tf_op jit(solution)/shard_map/ppermute | solution.py:59
  45.1 5.7 %collective-permute-start.10 = (f32[8,2,8,384]{3,2,1,0:T(8,128)S(1)}, f32[8,2,8,384]{3,2,1,0:T(8,128)S(1)}, u32[]{:S(2)}, u32[]{:S(2)}) collective-permute-start(f32[8,2,8,384]{3,2,1,0:T(8,128)S(1)} %get-tuple-element.56.near_ref.corrections_ref), channel_id=1, source_target_pairs={{4,0},{14,2},{8,4},{2,6},{12,8},{6,10},{0,12},{10,14},{5,1},{15,3}... | collective-permute-start | bytes 589832 | tf_op jit(solution)/shard_map/ppermute | solution.py:44
  46.1 4.6 %collective-permute-start.11 = (f32[8,8,384]{2,1,0:T(8,128)S(1)}, f32[8,8,384]{2,1,0:T(8,128)S(1)}, u32[]{:S(2)}, u32[]{:S(2)}) collective-permute-start(f32[8,8,384]{2,1,0:T(8,128)S(1)} %get-tuple-element.58), channel_id=1, source_target_pairs={{0,2},{2,0},{4,6},{6,4},{8,10},{10,8},{12,14},{14,12},{1,3},{3,1},... | collective-permute-start | bytes 294920 | tf_op jit(solution)/shard_map/ppermute | solution.py:35
  47.2 3.5 %collective-permute-start.12 = (f32[8,8,384]{2,1,0:T(8,128)S(1)}, f32[8,8,384]{2,1,0:T(8,128)S(1)}, u32[]{:S(2)}, u32[]{:S(2)}) collective-permute-start(f32[8,8,384]{2,1,0:T(8,128)S(1)} %get-tuple-element.59), channel_id=1, source_target_pairs={{0,1},{1,0},{2,3},{3,2},{4,5},{5,4},{6,7},{7,6},{8,9},{9,8},{10,11... | collective-permute-start | bytes 294920 | tf_op jit(solution)/shard_map/ppermute | solution.py:39
  50.8 9.0 %collective-permute-start.15 = (f32[8,2,8,384]{3,2,1,0:T(8,128)S(1)}, f32[8,2,8,384]{3,2,1,0:T(8,128)S(1)}, u32[]{:S(2)}, u32[]{:S(2)}) collective-permute-start(f32[8,2,8,384]{3,2,1,0:T(8,128)S(1)} %get-tuple-element.68.far_ref.corrections_ref), channel_id=1, source_target_pairs={{12,0},{6,2},{0,4},{10,6},{4,8},{14,10},{8,12},{2,14},{13,1},{7,3}... | collective-permute-start | bytes 589832 | tf_op jit(solution)/shard_map/ppermute | solution.py:49
  53.9 1.2 %collective-permute-start.13 = (f32[8,128]{1,0:T(8,128)S(1)}, f32[8,128]{1,0:T(8,128)S(1)}, u32[]{:S(2)}, u32[]{:S(2)}) collective-permute-start(f32[8,128]{1,0:T(8,128)S(1)} %second_across.1), channel_id=1, source_target_pairs={{0,1},{1,0},{2,3},{3,2},{4,5},{5,4},{6,7},{7,6},{8,9},{9,8},{10,11... | collective-permute-start | bytes 12296 | tf_op jit(solution)/shard_map/ppermute | solution.py:59
  55.0 4.8 %collective-permute-start.14 = (f32[8,128]{1,0:T(8,128)S(1)}, f32[8,128]{1,0:T(8,128)S(1)}, u32[]{:S(2)}, u32[]{:S(2)}) collective-permute-start(f32[8,128]{1,0:T(8,128)S(1)} %add.32), channel_id=1, source_target_pairs={{0,2},{1,3},{2,0},{3,1},{4,6},{5,7},{6,4},{7,5},{8,10},{9,11},{10,... | collective-permute-start | bytes 12296 | tf_op jit(solution)/shard_map/ppermute | solution.py:59
  59.8 5.8 %collective-permute-start.18 = (f32[8,128]{1,0:T(8,128)S(1)}, f32[8,128]{1,0:T(8,128)S(1)}, u32[]{:S(2)}, u32[]{:S(2)}) collective-permute-start(f32[8,128]{1,0:T(8,128)S(1)} %add.33), channel_id=1, source_target_pairs={{0,12},{1,13},{2,14},{3,15},{4,8},{5,9},{6,10},{7,11},{8,4},{9,5},... | collective-permute-start | bytes 12296 | tf_op jit(solution)/shard_map/ppermute | solution.py:59
  61.5 4.5 %collective-permute-start.17 = (f32[8,128]{1,0:T(8,128)S(1)}, f32[8,128]{1,0:T(8,128)S(1)}, u32[]{:S(2)}, u32[]{:S(2)}) collective-permute-start(f32[8,128]{1,0:T(8,128)S(1)} %add.33), channel_id=1, source_target_pairs={{0,8},{1,9},{2,10},{3,11},{4,12},{5,13},{6,14},{7,15},{8,0},{9,1},... | collective-permute-start | bytes 12296 | tf_op jit(solution)/shard_map/ppermute | solution.py:59
  62.3 3.7 %collective-permute-start.16 = (f32[8,128]{1,0:T(8,128)S(1)}, f32[8,128]{1,0:T(8,128)S(1)}, u32[]{:S(2)}, u32[]{:S(2)}) collective-permute-start(f32[8,128]{1,0:T(8,128)S(1)} %add.33), channel_id=1, source_target_pairs={{0,4},{1,5},{2,6},{3,7},{4,0},{5,1},{6,2},{7,3},{8,12},{9,13},{10,... | collective-permute-start | bytes 12296 | tf_op jit(solution)/shard_map/ppermute | solution.py:59
  72.7 4.2 %collective-permute-start.19 = (f32[2,2,8,384]{3,2,1,0:T(8,128)S(1)}, f32[2,2,8,384]{3,2,1,0:T(8,128)S(1)}, u32[]{:S(2)}, u32[]{:S(2)}) collective-permute-start(f32[2,2,8,384]{3,2,1,0:T(8,128)S(1)} %densities.3), channel_id=1, source_target_pairs={{0,2},{2,0},{4,6},{6,4},{8,10},{10,8},{12,14},{14,12},{1,3},{3,1},... | collective-permute-start | bytes 147464 | tf_op jit(solution)/shard_map/ppermute | solution.py:35

commit v8 on v7

--- a/solution.py
+++ b/solution.py
@@ -11,6 +11,7 @@
 MODES = 8
 HALF = BLOCK // 2
 LANES = 128
+EARLY_SWEEPS = 4
 MAX_SWEEPS = 14
 HIGHEST = lax.Precision.HIGHEST
 VMEM = pl.BlockSpec(memory_space=pltpu.VMEM)
@@ -184,8 +185,7 @@
         )
         return top, bottom
 
-    def sweep(carry):
-        count, _, upper, lower = carry
+    def sweep(upper, lower):
         upper, lower = list(upper), list(lower)
         top, bottom = squares(upper, lower)
         worst = zero
@@ -215,14 +215,25 @@
             )
             bottom = jnp.where(row == 7, top, pltpu.roll(bottom, 7, 0))
             top = next_top
-        return count + 1, jnp.max(worst), tuple(upper), tuple(lower)
+        return worst, tuple(upper), tuple(lower)
+
+    def early(_, carry):
+        return sweep(*carry)[1:]
+
+    def late(carry):
+        count, _, upper, lower = carry
+        worst, upper, lower = sweep(upper, lower)
+        for step in (4, 2, 1):
+            worst = jnp.maximum(worst, pltpu.roll(worst, step, 0))
+        return count + 1, worst[0, 0], upper, lower
 
     def unfinished(carry):
         count, worst, _, _ = carry
         return jnp.logical_and(count < MAX_SWEEPS, worst > 1.6e-7)
 
+    upper, lower = lax.fori_loop(0, EARLY_SWEEPS, early, (tuple(upper), tuple(lower)))
     _, _, upper, lower = lax.while_loop(
-        unfinished, sweep, (jnp.int32(0), jnp.float32(1.0), tuple(upper), tuple(lower))
+        unfinished, late, (jnp.int32(EARLY_SWEEPS), jnp.float32(1.0), upper, lower)
     )
 
     top, bottom = squares(upper, lower)

time: 77.3 us -> 75.4 us (0.975)
  Pallas kernels: 33.1 us -> 30.7 us
    pallas_call x13, Pallas kernels: 30.7 us -> 28.3 us  [call(): pl.pallas_call(kernel, out_shape=out_shape, in_specs=[VMEM] * len(args),...]
  transfers between devices with their start and end apart: 20 -> 20, of which waited for: 11 -> 12; matrix products, arithmetic and copies ran while one was open for 0% -> 0% of each run, Pallas kernels for 21% -> 21%
where the time goes in v8:
time: 75.4 us; the launch traced here: 75.2 us
  Pallas kernels  30.7 us (41%)
  starting transfers between devices  25.8 us (34%)
  waiting for transfers between devices  17 us (23%)
  between operations  0.78 us (1%)
    pallas_call x13, Pallas kernels, call(): pl.pallas_call(kernel, out_shape=out_shape, in_specs=[VMEM] * len(args),...  28.3 us
    ppermute x9, waiting for transfers between devices, other(): return lax.ppermute(x, axes, [(i, i ^ mask) for i in range(total)])  10.9 us
    ppermute x9, starting transfers between devices, other(): return lax.ppermute(x, axes, [(i, i ^ mask) for i in range(total)])  10.8 us
    ppermute x4, starting transfers between devices, pair_swap(): lax.ppermute(x, 'gz', [(i, i ^ 1) for i in range(lax.axis_size('gz'))])  8.65 us
    ppermute x2, starting transfers between devices, from_beyond(): lax.ppermute(x, 'gz', [((i + (2 if i % 2 == 0 else size - 2)) % size, i)...  4.85 us
    ppermute x2, waiting for transfers between devices, from_beyond(): lax.ppermute(x, 'gz', [((i + (2 if i % 2 == 0 else size - 2)) % size, i)...  3 us
    pallas_call x1, Pallas kernels, prepare(): pl.pallas_call(prepare_kernel, out_shape=(shape, shape), in_specs=[pl.Blo...  2.41 us
    ppermute x4, waiting for transfers between devices, pair_swap(): lax.ppermute(x, 'gz', [(i, i ^ 1) for i in range(lax.axis_size('gz'))])  2.29 us
  transfers between devices with their start and end apart: 20, of which 12 were waited for; matrix products, arithmetic and copies ran while one was open for 0% of the time, Pallas kernels for 21%

profile of v8, /device:TPU:0, one launch (start us, length us, event | category | flops | bytes accessed | tf_op | source)
XLA Modules:
  0.0 75.2 jit_solution(665197093907709767)
XLA Ops:
  0.6 2.4 %prepare.1 = (f32[18,2,8,384]{3,2,1,0:T(8,128)}, f32[18,2,8,384]{3,2,1,0:T(8,128)}) custom-call(f32[16,2,16,384]{3,2,1,0:T(8,128)} %block_ref.3, f32[2,16,384]{2,1,0:T(8,128)} %stiffness_ref.3, f32[2,16,384]{2,1,0:T(8,128)} %concentration_ref.1), custom_call_target="tpu_custom_call" | custom-call | tf_op jit(solution)/shard_map/prepare/pallas_call | solution.py:360
  3.1 3.0 %collective-permute-start = (f32[18,2,8,384]{3,2,1,0:T(8,128)}, f32[18,2,8,384]{3,2,1,0:T(8,128)S(1)}, u32[]{:S(2)}, u32[]{:S(2)}) collective-permute-start(f32[18,2,8,384]{3,2,1,0:T(8,128)} %get-tuple-element.41), channel_id=1, source_target_pairs={{0,2},{2,0},{4,6},{6,4},{8,10},{10,8},{12,14},{14,12},{1,3},{3,1},... | collective-permute-start | bytes 1327112 | tf_op jit(solution)/shard_map/ppermute | solution.py:36
  6.1 3.6 %collective-permute-start.2 = (f32[18,2,8,384]{3,2,1,0:T(8,128)}, f32[18,2,8,384]{3,2,1,0:T(8,128)S(1)}, u32[]{:S(2)}, u32[]{:S(2)}) collective-permute-start(f32[18,2,8,384]{3,2,1,0:T(8,128)} %get-tuple-element.40.mine_ref), channel_id=1, source_target_pairs={{4,0},{14,2},{8,4},{2,6},{12,8},{6,10},{0,12},{10,14},{5,1},{15,3}... | collective-permute-start | bytes 1327112 | tf_op jit(solution)/shard_map/ppermute | solution.py:45
  10.0 0.6 copy-done.3
  10.6 0.8 %collective-permute-done.1.beside_ref = f32[16,2,4,384]{3,2,1,0:T(4,128)S(1)} collective-permute-done((f32[16,2,4,384]{3,2,1,0:T(4,128)S(1)}, f32[16,2,4,384]{3,2,1,0:T(4,128)S(1)}, u32[]{:S(2)}, u32[]{:S(2)}) %collective-permute-start.1) | collective-permute-done | bytes 196640 | tf_op jit(solution)/shard_map/ppermute | solution.py:40
  11.4 4.9 %first_local.1.tile_ref = f32[8,128]{1,0:T(8,128)S(1)} custom-call(f32[16,2,16,384]{3,2,1,0:T(8,128)S(1)} %copy-done.1, f32[16,2,4,384]{3,2,1,0:T(4,128)S(1)} %collective-permute-done.1.beside_ref, f32[2,16,384]{2,1,0:T(8,128)S(1)} %fusion.curvature_ref, f32[2,16,384]{2,1,0:T(8,128)S(1)} %copy-done.2), custom_call_target="tpu_custom_call" | custom-call | flops 100000000 | bytes 1085440 | tf_op jit(solution)/shard_map/first_local/pallas_call | solution.py:23
  16.9 3.0 %collective-permute-done.2.beyond_ref = f32[18,2,8,384]{3,2,1,0:T(8,128)S(1)} collective-permute-done((f32[18,2,8,384]{3,2,1,0:T(8,128)}, f32[18,2,8,384]{3,2,1,0:T(8,128)S(1)}, u32[]{:S(2)}, u32[]{:S(2)}) %collective-permute-start.2) | collective-permute-done | bytes 442400 | tf_op jit(solution)/shard_map/ppermute | solution.py:45
  19.9 2.4 %collective-permute-start.7 = (f32[17,8,384]{2,1,0:T(8,128)S(1)}, f32[17,8,384]{2,1,0:T(8,128)S(1)}, u32[]{:S(2)}, u32[]{:S(2)}) collective-permute-start(f32[17,8,384]{2,1,0:T(8,128)S(1)} %get-tuple-element.43), channel_id=1, source_target_pairs={{0,2},{2,0},{4,6},{6,4},{8,10},{10,8},{12,14},{14,12},{1,3},{3,1},... | collective-permute-start | bytes 626696 | tf_op jit(solution)/shard_map/ppermute | solution.py:36
  22.3 1.4 %first_across.1 = f32[8,128]{1,0:T(8,128)S(1)} custom-call(f32[18,2,8,384]{3,2,1,0:T(8,128)S(1)} %copy-done, f32[18,2,8,384]{3,2,1,0:T(8,128)S(1)} %collective-permute-done.theirs_ref, f32[18,2,8,384]{3,2,1,0:T(8,128)S(1)} %collective-permute-done.2.beyond_ref, f32[8,128]{1,0:T(8,128)S(1)} %first_local.1.tile_ref), custom_call_target="tpu_custom_call" | custom-call | flops 25000000 | bytes 1335296 | tf_op jit(solution)/shard_map/first_across/pallas_call | solution.py:23
  24.3 0.8 %collective-permute-done.3 = f32[8,128]{1,0:T(8,128)S(1)} collective-permute-done((f32[8,128]{1,0:T(8,128)S(1)}, f32[8,128]{1,0:T(8,128)S(1)}, u32[]{:S(2)}, u32[]{:S(2)}) %collective-permute-start.3) | collective-permute-done | bytes 4128 | tf_op jit(solution)/shard_map/ppermute | solution.py:60
  25.1 3.6 %collective-permute-done.4 = f32[8,128]{1,0:T(8,128)S(1)} collective-permute-done((f32[8,128]{1,0:T(8,128)S(1)}, f32[8,128]{1,0:T(8,128)S(1)}, u32[]{:S(2)}, u32[]{:S(2)}) %collective-permute-start.4) | collective-permute-done | bytes 4128 | tf_op jit(solution)/shard_map/ppermute | solution.py:60
  28.7 3.7 %collective-permute-done.5 = f32[8,128]{1,0:T(8,128)S(1)} collective-permute-done((f32[8,128]{1,0:T(8,128)S(1)}, f32[8,128]{1,0:T(8,128)S(1)}, u32[]{:S(2)}, u32[]{:S(2)}) %collective-permute-start.5) | collective-permute-done | bytes 4128 | tf_op jit(solution)/shard_map/ppermute | solution.py:60
  32.4 2.3 %collective-permute-start.9 = (f32[8,128]{1,0:T(8,128)S(1)}, f32[8,128]{1,0:T(8,128)S(1)}, u32[]{:S(2)}, u32[]{:S(2)}) collective-permute-start(f32[8,128]{1,0:T(8,128)S(1)} %add.30), channel_id=1, source_target_pairs={{0,8},{1,9},{2,10},{3,11},{4,12},{5,13},{6,14},{7,15},{8,0},{9,1},... | collective-permute-start | bytes 12296 | tf_op jit(solution)/shard_map/ppermute | solution.py:60
  34.7 3.0 %first_images.1 = (f32[16,4,8,384]{3,2,1,0:T(8,128)S(1)}, f32[4,8,384]{2,1,0:T(8,128)S(1)}, f32[4,8,384]{2,1,0:T(8,128)S(1)}, f32[6,8,384]{2,1,0:T(8,128)S(1)}, f32[4,24,384]{2,1,0:T(8,128)S(1)}) custom-call(f32[18,2,8,384]{3,2,1,0:T(8,128)S(1)} %copy-done, f32[18,2,8,384]{3,2,1,0:T(8,128)S(1)} %collective-permute-done.theirs_ref, ...), custom_call_target="tpu_custom_call" | custom-call | flops 6000000 | bytes 3293184 | tf_op jit(solution)/shard_map/first_images/pallas_call | solution.py:23
  37.7 4.9 %ritz_pairs.2 = (f32[8]{0:T(128)}, f32[8,128]{1,0:T(8,128)S(1)}, f32[8,16,128]{2,1,0:T(8,128)S(1)}) custom-call(f32[8,128]{1,0:T(8,128)S(1)} %add.31.pencil_ref), custom_call_target="tpu_custom_call" | custom-call | flops 10000000 | bytes 73760 | tf_op jit(solution)/shard_map/ritz_pairs/pallas_call | solution.py:23
  42.7 1.2 %update.1 = (f32[8,4,8,384]{3,2,1,0:T(8,128)S(1)}, f32[8,4,8,384]{3,2,1,0:T(8,128)S(1)}, f32[8,2,8,384]{3,2,1,0:T(8,128)S(1)}, f32[8,2,8,384]{3,2,1,0:T(8,128)S(...) custom-call(f32[8,16,128]{2,1,0:T(8,128)S(1)} %get-tuple-element.49.mix_ref, ...), custom_call_target="tpu_custom_call" | custom-call | flops 1000000 | bytes 3166208 | tf_op jit(solution)/shard_map/update/pallas_call | solution.py:23
  43.8 1.2 %collective-permute-start.10 = (f32[8,2,8,384]{3,2,1,0:T(8,128)S(1)}, f32[8,2,8,384]{3,2,1,0:T(8,128)S(1)}, u32[]{:S(2)}, u32[]{:S(2)}) collective-permute-start(f32[8,2,8,384]{3,2,1,0:T(8,128)S(1)} %get-tuple-element.56.near_ref.corrections_ref), channel_id=1, source_target_pairs={{4,0},{14,2},{8,4},{2,6},{12,8},{6,10},{0,12},{10,14},{5,1},{15,3}... | collective-permute-start | bytes 589832 | tf_op jit(solution)/shard_map/ppermute | solution.py:45
  45.1 1.1 %collective-permute-start.11 = (f32[8,8,384]{2,1,0:T(8,128)S(1)}, f32[8,8,384]{2,1,0:T(8,128)S(1)}, u32[]{:S(2)}, u32[]{:S(2)}) collective-permute-start(f32[8,8,384]{2,1,0:T(8,128)S(1)} %get-tuple-element.58), channel_id=1, source_target_pairs={{0,2},{2,0},{4,6},{6,4},{8,10},{10,8},{12,14},{14,12},{1,3},{3,1},... | collective-permute-start | bytes 294920 | tf_op jit(solution)/shard_map/ppermute | solution.py:36
  46.2 2.9 %second_local.1.tile_ref = f32[8,128]{1,0:T(8,128)S(1)} custom-call(f32[8,4,8,384]{3,2,1,0:T(8,128)S(1)} %get-tuple-element.60.modes_ref, f32[8,4,8,384]{3,2,1,0:T(8,128)S(1)} %get-tuple-element.61.images_ref.first_ref, f32[8,2,8,384]{3,2,1,0:T(8,128)S(1)} %get-tuple-element.56.near_ref.corrections_ref, ...), custom_call_target="tpu_custom_call" | custom-call | flops 80000000 | bytes 1306624 | tf_op jit(solution)/shard_map/second_local/pallas_call | solution.py:23
  49.8 1.4 %collective-permute-start.15 = (f32[8,2,8,384]{3,2,1,0:T(8,128)S(1)}, f32[8,2,8,384]{3,2,1,0:T(8,128)S(1)}, u32[]{:S(2)}, u32[]{:S(2)}) collective-permute-start(f32[8,2,8,384]{3,2,1,0:T(8,128)S(1)} %get-tuple-element.68.far_ref.corrections_ref), channel_id=1, source_target_pairs={{12,0},{6,2},{0,4},{10,6},{4,8},{14,10},{8,12},{2,14},{13,1},{7,3}... | collective-permute-start | bytes 589832 | tf_op jit(solution)/shard_map/ppermute | solution.py:50
  51.2 1.4 %second_across.1 = f32[8,128]{1,0:T(8,128)S(1)} custom-call(f32[8,2,8,384]{3,2,1,0:T(8,128)S(1)} %get-tuple-element.56.near_ref.corrections_ref, f32[8,2,8,384]{3,2,1,0:T(8,128)S(1)} %get-tuple-element.68.far_ref.corrections_ref, f32[8,2,8,384]{3,2,1,0:T(8,128)S(1)} %collective-permute-done.10.beyond_ref, f32[8,8,384]{2,1,0:T(8,128)S(1)} %collective-permute-done.11.pair_ref, ...), custom_call_target="tpu_custom_call" | custom-call | flops 25000000 | bytes 868352 | tf_op jit(solution)/shard_map/second_across/pallas_call | solution.py:23
  52.9 0.9 %collective-permute-done.13 = f32[8,128]{1,0:T(8,128)S(1)} collective-permute-done((f32[8,128]{1,0:T(8,128)S(1)}, f32[8,128]{1,0:T(8,128)S(1)}, u32[]{:S(2)}, u32[]{:S(2)}) %collective-permute-start.13) | collective-permute-done | bytes 4128 | tf_op jit(solution)/shard_map/ppermute | solution.py:60
  53.8 3.4 %collective-permute-start.14 = (f32[8,128]{1,0:T(8,128)S(1)}, f32[8,128]{1,0:T(8,128)S(1)}, u32[]{:S(2)}, u32[]{:S(2)}) collective-permute-start(f32[8,128]{1,0:T(8,128)S(1)} %add.32), channel_id=1, source_target_pairs={{0,2},{1,3},{2,0},{3,1},{4,6},{5,7},{6,4},{7,5},{8,10},{9,11},{10,... | collective-permute-start | bytes 12296 | tf_op jit(solution)/shard_map/ppermute | solution.py:60
  57.2 1.6 %collective-permute-done.14 = f32[8,128]{1,0:T(8,128)S(1)} collective-permute-done((f32[8,128]{1,0:T(8,128)S(1)}, f32[8,128]{1,0:T(8,128)S(1)}, u32[]{:S(2)}, u32[]{:S(2)}) %collective-permute-start.14) | collective-permute-done | bytes 4128 | tf_op jit(solution)/shard_map/ppermute | solution.py:60
  58.8 1.5 %collective-permute-start.18 = (f32[8,128]{1,0:T(8,128)S(1)}, f32[8,128]{1,0:T(8,128)S(1)}, u32[]{:S(2)}, u32[]{:S(2)}) collective-permute-start(f32[8,128]{1,0:T(8,128)S(1)} %add.33), channel_id=1, source_target_pairs={{0,12},{1,13},{2,14},{3,15},{4,8},{5,9},{6,10},{7,11},{8,4},{9,5},... | collective-permute-start | bytes 12296 | tf_op jit(solution)/shard_map/ppermute | solution.py:60
  60.3 1.1 %collective-permute-start.17 = (f32[8,128]{1,0:T(8,128)S(1)}, f32[8,128]{1,0:T(8,128)S(1)}, u32[]{:S(2)}, u32[]{:S(2)}) collective-permute-start(f32[8,128]{1,0:T(8,128)S(1)} %add.33), channel_id=1, source_target_pairs={{0,8},{1,9},{2,10},{3,11},{4,12},{5,13},{6,14},{7,15},{8,0},{9,1},... | collective-permute-start | bytes 12296 | tf_op jit(solution)/shard_map/ppermute | solution.py:60
  61.3 1.8 %collective-permute-start.16 = (f32[8,128]{1,0:T(8,128)S(1)}, f32[8,128]{1,0:T(8,128)S(1)}, u32[]{:S(2)}, u32[]{:S(2)}) collective-permute-start(f32[8,128]{1,0:T(8,128)S(1)} %add.33), channel_id=1, source_target_pairs={{0,4},{1,5},{2,6},{3,7},{4,0},{5,1},{6,2},{7,3},{8,12},{9,13},{10,... | collective-permute-start | bytes 12296 | tf_op jit(solution)/shard_map/ppermute | solution.py:60
  63.2 1.4 %images.1.second_ref = f32[8,4,8,384]{3,2,1,0:T(8,128)S(1)} custom-call(f32[8,2,8,384]{3,2,1,0:T(8,128)S(1)} %get-tuple-element.56.near_ref.corrections_ref, f32[8,2,8,384]{3,2,1,0:T(8,128)S(1)} %get-tuple-element.68.far_ref.corrections_ref, f32[8,2,8,384]{3,2,1,0:T(8,128)S(1)} %collective-permute-done.15.behind_ref, ...), custom_call_target="tpu_custom_call" | custom-call | flops 1000000 | bytes 1646592 | tf_op jit(solution)/shard_map/images/pallas_call | solution.py:23
  64.9 4.9 %ritz_pairs.3 = (f32[8]{0:T(128)}, f32[8,128]{1,0:T(8,128)S(1)}, f32[8,16,128]{2,1,0:T(8,128)S(1)}) custom-call(f32[8,128]{1,0:T(8,128)S(1)} %add_add_fusion.pencil_ref), custom_call_target="tpu_custom_call" | custom-call | flops 10000000 | bytes 73760 | tf_op jit(solution)/shard_map/ritz_pairs/pallas_call | solution.py:23
  70.4 2.1 %collective-permute-start.19 = (f32[2,2,8,384]{3,2,1,0:T(8,128)S(1)}, f32[2,2,8,384]{3,2,1,0:T(8,128)S(1)}, u32[]{:S(2)}, u32[]{:S(2)}) collective-permute-start(f32[2,2,8,384]{3,2,1,0:T(8,128)S(1)} %densities.3), channel_id=1, source_target_pairs={{0,2},{2,0},{4,6},{6,4},{8,10},{10,8},{12,14},{14,12},{1,3},{3,1},... | collective-permute-start | bytes 147464 | tf_op jit(solution)/shard_map/ppermute | solution.py:36
  73.0 1.6 %collective-permute-done.19.other_ref = f32[2,2,8,384]{3,2,1,0:T(8,128)S(1)} collective-permute-done((f32[2,2,8,384]{3,2,1,0:T(8,128)S(1)}, f32[2,2,8,384]{3,2,1,0:T(8,128)S(1)}, u32[]{:S(2)}, u32[]{:S(2)}) %collective-permute-start.19) | collective-permute-done | bytes 49184 | tf_op jit(solution)/shard_map/ppermute | solution.py:36
  74.5 0.7 merge.1
  (40 shorter events, 3.6 us)
Async XLA Ops:
  0.6 9.1 %copy-start.1 = (f32[16,2,16,384]{3,2,1,0:T(8,128)S(1)}, f32[16,2,16,384]{3,2,1,0:T(8,128)}, u32[]{:S(2)}) copy-start(f32[16,2,16,384]{3,2,1,0:T(8,128)} %block_ref.3) | copy-start | bytes 2359300
  3.1 13.4 %collective-permute-start = (f32[18,2,8,384]{3,2,1,0:T(8,128)}, f32[18,2,8,384]{3,2,1,0:T(8,128)S(1)}, u32[]{:S(2)}, u32[]{:S(2)}) collective-permute-start(f32[18,2,8,384]{3,2,1,0:T(8,128)} %get-tuple-element.41), channel_id=1, source_target_pairs={{0,2},{2,0},{4,6},{6,4},{8,10},{10,8},{12,14},{14,12},{1,3},{3,1},... | collective-permute-start | bytes 1327112 | tf_op jit(solution)/shard_map/ppermute | solution.py:36
  6.1 13.8 %collective-permute-start.2 = (f32[18,2,8,384]{3,2,1,0:T(8,128)}, f32[18,2,8,384]{3,2,1,0:T(8,128)S(1)}, u32[]{:S(2)}, u32[]{:S(2)}) collective-permute-start(f32[18,2,8,384]{3,2,1,0:T(8,128)} %get-tuple-element.40.mine_ref), channel_id=1, source_target_pairs={{4,0},{14,2},{8,4},{2,6},{12,8},{6,10},{0,12},{10,14},{5,1},{15,3}... | collective-permute-start | bytes 1327112 | tf_op jit(solution)/shard_map/ppermute | solution.py:45
  9.8 0.8 %copy-start.3 = (f32[2,16,384]{2,1,0:T(8,128)S(1)}, f32[2,16,384]{2,1,0:T(8,128)}, u32[]{:S(2)}) copy-start(f32[2,16,384]{2,1,0:T(8,128)} %concentration_ref.1) | copy-start | bytes 147460
  9.9 1.5 %copy-start.2 = (f32[2,16,384]{2,1,0:T(8,128)S(1)}, f32[2,16,384]{2,1,0:T(8,128)}, u32[]{:S(2)}) copy-start(f32[2,16,384]{2,1,0:T(8,128)} %stiffness_ref.3) | copy-start | bytes 147460
  9.9 1.5 %collective-permute-start.1 = (f32[16,2,4,384]{3,2,1,0:T(4,128)S(1)}, f32[16,2,4,384]{3,2,1,0:T(4,128)S(1)}, u32[]{:S(2)}, u32[]{:S(2)}) collective-permute-start(f32[16,2,4,384]{3,2,1,0:T(4,128)S(1)} %pad_maximum_fusion), channel_id=1, source_target_pairs={{0,1},{1,0},{2,3},{3,2},{4,5},{5,4},{6,7},{7,6},{8,9},{9,8},{10,11... | collective-permute-start | bytes 589832 | tf_op jit(solution)/shard_map/ppermute | solution.py:40
  10.6 5.9 %copy-start = (f32[18,2,8,384]{3,2,1,0:T(8,128)S(1)}, f32[18,2,8,384]{3,2,1,0:T(8,128)}, u32[]{:S(2)}) copy-start(f32[18,2,8,384]{3,2,1,0:T(8,128)} %get-tuple-element.40.mine_ref) | copy-start | bytes 1327108
  19.9 12.5 %collective-permute-start.6 = (f32[18,2,8,384]{3,2,1,0:T(8,128)S(1)}, f32[18,2,8,384]{3,2,1,0:T(8,128)S(1)}, u32[]{:S(2)}, u32[]{:S(2)}) collective-permute-start(f32[18,2,8,384]{3,2,1,0:T(8,128)S(1)} %collective-permute-done.theirs_ref), channel_id=1, source_target_pairs={{12,0},{6,2},{0,4},{10,6},{4,8},{14,10},{8,12},{2,14},{13,1},{7,3}... | collective-permute-start | bytes 1327112 | tf_op jit(solution)/shard_map/ppermute | solution.py:50
  19.9 12.5 %collective-permute-start.7 = (f32[17,8,384]{2,1,0:T(8,128)S(1)}, f32[17,8,384]{2,1,0:T(8,128)S(1)}, u32[]{:S(2)}, u32[]{:S(2)}) collective-permute-start(f32[17,8,384]{2,1,0:T(8,128)S(1)} %get-tuple-element.43), channel_id=1, source_target_pairs={{0,2},{2,0},{4,6},{6,4},{8,10},{10,8},{12,14},{14,12},{1,3},{3,1},... | collective-permute-start | bytes 626696 | tf_op jit(solution)/shard_map/ppermute | solution.py:36
  22.3 10.1 %collective-permute-start.8 = (f32[17,8,384]{2,1,0:T(8,128)S(1)}, f32[17,8,384]{2,1,0:T(8,128)S(1)}, u32[]{:S(2)}, u32[]{:S(2)}) collective-permute-start(f32[17,8,384]{2,1,0:T(8,128)S(1)} %get-tuple-element.44), channel_id=1, source_target_pairs={{0,1},{1,0},{2,3},{3,2},{4,5},{5,4},{6,7},{7,6},{8,9},{9,8},{10,11... | collective-permute-start | bytes 626696 | tf_op jit(solution)/shard_map/ppermute | solution.py:40
  23.8 1.3 %collective-permute-start.3 = (f32[8,128]{1,0:T(8,128)S(1)}, f32[8,128]{1,0:T(8,128)S(1)}, u32[]{:S(2)}, u32[]{:S(2)}) collective-permute-start(f32[8,128]{1,0:T(8,128)S(1)} %first_across.1), channel_id=1, source_target_pairs={{0,1},{1,0},{2,3},{3,2},{4,5},{5,4},{6,7},{7,6},{8,9},{9,8},{10,11... | collective-permute-start | bytes 12296 | tf_op jit(solution)/shard_map/ppermute | solution.py:60
  25.1 3.6 %collective-permute-start.4 = (f32[8,128]{1,0:T(8,128)S(1)}, f32[8,128]{1,0:T(8,128)S(1)}, u32[]{:S(2)}, u32[]{:S(2)}) collective-permute-start(f32[8,128]{1,0:T(8,128)S(1)} %add.28), channel_id=1, source_target_pairs={{0,2},{1,3},{2,0},{3,1},{4,6},{5,7},{6,4},{7,5},{8,10},{9,11},{10,... | collective-permute-start | bytes 12296 | tf_op jit(solution)/shard_map/ppermute | solution.py:60
  28.7 3.7 %collective-permute-start.5 = (f32[8,128]{1,0:T(8,128)S(1)}, f32[8,128]{1,0:T(8,128)S(1)}, u32[]{:S(2)}, u32[]{:S(2)}) collective-permute-start(f32[8,128]{1,0:T(8,128)S(1)} %add.29), channel_id=1, source_target_pairs={{0,4},{1,5},{2,6},{3,7},{4,0},{5,1},{6,2},{7,3},{8,12},{9,13},{10,... | collective-permute-start | bytes 12296 | tf_op jit(solution)/shard_map/ppermute | solution.py:60
  32.4 5.3 %collective-permute-start.9 = (f32[8,128]{1,0:T(8,128)S(1)}, f32[8,128]{1,0:T(8,128)S(1)}, u32[]{:S(2)}, u32[]{:S(2)}) collective-permute-start(f32[8,128]{1,0:T(8,128)S(1)} %add.30), channel_id=1, source_target_pairs={{0,8},{1,9},{2,10},{3,11},{4,12},{5,13},{6,14},{7,15},{8,0},{9,1},... | collective-permute-start | bytes 12296 | tf_op jit(solution)/shard_map/ppermute | solution.py:60
  43.8 5.9 %collective-permute-start.10 = (f32[8,2,8,384]{3,2,1,0:T(8,128)S(1)}, f32[8,2,8,384]{3,2,1,0:T(8,128)S(1)}, u32[]{:S(2)}, u32[]{:S(2)}) collective-permute-start(f32[8,2,8,384]{3,2,1,0:T(8,128)S(1)} %get-tuple-element.56.near_ref.corrections_ref), channel_id=1, source_target_pairs={{4,0},{14,2},{8,4},{2,6},{12,8},{6,10},{0,12},{10,14},{5,1},{15,3}... | collective-permute-start | bytes 589832 | tf_op jit(solution)/shard_map/ppermute | solution.py:45
  45.1 4.6 %collective-permute-start.11 = (f32[8,8,384]{2,1,0:T(8,128)S(1)}, f32[8,8,384]{2,1,0:T(8,128)S(1)}, u32[]{:S(2)}, u32[]{:S(2)}) collective-permute-start(f32[8,8,384]{2,1,0:T(8,128)S(1)} %get-tuple-element.58), channel_id=1, source_target_pairs={{0,2},{2,0},{4,6},{6,4},{8,10},{10,8},{12,14},{14,12},{1,3},{3,1},... | collective-permute-start | bytes 294920 | tf_op jit(solution)/shard_map/ppermute | solution.py:36
  46.2 3.5 %collective-permute-start.12 = (f32[8,8,384]{2,1,0:T(8,128)S(1)}, f32[8,8,384]{2,1,0:T(8,128)S(1)}, u32[]{:S(2)}, u32[]{:S(2)}) collective-permute-start(f32[8,8,384]{2,1,0:T(8,128)S(1)} %get-tuple-element.59), channel_id=1, source_target_pairs={{0,1},{1,0},{2,3},{3,2},{4,5},{5,4},{6,7},{7,6},{8,9},{9,8},{10,11... | collective-permute-start | bytes 294920 | tf_op jit(solution)/shard_map/ppermute | solution.py:40
  49.8 9.0 %collective-permute-start.15 = (f32[8,2,8,384]{3,2,1,0:T(8,128)S(1)}, f32[8,2,8,384]{3,2,1,0:T(8,128)S(1)}, u32[]{:S(2)}, u32[]{:S(2)}) collective-permute-start(f32[8,2,8,384]{3,2,1,0:T(8,128)S(1)} %get-tuple-element.68.far_ref.corrections_ref), channel_id=1, source_target_pairs={{12,0},{6,2},{0,4},{10,6},{4,8},{14,10},{8,12},{2,14},{13,1},{7,3}... | collective-permute-start | bytes 589832 | tf_op jit(solution)/shard_map/ppermute | solution.py:50
  52.6 1.2 %collective-permute-start.13 = (f32[8,128]{1,0:T(8,128)S(1)}, f32[8,128]{1,0:T(8,128)S(1)}, u32[]{:S(2)}, u32[]{:S(2)}) collective-permute-start(f32[8,128]{1,0:T(8,128)S(1)} %second_across.1), channel_id=1, source_target_pairs={{0,1},{1,0},{2,3},{3,2},{4,5},{5,4},{6,7},{7,6},{8,9},{9,8},{10,11... | collective-permute-start | bytes 12296 | tf_op jit(solution)/shard_map/ppermute | solution.py:60
  53.8 4.9 %collective-permute-start.14 = (f32[8,128]{1,0:T(8,128)S(1)}, f32[8,128]{1,0:T(8,128)S(1)}, u32[]{:S(2)}, u32[]{:S(2)}) collective-permute-start(f32[8,128]{1,0:T(8,128)S(1)} %add.32), channel_id=1, source_target_pairs={{0,2},{1,3},{2,0},{3,1},{4,6},{5,7},{6,4},{7,5},{8,10},{9,11},{10,... | collective-permute-start | bytes 12296 | tf_op jit(solution)/shard_map/ppermute | solution.py:60
  58.8 5.8 %collective-permute-start.18 = (f32[8,128]{1,0:T(8,128)S(1)}, f32[8,128]{1,0:T(8,128)S(1)}, u32[]{:S(2)}, u32[]{:S(2)}) collective-permute-start(f32[8,128]{1,0:T(8,128)S(1)} %add.33), channel_id=1, source_target_pairs={{0,12},{1,13},{2,14},{3,15},{4,8},{5,9},{6,10},{7,11},{8,4},{9,5},... | collective-permute-start | bytes 12296 | tf_op jit(solution)/shard_map/ppermute | solution.py:60
  60.3 4.5 %collective-permute-start.17 = (f32[8,128]{1,0:T(8,128)S(1)}, f32[8,128]{1,0:T(8,128)S(1)}, u32[]{:S(2)}, u32[]{:S(2)}) collective-permute-start(f32[8,128]{1,0:T(8,128)S(1)} %add.33), channel_id=1, source_target_pairs={{0,8},{1,9},{2,10},{3,11},{4,12},{5,13},{6,14},{7,15},{8,0},{9,1},... | collective-permute-start | bytes 12296 | tf_op jit(solution)/shard_map/ppermute | solution.py:60
  61.3 3.6 %collective-permute-start.16 = (f32[8,128]{1,0:T(8,128)S(1)}, f32[8,128]{1,0:T(8,128)S(1)}, u32[]{:S(2)}, u32[]{:S(2)}) collective-permute-start(f32[8,128]{1,0:T(8,128)S(1)} %add.33), channel_id=1, source_target_pairs={{0,4},{1,5},{2,6},{3,7},{4,0},{5,1},{6,2},{7,3},{8,12},{9,13},{10,... | collective-permute-start | bytes 12296 | tf_op jit(solution)/shard_map/ppermute | solution.py:60
  70.4 4.2 %collective-permute-start.19 = (f32[2,2,8,384]{3,2,1,0:T(8,128)S(1)}, f32[2,2,8,384]{3,2,1,0:T(8,128)S(1)}, u32[]{:S(2)}, u32[]{:S(2)}) collective-permute-start(f32[2,2,8,384]{3,2,1,0:T(8,128)S(1)} %densities.3), channel_id=1, source_target_pairs={{0,2},{2,0},{4,6},{6,4},{8,10},{10,8},{12,14},{14,12},{1,3},{3,1},... | collective-permute-start | bytes 147464 | tf_op jit(solution)/shard_map/ppermute | solution.py:36

commit v9 on v8

--- a/solution.py
+++ b/solution.py
@@ -11,7 +11,7 @@
 MODES = 8
 HALF = BLOCK // 2
 LANES = 128
-EARLY_SWEEPS = 4
+EARLY_SWEEPS = 5
 MAX_SWEEPS = 14
 HIGHEST = lax.Precision.HIGHEST
 VMEM = pl.BlockSpec(memory_space=pltpu.VMEM)

time: 75.4 us -> 76.8 us (1.019)
  Pallas kernels: 30.7 us -> 32.1 us
    pallas_call x13, Pallas kernels: 28.3 us -> 29.7 us  [call(): pl.pallas_call(kernel, out_shape=out_shape, in_specs=[VMEM] * len(args),...]
where the time goes in v9:
time: 76.8 us; the launch traced here: 76.6 us
  Pallas kernels  32.1 us (42%)
  starting transfers between devices  25.8 us (34%)
  waiting for transfers between devices  17 us (22%)
  between operations  0.78 us (1%)
    pallas_call x13, Pallas kernels, call(): pl.pallas_call(kernel, out_shape=out_shape, in_specs=[VMEM] * len(args),...  29.7 us
    ppermute x9, waiting for transfers between devices, other(): return lax.ppermute(x, axes, [(i, i ^ mask) for i in range(total)])  10.9 us
    ppermute x9, starting transfers between devices, other(): return lax.ppermute(x, axes, [(i, i ^ mask) for i in range(total)])  10.8 us
    ppermute x4, starting transfers between devices, pair_swap(): lax.ppermute(x, 'gz', [(i, i ^ 1) for i in range(lax.axis_size('gz'))])  8.65 us
    ppermute x2, starting transfers between devices, from_beyond(): lax.ppermute(x, 'gz', [((i + (2 if i % 2 == 0 else size - 2)) % size, i)...  4.85 us
    ppermute x2, waiting for transfers between devices, from_beyond(): lax.ppermute(x, 'gz', [((i + (2 if i % 2 == 0 else size - 2)) % size, i)...  3 us
    pallas_call x1, Pallas kernels, prepare(): pl.pallas_call(prepare_kernel, out_shape=(shape, shape), in_specs=[pl.Blo...  2.41 us
    ppermute x4, waiting for transfers between devices, pair_swap(): lax.ppermute(x, 'gz', [(i, i ^ 1) for i in range(lax.axis_size('gz'))])  2.29 us
  transfers between devices with their start and end apart: 20, of which 12 were waited for; matrix products, arithmetic and copies ran while one was open for 0% of the time, Pallas kernels for 21%

profile of v9, /device:TPU:0, one launch (start us, length us, event | category | flops | bytes accessed | tf_op | source)
XLA Modules:
  0.0 76.6 jit_solution(14250926455748962469)
XLA Ops:
  0.6 2.4 %prepare.1 = (f32[18,2,8,384]{3,2,1,0:T(8,128)}, f32[18,2,8,384]{3,2,1,0:T(8,128)}) custom-call(f32[16,2,16,384]{3,2,1,0:T(8,128)} %block_ref.3, f32[2,16,384]{2,1,0:T(8,128)} %stiffness_ref.3, f32[2,16,384]{2,1,0:T(8,128)} %concentration_ref.1), custom_call_target="tpu_custom_call" | custom-call | tf_op jit(solution)/shard_map/prepare/pallas_call | solution.py:360
  3.1 3.0 %collective-permute-start = (f32[18,2,8,384]{3,2,1,0:T(8,128)}, f32[18,2,8,384]{3,2,1,0:T(8,128)S(1)}, u32[]{:S(2)}, u32[]{:S(2)}) collective-permute-start(f32[18,2,8,384]{3,2,1,0:T(8,128)} %get-tuple-element.41), channel_id=1, source_target_pairs={{0,2},{2,0},{4,6},{6,4},{8,10},{10,8},{12,14},{14,12},{1,3},{3,1},... | collective-permute-start | bytes 1327112 | tf_op jit(solution)/shard_map/ppermute | solution.py:36
  6.1 3.6 %collective-permute-start.2 = (f32[18,2,8,384]{3,2,1,0:T(8,128)}, f32[18,2,8,384]{3,2,1,0:T(8,128)S(1)}, u32[]{:S(2)}, u32[]{:S(2)}) collective-permute-start(f32[18,2,8,384]{3,2,1,0:T(8,128)} %get-tuple-element.40.mine_ref), channel_id=1, source_target_pairs={{4,0},{14,2},{8,4},{2,6},{12,8},{6,10},{0,12},{10,14},{5,1},{15,3}... | collective-permute-start | bytes 1327112 | tf_op jit(solution)/shard_map/ppermute | solution.py:45
  10.0 0.6 copy-done.3
  10.6 0.8 %collective-permute-done.1.beside_ref = f32[16,2,4,384]{3,2,1,0:T(4,128)S(1)} collective-permute-done((f32[16,2,4,384]{3,2,1,0:T(4,128)S(1)}, f32[16,2,4,384]{3,2,1,0:T(4,128)S(1)}, u32[]{:S(2)}, u32[]{:S(2)}) %collective-permute-start.1) | collective-permute-done | bytes 196640 | tf_op jit(solution)/shard_map/ppermute | solution.py:40
  11.4 4.9 %first_local.1.tile_ref = f32[8,128]{1,0:T(8,128)S(1)} custom-call(f32[16,2,16,384]{3,2,1,0:T(8,128)S(1)} %copy-done.1, f32[16,2,4,384]{3,2,1,0:T(4,128)S(1)} %collective-permute-done.1.beside_ref, f32[2,16,384]{2,1,0:T(8,128)S(1)} %fusion.curvature_ref, f32[2,16,384]{2,1,0:T(8,128)S(1)} %copy-done.2), custom_call_target="tpu_custom_call" | custom-call | flops 100000000 | bytes 1085440 | tf_op jit(solution)/shard_map/first_local/pallas_call | solution.py:23
  16.9 3.0 %collective-permute-done.2.beyond_ref = f32[18,2,8,384]{3,2,1,0:T(8,128)S(1)} collective-permute-done((f32[18,2,8,384]{3,2,1,0:T(8,128)}, f32[18,2,8,384]{3,2,1,0:T(8,128)S(1)}, u32[]{:S(2)}, u32[]{:S(2)}) %collective-permute-start.2) | collective-permute-done | bytes 442400 | tf_op jit(solution)/shard_map/ppermute | solution.py:45
  19.9 2.4 %collective-permute-start.7 = (f32[17,8,384]{2,1,0:T(8,128)S(1)}, f32[17,8,384]{2,1,0:T(8,128)S(1)}, u32[]{:S(2)}, u32[]{:S(2)}) collective-permute-start(f32[17,8,384]{2,1,0:T(8,128)S(1)} %get-tuple-element.43), channel_id=1, source_target_pairs={{0,2},{2,0},{4,6},{6,4},{8,10},{10,8},{12,14},{14,12},{1,3},{3,1},... | collective-permute-start | bytes 626696 | tf_op jit(solution)/shard_map/ppermute | solution.py:36
  22.3 1.4 %first_across.1 = f32[8,128]{1,0:T(8,128)S(1)} custom-call(f32[18,2,8,384]{3,2,1,0:T(8,128)S(1)} %copy-done, f32[18,2,8,384]{3,2,1,0:T(8,128)S(1)} %collective-permute-done.theirs_ref, f32[18,2,8,384]{3,2,1,0:T(8,128)S(1)} %collective-permute-done.2.beyond_ref, f32[8,128]{1,0:T(8,128)S(1)} %first_local.1.tile_ref), custom_call_target="tpu_custom_call" | custom-call | flops 25000000 | bytes 1335296 | tf_op jit(solution)/shard_map/first_across/pallas_call | solution.py:23
  24.3 0.8 %collective-permute-done.3 = f32[8,128]{1,0:T(8,128)S(1)} collective-permute-done((f32[8,128]{1,0:T(8,128)S(1)}, f32[8,128]{1,0:T(8,128)S(1)}, u32[]{:S(2)}, u32[]{:S(2)}) %collective-permute-start.3) | collective-permute-done | bytes 4128 | tf_op jit(solution)/shard_map/ppermute | solution.py:60
  25.1 3.6 %collective-permute-done.4 = f32[8,128]{1,0:T(8,128)S(1)} collective-permute-done((f32[8,128]{1,0:T(8,128)S(1)}, f32[8,128]{1,0:T(8,128)S(1)}, u32[]{:S(2)}, u32[]{:S(2)}) %collective-permute-start.4) | collective-permute-done | bytes 4128 | tf_op jit(solution)/shard_map/ppermute | solution.py:60
  28.7 3.7 %collective-permute-done.5 = f32[8,128]{1,0:T(8,128)S(1)} collective-permute-done((f32[8,128]{1,0:T(8,128)S(1)}, f32[8,128]{1,0:T(8,128)S(1)}, u32[]{:S(2)}, u32[]{:S(2)}) %collective-permute-start.5) | collective-permute-done | bytes 4128 | tf_op jit(solution)/shard_map/ppermute | solution.py:60
  32.4 2.3 %collective-permute-start.9 = (f32[8,128]{1,0:T(8,128)S(1)}, f32[8,128]{1,0:T(8,128)S(1)}, u32[]{:S(2)}, u32[]{:S(2)}) collective-permute-start(f32[8,128]{1,0:T(8,128)S(1)} %add.30), channel_id=1, source_target_pairs={{0,8},{1,9},{2,10},{3,11},{4,12},{5,13},{6,14},{7,15},{8,0},{9,1},... | collective-permute-start | bytes 12296 | tf_op jit(solution)/shard_map/ppermute | solution.py:60
  34.7 3.0 %first_images.1 = (f32[16,4,8,384]{3,2,1,0:T(8,128)S(1)}, f32[4,8,384]{2,1,0:T(8,128)S(1)}, f32[4,8,384]{2,1,0:T(8,128)S(1)}, f32[6,8,384]{2,1,0:T(8,128)S(1)}, f32[4,24,384]{2,1,0:T(8,128)S(1)}) custom-call(f32[18,2,8,384]{3,2,1,0:T(8,128)S(1)} %copy-done, f32[18,2,8,384]{3,2,1,0:T(8,128)S(1)} %collective-permute-done.theirs_ref, ...), custom_call_target="tpu_custom_call" | custom-call | flops 6000000 | bytes 3293184 | tf_op jit(solution)/shard_map/first_images/pallas_call | solution.py:23
  37.7 5.7 %ritz_pairs.2 = (f32[8]{0:T(128)}, f32[8,128]{1,0:T(8,128)S(1)}, f32[8,16,128]{2,1,0:T(8,128)S(1)}) custom-call(f32[8,128]{1,0:T(8,128)S(1)} %add.31.pencil_ref), custom_call_target="tpu_custom_call" | custom-call | flops 10000000 | bytes 73760 | tf_op jit(solution)/shard_map/ritz_pairs/pallas_call | solution.py:23
  43.4 1.2 %update.1 = (f32[8,4,8,384]{3,2,1,0:T(8,128)S(1)}, f32[8,4,8,384]{3,2,1,0:T(8,128)S(1)}, f32[8,2,8,384]{3,2,1,0:T(8,128)S(1)}, f32[8,2,8,384]{3,2,1,0:T(8,128)S(...) custom-call(f32[8,16,128]{2,1,0:T(8,128)S(1)} %get-tuple-element.49.mix_ref, ...), custom_call_target="tpu_custom_call" | custom-call | flops 1000000 | bytes 3166208 | tf_op jit(solution)/shard_map/update/pallas_call | solution.py:23
  44.6 1.2 %collective-permute-start.10 = (f32[8,2,8,384]{3,2,1,0:T(8,128)S(1)}, f32[8,2,8,384]{3,2,1,0:T(8,128)S(1)}, u32[]{:S(2)}, u32[]{:S(2)}) collective-permute-start(f32[8,2,8,384]{3,2,1,0:T(8,128)S(1)} %get-tuple-element.56.near_ref.corrections_ref), channel_id=1, source_target_pairs={{4,0},{14,2},{8,4},{2,6},{12,8},{6,10},{0,12},{10,14},{5,1},{15,3}... | collective-permute-start | bytes 589832 | tf_op jit(solution)/shard_map/ppermute | solution.py:45
  45.8 1.1 %collective-permute-start.11 = (f32[8,8,384]{2,1,0:T(8,128)S(1)}, f32[8,8,384]{2,1,0:T(8,128)S(1)}, u32[]{:S(2)}, u32[]{:S(2)}) collective-permute-start(f32[8,8,384]{2,1,0:T(8,128)S(1)} %get-tuple-element.58), channel_id=1, source_target_pairs={{0,2},{2,0},{4,6},{6,4},{8,10},{10,8},{12,14},{14,12},{1,3},{3,1},... | collective-permute-start | bytes 294920 | tf_op jit(solution)/shard_map/ppermute | solution.py:36
  46.9 2.9 %second_local.1.tile_ref = f32[8,128]{1,0:T(8,128)S(1)} custom-call(f32[8,4,8,384]{3,2,1,0:T(8,128)S(1)} %get-tuple-element.60.modes_ref, f32[8,4,8,384]{3,2,1,0:T(8,128)S(1)} %get-tuple-element.61.images_ref.first_ref, f32[8,2,8,384]{3,2,1,0:T(8,128)S(1)} %get-tuple-element.56.near_ref.corrections_ref, ...), custom_call_target="tpu_custom_call" | custom-call | flops 80000000 | bytes 1306624 | tf_op jit(solution)/shard_map/second_local/pallas_call | solution.py:23
  50.5 1.4 %collective-permute-start.15 = (f32[8,2,8,384]{3,2,1,0:T(8,128)S(1)}, f32[8,2,8,384]{3,2,1,0:T(8,128)S(1)}, u32[]{:S(2)}, u32[]{:S(2)}) collective-permute-start(f32[8,2,8,384]{3,2,1,0:T(8,128)S(1)} %get-tuple-element.68.far_ref.corrections_ref), channel_id=1, source_target_pairs={{12,0},{6,2},{0,4},{10,6},{4,8},{14,10},{8,12},{2,14},{13,1},{7,3}... | collective-permute-start | bytes 589832 | tf_op jit(solution)/shard_map/ppermute | solution.py:50
  51.9 1.4 %second_across.1 = f32[8,128]{1,0:T(8,128)S(1)} custom-call(f32[8,2,8,384]{3,2,1,0:T(8,128)S(1)} %get-tuple-element.56.near_ref.corrections_ref, f32[8,2,8,384]{3,2,1,0:T(8,128)S(1)} %get-tuple-element.68.far_ref.corrections_ref, f32[8,2,8,384]{3,2,1,0:T(8,128)S(1)} %collective-permute-done.10.beyond_ref, f32[8,8,384]{2,1,0:T(8,128)S(1)} %collective-permute-done.11.pair_ref, ...), custom_call_target="tpu_custom_call" | custom-call | flops 25000000 | bytes 868352 | tf_op jit(solution)/shard_map/second_across/pallas_call | solution.py:23
  53.6 0.9 %collective-permute-done.13 = f32[8,128]{1,0:T(8,128)S(1)} collective-permute-done((f32[8,128]{1,0:T(8,128)S(1)}, f32[8,128]{1,0:T(8,128)S(1)}, u32[]{:S(2)}, u32[]{:S(2)}) %collective-permute-start.13) | collective-permute-done | bytes 4128 | tf_op jit(solution)/shard_map/ppermute | solution.py:60
  54.6 3.4 %collective-permute-start.14 = (f32[8,128]{1,0:T(8,128)S(1)}, f32[8,128]{1,0:T(8,128)S(1)}, u32[]{:S(2)}, u32[]{:S(2)}) collective-permute-start(f32[8,128]{1,0:T(8,128)S(1)} %add.32), channel_id=1, source_target_pairs={{0,2},{1,3},{2,0},{3,1},{4,6},{5,7},{6,4},{7,5},{8,10},{9,11},{10,... | collective-permute-start | bytes 12296 | tf_op jit(solution)/shard_map/ppermute | solution.py:60
  57.9 1.6 %collective-permute-done.14 = f32[8,128]{1,0:T(8,128)S(1)} collective-permute-done((f32[8,128]{1,0:T(8,128)S(1)}, f32[8,128]{1,0:T(8,128)S(1)}, u32[]{:S(2)}, u32[]{:S(2)}) %collective-permute-start.14) | collective-permute-done | bytes 4128 | tf_op jit(solution)/shard_map/ppermute | solution.py:60
  59.5 1.5 %collective-permute-start.18 = (f32[8,128]{1,0:T(8,128)S(1)}, f32[8,128]{1,0:T(8,128)S(1)}, u32[]{:S(2)}, u32[]{:S(2)}) collective-permute-start(f32[8,128]{1,0:T(8,128)S(1)} %add.33), channel_id=1, source_target_pairs={{0,12},{1,13},{2,14},{3,15},{4,8},{5,9},{6,10},{7,11},{8,4},{9,5},... | collective-permute-start | bytes 12296 | tf_op jit(solution)/shard_map/ppermute | solution.py:60
  61.0 1.1 %collective-permute-start.17 = (f32[8,128]{1,0:T(8,128)S(1)}, f32[8,128]{1,0:T(8,128)S(1)}, u32[]{:S(2)}, u32[]{:S(2)}) collective-permute-start(f32[8,128]{1,0:T(8,128)S(1)} %add.33), channel_id=1, source_target_pairs={{0,8},{1,9},{2,10},{3,11},{4,12},{5,13},{6,14},{7,15},{8,0},{9,1},... | collective-permute-start | bytes 12296 | tf_op jit(solution)/shard_map/ppermute | solution.py:60
  62.0 1.8 %collective-permute-start.16 = (f32[8,128]{1,0:T(8,128)S(1)}, f32[8,128]{1,0:T(8,128)S(1)}, u32[]{:S(2)}, u32[]{:S(2)}) collective-permute-start(f32[8,128]{1,0:T(8,128)S(1)} %add.33), channel_id=1, source_target_pairs={{0,4},{1,5},{2,6},{3,7},{4,0},{5,1},{6,2},{7,3},{8,12},{9,13},{10,... | collective-permute-start | bytes 12296 | tf_op jit(solution)/shard_map/ppermute | solution.py:60
  63.9 1.4 %images.1.second_ref = f32[8,4,8,384]{3,2,1,0:T(8,128)S(1)} custom-call(f32[8,2,8,384]{3,2,1,0:T(8,128)S(1)} %get-tuple-element.56.near_ref.corrections_ref, f32[8,2,8,384]{3,2,1,0:T(8,128)S(1)} %get-tuple-element.68.far_ref.corrections_ref, f32[8,2,8,384]{3,2,1,0:T(8,128)S(1)} %collective-permute-done.15.behind_ref, ...), custom_call_target="tpu_custom_call" | custom-call | flops 1000000 | bytes 1646592 | tf_op jit(solution)/shard_map/images/pallas_call | solution.py:23
  65.7 5.7 %ritz_pairs.3 = (f32[8]{0:T(128)}, f32[8,128]{1,0:T(8,128)S(1)}, f32[8,16,128]{2,1,0:T(8,128)S(1)}) custom-call(f32[8,128]{1,0:T(8,128)S(1)} %add_add_fusion.pencil_ref), custom_call_target="tpu_custom_call" | custom-call | flops 10000000 | bytes 73760 | tf_op jit(solution)/shard_map/ritz_pairs/pallas_call | solution.py:23
  71.8 2.1 %collective-permute-start.19 = (f32[2,2,8,384]{3,2,1,0:T(8,128)S(1)}, f32[2,2,8,384]{3,2,1,0:T(8,128)S(1)}, u32[]{:S(2)}, u32[]{:S(2)}) collective-permute-start(f32[2,2,8,384]{3,2,1,0:T(8,128)S(1)} %densities.3), channel_id=1, source_target_pairs={{0,2},{2,0},{4,6},{6,4},{8,10},{10,8},{12,14},{14,12},{1,3},{3,1},... | collective-permute-start | bytes 147464 | tf_op jit(solution)/shard_map/ppermute | solution.py:36
  74.4 1.6 %collective-permute-done.19.other_ref = f32[2,2,8,384]{3,2,1,0:T(8,128)S(1)} collective-permute-done((f32[2,2,8,384]{3,2,1,0:T(8,128)S(1)}, f32[2,2,8,384]{3,2,1,0:T(8,128)S(1)}, u32[]{:S(2)}, u32[]{:S(2)}) %collective-permute-start.19) | collective-permute-done | bytes 49184 | tf_op jit(solution)/shard_map/ppermute | solution.py:36
  76.0 0.7 merge.1
  (40 shorter events, 3.6 us)
Async XLA Ops:
  0.6 9.1 %copy-start.1 = (f32[16,2,16,384]{3,2,1,0:T(8,128)S(1)}, f32[16,2,16,384]{3,2,1,0:T(8,128)}, u32[]{:S(2)}) copy-start(f32[16,2,16,384]{3,2,1,0:T(8,128)} %block_ref.3) | copy-start | bytes 2359300
  3.1 13.4 %collective-permute-start = (f32[18,2,8,384]{3,2,1,0:T(8,128)}, f32[18,2,8,384]{3,2,1,0:T(8,128)S(1)}, u32[]{:S(2)}, u32[]{:S(2)}) collective-permute-start(f32[18,2,8,384]{3,2,1,0:T(8,128)} %get-tuple-element.41), channel_id=1, source_target_pairs={{0,2},{2,0},{4,6},{6,4},{8,10},{10,8},{12,14},{14,12},{1,3},{3,1},... | collective-permute-start | bytes 1327112 | tf_op jit(solution)/shard_map/ppermute | solution.py:36
  6.1 13.8 %collective-permute-start.2 = (f32[18,2,8,384]{3,2,1,0:T(8,128)}, f32[18,2,8,384]{3,2,1,0:T(8,128)S(1)}, u32[]{:S(2)}, u32[]{:S(2)}) collective-permute-start(f32[18,2,8,384]{3,2,1,0:T(8,128)} %get-tuple-element.40.mine_ref), channel_id=1, source_target_pairs={{4,0},{14,2},{8,4},{2,6},{12,8},{6,10},{0,12},{10,14},{5,1},{15,3}... | collective-permute-start | bytes 1327112 | tf_op jit(solution)/shard_map/ppermute | solution.py:45
  9.8 0.8 %copy-start.3 = (f32[2,16,384]{2,1,0:T(8,128)S(1)}, f32[2,16,384]{2,1,0:T(8,128)}, u32[]{:S(2)}) copy-start(f32[2,16,384]{2,1,0:T(8,128)} %concentration_ref.1) | copy-start | bytes 147460
  9.9 1.5 %copy-start.2 = (f32[2,16,384]{2,1,0:T(8,128)S(1)}, f32[2,16,384]{2,1,0:T(8,128)}, u32[]{:S(2)}) copy-start(f32[2,16,384]{2,1,0:T(8,128)} %stiffness_ref.3) | copy-start | bytes 147460
  9.9 1.5 %collective-permute-start.1 = (f32[16,2,4,384]{3,2,1,0:T(4,128)S(1)}, f32[16,2,4,384]{3,2,1,0:T(4,128)S(1)}, u32[]{:S(2)}, u32[]{:S(2)}) collective-permute-start(f32[16,2,4,384]{3,2,1,0:T(4,128)S(1)} %pad_maximum_fusion), channel_id=1, source_target_pairs={{0,1},{1,0},{2,3},{3,2},{4,5},{5,4},{6,7},{7,6},{8,9},{9,8},{10,11... | collective-permute-start | bytes 589832 | tf_op jit(solution)/shard_map/ppermute | solution.py:40
  10.6 5.9 %copy-start = (f32[18,2,8,384]{3,2,1,0:T(8,128)S(1)}, f32[18,2,8,384]{3,2,1,0:T(8,128)}, u32[]{:S(2)}) copy-start(f32[18,2,8,384]{3,2,1,0:T(8,128)} %get-tuple-element.40.mine_ref) | copy-start | bytes 1327108
  19.9 12.5 %collective-permute-start.6 = (f32[18,2,8,384]{3,2,1,0:T(8,128)S(1)}, f32[18,2,8,384]{3,2,1,0:T(8,128)S(1)}, u32[]{:S(2)}, u32[]{:S(2)}) collective-permute-start(f32[18,2,8,384]{3,2,1,0:T(8,128)S(1)} %collective-permute-done.theirs_ref), channel_id=1, source_target_pairs={{12,0},{6,2},{0,4},{10,6},{4,8},{14,10},{8,12},{2,14},{13,1},{7,3}... | collective-permute-start | bytes 1327112 | tf_op jit(solution)/shard_map/ppermute | solution.py:50
  19.9 12.5 %collective-permute-start.7 = (f32[17,8,384]{2,1,0:T(8,128)S(1)}, f32[17,8,384]{2,1,0:T(8,128)S(1)}, u32[]{:S(2)}, u32[]{:S(2)}) collective-permute-start(f32[17,8,384]{2,1,0:T(8,128)S(1)} %get-tuple-element.43), channel_id=1, source_target_pairs={{0,2},{2,0},{4,6},{6,4},{8,10},{10,8},{12,14},{14,12},{1,3},{3,1},... | collective-permute-start | bytes 626696 | tf_op jit(solution)/shard_map/ppermute | solution.py:36
  22.3 10.1 %collective-permute-start.8 = (f32[17,8,384]{2,1,0:T(8,128)S(1)}, f32[17,8,384]{2,1,0:T(8,128)S(1)}, u32[]{:S(2)}, u32[]{:S(2)}) collective-permute-start(f32[17,8,384]{2,1,0:T(8,128)S(1)} %get-tuple-element.44), channel_id=1, source_target_pairs={{0,1},{1,0},{2,3},{3,2},{4,5},{5,4},{6,7},{7,6},{8,9},{9,8},{10,11... | collective-permute-start | bytes 626696 | tf_op jit(solution)/shard_map/ppermute | solution.py:40
  23.8 1.3 %collective-permute-start.3 = (f32[8,128]{1,0:T(8,128)S(1)}, f32[8,128]{1,0:T(8,128)S(1)}, u32[]{:S(2)}, u32[]{:S(2)}) collective-permute-start(f32[8,128]{1,0:T(8,128)S(1)} %first_across.1), channel_id=1, source_target_pairs={{0,1},{1,0},{2,3},{3,2},{4,5},{5,4},{6,7},{7,6},{8,9},{9,8},{10,11... | collective-permute-start | bytes 12296 | tf_op jit(solution)/shard_map/ppermute | solution.py:60
  25.1 3.6 %collective-permute-start.4 = (f32[8,128]{1,0:T(8,128)S(1)}, f32[8,128]{1,0:T(8,128)S(1)}, u32[]{:S(2)}, u32[]{:S(2)}) collective-permute-start(f32[8,128]{1,0:T(8,128)S(1)} %add.28), channel_id=1, source_target_pairs={{0,2},{1,3},{2,0},{3,1},{4,6},{5,7},{6,4},{7,5},{8,10},{9,11},{10,... | collective-permute-start | bytes 12296 | tf_op jit(solution)/shard_map/ppermute | solution.py:60
  28.7 3.7 %collective-permute-start.5 = (f32[8,128]{1,0:T(8,128)S(1)}, f32[8,128]{1,0:T(8,128)S(1)}, u32[]{:S(2)}, u32[]{:S(2)}) collective-permute-start(f32[8,128]{1,0:T(8,128)S(1)} %add.29), channel_id=1, source_target_pairs={{0,4},{1,5},{2,6},{3,7},{4,0},{5,1},{6,2},{7,3},{8,12},{9,13},{10,... | collective-permute-start | bytes 12296 | tf_op jit(solution)/shard_map/ppermute | solution.py:60
  32.4 5.3 %collective-permute-start.9 = (f32[8,128]{1,0:T(8,128)S(1)}, f32[8,128]{1,0:T(8,128)S(1)}, u32[]{:S(2)}, u32[]{:S(2)}) collective-permute-start(f32[8,128]{1,0:T(8,128)S(1)} %add.30), channel_id=1, source_target_pairs={{0,8},{1,9},{2,10},{3,11},{4,12},{5,13},{6,14},{7,15},{8,0},{9,1},... | collective-permute-start | bytes 12296 | tf_op jit(solution)/shard_map/ppermute | solution.py:60
  44.6 5.9 %collective-permute-start.10 = (f32[8,2,8,384]{3,2,1,0:T(8,128)S(1)}, f32[8,2,8,384]{3,2,1,0:T(8,128)S(1)}, u32[]{:S(2)}, u32[]{:S(2)}) collective-permute-start(f32[8,2,8,384]{3,2,1,0:T(8,128)S(1)} %get-tuple-element.56.near_ref.corrections_ref), channel_id=1, source_target_pairs={{4,0},{14,2},{8,4},{2,6},{12,8},{6,10},{0,12},{10,14},{5,1},{15,3}... | collective-permute-start | bytes 589832 | tf_op jit(solution)/shard_map/ppermute | solution.py:45
  45.8 4.6 %collective-permute-start.11 = (f32[8,8,384]{2,1,0:T(8,128)S(1)}, f32[8,8,384]{2,1,0:T(8,128)S(1)}, u32[]{:S(2)}, u32[]{:S(2)}) collective-permute-start(f32[8,8,384]{2,1,0:T(8,128)S(1)} %get-tuple-element.58), channel_id=1, source_target_pairs={{0,2},{2,0},{4,6},{6,4},{8,10},{10,8},{12,14},{14,12},{1,3},{3,1},... | collective-permute-start | bytes 294920 | tf_op jit(solution)/shard_map/ppermute | solution.py:36
  46.9 3.5 %collective-permute-start.12 = (f32[8,8,384]{2,1,0:T(8,128)S(1)}, f32[8,8,384]{2,1,0:T(8,128)S(1)}, u32[]{:S(2)}, u32[]{:S(2)}) collective-permute-start(f32[8,8,384]{2,1,0:T(8,128)S(1)} %get-tuple-element.59), channel_id=1, source_target_pairs={{0,1},{1,0},{2,3},{3,2},{4,5},{5,4},{6,7},{7,6},{8,9},{9,8},{10,11... | collective-permute-start | bytes 294920 | tf_op jit(solution)/shard_map/ppermute | solution.py:40
  50.5 9.0 %collective-permute-start.15 = (f32[8,2,8,384]{3,2,1,0:T(8,128)S(1)}, f32[8,2,8,384]{3,2,1,0:T(8,128)S(1)}, u32[]{:S(2)}, u32[]{:S(2)}) collective-permute-start(f32[8,2,8,384]{3,2,1,0:T(8,128)S(1)} %get-tuple-element.68.far_ref.corrections_ref), channel_id=1, source_target_pairs={{12,0},{6,2},{0,4},{10,6},{4,8},{14,10},{8,12},{2,14},{13,1},{7,3}... | collective-permute-start | bytes 589832 | tf_op jit(solution)/shard_map/ppermute | solution.py:50
  53.4 1.2 %collective-permute-start.13 = (f32[8,128]{1,0:T(8,128)S(1)}, f32[8,128]{1,0:T(8,128)S(1)}, u32[]{:S(2)}, u32[]{:S(2)}) collective-permute-start(f32[8,128]{1,0:T(8,128)S(1)} %second_across.1), channel_id=1, source_target_pairs={{0,1},{1,0},{2,3},{3,2},{4,5},{5,4},{6,7},{7,6},{8,9},{9,8},{10,11... | collective-permute-start | bytes 12296 | tf_op jit(solution)/shard_map/ppermute | solution.py:60
  54.6 4.9 %collective-permute-start.14 = (f32[8,128]{1,0:T(8,128)S(1)}, f32[8,128]{1,0:T(8,128)S(1)}, u32[]{:S(2)}, u32[]{:S(2)}) collective-permute-start(f32[8,128]{1,0:T(8,128)S(1)} %add.32), channel_id=1, source_target_pairs={{0,2},{1,3},{2,0},{3,1},{4,6},{5,7},{6,4},{7,5},{8,10},{9,11},{10,... | collective-permute-start | bytes 12296 | tf_op jit(solution)/shard_map/ppermute | solution.py:60
  59.5 5.8 %collective-permute-start.18 = (f32[8,128]{1,0:T(8,128)S(1)}, f32[8,128]{1,0:T(8,128)S(1)}, u32[]{:S(2)}, u32[]{:S(2)}) collective-permute-start(f32[8,128]{1,0:T(8,128)S(1)} %add.33), channel_id=1, source_target_pairs={{0,12},{1,13},{2,14},{3,15},{4,8},{5,9},{6,10},{7,11},{8,4},{9,5},... | collective-permute-start | bytes 12296 | tf_op jit(solution)/shard_map/ppermute | solution.py:60
  61.0 4.5 %collective-permute-start.17 = (f32[8,128]{1,0:T(8,128)S(1)}, f32[8,128]{1,0:T(8,128)S(1)}, u32[]{:S(2)}, u32[]{:S(2)}) collective-permute-start(f32[8,128]{1,0:T(8,128)S(1)} %add.33), channel_id=1, source_target_pairs={{0,8},{1,9},{2,10},{3,11},{4,12},{5,13},{6,14},{7,15},{8,0},{9,1},... | collective-permute-start | bytes 12296 | tf_op jit(solution)/shard_map/ppermute | solution.py:60
  62.0 3.6 %collective-permute-start.16 = (f32[8,128]{1,0:T(8,128)S(1)}, f32[8,128]{1,0:T(8,128)S(1)}, u32[]{:S(2)}, u32[]{:S(2)}) collective-permute-start(f32[8,128]{1,0:T(8,128)S(1)} %add.33), channel_id=1, source_target_pairs={{0,4},{1,5},{2,6},{3,7},{4,0},{5,1},{6,2},{7,3},{8,12},{9,13},{10,... | collective-permute-start | bytes 12296 | tf_op jit(solution)/shard_map/ppermute | solution.py:60
  71.8 4.2 %collective-permute-start.19 = (f32[2,2,8,384]{3,2,1,0:T(8,128)S(1)}, f32[2,2,8,384]{3,2,1,0:T(8,128)S(1)}, u32[]{:S(2)}, u32[]{:S(2)}) collective-permute-start(f32[2,2,8,384]{3,2,1,0:T(8,128)S(1)} %densities.3), channel_id=1, source_target_pairs={{0,2},{2,0},{4,6},{6,4},{8,10},{10,8},{12,14},{14,12},{1,3},{3,1},... | collective-permute-start | bytes 147464 | tf_op jit(solution)/shard_map/ppermute | solution.py:36
